TPU v7x, 32 devices: a whole 2x2x4 slice. The times are simulated.
32 devices in a mesh: dp: 4 (over z), row: 4 (over y, core), col: 2 (over x).
Axes of the slice: x: 2, y: 2, z: 4, core: 2. Of those that a mesh axis runs over, the one named last changes fastest.
Arguments:
- tokens: bfloat16 [20480, 1024], P(('dp', 'row'), 'col'), may hold values from -6 to 6
- segments: int32 [20480], P('dp'), may hold values from 0 to 159, never falling along the last dimension, each value on 1 to 512 neighbouring positions
- qkv_weight: bfloat16 [1024, 3072], P('col', 'row'), may hold values from -0.1875 to 0.1875
- qv_bias: float32 [16, 128], P(('row', 'col')), may hold values from -6 to 6
- out_weight: bfloat16 [1024, 1024], P('row', 'col'), may hold values from -1.5 to 1.5
- out_bias: float32 [1024], P('col'), may hold values from -6 to 6
- ln1_gain: float32 [1024], P('col'), may hold values from 0.25 to 1.75
- ln1_bias: float32 [1024], P('col'), may hold values from -6 to 6
- ff_in_weight: bfloat16 [1024, 4096], P('col', 'row'), may hold values from -0.1875 to 0.1875
- ff_in_bias: float32 [4096], P(('row', 'col')), may hold values from -6 to 6
- ff_out_weight: bfloat16 [4096, 1024], P('row', 'col'), may hold values from -0.09375 to 0.09375
- ff_out_bias: float32 [1024], P('col'), may hold values from -6 to 6
- ln2_gain: float32 [1024], P('col'), may hold values from 0.25 to 1.75
- ln2_bias: float32 [1024], P('col'), may hold values from -6 to 6
- out_grad: bfloat16 [20480, 1024], P(('dp', 'row'), 'col'), may hold values from -6 to 6
Outputs:
- layer_out: float32 [20480, 1024], P(('dp', 'row'), 'col')
- input_grad: float32 [20480, 1024], P(('dp', 'row'), 'col')
- qkv_weight_grad: float32 [1024, 3072], P('col', 'row')
- qv_bias_grad: float32 [16, 128], P(('row', 'col'))
- out_weight_grad: float32 [1024, 1024], P('row', 'col')
- out_bias_grad: float32 [1024], P('col')
- ln1_gain_grad: float32 [1024], P('col')
- ln1_bias_grad: float32 [1024], P('col')
- ff_in_weight_grad: float32 [1024, 4096], P('col', 'row')
- ff_in_bias_grad: float32 [4096], P(('row', 'col'))
- ff_out_weight_grad: float32 [4096, 1024], P('row', 'col')
- ff_out_bias_grad: float32 [1024], P('col')
- ln2_gain_grad: float32 [1024], P('col')
- ln2_bias_grad: float32 [1024], P('col')
Inputs may be any that keep to these rules, and one draw needn't show every extreme that they name: `segments`: segment numbers never fall along the tokens; one segment holds at most 512 tokens.
All inputs are finite; a program needn't handle non-finite values.
Results may differ from a plain program's by a relative error of at most 0.02.
Values may be sent and summed in bfloat16 or wider, within the bound.
No kernel may reach another device: no remote copies, remote signals or barrier semaphores. Data moves between devices by JAX's collectives and lax.ppermute only.
A program may use at most 192 MiB of HBM per device.

v0:
```python
import math

import jax
import jax.numpy as jnp
from jax import lax
from jax.sharding import PartitionSpec as P

D = 1024
HD = 64
SEQ = 512


EPSILON = 1e-06
NEGATIVE = -1e30
ROWS_FIRST = (((0,), (0,)), ((), ()))
PLAIN = (((1,), (0,)), ((), ()))
TRANSPOSED = (((1,), (1,)), ((), ()))


def matmul(left, right, contract):
    return lax.dot_general(left, right, contract, preferred_element_type=jnp.float32)


def gelu_exact(value):
    return jax.nn.gelu(value, approximate=False)


def gather_rows(value):
    return lax.all_gather(value, "row", axis=0, tiled=True)


def gather_cols(value):
    return lax.all_gather(value, "col", axis=1, tiled=True)


def project_cols(rows_value, weight, upward):
    whole = lax.all_gather(rows_value, "col", axis=1, tiled=True)
    if upward:
        block = lax.all_to_all(weight, "col", split_axis=1, concat_axis=0, tiled=True)
        return matmul(whole, block, PLAIN)
    block = lax.all_to_all(weight, "col", split_axis=0, concat_axis=1, tiled=True)
    return matmul(whole, block, TRANSPOSED)


def sum_rows(whole, weight, contract):
    return lax.psum_scatter(
        matmul(whole, weight, contract).astype(jnp.bfloat16), "row", scatter_dimension=0, tiled=True
    ).astype(jnp.float32)


def row_totals(first, second):
    return lax.psum((first, second), "col")


def norm_forward(value, gain, bias):
    total, squares = row_totals(
        jnp.sum(value, 1, keepdims=True), jnp.sum(value * value, 1, keepdims=True)
    )
    center = total / D
    inverse = lax.rsqrt(squares / D - center * center + EPSILON)
    unit = (value - center) * inverse
    return (unit * gain + bias, unit, inverse)


def norm_backward(grad, unit, inverse, gain):
    scaled = grad * gain
    total, paired = row_totals(
        jnp.sum(scaled, 1, keepdims=True), jnp.sum(scaled * unit, 1, keepdims=True)
    )
    back = inverse * (scaled - total / D - unit * (paired / D))
    return (back, jnp.sum(grad * unit, 0), jnp.sum(grad, 0))


def to_blocks(qkv_low, segments):
    count = qkv_low.shape[0]
    local_heads = qkv_low.shape[1] // (3 * HD)
    blocks = qkv_low.reshape(count // SEQ, SEQ, local_heads, 3, HD)
    return (blocks, segments.reshape(count // SEQ, SEQ), local_heads)


def scores_for(block, labels):
    scores = jnp.einsum(
        "qhd,khd->hqk", block[:, :, 0], block[:, :, 1], preferred_element_type=jnp.float32
    ) / math.sqrt(HD)
    same_doc = labels[:, None] == labels[None, :]
    return jnp.where(same_doc[None], scores, NEGATIVE)


def attention_forward(qkv_low, segments):
    blocks, labels, local_heads = to_blocks(qkv_low, segments)

    def one_sequence(item):
        block, marks = item
        scores = scores_for(block, marks)
        highest = jnp.max(scores, 2, keepdims=True)
        powers = jnp.exp(scores - highest)
        total = jnp.sum(powers, 2, keepdims=True)
        probs = (powers / total).astype(jnp.bfloat16)
        mixed = jnp.einsum(
            "hqk,khd->qhd", probs, block[:, :, 2], preferred_element_type=jnp.float32
        )
        return (mixed.astype(jnp.bfloat16), highest[:, :, 0] + jnp.log(total[:, :, 0]))

    mixed, log_totals = lax.map(one_sequence, (blocks, labels))
    return (mixed.reshape(qkv_low.shape[0], local_heads * HD), log_totals)


def attention_backward(qkv_low, segments, log_totals, grad_heads):
    blocks, labels, local_heads = to_blocks(qkv_low, segments)
    grad_blocks = grad_heads.reshape(blocks.shape[0], SEQ, local_heads, HD)

    def one_sequence(item):
        block, marks, log_block, grad_block = item
        scores = scores_for(block, marks)
        weights = jnp.exp(scores - log_block[:, :, None])
        probs = weights.astype(jnp.bfloat16)
        d_value = jnp.einsum("hqk,qhd->khd", probs, grad_block, preferred_element_type=jnp.float32)
        d_probs = jnp.einsum(
            "qhd,khd->hqk", grad_block, block[:, :, 2], preferred_element_type=jnp.float32
        )
        delta = jnp.sum(weights * d_probs, 2, keepdims=True)
        d_scores = (weights * (d_probs - delta)).astype(jnp.bfloat16)
        d_query = jnp.einsum(
            "hqk,khd->qhd", d_scores, block[:, :, 1], preferred_element_type=jnp.float32
        ) / math.sqrt(HD)
        d_key = jnp.einsum(
            "hqk,qhd->khd", d_scores, block[:, :, 0], preferred_element_type=jnp.float32
        ) / math.sqrt(HD)
        return jnp.stack([d_query, d_key, d_value], 2).astype(jnp.bfloat16)

    d_qkv = lax.map(one_sequence, (blocks, labels, log_totals, grad_blocks))
    return d_qkv.reshape(qkv_low.shape[0], local_heads * 3 * HD)


def local(
    tokens,
    segments,
    qkv_weight,
    qv_bias,
    out_weight,
    out_bias,
    ln1_gain,
    ln1_bias,
    ff_in_weight,
    ff_in_bias,
    ff_out_weight,
    ff_out_bias,
    ln2_gain,
    ln2_bias,
    out_grad,
):
    local_heads = qv_bias.shape[0]
    hollow = jnp.zeros((local_heads, 1, HD), jnp.float32)
    full_bias = jnp.concatenate([qv_bias[:, None, :HD], hollow, qv_bias[:, None, HD:]], 1).reshape(
        -1
    )
    rows_tokens = gather_rows(tokens)
    qkv_low = (project_cols(rows_tokens, qkv_weight, True) + full_bias).astype(jnp.bfloat16)
    heads, log_totals = attention_forward(qkv_low, segments)
    cols_heads = gather_cols(heads)
    branch_one = sum_rows(cols_heads, out_weight, PLAIN) + out_bias
    middle, unit_one, inverse_one = norm_forward(
        tokens.astype(jnp.float32) + branch_one, ln1_gain, ln1_bias
    )
    rows_middle = gather_rows(middle.astype(jnp.bfloat16))
    hidden = project_cols(rows_middle, ff_in_weight, True) + ff_in_bias
    gelu_value, pullback = jax.vjp(gelu_exact, hidden)
    active = gelu_value.astype(jnp.bfloat16)
    cols_active = gather_cols(active)
    branch_two = sum_rows(cols_active, ff_out_weight, PLAIN) + ff_out_bias
    layer_out, unit_two, inverse_two = norm_forward(middle + branch_two, ln2_gain, ln2_bias)
    back_two, ln2_gain_part, ln2_bias_part = norm_backward(
        out_grad.astype(jnp.float32), unit_two, inverse_two, ln2_gain
    )
    d_two = back_two.astype(jnp.bfloat16)
    ff_out_bias_part = jnp.sum(d_two, 0, dtype=jnp.float32)
    rows_two = gather_rows(d_two)
    ff_out_weight_part = matmul(cols_active, rows_two, ROWS_FIRST)
    d_active = project_cols(rows_two, ff_out_weight, False)
    d_hidden = pullback(d_active)[0].astype(jnp.bfloat16)
    ff_in_bias_part = jnp.sum(d_hidden, 0, dtype=jnp.float32)
    cols_hidden = gather_cols(d_hidden)
    ff_in_weight_part = matmul(rows_middle, cols_hidden, ROWS_FIRST)
    back_middle = back_two + sum_rows(cols_hidden, ff_in_weight, TRANSPOSED)
    ff_weights = (ff_in_weight_part, ff_in_bias_part, ff_out_weight_part)
    ff_vectors = (ff_out_bias_part, ln2_gain_part, ln2_bias_part)
    back_one, ln1_gain_part, ln1_bias_part = norm_backward(
        back_middle, unit_one, inverse_one, ln1_gain
    )
    d_one = back_one.astype(jnp.bfloat16)
    out_bias_part = jnp.sum(d_one, 0, dtype=jnp.float32)
    rows_one = gather_rows(d_one)
    out_weight_part = matmul(cols_heads, rows_one, ROWS_FIRST)
    d_heads = project_cols(rows_one, out_weight, False).astype(jnp.bfloat16)
    d_qkv = attention_backward(qkv_low, segments, log_totals, d_heads)
    column_sums = jnp.sum(d_qkv, 0, dtype=jnp.float32).reshape(local_heads, 3, HD)
    qv_bias_part = jnp.concatenate([column_sums[:, 0], column_sums[:, 2]], 1)
    cols_qkv = gather_cols(d_qkv)
    qkv_weight_part = matmul(rows_tokens, cols_qkv, ROWS_FIRST)
    input_grad = back_one + sum_rows(cols_qkv, qkv_weight, TRANSPOSED)
    summed_weights = (
        lax.psum(qkv_weight_part.astype(jnp.bfloat16), "dp").astype(jnp.float32),
        lax.psum(qv_bias_part.astype(jnp.bfloat16), "dp").astype(jnp.float32),
        lax.psum(out_weight_part.astype(jnp.bfloat16), "dp").astype(jnp.float32),
        lax.psum(ff_weights[0].astype(jnp.bfloat16), "dp").astype(jnp.float32),
        lax.psum(ff_weights[1].astype(jnp.bfloat16), "dp").astype(jnp.float32),
        lax.psum(ff_weights[2].astype(jnp.bfloat16), "dp").astype(jnp.float32),
    )
    summed_vectors = lax.psum(
        (out_bias_part, ln1_gain_part, ln1_bias_part, ff_vectors[0], ff_vectors[1], ff_vectors[2]),
        ("dp", "row"),
    )
    attn_weights = summed_weights[:3]
    ff_weights = summed_weights[3:]
    attn_vectors = summed_vectors[:3]
    ff_vectors = summed_vectors[3:]
    return (
        layer_out,
        input_grad,
        attn_weights[0],
        attn_weights[1],
        attn_weights[2],
        attn_vectors[0],
        attn_vectors[1],
        attn_vectors[2],
        ff_weights[0],
        ff_weights[1],
        ff_weights[2],
        ff_vectors[0],
        ff_vectors[1],
        ff_vectors[2],
    )


def solution(mesh):
    in_specs = (
        P(("dp", "row"), "col"),
        P("dp"),
        P("col", "row"),
        P(("row", "col"), None),
        P("row", "col"),
        P("col"),
        P("col"),
        P("col"),
        P("col", "row"),
        P(("row", "col")),
        P("row", "col"),
        P("col"),
        P("col"),
        P("col"),
        P(("dp", "row"), "col"),
    )
    out_specs = (
        P(("dp", "row"), "col"),
        P(("dp", "row"), "col"),
        P("col", "row"),
        P(("row", "col"), None),
        P("row", "col"),
        P("col"),
        P("col"),
        P("col"),
        P("col", "row"),
        P(("row", "col")),
        P("row", "col"),
        P("col"),
        P("col"),
        P("col"),
    )
    return jax.shard_map(local, mesh=mesh, in_specs=in_specs, out_specs=out_specs, check_vma=False)
```

profile of v0, /device:TPU:0, one launch (start us, length us, event | category | flops | bytes accessed | tf_op | source)
XLA Modules:
  0.0 1772.8 jit_solution(9874035962422532805)
XLA Ops:
  8.0 44.8 %all-gather.13.cloned.1.call-done = bf16[5120,512]{1,0:T(8,128)(2,1)} async-done(((bf16[1280,512]{1,0:T(8,128)(2,1)}), bf16[5120,512]{1,0:T(8,128)(2,1)}) %all-gather.13.cloned.1.call-update) | async-done | bytes 5242896 | tf_op jit(solution)/shard_map/all_gather | solution.py:29
  59.0 11.1 all-to-all-done
  70.4 113.4 %all-gather.15.cloned.1.call-done = bf16[5120,1024]{1,0:T(8,128)(2,1)} async-done(((bf16[5120,512]{1,0:T(8,128)(2,1)}), bf16[5120,1024]{1,0:T(8,128)(2,1)}) %all-gather.15.cloned.1.call-update) | async-done | bytes 10485776 | tf_op jit(solution)/shard_map/all_gather | solution.py:37
  183.8 10.9 add_convert_fusion.1
  194.8 19.6 %reshape.205 = bf16[10,512,2,3,64]{4,3,2,1,0:T(4,128)(2,1)} reshape(bf16[5120,384]{1,0:T(8,128)(2,1)} %add_convert_fusion.1) | data formatting | bytes 7864320 | tf_op jit(solution)/shard_map/reshape | solution.py:77
  214.4 12.8 copy.58
  227.2 37.6 %while.22 = (s32[]{:T(128)}, bf16[10,512,2,64]{1,3,2,0:T(8,128)(2,1)S(1)}, f32[10,2,512]{2,1,0:T(2,128)}, bf16[10,512,2,3,64]{1,4,2,3,0:T(8,128)(2,1)}, s32[10,512]{1,0:T(8,128)S(1)}, /*index=5*/s32[]{:T(128)}) while((s32[]{:T(128)}, bf16[10,512,2,64]{1,3,2,0:T(8,128)(2,1)S(1)}, f32[10,2,512]{2,1,0:T(2,128)}, ...), condition=%wide.region_3.4_spmd, body=%wide.region_0.3_spmd.sunk | while | flops 140835840 | bytes 8689757 | solution.py:104
  267.6 39.1 %all-gather.17.cloned.1.call-done = bf16[5120,256]{0,1:T(8,128)(2,1)} async-done(((bf16[5120,128]{0,1:T(8,128)(2,1)}), bf16[5120,256]{0,1:T(8,128)(2,1)}) %all-gather.17.cloned.1.call-update) | async-done | bytes 2621456 | tf_op jit(solution)/shard_map/all_gather | solution.py:33
  306.7 5.6 convolution_convert_fusion.2
  312.5 51.5 %reduce-scatter.5.cloned.1.call-done = bf16[1280,512]{1,0:T(8,128)(2,1)} async-done(((bf16[5120,512]{1,0:T(8,128)(2,1)}), bf16[1280,512]{1,0:T(8,128)(2,1)}) %reduce-scatter.5.cloned.1.call-update) | async-done | bytes 1310736 | tf_op jit(solution)/shard_map/reduce_scatter | solution.py:46
  366.1 8.2 all-reduce.4
  376.2 39.7 %all-gather.19.cloned.1.call-done = bf16[5120,512]{1,0:T(8,128)(2,1)} async-done(((bf16[1280,512]{1,0:T(8,128)(2,1)}), bf16[5120,512]{1,0:T(8,128)(2,1)}) %all-gather.19.cloned.1.call-update) | async-done | bytes 5242896 | tf_op jit(solution)/shard_map/all_gather | solution.py:29
  418.2 22.1 %all_to_all.76 = bf16[512,2,512]{0,2,1:T(8,128)(2,1)} all-to-all(bf16[512,2,512]{0,2,1:T(8,128)(2,1)} %bitcast.169), channel_id=1, replica_groups=mesh['dp'=4,'row'=4,'col'=2] {'col'}, dimensions={1} | all-to-all | bytes 2097152 | tf_op jit(solution)/shard_map/all_to_all | solution.py:39
  442.6 107.0 %all-gather.21.cloned.1.call-done = bf16[5120,1024]{1,0:T(8,128)(2,1)} async-done(((bf16[5120,512]{1,0:T(8,128)(2,1)}), bf16[5120,1024]{1,0:T(8,128)(2,1)}) %all-gather.21.cloned.1.call-update) | async-done | bytes 10485776 | tf_op jit(solution)/shard_map/all_gather | solution.py:37
  549.6 31.6 %multiply_convert_fusion.1 = (bf16[5120,512]{1,0:T(8,128)(2,1)}, f32[5120,512]{1,0:T(8,128)}, f32[5120,512]{1,0:T(8,128)}) fusion(f32[512]{0:T(512)S(1)} %copy-done.16, bf16[5120,1024]{1,0:T(8,128)(2,1)} %all-gather.21.cloned.1.call-done, bf16[1024,512]{1,0:T(8,128)(2,1)} %bitcast.174), kind=kOutput, calls=%fused_computation.49 | convolution fusion | flops 5541724160 | bytes 37750784 | tf_op jit(solution)/shard_map/dot_general | solution.py:21
  581.3 128.7 %all-gather.23.cloned.1.call-done = bf16[5120,1024]{1,0:T(8,128)(2,1)} async-done(((bf16[5120,512]{1,0:T(8,128)(2,1)}), bf16[5120,1024]{1,0:T(8,128)(2,1)}) %all-gather.23.cloned.1.call-update) | async-done | bytes 10485776 | tf_op jit(solution)/shard_map/all_gather | solution.py:33
  710.0 10.0 convolution_convert_fusion.5
  720.1 51.5 %reduce-scatter.7.cloned.1.call-done = bf16[1280,512]{1,0:T(8,128)(2,1)} async-done(((bf16[5120,512]{1,0:T(8,128)(2,1)}), bf16[1280,512]{1,0:T(8,128)(2,1)}) %reduce-scatter.7.cloned.1.call-update) | async-done | bytes 1310736 | tf_op jit(solution)/shard_map/reduce_scatter | solution.py:46
  775.3 8.1 all-reduce.3
  786.4 7.2 all-reduce.2
  793.6 5.0 convert_reduce_fusion.1
  798.6 40.5 %all-gather.25.cloned.1.call-done = bf16[5120,512]{1,0:T(8,128)(2,1)} async-done(((bf16[1280,512]{1,0:T(8,128)(2,1)}), bf16[5120,512]{1,0:T(8,128)(2,1)}) %all-gather.25.cloned.1.call-update) | async-done | bytes 5242896 | tf_op jit(solution)/shard_map/all_gather | solution.py:29
  839.2 20.4 %all_to_all.77 = bf16[2,512,512]{2,1,0:T(8,128)(2,1)} all-to-all(bf16[2,512,512]{2,1,0:T(8,128)(2,1)} %bitcast.172), channel_id=1, replica_groups=mesh['dp'=4,'row'=4,'col'=2] {'col'}, dimensions={0} | all-to-all | bytes 2097152 | tf_op jit(solution)/shard_map/all_to_all | solution.py:41
  862.0 108.9 %all-gather.27.cloned.1.call-done = bf16[5120,1024]{1,0:T(8,128)(2,1)} async-done(((bf16[5120,512]{1,0:T(8,128)(2,1)}), bf16[5120,1024]{1,0:T(8,128)(2,1)}) %all-gather.27.cloned.1.call-update) | async-done | bytes 10485776 | tf_op jit(solution)/shard_map/all_gather | solution.py:37
  970.8 18.7 %fusion.40 = (bf16[512]{0:T(512)(128)(2,1)S(1)}, bf16[5120,512]{1,0:T(8,128)(2,1)}) fusion(f32[5120,512]{1,0:T(8,128)} %get-tuple-element.220, f32[5120,512]{1,0:T(8,128)} %get-tuple-element.230, f32[512]{0:T(512)S(1)} %copy-done.16, bf16[5120,1024]{1,0:T(8,128)(2,1)} %all-gather.27.cloned.1.call-done, bf16[512,1024]{0,1:T(8,128)(2,1)} %bitcast.173), kind=kOutput, calls=%fused_computation.118 | convolution fusion | flops 5410651648 | bytes 37751808 | tf_op jit(solution)/shard_map/dot_general | solution.py:21
  989.6 128.9 %all-gather.29.cloned.1.call-done = bf16[5120,1024]{1,0:T(8,128)(2,1)} async-done(((bf16[5120,512]{1,0:T(8,128)(2,1)}), bf16[5120,1024]{1,0:T(8,128)(2,1)}) %all-gather.29.cloned.1.call-update) | async-done | bytes 10485776 | tf_op jit(solution)/shard_map/all_gather | solution.py:33
  1118.5 10.2 convolution_convert_fusion.4
  1128.8 51.5 %reduce-scatter.9.cloned.1.call-done = bf16[1280,512]{1,0:T(8,128)(2,1)} async-done(((bf16[5120,512]{1,0:T(8,128)(2,1)}), bf16[1280,512]{1,0:T(8,128)(2,1)}) %reduce-scatter.9.cloned.1.call-update) | async-done | bytes 1310736 | tf_op jit(solution)/shard_map/reduce_scatter | solution.py:46
  1183.7 8.1 all-reduce.1
  1191.8 4.2 convert_reduce_fusion.2
  1196.1 39.6 %all-gather.31.cloned.1.call-done = bf16[5120,512]{1,0:T(8,128)(2,1)} async-done(((bf16[1280,512]{1,0:T(8,128)(2,1)}), bf16[5120,512]{1,0:T(8,128)(2,1)}) %all-gather.31.cloned.1.call-update) | async-done | bytes 5242896 | tf_op jit(solution)/shard_map/all_gather | solution.py:29
  1239.3 5.8 all-to-all-done.3
  1245.2 121.5 %all-gather.33.cloned.1.call-done = bf16[5120,1024]{1,0:T(8,128)(2,1)} async-done(((bf16[5120,512]{1,0:T(8,128)(2,1)}), bf16[5120,1024]{1,0:T(8,128)(2,1)}) %all-gather.33.cloned.1.call-update) | async-done | bytes 10485776 | tf_op jit(solution)/shard_map/all_gather | solution.py:37
  1366.8 7.9 convolution_convert_fusion.6
  1374.7 4.7 reshape.204
  1383.0 84.4 %while.23 = (s32[]{:T(128)}, bf16[10,512,2,3,64]{1,4,2,3,0:T(8,128)(2,1)}, bf16[10,512,2,3,64]{1,4,2,3,0:T(8,128)(2,1)}, s32[10,512]{1,0:T(8,128)}, f32[10,2,512...) while((s32[]{:T(128)}, bf16[10,512,2,3,64]{1,4,2,3,0:T(8,128)(2,1)}, ...), condition=%wide.region_25.26_spmd, body=%wide.region_23.25_spmd.sunk | while | flops 342031360 | bytes 19163244 | solution.py:131
  1467.4 4.8 copy.67
  1472.2 6.5 copy.78
  1478.8 10.9 convolution_convert_fusion.7
  1489.6 11.8 convolution_convert_fusion.8
  1501.4 4.8 convolution_convert_fusion.10
  1506.2 70.8 %all-gather.35.cloned.1.call-done = bf16[5120,768]{0,1:T(8,128)(2,1)} async-done(((bf16[5120,384]{0,1:T(8,128)(2,1)}), bf16[5120,768]{0,1:T(8,128)(2,1)}) %all-gather.35.cloned.1.call-update) | async-done | bytes 7864336 | tf_op jit(solution)/shard_map/all_gather | solution.py:33
  1577.0 9.8 fusion.36
  1587.9 9.3 convolution_convert_fusion.3
  1597.2 65.1 %all-reduce = (f32[512]{0:T(512)}, f32[512]{0:T(512)}, f32[512]{0:T(512)}, f32[512]{0:T(512)}, f32[512]{0:T(512)}, /*index=5*/f32[512]{0:T(512)}) all-reduce(f32[512]{0:T(512)S(1)} %get-tuple-element.213, f32[512]{0:T(512)S(1)} %get-tuple-element.152, ...), channel_id=1, replica_groups=mesh['dp'=4,'row'=4,'col'=2] {'dp','row'}, use_global_device_ids=true, to_apply=%region_32.33 | all-reduce | flops 3072 | bytes 24576 | tf_op jit(solution)/shard_map/psum | solution.py:209
  1665.2 8.7 all-reduce.5
  1675.0 34.8 %all-reduce.9.cloned.1.call-done = (bf16[512,768]{0,1:T(8,128)(2,1)}, bf16[256,512]{1,0:T(8,128)(2,1)}, bf16[512,1024]{1,0:T(8,128)(2,1)}, bf16[1024,512]{1,0:T(8,128)(2,1)}) async-done(((bf16[512,768]{0,1:T(8,128)(2,1)}, bf16[256,512]{1,0:T(8,128)(2,1)}, bf16[512,1024]{1,0:T(8,128)(2,1)}, bf16[1024,512]{1,0:T(8,128)(2,1)}), (bf16[512,768]{0,1:T(8,128)(2,1)}, bf16[256,512]{1,0:T(8,128)(2,1)}, ...) | async-done | bytes 3145744 | tf_op jit(solution)/shard_map/psum | solution.py:202
  1718.8 44.0 %reduce-scatter.11.cloned.1.call-done = bf16[1280,512]{1,0:T(8,128)(2,1)} async-done(((bf16[5120,512]{1,0:T(8,128)(2,1)}), bf16[1280,512]{1,0:T(8,128)(2,1)}) %reduce-scatter.11.cloned.1.call-update) | async-done | bytes 1310736 | tf_op jit(solution)/shard_map/reduce_scatter | solution.py:46
  (296 shorter events, 177.7 us)
Async XLA Ops:
  7.2 45.6 %all-gather.13.cloned.1.call-start = ((), (), s32[]{:S(2)}) async-start(), calls=%async_computation.8 | async-start | bytes 6553600 | tf_op jit(solution)/shard_map/all_gather | solution.py:29
  7.9 175.9 %all-gather.15.cloned.1.call-start = ((), (), s32[]{:S(2)}) async-start(), calls=%async_computation.9 | async-start | bytes 15728640 | tf_op jit(solution)/shard_map/all_gather | solution.py:37
  52.7 1.1 copy-start.5
  53.9 4.9 copy-start.13
  53.9 5.1 copy-start.10
  55.0 15.0 all-to-all-start
  58.6 248.2 %all-gather.17.cloned.1.call-start = ((), (), s32[]{:S(2)}) async-start(), calls=%async_computation.10 | async-start | bytes 3932160 | tf_op jit(solution)/shard_map/all_gather | solution.py:33
  264.8 2.7 copy-start.7
  267.6 96.4 %reduce-scatter.5.cloned.1.call-start = ((), (), s32[]{:S(2)}) async-start(), calls=%async_computation.11 | async-start | bytes 6553600 | tf_op jit(solution)/shard_map/reduce_scatter | solution.py:46
  312.4 51.6 %copy-start = (bf16[1280,512]{1,0:T(8,128)(2,1)S(1)}, bf16[1280,512]{1,0:T(8,128)(2,1)}, u32[]{:S(2)}) copy-start(bf16[1280,512]{1,0:T(8,128)(2,1)} %param.19) | copy-start | bytes 3932164
  312.4 51.6 %copy-start.8 = (f32[512]{0:T(512)S(1)}, f32[512]{0:T(512)}, u32[]{:S(2)}) copy-start(f32[512]{0:T(512)} %param.24) | copy-start | bytes 6148
  312.4 62.0 %copy-start.9 = (f32[512]{0:T(512)S(1)}, f32[512]{0:T(512)}, u32[]{:S(2)}) copy-start(f32[512]{0:T(512)} %param.25) | copy-start | bytes 6148
  312.4 61.9 %copy-start.11 = (f32[512]{0:T(512)S(1)}, f32[512]{0:T(512)}, u32[]{:S(2)}) copy-start(f32[512]{0:T(512)} %param.26) | copy-start | bytes 6148
  312.4 103.5 %all-gather.19.cloned.1.call-start = ((), (), s32[]{:S(2)}) async-start(), calls=%async_computation.12 | async-start | bytes 6553600 | tf_op jit(solution)/shard_map/all_gather | solution.py:29
  363.9 10.4 copy-start.1
  376.2 173.4 %all-gather.21.cloned.1.call-start = ((), (), s32[]{:S(2)}) async-start(), calls=%async_computation.13 | async-start | bytes 15728640 | tf_op jit(solution)/shard_map/all_gather | solution.py:37
  415.9 294.1 %all-gather.23.cloned.1.call-start = ((), (), s32[]{:S(2)}) async-start(), calls=%async_computation.14 | async-start | bytes 15728640 | tf_op jit(solution)/shard_map/all_gather | solution.py:33
  418.2 131.4 %copy-start.16 = (f32[512]{0:T(512)S(1)}, f32[512]{0:T(512)}, u32[]{:S(2)}) copy-start(f32[512]{0:T(512)} %param.28) | copy-start | bytes 6148
  581.2 190.4 %reduce-scatter.7.cloned.1.call-start = ((), (), s32[]{:S(2)}) async-start(), calls=%async_computation.15 | async-start | bytes 6553600 | tf_op jit(solution)/shard_map/reduce_scatter | solution.py:46
  720.0 51.6 %copy-start.14 = (f32[512]{0:T(512)S(1)}, f32[512]{0:T(512)}, u32[]{:S(2)}) copy-start(f32[512]{0:T(512)} %param.30) | copy-start | bytes 6148
  720.0 63.4 %copy-start.12 = (f32[512]{0:T(512)S(1)}, f32[512]{0:T(512)}, u32[]{:S(2)}) copy-start(f32[512]{0:T(512)} %param.31) | copy-start | bytes 6148
  720.1 119.1 %all-gather.25.cloned.1.call-start = ((), (), s32[]{:S(2)}) async-start(), calls=%async_computation.16 | async-start | bytes 6553600 | tf_op jit(solution)/shard_map/all_gather | solution.py:29
  775.3 18.3 %copy-start.15 = (f32[512]{0:T(512)S(1)}, f32[512]{0:T(512)}, u32[]{:S(2)}) copy-start(f32[512]{0:T(512)} %param.32) | copy-start | bytes 6148
  798.6 172.3 %all-gather.27.cloned.1.call-start = ((), (), s32[]{:S(2)}) async-start(), calls=%async_computation.17 | async-start | bytes 15728640 | tf_op jit(solution)/shard_map/all_gather | solution.py:37
  839.2 279.3 %all-gather.29.cloned.1.call-start = ((), (), s32[]{:S(2)}) async-start(), calls=%async_computation.18 | async-start | bytes 15728640 | tf_op jit(solution)/shard_map/all_gather | solution.py:33
  989.6 190.7 %reduce-scatter.9.cloned.1.call-start = ((), (), s32[]{:S(2)}) async-start(), calls=%async_computation.19 | async-start | bytes 6553600 | tf_op jit(solution)/shard_map/reduce_scatter | solution.py:46
  1128.7 107.0 %all-gather.31.cloned.1.call-start = ((), (), s32[]{:S(2)}) async-start(), calls=%async_computation.20 | async-start | bytes 6553600 | tf_op jit(solution)/shard_map/all_gather | solution.py:29
  1196.0 170.7 %all-gather.33.cloned.1.call-start = ((), (), s32[]{:S(2)}) async-start(), calls=%async_computation.21 | async-start | bytes 15728640 | tf_op jit(solution)/shard_map/all_gather | solution.py:37
  1235.7 9.3 all-to-all-start.3
  1239.2 337.7 %all-gather.35.cloned.1.call-start = ((), (), s32[]{:S(2)}) async-start(), calls=%async_computation.22 | async-start | bytes 11796480 | tf_op jit(solution)/shard_map/all_gather | solution.py:33
  1478.7 231.1 %all-reduce.9.cloned.1.call-start = ((), (), s32[]{:S(2)}) async-start(), calls=%async_computation.24 | async-start | bytes 6291456 | tf_op jit(solution)/shard_map/psum | solution.py:202
  1489.6 11.8 copy-start.3
  1586.8 1.1 copy-start.6
  1586.8 176.0 %reduce-scatter.11.cloned.1.call-start = ((), (), s32[]{:S(2)}) async-start(), calls=%async_computation.23 | async-start | bytes 6553600 | tf_op jit(solution)/shard_map/reduce_scatter | solution.py:46
  1714.2 3.0 copy-start.4
  1714.2 48.6 %copy-start.2 = (f32[1280,512]{1,0:T(8,128)S(1)}, f32[1280,512]{1,0:T(8,128)}, u32[]{:S(2)}) copy-start(f32[1280,512]{1,0:T(8,128)} %get-tuple-element.215) | copy-start | bytes 7864324
Sparse Core Ops, SparseCore 0:
  9.6 43.1 all-gather.12
  54.3 129.4 all-gather.14
  267.7 39.0 all-gather.16
  312.5 51.3 reduce-scatter.4
  376.3 39.5 all-gather.18
  417.4 132.1 all-gather.20
  581.3 128.5 all-gather.22
  720.2 51.3 reduce-scatter.6
  798.7 40.4 all-gather.24
  840.6 130.2 all-gather.26
  989.7 128.7 all-gather.28
  1128.8 51.3 reduce-scatter.8
  1196.1 39.5 all-gather.30
  1237.2 129.4 all-gather.32
  1478.8 98.0 all-gather.34
  1586.9 122.8 all-reduce.8
  1712.4 50.4 reduce-scatter.10
where the time goes:
time: 1780 us; the launch traced here: 1770 us
  waiting for transfers between devices  1230 us (69%)
  matrix products  199 us (11%)
  blocking collectives  148 us (8%)
  local copies, waits for them, and re-layouts  103 us (6%)
  other arithmetic  65.8 us (4%)
    all_gather x4, waiting for transfers between devices, project_cols(): whole = lax.all_gather(rows_value, 'col', axis=1, tiled=True)  451 us
    all_gather x4, waiting for transfers between devices, gather_cols(): return lax.all_gather(value, 'col', axis=1, tiled=True)  367 us
    reduce_scatter x4, waiting for transfers between devices, sum_rows(): lax.psum_scatter(matmul(whole, weight, contract).astype(jnp.bfloat16), 'r...  198 us
    all_gather x4, waiting for transfers between devices, gather_rows(): return lax.all_gather(value, 'row', axis=0, tiled=True)  165 us
    dot_general x12, matrix products, matmul(): lax.dot_general(left, right, contract, preferred_element_type=jnp.float32)  142 us
    psum x1, blocking collectives, local(): lax.psum((out_bias_part, ln1_gain_part, ln1_bias_part, ff_vectors[0], ff_...  65.1 us
  transfers between devices with their start and end apart: 19, of which 19 were waited for; matrix products, arithmetic and copies ran while one was open for 3% of the time, Pallas kernels for 0%

commit v1 on v0

v1 whole, which is shorter than its diff:
```python
import math

import jax
import jax.numpy as jnp
from jax import lax
from jax.experimental import pallas as pl
from jax.experimental.pallas import tpu as pltpu
from jax.sharding import PartitionSpec as P

D = 1024
HD = 64
SEQ = 512
QUARTER = SEQ // 4
GRID = ("row", "col")

EPSILON = 1e-06
NEGATIVE = -1e30
F32 = jnp.float32
BF16 = jnp.bfloat16
NN = (((1,), (0,)), ((), ()))
NT = (((1,), (1,)), ((), ()))
TN = (((0,), (0,)), ((), ()))
MIB = 1 << 20


def mm(left, right, contract):
    return lax.dot_general(left, right, contract, preferred_element_type=F32)


def attend_kernel(qkv_ref, column_ref, line_ref, heads_ref, probs_ref, mask):
    @pl.when(pl.program_id(0) == 0)
    def _():
        mask[...] = jnp.where(column_ref[...] == line_ref[...], 0.0, NEGATIVE)

    mixed = []
    for head in range(2):
        base = head * 3 * HD
        query = qkv_ref[:, base : base + HD] * jnp.asarray(1 / math.sqrt(HD), BF16)
        key = qkv_ref[:, base + HD : base + 2 * HD]
        value = qkv_ref[:, base + 2 * HD : base + 3 * HD]
        scores = mm(key, query, NT) + mask[...]
        powers = jnp.exp(scores - jnp.max(scores, 0, keepdims=True))
        total = jnp.sum(powers, 0, keepdims=True)
        probs = (powers * (1.0 / total)).astype(BF16)
        probs_ref[head] = probs
        mixed.append(mm(value, probs, TN))
    heads_ref[...] = jnp.concatenate(mixed, 0).T.astype(BF16)


def attend(qkv, labels):
    pairs = qkv.shape[1] // (6 * HD)
    return pl.pallas_call(
        attend_kernel,
        grid=(pairs,),
        in_specs=[
            pl.BlockSpec((SEQ, 6 * HD), lambda i: (0, i)),
            pl.BlockSpec((SEQ, 1), lambda i: (0, 0)),
            pl.BlockSpec((1, SEQ), lambda i: (0, 0)),
        ],
        out_specs=[
            pl.BlockSpec((SEQ, 2 * HD), lambda i: (0, i)),
            pl.BlockSpec((2, SEQ, SEQ), lambda i: (i, 0, 0)),
        ],
        out_shape=[
            jax.ShapeDtypeStruct((SEQ, pairs * 2 * HD), BF16),
            jax.ShapeDtypeStruct((pairs * 2, SEQ, SEQ), BF16),
        ],
        scratch_shapes=[pltpu.VMEM((SEQ, SEQ), F32)],
        compiler_params=pltpu.CompilerParams(vmem_limit_bytes=32 * MIB),
        cost_estimate=pl.CostEstimate(
            flops=pairs * 2 * 4 * SEQ * SEQ * 256, bytes_accessed=pairs * 2 * SEQ * SEQ * 2, transcendentals=pairs * 2 * SEQ * SEQ
        ),
        name="attend",
    )(qkv, labels[:, None], labels[None, :])


def attend_back_kernel(qkv_ref, probs_ref, grad_ref, out_ref):
    for head in range(2):
        base = head * 3 * HD
        scale = jnp.asarray(1 / math.sqrt(HD), BF16)
        query = qkv_ref[:, base : base + HD] * scale
        key = qkv_ref[:, base + HD : base + 2 * HD] * scale
        value = qkv_ref[:, base + 2 * HD : base + 3 * HD]
        grad = grad_ref[:, head * HD : (head + 1) * HD]
        probs = probs_ref[head]
        d_value = mm(probs, grad, NN)
        d_probs = mm(value, grad, NT)
        wide = probs.astype(F32)
        delta = jnp.sum(wide * d_probs, 0, keepdims=True)
        d_scores = (wide * (d_probs - delta)).astype(BF16)
        d_key = mm(d_scores, query, NN)
        d_query = mm(key, d_scores, TN).T
        out_ref[:, base : base + HD] = d_query.astype(BF16)
        out_ref[:, base + HD : base + 2 * HD] = d_key.astype(BF16)
        out_ref[:, base + 2 * HD : base + 3 * HD] = d_value.astype(BF16)


def attend_back(qkv, probs, grad):
    pairs = qkv.shape[1] // (6 * HD)
    return pl.pallas_call(
        attend_back_kernel,
        grid=(pairs,),
        in_specs=[
            pl.BlockSpec((SEQ, 6 * HD), lambda i: (0, i)),
            pl.BlockSpec((2, SEQ, SEQ), lambda i: (i, 0, 0)),
            pl.BlockSpec((SEQ, 2 * HD), lambda i: (0, i)),
        ],
        out_specs=pl.BlockSpec((SEQ, 6 * HD), lambda i: (0, i)),
        out_shape=jax.ShapeDtypeStruct(qkv.shape, BF16),
        compiler_params=pltpu.CompilerParams(vmem_limit_bytes=32 * MIB),
        cost_estimate=pl.CostEstimate(
            flops=pairs * 2 * 10 * SEQ * SEQ * 256, bytes_accessed=pairs * 2 * SEQ * SEQ * 2, transcendentals=0
        ),
        name="attend_back",
    )(qkv, probs, grad)


def own_rows(value, odd, col):
    rolled = jnp.where(odd, jnp.roll(value, -2 * QUARTER, 0), value)
    first = jnp.concatenate([rolled[:SEQ], rolled[2 * SEQ : 2 * SEQ + QUARTER]], 0)
    second = jnp.concatenate([rolled[SEQ : 2 * SEQ], rolled[2 * SEQ + QUARTER :]], 0)
    mine = jnp.where(col == 0, first, second)
    other = lax.ppermute(jnp.where(col == 0, second, first), "col", [(0, 1), (1, 0)])
    return jnp.concatenate([jnp.where(col == 0, mine, other), jnp.where(col == 0, other, mine)], 1)


def give_back(value, odd, col):
    half = D // 2
    mine = jnp.where(col == 0, value[:, :half], value[:, half:])
    leaving = jnp.where(col == 0, value[:, half:], value[:, :half])
    other = lax.ppermute(leaving.astype(BF16), "col", [(0, 1), (1, 0)]).astype(F32)
    first = jnp.where(col == 0, mine, other)
    second = jnp.where(col == 0, other, mine)
    rolled = jnp.concatenate([first[:SEQ], second[:SEQ], first[SEQ:], second[SEQ:]], 0)
    return jnp.where(odd, jnp.roll(rolled, 2 * QUARTER, 0), rolled)


def swap(offset):
    return [(i, i ^ offset) for i in range(8)]


def spread_heads(value, member):
    width = value.shape[1] // 4
    pieces = []
    for offset in range(4):
        piece = lax.dynamic_slice_in_dim(value, (member ^ offset) * width, width, 1)
        pieces.append(piece if offset == 0 else lax.ppermute(piece, GRID, swap(offset)))
    return jnp.concatenate(pieces, 0)


def collect_heads(value, member):
    width = value.shape[1]
    whole = jnp.zeros((QUARTER, 4 * width), value.dtype)
    for offset in range(4):
        piece = value[offset * QUARTER : (offset + 1) * QUARTER]
        if offset:
            piece = lax.ppermute(piece, GRID, swap(offset))
        whole = lax.dynamic_update_slice_in_dim(whole, piece, (member ^ offset) * width, 1)
    return whole


def gather_weight(shard):
    return lax.all_gather(shard, GRID, axis=0, tiled=False)


def whole_up(stack):
    _, depth, width = stack.shape
    return stack.reshape(4, 2, depth, width).transpose(1, 2, 0, 3).reshape(2 * depth, 4 * width)


def whole_down(stack):
    _, depth, width = stack.shape
    return stack.reshape(4, 2, depth, width).transpose(0, 2, 1, 3).reshape(4 * depth, 2 * width)


def reduce_up(grad):
    depth, width = grad.shape
    stack = grad.astype(BF16).reshape(2, depth // 2, 4, width // 4).transpose(2, 0, 1, 3)
    return reduce_stack(stack.reshape(8, depth // 2, width // 4))


def reduce_down(grad):
    depth, width = grad.shape
    stack = grad.astype(BF16).reshape(4, depth // 4, 2, width // 2).transpose(0, 2, 1, 3)
    return reduce_stack(stack.reshape(8, depth // 4, width // 2))


def reduce_stack(stack):
    share = lax.psum_scatter(stack, GRID, scatter_dimension=0, tiled=False)
    return lax.psum(share, "dp").astype(F32)


def norm_forward(value, gain, bias):
    center = jnp.sum(value, 1, keepdims=True) / D
    squares = jnp.sum(value * value, 1, keepdims=True) / D
    inverse = lax.rsqrt(squares - center * center + EPSILON)
    unit = (value - center) * inverse
    return (unit * gain + bias, unit, inverse)


def norm_backward(grad, unit, inverse, gain):
    scaled = grad * gain
    total = jnp.sum(scaled, 1, keepdims=True)
    paired = jnp.sum(scaled * unit, 1, keepdims=True)
    back = inverse * (scaled - total / D - unit * (paired / D))
    return (back, jnp.sum(grad * unit, 0), jnp.sum(grad, 0))


def gelu_exact(value):
    return jax.nn.gelu(value, approximate=False)


def local(
    tokens,
    segments,
    qkv_weight,
    qv_bias,
    out_weight,
    out_bias,
    ln1_gain,
    ln1_bias,
    ff_in_weight,
    ff_in_bias,
    ff_out_weight,
    ff_out_bias,
    ln2_gain,
    ln2_bias,
    out_grad,
):
    row, col = lax.axis_index("row"), lax.axis_index("col")
    odd = row % 2 == 1
    member = (row % 2) * 2 + col

    qkv_w = whole_up(gather_weight(qkv_weight))
    out_w = whole_down(gather_weight(out_weight))
    ff_in_w = whole_up(gather_weight(ff_in_weight))
    ff_out_w = whole_down(gather_weight(ff_out_weight))

    packed = jnp.concatenate(
        [out_bias, ln1_gain, ln1_bias, ff_out_bias, ln2_gain, ln2_bias, ff_in_bias, qv_bias.reshape(-1)]
    )
    packed = lax.all_gather(packed, GRID, axis=0, tiled=False)
    vectors = packed[:2, : 6 * 512].reshape(2, 6, 512).transpose(1, 0, 2).reshape(6, D)
    out_b, gain_one, bias_one, ff_out_b, gain_two, bias_two = [vectors[i] for i in range(6)]
    ff_in_b = packed[:, 6 * 512 : 7 * 512].reshape(-1)
    qv_b = packed[:, 7 * 512 :].reshape(-1, 2 * HD)
    hollow = jnp.zeros((qv_b.shape[0], HD), F32)
    qkv_b = jnp.concatenate([qv_b[:, :HD], hollow, qv_b[:, HD:]], 1).reshape(-1)

    x = own_rows(tokens, odd, col)
    incoming = own_rows(out_grad, odd, col)

    group = (row // 2) * 5
    labels = lax.dynamic_slice_in_dim(segments, (group + (row % 2) * 3 + col) * SEQ, SEQ)
    shared = lax.dynamic_slice_in_dim(segments, (group + 2) * SEQ, SEQ)
    shared = jnp.concatenate(
        [lax.dynamic_slice_in_dim(shared, (member ^ offset) * QUARTER, QUARTER) for offset in range(4)]
    )

    qkv = (mm(x, qkv_w, NN) + qkv_b).astype(BF16)
    qkv_shared = spread_heads(qkv[SEQ:], member)
    heads_own, probs_own = attend(qkv[:SEQ], labels)
    heads_shared, probs_shared = attend(qkv_shared, shared)
    heads = jnp.concatenate([heads_own, collect_heads(heads_shared, member)], 0)
    branch_one = mm(heads, out_w, NN) + out_b
    middle, unit_one, inverse_one = norm_forward(x.astype(F32) + branch_one, gain_one, bias_one)
    middle_low = middle.astype(BF16)
    hidden = mm(middle_low, ff_in_w, NN) + ff_in_b
    gelu_value, pullback = jax.vjp(gelu_exact, hidden)
    active = gelu_value.astype(BF16)
    branch_two = mm(active, ff_out_w, NN) + ff_out_b
    layer_out, unit_two, inverse_two = norm_forward(middle + branch_two, gain_two, bias_two)
    layer_out = give_back(layer_out, odd, col)

    back_two, ln2_gain_part, ln2_bias_part = norm_backward(incoming.astype(F32), unit_two, inverse_two, gain_two)
    d_two = back_two.astype(BF16)
    ff_out_bias_part = jnp.sum(d_two, 0, dtype=F32)
    ff_out_grad = reduce_down(mm(active, d_two, TN))
    d_hidden = pullback(mm(d_two, ff_out_w, NT))[0].astype(BF16)
    ff_in_bias_part = jnp.sum(d_hidden, 0, dtype=F32)
    ff_in_grad = reduce_up(mm(middle_low, d_hidden, TN))
    back_middle = back_two + mm(d_hidden, ff_in_w, NT)
    back_one, ln1_gain_part, ln1_bias_part = norm_backward(back_middle, unit_one, inverse_one, gain_one)
    d_one = back_one.astype(BF16)
    out_bias_part = jnp.sum(d_one, 0, dtype=F32)
    out_grad_w = reduce_down(mm(heads, d_one, TN))
    d_heads = mm(d_one, out_w, NT).astype(BF16)
    d_shared = spread_heads(d_heads[SEQ:], member)
    d_qkv_own = attend_back(qkv[:SEQ], probs_own, d_heads[:SEQ])
    d_qkv_shared = attend_back(qkv_shared, probs_shared, d_shared)
    d_qkv = jnp.concatenate([d_qkv_own, collect_heads(d_qkv_shared, member)], 0)
    qkv_grad = reduce_up(mm(x, d_qkv, TN))
    column_sums = jnp.sum(d_qkv, 0, dtype=F32).reshape(-1, 3, HD)
    qv_part = jnp.concatenate([column_sums[:, 0], column_sums[:, 2]], 1).reshape(-1)
    input_grad = give_back(back_one + mm(d_qkv, qkv_w, NT), odd, col)

    sums = lax.psum(
        jnp.concatenate(
            [
                out_bias_part,
                ln1_gain_part,
                ln1_bias_part,
                ff_out_bias_part,
                ln2_gain_part,
                ln2_bias_part,
                ff_in_bias_part,
                qv_part,
            ]
        ),
        ("dp", "row", "col"),
    )
    halves = lax.dynamic_slice_in_dim(sums[: 6 * D].reshape(6, 2, D // 2), col, 1, 1)[:, 0]
    place = row * 2 + col
    ff_in_part = lax.dynamic_slice_in_dim(sums, 6 * D + place * 512, 512)
    qv_mine = lax.dynamic_slice_in_dim(sums, 6 * D + 4 * D + place * 256, 256).reshape(2, 2 * HD)
    return (
        layer_out,
        input_grad,
        qkv_grad,
        qv_mine,
        out_grad_w,
        halves[0],
        halves[1],
        halves[2],
        ff_in_grad,
        ff_in_part,
        ff_out_grad,
        halves[3],
        halves[4],
        halves[5],
    )


def solution(mesh):
    in_specs = (
        P(("dp", "row"), "col"),
        P("dp"),
        P("col", "row"),
        P(("row", "col"), None),
        P("row", "col"),
        P("col"),
        P("col"),
        P("col"),
        P("col", "row"),
        P(("row", "col")),
        P("row", "col"),
        P("col"),
        P("col"),
        P("col"),
        P(("dp", "row"), "col"),
    )
    out_specs = (
        P(("dp", "row"), "col"),
        P(("dp", "row"), "col"),
        P("col", "row"),
        P(("row", "col"), None),
        P("row", "col"),
        P("col"),
        P("col"),
        P("col"),
        P("col", "row"),
        P(("row", "col")),
        P("row", "col"),
        P("col"),
        P("col"),
        P("col"),
    )
    return jax.shard_map(local, mesh=mesh, in_specs=in_specs, out_specs=out_specs, check_vma=False)
```

time: 1780 us -> 752 us (0.42)
  waiting for transfers between devices: 1230 us -> 261 us
  matrix products: 199 us -> 124 us
  local copies, waits for them, and re-layouts: 103 us -> 159 us
  blocking collectives: 148 us -> 105 us
  other arithmetic: 65.8 us -> 30.1 us
  Pallas kernels: 0 us -> 32.3 us
    all_gather x12 -> x4, waiting for transfers between devices: 983 us -> 58.8 us  [gather_weight(): return lax.all_gather(shard, GRID, axis=0, tiled=False)]
    dot_general x82 -> x12, matrix products: 199 us -> 124 us  [mm(): return lax.dot_general(left, right, contract, preferred_element_type=F32)]
    reshape x3 -> x12, local copies, waits for them, and re-layouts: 24.3 us -> 90.1 us  [the longest x2 27.1 us: reduce_up(): grad.astype(BF16).reshape(2, depth // 2, 4, width // 4)]
    reduce_scatter x4, waiting for transfers between devices: 198 us -> 136 us  [reduce_stack(): share = lax.psum_scatter(stack, GRID, scatter_dimension=0, tiled=False)]
    all_gather x0 -> x1, blocking collectives: none -> 52.2 us  [local(): packed = lax.all_gather(packed, GRID, axis=0, tiled=False)]
    psum x6 -> x1, blocking collectives: 105 us -> 53.1 us  [local(): lax.psum(jnp.concatenate([out_bias_part, ln1_gain_part, ln1_bias_part, ff...]
    all_to_all x2 -> x0, blocking collectives: 42.5 us -> none  [the longest x1 22.1 us: project_cols(): lax.all_to_all(weight, 'col', split_axis=1, concat_axis=0, tiled=True)]
    pallas_call x0 -> x4, Pallas kernels: none -> 32.3 us  [the longest x2 16.9 us: attend_back(): pl.pallas_call(attend_back_kernel, grid=(pairs,), in_specs=[pl.BlockSpec(...]
  transfers between devices with their start and end apart: 19 -> 25, of which waited for: 19 -> 12; matrix products, arithmetic and copies ran while one was open for 3% -> 25% of each run, Pallas kernels for 0% -> 4%
where the time goes in v1:
time: 752 us; the launch traced here: 743 us
  waiting for transfers between devices  261 us (35%)
  local copies, waits for them, and re-layouts  159 us (21%)
  matrix products  124 us (16%)
  blocking collectives  105 us (14%)
  Pallas kernels  32.3 us (4%)
  other arithmetic  30.1 us (4%)
  starting transfers between devices  15.7 us (2%)
  between operations  15.6 us (2%)
    reduce_scatter x4, waiting for transfers between devices, reduce_stack(): share = lax.psum_scatter(stack, GRID, scatter_dimension=0, tiled=False)  136 us
    dot_general x12, matrix products, mm(): return lax.dot_general(left, right, contract, preferred_element_type=F32)  124 us
    all_gather x4, waiting for transfers between devices, gather_weight(): return lax.all_gather(shard, GRID, axis=0, tiled=False)  58.8 us
    psum x1, blocking collectives, local(): lax.psum(jnp.concatenate([out_bias_part, ln1_gain_part, ln1_bias_part, ff...  53.1 us
    all_gather x1, blocking collectives, local(): packed = lax.all_gather(packed, GRID, axis=0, tiled=False)  52.2 us
    psum x1, waiting for transfers between devices, reduce_stack(): return lax.psum(share, 'dp').astype(F32)  49.5 us
    unnamed x122, local copies, waits for them, and re-layouts  34.8 us
    reshape x2, local copies, waits for them, and re-layouts, reduce_up(): grad.astype(BF16).reshape(2, depth // 2, 4, width // 4)  27.1 us
  transfers between devices with their start and end apart: 25, of which 12 were waited for; matrix products, arithmetic and copies ran while one was open for 25% of the time, Pallas kernels for 4%

profile of v1, /device:TPU:0, one launch (start us, length us, event | category | flops | bytes accessed | tf_op | source)
XLA Modules:
  0.0 743.0 jit_solution(17011197319322192364)
XLA Ops:
  11.6 2.9 collective-permute-start
  17.2 52.2 %all-gather.5 = f32[8,1,3840]{2,1,0:T(1,128)S(1)} all-gather(f32[1,1,3840]{2,1,0:T(1,128)S(1)} %reshape.213), channel_id=3, replica_groups=mesh['dp'=4,'row'=4,'col'=2] {'row','col'}, dimensions={0}, use_global_device_ids=true | all-gather | bytes 138240 | tf_op jit(solution)/shard_map/all_gather | solution.py:242
  73.7 2.5 broadcast_select_fusion.5
  76.1 10.3 %copy.45 = bf16[4,2,512,768]{3,0,2,1:T(4,128)(2,1)} copy(bf16[4,2,512,768]{3,2,1,0:T(8,128)(2,1)} %bitcast.105) | data formatting | bytes 12582912 | tf_op jit(solution)/shard_map/reshape | solution.py:168
  86.4 4.4 copy.58
  90.9 4.7 add_convert_fusion.1
  99.9 2.2 broadcast_select_fusion.1
  103.0 3.7 copy.48
  109.5 3.2 attend.3
  114.4 12.2 %attend.2 = (bf16[512,1024]{1,0:T(8,128)(2,1)S(1)}, bf16[16,512,512]{2,1,0:T(8,128)(2,1)S(1)}) custom-call(bf16[512,3072]{1,0:T(8,128)(2,1)S(1)} %slice.271.qkv_ref, s32[512,1]{1,0:T(8,128)S(1)} %copy.46.column_ref, s32[1,512]{1,0:T(1,128)S(1)} %bitcast.80), custom_call_target="tpu_custom_call" | custom-call | flops 4294967296 | bytes 8388608 | tf_op jit(solution)/shard_map/attend/pallas_call | solution.py:52
  127.9 2.6 collective-permute-done.6
  130.6 3.2 fusion.31
  133.8 26.5 %all-gather.15.cloned.1.call-done = bf16[4096,1024]{1,0:T(8,128)(2,1)} async-done(((bf16[512,1024]{1,0:T(8,128)(2,1)}), bf16[4096,1024]{1,0:T(8,128)(2,1)}) %all-gather.15.cloned.1.call-update) | async-done | bytes 8388624 | tf_op jit(solution)/shard_map/all_gather | solution.py:163
  160.3 12.5 %copy.49 = bf16[4,2,512,1024]{3,0,2,1:T(4,128)(2,1)} copy(bf16[4,2,512,1024]{3,2,1,0:T(8,128)(2,1)} %bitcast.94) | data formatting | bytes 16777216 | tf_op jit(solution)/shard_map/reshape | solution.py:168
  172.8 12.2 %copy.60 = bf16[128,8,4,1024]{3,1,2,0:T(8,128)(2,1)} copy(bf16[128,8,4,1024]{3,2,1,0:T(4,128)(2,1)} %bitcast.87) | data formatting | bytes 16777216
  185.1 31.4 %all-gather.17.cloned.1.call-done = bf16[8192,512]{1,0:T(8,128)(2,1)} async-done(((bf16[1024,512]{1,0:T(8,128)(2,1)}), bf16[8192,512]{1,0:T(8,128)(2,1)}) %all-gather.17.cloned.1.call-update) | async-done | bytes 8388624 | tf_op jit(solution)/shard_map/all_gather | solution.py:163
  216.5 16.4 %copy.50 = bf16[4,2,1024,512]{3,1,2,0:T(2,128)(2,1)} copy(bf16[4,2,1024,512]{3,2,1,0:T(8,128)(2,1)} %bitcast.95) | data formatting | bytes 16777216 | tf_op jit(solution)/shard_map/reshape | solution.py:173
  232.9 9.5 %copy.62 = bf16[512,8,2,512]{3,1,2,0:T(8,128)(2,1)} copy(bf16[512,8,2,512]{3,2,1,0:T(2,128)(2,1)} %bitcast.88) | data formatting | bytes 16777216
  242.5 33.3 %multiply_convert_fusion = (bf16[640,4096]{1,0:T(8,128)(2,1)S(1)}, f32[640,4096]{1,0:T(8,128)}, f32[640,4096]{1,0:T(8,128)}) fusion(f32[4096]{0:T(1024)S(1)} %bitcast.127, bf16[1024,4096]{1,0:T(8,128)(2,1)} %bitcast.96, f32[640,1024]{1,0:T(8,128)S(1)} %copy-done.19, f32[1024]{0:T(1024)S(1)} %bitcast.129, f32[1024]{0:T(1024)S(1)} %bitcast.122, ...), kind=kOutput, calls=%fused_computation.4 | convolution fusion | flops 5545000960 | bytes 37254144 | tf_op jit(solution)/shard_map/dot_general | solution.py:27
  275.8 6.1 fusion.30
  283.2 3.0 convert_reduce_fusion.3
  286.2 18.1 %convert_reduce_fusion = (f32[4096]{0:T(1024)S(1)}, bf16[640,4096]{1,0:T(8,128)(2,1)}) fusion(f32[640,4096]{1,0:T(8,128)} %get-tuple-element.43, bf16[4096,1024]{1,0:T(8,128)(2,1)} %bitcast.98, f32[640,1024]{1,0:T(8,128)} %get-tuple-element.39, f32[640,4096]{1,0:T(8,128)} %get-tuple-element.102, f32[4096]{0:T(1024)S(1)} %bitcast.128), kind=kOutput, calls=%fused_computation.2 | convolution fusion | flops 5413924864 | bytes 37257216 | tf_op jit(solution)/shard_map/dot_general | solution.py:27
  304.3 12.1 %multiply_reduce_fusion = (f32[1024]{0:T(1024)S(1)}, f32[640]{0:T(1024)S(1)}, f32[640]{0:T(1024)S(1)}, f32[1024]{0:T(1024)S(1)}, f32[640,1024]{1,0:T(8,128)S(1)}) fusion(f32[640,1024]{1,0:T(8,128)} %get-tuple-element.101, f32[640]{0:T(1024)S(1)} %get-tuple-element.100, f32[640]{0:T(1024)S(1)} %get-tuple-element.99, f32[1024]{0:T(1024)S(1)} %bitcast.124, ...), kind=kOutput, calls=%fused_computation.37 | convolution fusion | flops 5375259648 | bytes 21518336 | tf_op jit(solution)/shard_map/dot_general | solution.py:27
  318.8 3.2 convolution_convert_fusion.3
  322.0 4.5 reshape.198
  326.5 3.3 copy.53
  329.8 4.1 convolution_convert_fusion.4
  340.2 3.5 attend_back.3
  345.4 13.4 %attend_back.2 = bf16[512,3072]{1,0:T(8,128)(2,1)S(1)} custom-call(bf16[512,3072]{1,0:T(8,128)(2,1)S(1)} %copy-done.1, bf16[16,512,512]{2,1,0:T(8,128)(2,1)S(1)} %bitcast.84, bf16[512,1024]{1,0:T(8,128)(2,1)S(1)} %slice.291.grad_ref), custom_call_target="tpu_custom_call" | custom-call | flops 10737418240 | bytes 8388608 | tf_op jit(solution)/shard_map/attend_back/pallas_call | solution.py:100
  359.6 5.9 collective-permute-done.14
  366.4 7.1 convolution_convert_fusion.2
  373.5 12.3 %reshape.193 = bf16[2,512,4,768]{3,2,1,0:T(4,128)(2,1)} reshape(bf16[1024,3072]{1,0:T(8,128)(2,1)} %convolution_convert_fusion.2) | data formatting | bytes 12582912 | tf_op jit(solution)/shard_map/reshape | solution.py:178
  385.8 6.3 copy.51
  392.2 12.0 %convolution_convert_fusion.1 = bf16[4096,1024]{1,0:T(8,128)(2,1)} fusion(bf16[640,4096]{1,0:T(8,128)(2,1)} %copy-done.47, f32[640,1024]{1,0:T(8,128)} %get-tuple-element.39), kind=kOutput, calls=%fused_computation.21 | convolution fusion | flops 5373558784 | bytes 16252928 | tf_op jit(solution)/shard_map/dot_general | solution.py:27
  404.2 14.7 %reshape.202 = bf16[4,1024,2,512]{3,2,1,0:T(2,128)(2,1)} reshape(bf16[4096,1024]{1,0:T(8,128)(2,1)} %convolution_convert_fusion.1) | data formatting | bytes 16777216 | tf_op jit(solution)/shard_map/reshape | solution.py:184
  418.9 8.2 %copy.55 = bf16[4,2,1024,512]{3,2,1,0:T(8,128)(2,1)} copy(bf16[4,2,1024,512]{3,1,2,0:T(2,128)(2,1)} %bitcast.89) | data formatting | bytes 16777216 | tf_op jit(solution)/shard_map/transpose | solution.py:184
  427.2 12.2 %convolution_convert_fusion = bf16[1024,4096]{1,0:T(8,128)(2,1)} fusion(bf16[640,4096]{1,0:T(8,128)(2,1)} %get-tuple-element.106, f32[640,1024]{1,0:T(8,128)} %get-tuple-element.101, f32[1024]{0:T(1024)S(1)} %bitcast.131, f32[1024]{0:T(1024)S(1)} %bitcast.126, f32[640]{0:T(1024)S(1)} %get-tuple-element.100, f32[640]{0:T(1024)S(1)} %get-tuple-element.99), kind=kOutput, calls=%fused_computation.20 | convolution fusion | flops 5376180224 | bytes 16266240 | tf_op jit(solution)/shard_map/dot_general | solution.py:27
  439.4 14.7 %reshape.200 = bf16[2,512,4,1024]{3,2,1,0:T(4,128)(2,1)} reshape(bf16[1024,4096]{1,0:T(8,128)(2,1)} %convolution_convert_fusion) | data formatting | bytes 16777216 | tf_op jit(solution)/shard_map/reshape | solution.py:178
  454.1 9.7 %copy.54 = bf16[4,2,512,1024]{3,2,1,0:T(8,128)(2,1)} copy(bf16[4,2,512,1024]{3,0,2,1:T(4,128)(2,1)} %bitcast.90) | data formatting | bytes 16777216 | tf_op jit(solution)/shard_map/transpose | solution.py:178
  463.9 3.2 select_convert_fusion.1
  467.3 61.2 %reduce-scatter.11.cloned.1.call-done = bf16[1,1024,512]{2,1,0:T(8,128)(2,1)} async-done(((bf16[8,1024,512]{2,1,0:T(8,128)(2,1)}), bf16[1,1024,512]{2,1,0:T(8,128)(2,1)}) %reduce-scatter.11.cloned.1.call-update) | async-done | bytes 1048592 | tf_op jit(solution)/shard_map/reduce_scatter | solution.py:189
  528.5 75.1 %reduce-scatter.9.cloned.1.call-done = bf16[1,512,1024]{2,1,0:T(8,128)(2,1)} async-done(((bf16[8,512,1024]{2,1,0:T(8,128)(2,1)}), bf16[1,512,1024]{2,1,0:T(8,128)(2,1)}) %reduce-scatter.9.cloned.1.call-update) | async-done | bytes 1048592 | tf_op jit(solution)/shard_map/reduce_scatter | solution.py:189
  603.7 8.1 %convolution_add_fusion.1 = f32[640,1024]{1,0:T(8,128)S(1)} fusion(f32[640,1024]{1,0:T(8,128)} %copy-done.18, bf16[1024,3072]{1,0:T(8,128)(2,1)} %bitcast.104, bf16[128,3072]{1,0:T(8,128)(2,1)} %copy-done.16, bf16[512,3072]{1,0:T(8,128)(2,1)S(1)} %attend_back.2), kind=kOutput, calls=%fused_computation.57 | convolution fusion | flops 4035051520 | bytes 15466496 | tf_op jit(solution)/shard_map/dot_general | solution.py:27
  616.7 53.1 %psum.36 = f32[12288]{0:T(1024)S(1)} all-reduce(f32[12288]{0:T(1024)S(1)} %fusion.14), channel_id=1, replica_groups=mesh['dp'=4,'row'=4,'col'=2] {'dp','row','col'}, use_global_device_ids=true, to_apply=%region_18.19 | all-reduce | flops 12288 | bytes 98304 | tf_op jit(solution)/shard_map/psum | solution.py:297
  671.7 2.4 convert_select_fusion.3
  676.8 3.0 maximum_select_fusion
  679.8 49.5 %all-reduce.3.cloned.1.call-done = (bf16[512,768]{1,0:T(8,128)(2,1)}, bf16[256,512]{1,0:T(8,128)(2,1)}, bf16[512,1024]{1,0:T(8,128)(2,1)}, bf16[1024,512]{1,0:T(8,128)(2,1)}) async-done(((bf16[512,768]{1,0:T(8,128)(2,1)}, bf16[256,512]{1,0:T(8,128)(2,1)}, bf16[512,1024]{1,0:T(8,128)(2,1)}, bf16[1024,512]{1,0:T(8,128)(2,1)}), (bf16[512,768]{1,0:T(8,128)(2,1)}, bf16[256,512]{1,0:T(8,128)(2,1)}, ...) | async-done | bytes 3145744 | tf_op jit(solution)/shard_map/psum | solution.py:190
  729.3 2.9 convert_element_type.97
  (252 shorter events, 48.4 us)
Async XLA Ops:
  7.2 68.9 %all-gather.11.cloned.1.call-start = ((), (), s32[]{:S(2)}) async-start(), calls=%async_computation.8 | async-start | bytes 7077888 | tf_op jit(solution)/shard_map/all_gather | solution.py:163
  7.9 95.1 %all-gather.13.cloned.1.call-start = ((), (), s32[]{:S(2)}) async-start(), calls=%async_computation.9 | async-start | bytes 2359296 | tf_op jit(solution)/shard_map/all_gather | solution.py:163
  8.7 151.6 %all-gather.15.cloned.1.call-start = ((), (), s32[]{:S(2)}) async-start(), calls=%async_computation.10 | async-start | bytes 9437184 | tf_op jit(solution)/shard_map/all_gather | solution.py:163
  9.4 207.1 %all-gather.17.cloned.1.call-start = ((), (), s32[]{:S(2)}) async-start(), calls=%async_computation.11 | async-start | bytes 9437184 | tf_op jit(solution)/shard_map/all_gather | solution.py:163
  10.0 457.2 %reduce-scatter.7.cloned.1.call-start = ((), (), s32[]{:S(2)}) async-start(), calls=%async_computation.5 | async-start | bytes 2359296 | tf_op jit(solution)/shard_map/reduce_scatter | solution.py:189
  11.6 62.0 %collective-permute-start = (bf16[640,512]{1,0:T(8,128)(2,1)}, bf16[640,512]{1,0:T(8,128)(2,1)}, u32[]{:S(2)}, u32[]{:S(2)}) collective-permute-start(bf16[640,512]{1,0:T(8,128)(2,1)} %broadcast_select_fusion.6), channel_id=1, source_target_pairs={{0,1},{1,0},{2,3},{3,2},{4,5},{5,4},{6,7},{7,6},{8,9},{9,8},{10,11... | collective-permute-start | bytes 1966088 | tf_op jit(solution)/shard_map/ppermute | solution.py:123
  16.1 83.8 %collective-permute-start.8 = (bf16[640,512]{1,0:T(8,128)(2,1)}, bf16[640,512]{1,0:T(8,128)(2,1)}, u32[]{:S(2)}, u32[]{:S(2)}) collective-permute-start(bf16[640,512]{1,0:T(8,128)(2,1)} %broadcast_select_fusion.2), channel_id=1, source_target_pairs={{0,1},{1,0},{2,3},{3,2},{4,5},{5,4},{6,7},{7,6},{8,9},{9,8},{10,11... | collective-permute-start | bytes 1966088 | tf_op jit(solution)/shard_map/ppermute | solution.py:123
  96.6 12.5 %collective-permute-start.1 = (bf16[128,768]{1,0:T(8,128)(2,1)}, bf16[128,768]{1,0:T(8,128)(2,1)S(1)}, u32[]{:S(2)}, u32[]{:S(2)}) collective-permute-start(bf16[128,768]{1,0:T(8,128)(2,1)} %get-tuple-element.68), channel_id=1, source_target_pairs={{0,1},{1,0},{2,3},{3,2},{4,5},{5,4},{6,7},{7,6},{8,9},{9,8},{10,11... | collective-permute-start | bytes 589832 | tf_op jit(solution)/shard_map/ppermute | solution.py:147
  98.8 10.3 %collective-permute-start.2 = (bf16[128,768]{1,0:T(8,128)(2,1)}, bf16[128,768]{1,0:T(8,128)(2,1)S(1)}, u32[]{:S(2)}, u32[]{:S(2)}) collective-permute-start(bf16[128,768]{1,0:T(8,128)(2,1)} %get-tuple-element.67), channel_id=1, source_target_pairs={{0,2},{1,3},{2,0},{3,1},{4,6},{5,7},{6,4},{7,5},{8,10},{9,11},{10,... | collective-permute-start | bytes 589832 | tf_op jit(solution)/shard_map/ppermute | solution.py:147
  99.9 9.6 %collective-permute-start.3 = (bf16[128,768]{1,0:T(8,128)(2,1)}, bf16[128,768]{1,0:T(8,128)(2,1)S(1)}, u32[]{:S(2)}, u32[]{:S(2)}) collective-permute-start(bf16[128,768]{1,0:T(8,128)(2,1)} %get-tuple-element.66), channel_id=1, source_target_pairs={{0,3},{1,2},{2,1},{3,0},{4,7},{5,6},{6,5},{7,4},{8,11},{9,10},{10,... | collective-permute-start | bytes 589832 | tf_op jit(solution)/shard_map/ppermute | solution.py:147
  108.9 21.7 %copy-start.21 = (bf16[128,8,2,512]{3,1,2,0:T(8,128)(2,1)}, bf16[128,8,2,512]{3,1,2,0:T(8,128)(2,1)S(1)}, u32[]{:S(2)}) copy-start(bf16[128,8,2,512]{3,1,2,0:T(8,128)(2,1)S(1)} %copy.59) | copy-start | bytes 6291460
  109.1 5.3 copy-start
  109.5 17.1 %copy-start.2 = (bf16[512,768]{1,0:T(8,128)(2,1)}, bf16[512,768]{1,0:T(8,128)(2,1)S(1)}, u32[]{:S(2)}) copy-start(bf16[512,768]{1,0:T(8,128)(2,1)S(1)} %pad_maximum_fusion.8.qkv_ref) | copy-start | bytes 2359300
  112.8 14.5 %collective-permute-start.4 = (bf16[128,256]{1,0:T(8,128)(2,1)S(1)}, bf16[128,256]{1,0:T(8,128)(2,1)S(1)}, u32[]{:S(2)}, u32[]{:S(2)}) collective-permute-start(bf16[128,256]{1,0:T(8,128)(2,1)S(1)} %get-tuple-element.75), channel_id=1, source_target_pairs={{0,1},{1,0},{2,3},{3,2},{4,5},{5,4},{6,7},{7,6},{8,9},{9,8},{10,11... | collective-permute-start | bytes 196616 | tf_op jit(solution)/shard_map/ppermute | solution.py:157
  114.4 16.2 %copy-start.25 = (bf16[640,512]{1,0:T(8,128)(2,1)S(1)}, bf16[640,512]{1,0:T(8,128)(2,1)}, u32[]{:S(2)}) copy-start(bf16[640,512]{1,0:T(8,128)(2,1)} %get-tuple-element.51) | copy-start | bytes 1966084
  114.4 16.2 %copy-start.28 = (bf16[640,512]{1,0:T(8,128)(2,1)S(1)}, bf16[640,512]{1,0:T(8,128)(2,1)}, u32[]{:S(2)}) copy-start(bf16[640,512]{1,0:T(8,128)(2,1)} %get-tuple-element.52) | copy-start | bytes 1966084
  114.4 16.3 %copy-start.38 = (f32[1,2,512]{2,0,1:T(1,128)S(1)}, f32[1,2,512]{2,0,1:T(1,128)}, u32[]{:S(2)}) copy-start(f32[1,2,512]{2,0,1:T(1,128)} %get-tuple-element.84) | copy-start | bytes 12292
  126.6 7.2 copy-start.4
  126.6 7.2 copy-start.5
  126.6 1.3 collective-permute-start.5
  126.7 3.9 collective-permute-start.6
  232.9 9.6 %copy-start.19 = (f32[640,1024]{1,0:T(8,128)S(1)}, f32[640,1024]{1,0:T(8,128)}, u32[]{:S(2)}) copy-start(f32[640,1024]{1,0:T(8,128)} %get-tuple-element.101) | copy-start | bytes 7864324
  232.9 9.6 %copy-start.33 = (f32[1,2,512]{2,0,1:T(1,128)S(1)}, f32[1,2,512]{2,0,1:T(1,128)}, u32[]{:S(2)}) copy-start(f32[1,2,512]{2,0,1:T(1,128)} %get-tuple-element.83) | copy-start | bytes 12292
  232.9 9.6 %copy-start.34 = (f32[1,4,8,128]{3,1,2,0:T(4,128)S(1)}, f32[1,4,8,128]{3,1,2,0:T(4,128)}, u32[]{:S(2)}) copy-start(f32[1,4,8,128]{3,1,2,0:T(4,128)} %copy.61) | copy-start | bytes 49156
  232.9 9.6 %copy-start.36 = (f32[1,2,512]{2,0,1:T(1,128)S(1)}, f32[1,2,512]{2,0,1:T(1,128)}, u32[]{:S(2)}) copy-start(f32[1,2,512]{2,0,1:T(1,128)} %get-tuple-element.82) | copy-start | bytes 12292
  242.5 33.3 %copy-start.7 = (bf16[512,8,2,512]{3,1,2,0:T(8,128)(2,1)S(1)}, bf16[512,8,2,512]{3,1,2,0:T(8,128)(2,1)}, u32[]{:S(2)}) copy-start(bf16[512,8,2,512]{3,1,2,0:T(8,128)(2,1)} %copy.62) | copy-start | bytes 25165828
  242.5 33.3 %copy-start.37 = (f32[1,2,512]{2,0,1:T(1,128)S(1)}, f32[1,2,512]{2,0,1:T(1,128)}, u32[]{:S(2)}) copy-start(f32[1,2,512]{2,0,1:T(1,128)} %get-tuple-element.81) | copy-start | bytes 12292
  275.8 6.1 copy-start.47
  275.8 6.1 copy-start.9
  304.3 12.1 %copy-start.20 = (f32[640,1024]{1,0:T(8,128)S(1)}, f32[640,1024]{1,0:T(8,128)}, u32[]{:S(2)}) copy-start(f32[640,1024]{1,0:T(8,128)} %get-tuple-element.101) | copy-start | bytes 7864324
  329.8 137.5 %reduce-scatter.5.cloned.1.call-start = ((), (), s32[]{:S(2)}) async-start(), calls=%async_computation.4 | async-start | bytes 7077888 | tf_op jit(solution)/shard_map/reduce_scatter | solution.py:189
  329.8 15.6 %slice-start = ((s8[8388608]{0:T(1024)(128)(4,1)}), s8[4194304]{0:T(1024)(128)(4,1)S(1)}, s32[]{:S(2)}) async-start(s8[8388608]{0:T(1024)(128)(4,1)} %bitcast.83), calls=%async_computation.13 | async-start | bytes 8388608
  333.9 6.2 copy-start.3
  333.9 11.5 %slice-start.1 = ((s8[8388608]{0:T(1024)(128)(4,1)}), s8[4194304]{0:T(1024)(128)(4,1)S(1)}, s32[]{:S(2)}) async-start(s8[8388608]{0:T(1024)(128)(4,1)} %bitcast.83), calls=%async_computation.14 | async-start | bytes 8388608
  334.0 2.3 collective-permute-start.10
  334.3 4.0 collective-permute-start.11
  335.6 4.5 collective-permute-start.9
  343.9 15.7 %collective-permute-start.12 = (bf16[128,768]{1,0:T(8,128)(2,1)S(1)}, bf16[128,768]{1,0:T(8,128)(2,1)S(1)}, u32[]{:S(2)}, u32[]{:S(2)}) collective-permute-start(bf16[128,768]{1,0:T(8,128)(2,1)S(1)} %get-tuple-element.63), channel_id=1, source_target_pairs={{0,1},{1,0},{2,3},{3,2},{4,5},{5,4},{6,7},{7,6},{8,9},{9,8},{10,11... | collective-permute-start | bytes 589832 | tf_op jit(solution)/shard_map/ppermute | solution.py:157
  345.4 14.2 %collective-permute-start.13 = (bf16[128,768]{1,0:T(8,128)(2,1)S(1)}, bf16[128,768]{1,0:T(8,128)(2,1)S(1)}, u32[]{:S(2)}, u32[]{:S(2)}) collective-permute-start(bf16[128,768]{1,0:T(8,128)(2,1)S(1)} %get-tuple-element.62), channel_id=1, source_target_pairs={{0,2},{1,3},{2,0},{3,1},{4,6},{5,7},{6,4},{7,5},{8,10},{9,11},{10,... | collective-permute-start | bytes 589832 | tf_op jit(solution)/shard_map/ppermute | solution.py:157
  345.4 21.0 %copy-start.26 = (bf16[640,512]{1,0:T(8,128)(2,1)S(1)}, bf16[640,512]{1,0:T(8,128)(2,1)}, u32[]{:S(2)}) copy-start(bf16[640,512]{1,0:T(8,128)(2,1)} %get-tuple-element.51) | copy-start | bytes 1966084
  345.4 21.0 %copy-start.29 = (bf16[640,512]{1,0:T(8,128)(2,1)S(1)}, bf16[640,512]{1,0:T(8,128)(2,1)}, u32[]{:S(2)}) copy-start(bf16[640,512]{1,0:T(8,128)(2,1)} %get-tuple-element.52) | copy-start | bytes 1966084
  358.9 6.6 collective-permute-start.14
  392.1 136.4 %reduce-scatter.11.cloned.1.call-start = ((), (), s32[]{:S(2)}) async-start(), calls=%async_computation.7 | async-start | bytes 9437184 | tf_op jit(solution)/shard_map/reduce_scatter | solution.py:189
  427.1 176.5 %reduce-scatter.9.cloned.1.call-start = ((), (), s32[]{:S(2)}) async-start(), calls=%async_computation.6 | async-start | bytes 9437184 | tf_op jit(solution)/shard_map/reduce_scatter | solution.py:189
  463.9 265.5 %all-reduce.3.cloned.1.call-start = ((), (), s32[]{:S(2)}) async-start(), calls=%async_computation.12 | async-start | bytes 6291456 | tf_op jit(solution)/shard_map/psum | solution.py:190
  467.1 204.6 %collective-permute-start.7 = (bf16[640,512]{1,0:T(8,128)(2,1)}, bf16[640,512]{1,0:T(8,128)(2,1)}, u32[]{:S(2)}, u32[]{:S(2)}) collective-permute-start(bf16[640,512]{1,0:T(8,128)(2,1)} %select_convert_fusion.1), channel_id=1, source_target_pairs={{0,1},{1,0},{2,3},{3,2},{4,5},{5,4},{6,7},{7,6},{8,9},{9,8},{10,11... | collective-permute-start | bytes 1966088 | tf_op jit(solution)/shard_map/ppermute | solution.py:131
  603.7 10.6 %copy-start.17 = (bf16[128,3072]{1,0:T(8,128)(2,1)S(1)}, bf16[128,3072]{1,0:T(8,128)(2,1)}, u32[]{:S(2)}) copy-start(bf16[128,3072]{1,0:T(8,128)(2,1)} %copy-done.16) | copy-start | bytes 2359300
  615.2 59.2 %collective-permute-start.15 = (bf16[640,512]{1,0:T(8,128)(2,1)}, bf16[640,512]{1,0:T(8,128)(2,1)S(1)}, u32[]{:S(2)}, u32[]{:S(2)}) collective-permute-start(bf16[640,512]{1,0:T(8,128)(2,1)} %select_convert_fusion), channel_id=1, source_target_pairs={{0,1},{1,0},{2,3},{3,2},{4,5},{5,4},{6,7},{7,6},{8,9},{9,8},{10,11... | collective-permute-start | bytes 1966088 | tf_op jit(solution)/shard_map/ppermute | solution.py:131
  (31 other events, 89.0 us)
Sparse Core Ops, SparseCore 0:
  9.9 61.3 all-gather.10
  73.2 29.8 all-gather.12
  104.9 55.3 all-gather.14
  162.1 54.3 all-gather.16
  329.9 41.1 reduce-scatter.6
  392.2 61.4 reduce-scatter.4
  457.2 71.2 reduce-scatter.10
  532.4 71.2 reduce-scatter.8
  606.3 123.0 all-reduce.2

commit v2 on v1

--- a/solution.py
+++ b/solution.py
@@ -106,7 +106,7 @@
             pl.BlockSpec((SEQ, 2 * HD), lambda i: (0, i)),
         ],
         out_specs=pl.BlockSpec((SEQ, 6 * HD), lambda i: (0, i)),
-        out_shape=jax.ShapeDtypeStruct(qkv.shape, BF16),
+        out_shape=jax.ShapeDtypeStruct((SEQ, qkv.shape[1]), BF16),
         compiler_params=pltpu.CompilerParams(vmem_limit_bytes=32 * MIB),
         cost_estimate=pl.CostEstimate(
             flops=pairs * 2 * 10 * SEQ * SEQ * 256, bytes_accessed=pairs * 2 * SEQ * SEQ * 2, transcendentals=0
@@ -159,55 +159,372 @@
     return whole
 
 
+def dense(kernel, grid, in_specs, out_specs, out_shape, scratch, flops, name):
+    return pl.pallas_call(
+        kernel,
+        grid=(grid,),
+        in_specs=in_specs,
+        out_specs=out_specs,
+        out_shape=out_shape,
+        scratch_shapes=scratch,
+        compiler_params=pltpu.CompilerParams(vmem_limit_bytes=48 * MIB),
+        cost_estimate=pl.CostEstimate(flops=flops, bytes_accessed=flops // 640, transcendentals=0),
+        name=name,
+    )
+
+
+def whole(value):
+    return pl.BlockSpec(value.shape, lambda i: (0,) * value.ndim)
+
+
+def columns_of(value, parts=4):
+    return pl.BlockSpec((value.shape[0], value.shape[1] // parts), lambda i: (0, i))
+
+
+def pair_of(stack):
+    depth = stack.shape[1] // 256 * 256
+    return pl.BlockSpec((2, depth, stack.shape[2]), lambda i: (i, 0, 0))
+
+
+def shaped(shape, kind):
+    return jax.ShapeDtypeStruct(shape, kind)
+
+
+def halves_times(left_ref, weight_ref, start, width):
+    half = left_ref.shape[1] // 2
+    stop = start + width
+    return mm(left_ref[:, :half], weight_ref[0, :, start:stop], NN) + mm(
+        left_ref[:, half:], weight_ref[1, :, start:stop], NN
+    )
+
+
+def qkv_kernel(x_ref, weight_ref, bias_ref, out_ref):
+    for start in range(0, out_ref.shape[1], 256):
+        part = halves_times(x_ref, weight_ref, start, 256)
+        out_ref[:, start : start + 256] = (part + bias_ref[:, start : start + 256]).astype(BF16)
+
+
+def project_qkv(x, stack, bias):
+    width = 4 * stack.shape[2]
+    return dense(
+        qkv_kernel,
+        4,
+        [whole(x), pair_of(stack), columns_of(bias)],
+        pl.BlockSpec((x.shape[0], width // 4), lambda i: (0, i)),
+        shaped((x.shape[0], width), BF16),
+        [],
+        2 * x.shape[0] * D * width,
+        "project_qkv",
+    )(x, stack, bias)
+
+
+def hidden_kernel(x_ref, weight_ref, bias_ref, active_ref, slope_ref):
+    for start in range(0, active_ref.shape[1], 256):
+        stop = start + 256
+        hidden = halves_times(x_ref, weight_ref, start, 256) + bias_ref[:, start:stop]
+        share = 0.5 * (1.0 + lax.erf(hidden * math.sqrt(0.5)))
+        bell = jnp.exp(hidden * hidden * -0.5) * (1 / math.sqrt(2 * math.pi))
+        active_ref[:, start:stop] = (hidden * share).astype(BF16)
+        slope_ref[:, start:stop] = (share + hidden * bell).astype(BF16)
+
+
+def project_hidden(x, stack, bias):
+    width = 4 * stack.shape[2]
+    block = pl.BlockSpec((x.shape[0], width // 4), lambda i: (0, i))
+    return dense(
+        hidden_kernel,
+        4,
+        [whole(x), pair_of(stack), columns_of(bias)],
+        [block, block],
+        [shaped((x.shape[0], width), BF16)] * 2,
+        [],
+        4 * x.shape[0] * D * width,
+        "project_hidden",
+    )(x, stack, bias)
+
+
+def add_product(left_ref, weight_ref, total, contract):
+    step = pl.program_id(0)
+    half = D // 2
+    for col in range(2):
+        part = mm(left_ref[...], weight_ref[col], contract)
+        span = slice(col * half, (col + 1) * half)
+
+        @pl.when(step == 0)
+        def _():
+            total[:, span] = part
+
+        @pl.when(step > 0)
+        def _():
+            total[:, span] += part
+
+
+ROWS = 128
+
+
+def row_blocks(ref):
+    return [pl.ds(start, ROWS) for start in range(0, ref.shape[0], ROWS)]
+
+
+def norm_parts(value):
+    center = jnp.sum(value, 1, keepdims=True) * (1 / D)
+    squares = jnp.sum(value * value, 1, keepdims=True) * (1 / D)
+    inverse = lax.rsqrt(squares - center * center + EPSILON)
+    return ((value - center) * inverse, inverse)
+
+
+def norm_back(grad, unit, inverse, gain):
+    scaled = grad * gain
+    mean = jnp.sum(scaled, 1, keepdims=True) * (1 / D)
+    paired = jnp.sum(scaled * unit, 1, keepdims=True) * (1 / D)
+    return inverse * (scaled - mean - unit * paired)
+
+
+def total_of(value):
+    return jnp.sum(value, 0, keepdims=True)
+
+
+def first_norm_kernel(heads_ref, weight_ref, x_ref, vec_ref, unit_ref, inverse_ref, low_ref, total):
+    add_product(heads_ref, weight_ref, total, NN)
+
+    @pl.when(pl.program_id(0) == 3)
+    def _():
+        for rows in row_blocks(x_ref):
+            value = x_ref[rows, :].astype(F32) + (total[rows, :] + vec_ref[0:1, :])
+            unit, inverse = norm_parts(value)
+            unit_ref[rows, :] = unit
+            inverse_ref[rows, :] = inverse
+            low_ref[rows, :] = (unit * vec_ref[1:2, :] + vec_ref[2:3, :]).astype(BF16)
+
+
+def first_norm(heads, stack, x, vec):
+    rows = x.shape[0]
+    outs = [shaped((rows, D), F32), shaped((rows, 1), F32), shaped((rows, D), BF16)]
+    return dense(
+        first_norm_kernel,
+        4,
+        [columns_of(heads), pair_of(stack), whole(x), whole(vec)],
+        [whole(out) for out in outs],
+        outs,
+        [pltpu.VMEM((rows, D), F32)],
+        2 * rows * D * D,
+        "first_norm",
+    )(heads, stack, x, vec)
+
+
+def second_norm_kernel(
+    active_ref, weight_ref, unit_ref, incoming_ref, vec_ref, out_ref, back_ref, low_ref, sums_ref, total
+):
+    add_product(active_ref, weight_ref, total, NN)
+
+    @pl.when(pl.program_id(0) == 3)
+    def _():
+        sums = [jnp.zeros((1, D), F32)] * 3
+        for rows in row_blocks(out_ref):
+            middle = unit_ref[rows, :] * vec_ref[1:2, :] + vec_ref[2:3, :]
+            unit, inverse = norm_parts(middle + (total[rows, :] + vec_ref[3:4, :]))
+            out_ref[rows, :] = unit * vec_ref[4:5, :] + vec_ref[5:6, :]
+            grad = incoming_ref[rows, :].astype(F32)
+            back = norm_back(grad, unit, inverse, vec_ref[4:5, :])
+            low = back.astype(BF16)
+            back_ref[rows, :] = back
+            low_ref[rows, :] = low
+            news = [total_of(low.astype(F32)), total_of(grad * unit), total_of(grad)]
+            sums = [old + new for old, new in zip(sums, news)]
+        for place in range(3):
+            sums_ref[place : place + 1, :] = sums[place]
+
+
+def second_norm(active, stack, unit, incoming, vec):
+    rows = unit.shape[0]
+    outs = [shaped((rows, D), F32), shaped((rows, D), F32), shaped((rows, D), BF16), shaped((3, D), F32)]
+    return dense(
+        second_norm_kernel,
+        4,
+        [columns_of(active), pair_of(stack), whole(unit), whole(incoming), whole(vec)],
+        [whole(out) for out in outs],
+        outs,
+        [pltpu.VMEM((rows, D), F32)],
+        2 * rows * D * active.shape[1],
+        "second_norm",
+    )(active, stack, unit, incoming, vec)
+
+
+def first_back_kernel(
+    d_hidden_ref, weight_ref, back_ref, unit_ref, inverse_ref, vec_ref, out_ref, low_ref, sums_ref, total
+):
+    add_product(d_hidden_ref, weight_ref, total, NT)
+
+    @pl.when(pl.program_id(0) == 3)
+    def _():
+        sums = [jnp.zeros((1, D), F32)] * 3
+        for rows in row_blocks(out_ref):
+            grad = back_ref[rows, :] + total[rows, :]
+            unit = unit_ref[rows, :]
+            back = norm_back(grad, unit, inverse_ref[rows, :], vec_ref[1:2, :])
+            low = back.astype(BF16)
+            out_ref[rows, :] = back
+            low_ref[rows, :] = low
+            news = [total_of(low.astype(F32)), total_of(grad * unit), total_of(grad)]
+            sums = [old + new for old, new in zip(sums, news)]
+        for place in range(3):
+            sums_ref[place : place + 1, :] = sums[place]
+
+
+def first_back(d_hidden, stack, back, unit, inverse, vec):
+    rows = unit.shape[0]
+    outs = [shaped((rows, D), F32), shaped((rows, D), BF16), shaped((3, D), F32)]
+    return dense(
+        first_back_kernel,
+        4,
+        [columns_of(d_hidden), pair_of(stack), whole(back), whole(unit), whole(inverse), whole(vec)],
+        [whole(out) for out in outs],
+        outs,
+        [pltpu.VMEM((rows, D), F32)],
+        2 * rows * D * d_hidden.shape[1],
+        "first_back",
+    )(d_hidden, stack, back, unit, inverse, vec)
+
+
+def input_back_kernel(d_qkv_ref, weight_ref, back_ref, out_ref, sums_ref):
+    step = pl.program_id(0)
+    half = D // 2
+    sums_ref[...] = total_of(d_qkv_ref[...].astype(F32))
+    for col in range(2):
+        part = mm(d_qkv_ref[...], weight_ref[col], NT)
+        span = slice(col * half, (col + 1) * half)
+
+        @pl.when(step == 0)
+        def _():
+            out_ref[:, span] = back_ref[:, span] + part
+
+        @pl.when(step > 0)
+        def _():
+            out_ref[:, span] += part
+
+
+def input_back(d_qkv, stack, back):
+    rows, width = d_qkv.shape
+    outs = [shaped((rows, D), F32), shaped((1, width), F32)]
+    return dense(
+        input_back_kernel,
+        4,
+        [columns_of(d_qkv), pair_of(stack), whole(back)],
+        [whole(outs[0]), columns_of(outs[1])],
+        outs,
+        [],
+        2 * rows * D * width,
+        "input_back",
+    )(d_qkv, stack, back)
+
+
+def columns_back(grad_ref, weight_ref, start, stop):
+    half = D // 2
+    return mm(grad_ref[:, :half], weight_ref[0, start:stop, :], NT) + mm(
+        grad_ref[:, half:], weight_ref[1, start:stop, :], NT
+    )
+
+
+def hidden_back_kernel(grad_ref, weight_ref, slope_ref, out_ref, sums_ref):
+    for start in range(0, out_ref.shape[1], 256):
+        span = slice(start, start + 256)
+        part = columns_back(grad_ref, weight_ref, start, start + 256)
+        low = (part * slope_ref[:, span].astype(F32)).astype(BF16)
+        out_ref[:, span] = low
+        sums_ref[:, span] = total_of(low.astype(F32))
+
+
+def hidden_back(grad, stack, slope):
+    outs = [shaped(slope.shape, BF16), shaped((1, slope.shape[1]), F32)]
+    return dense(
+        hidden_back_kernel,
+        4,
+        [whole(grad), pair_of(stack), columns_of(slope)],
+        [columns_of(out) for out in outs],
+        outs,
+        [],
+        2 * grad.shape[0] * D * slope.shape[1],
+        "hidden_back",
+    )(grad, stack, slope)
+
+
+def heads_back_kernel(grad_ref, weight_ref, out_ref):
+    out_ref[...] = columns_back(grad_ref, weight_ref, 0, weight_ref.shape[1]).astype(BF16)
+
+
+def heads_back(grad, stack):
+    return dense(
+        heads_back_kernel,
+        4,
+        [whole(grad), pair_of(stack)],
+        columns_of(grad),
+        shaped(grad.shape, BF16),
+        [],
+        2 * grad.shape[0] * D * D,
+        "heads_back",
+    )(grad, stack)
+
+
+def grad_up_kernel(left_ref, right_ref, out_ref, turned):
+    @pl.when(pl.program_id(0) == 0)
+    def _():
+        turned[...] = left_ref[...].T
+
+    half = D // 2
+    for col in range(2):
+        out_ref[col] = mm(turned[col * half : (col + 1) * half, :], right_ref[...], NN).astype(BF16)
+
+
+def grad_up(left, right):
+    width = right.shape[1] // 4
+    out = shaped((8, D // 2, width), BF16)
+    return dense(
+        grad_up_kernel,
+        4,
+        [whole(left), columns_of(right)],
+        pair_of(out),
+        out,
+        [pltpu.VMEM((D, left.shape[0]), BF16)],
+        2 * left.shape[0] * D * right.shape[1],
+        "grad_up",
+    )(left, right)
+
+
+def grad_down_kernel(left_ref, right_ref, out_ref):
+    half = D // 2
+    turned = left_ref[...].T
+    for col in range(2):
+        out_ref[col] = mm(turned, right_ref[:, col * half : (col + 1) * half], NN).astype(BF16)
+
+
+def grad_down(left, right):
+    width = left.shape[1] // 4
+    out = shaped((8, width, D // 2), BF16)
+    return dense(
+        grad_down_kernel,
+        4,
+        [columns_of(left), whole(right)],
+        pair_of(out),
+        out,
+        [],
+        2 * left.shape[0] * D * left.shape[1],
+        "grad_down",
+    )(left, right)
+
+
 def gather_weight(shard):
     return lax.all_gather(shard, GRID, axis=0, tiled=False)
 
 
-def whole_up(stack):
-    _, depth, width = stack.shape
-    return stack.reshape(4, 2, depth, width).transpose(1, 2, 0, 3).reshape(2 * depth, 4 * width)
-
-
-def whole_down(stack):
-    _, depth, width = stack.shape
-    return stack.reshape(4, 2, depth, width).transpose(0, 2, 1, 3).reshape(4 * depth, 2 * width)
-
-
-def reduce_up(grad):
-    depth, width = grad.shape
-    stack = grad.astype(BF16).reshape(2, depth // 2, 4, width // 4).transpose(2, 0, 1, 3)
-    return reduce_stack(stack.reshape(8, depth // 2, width // 4))
-
-
-def reduce_down(grad):
-    depth, width = grad.shape
-    stack = grad.astype(BF16).reshape(4, depth // 4, 2, width // 2).transpose(0, 2, 1, 3)
-    return reduce_stack(stack.reshape(8, depth // 4, width // 2))
-
-
 def reduce_stack(stack):
-    share = lax.psum_scatter(stack, GRID, scatter_dimension=0, tiled=False)
-    return lax.psum(share, "dp").astype(F32)
-
-
-def norm_forward(value, gain, bias):
-    center = jnp.sum(value, 1, keepdims=True) / D
-    squares = jnp.sum(value * value, 1, keepdims=True) / D
-    inverse = lax.rsqrt(squares - center * center + EPSILON)
-    unit = (value - center) * inverse
-    return (unit * gain + bias, unit, inverse)
-
-
-def norm_backward(grad, unit, inverse, gain):
-    scaled = grad * gain
-    total = jnp.sum(scaled, 1, keepdims=True)
-    paired = jnp.sum(scaled * unit, 1, keepdims=True)
-    back = inverse * (scaled - total / D - unit * (paired / D))
-    return (back, jnp.sum(grad * unit, 0), jnp.sum(grad, 0))
-
-
-def gelu_exact(value):
-    return jax.nn.gelu(value, approximate=False)
+    return lax.psum_scatter(stack, GRID, scatter_dimension=0, tiled=False)
+
+
+def in_three(value):
+    high = lax.reduce_precision(value, 8, 7)
+    rest = value - high
+    mid = lax.reduce_precision(rest, 8, 7)
+    return jnp.stack([high, mid, rest - mid]).astype(BF16)
 
 
 def local(
@@ -231,21 +548,23 @@
     odd = row % 2 == 1
     member = (row % 2) * 2 + col
 
-    qkv_w = whole_up(gather_weight(qkv_weight))
-    out_w = whole_down(gather_weight(out_weight))
-    ff_in_w = whole_up(gather_weight(ff_in_weight))
-    ff_out_w = whole_down(gather_weight(ff_out_weight))
-
     packed = jnp.concatenate(
         [out_bias, ln1_gain, ln1_bias, ff_out_bias, ln2_gain, ln2_bias, ff_in_bias, qv_bias.reshape(-1)]
     )
-    packed = lax.all_gather(packed, GRID, axis=0, tiled=False)
-    vectors = packed[:2, : 6 * 512].reshape(2, 6, 512).transpose(1, 0, 2).reshape(6, D)
-    out_b, gain_one, bias_one, ff_out_b, gain_two, bias_two = [vectors[i] for i in range(6)]
-    ff_in_b = packed[:, 6 * 512 : 7 * 512].reshape(-1)
+    riders = in_three(packed).reshape(15, 768)
+    riders = jnp.concatenate([qkv_weight, riders, jnp.zeros((1, 768), BF16)], 0)
+    qkv_w = gather_weight(riders)
+    out_w = gather_weight(out_weight)
+    ff_in_w = gather_weight(ff_in_weight)
+    ff_out_w = gather_weight(ff_out_weight)
+
+    packed = qkv_w[:, D // 2 : D // 2 + 15].astype(F32).reshape(8, 3, packed.shape[0])
+    packed = (packed[:, 0] + packed[:, 1]) + packed[:, 2]
+    vec = packed[:2, : 6 * 512].reshape(2, 6, 512).transpose(1, 0, 2).reshape(6, D)
+    ff_in_b = packed[:, 6 * 512 : 7 * 512].reshape(1, -1)
     qv_b = packed[:, 7 * 512 :].reshape(-1, 2 * HD)
     hollow = jnp.zeros((qv_b.shape[0], HD), F32)
-    qkv_b = jnp.concatenate([qv_b[:, :HD], hollow, qv_b[:, HD:]], 1).reshape(-1)
+    qkv_b = jnp.concatenate([qv_b[:, :HD], hollow, qv_b[:, HD:]], 1).reshape(1, -1)
 
     x = own_rows(tokens, odd, col)
     incoming = own_rows(out_grad, odd, col)
@@ -257,58 +576,52 @@
         [lax.dynamic_slice_in_dim(shared, (member ^ offset) * QUARTER, QUARTER) for offset in range(4)]
     )
 
-    qkv = (mm(x, qkv_w, NN) + qkv_b).astype(BF16)
+    qkv = project_qkv(x, qkv_w, qkv_b)
     qkv_shared = spread_heads(qkv[SEQ:], member)
-    heads_own, probs_own = attend(qkv[:SEQ], labels)
+    heads_own, probs_own = attend(qkv, labels)
     heads_shared, probs_shared = attend(qkv_shared, shared)
     heads = jnp.concatenate([heads_own, collect_heads(heads_shared, member)], 0)
-    branch_one = mm(heads, out_w, NN) + out_b
-    middle, unit_one, inverse_one = norm_forward(x.astype(F32) + branch_one, gain_one, bias_one)
-    middle_low = middle.astype(BF16)
-    hidden = mm(middle_low, ff_in_w, NN) + ff_in_b
-    gelu_value, pullback = jax.vjp(gelu_exact, hidden)
-    active = gelu_value.astype(BF16)
-    branch_two = mm(active, ff_out_w, NN) + ff_out_b
-    layer_out, unit_two, inverse_two = norm_forward(middle + branch_two, gain_two, bias_two)
+    unit_one, inverse_one, middle_low = first_norm(heads, out_w, x, vec)
+    active, slope = project_hidden(middle_low, ff_in_w, ff_in_b)
+    layer_out, back_two, d_two, sums_two = second_norm(active, ff_out_w, unit_one, incoming, vec)
+
+    ff_out_grad = grad_down(active, d_two)
+    d_two, ff_out_grad = lax.optimization_barrier((d_two, ff_out_grad))
+    ff_out_grad = reduce_stack(ff_out_grad)
     layer_out = give_back(layer_out, odd, col)
-
-    back_two, ln2_gain_part, ln2_bias_part = norm_backward(incoming.astype(F32), unit_two, inverse_two, gain_two)
-    d_two = back_two.astype(BF16)
-    ff_out_bias_part = jnp.sum(d_two, 0, dtype=F32)
-    ff_out_grad = reduce_down(mm(active, d_two, TN))
-    d_hidden = pullback(mm(d_two, ff_out_w, NT))[0].astype(BF16)
-    ff_in_bias_part = jnp.sum(d_hidden, 0, dtype=F32)
-    ff_in_grad = reduce_up(mm(middle_low, d_hidden, TN))
-    back_middle = back_two + mm(d_hidden, ff_in_w, NT)
-    back_one, ln1_gain_part, ln1_bias_part = norm_backward(back_middle, unit_one, inverse_one, gain_one)
-    d_one = back_one.astype(BF16)
-    out_bias_part = jnp.sum(d_one, 0, dtype=F32)
-    out_grad_w = reduce_down(mm(heads, d_one, TN))
-    d_heads = mm(d_one, out_w, NT).astype(BF16)
+    d_hidden, ff_in_bias_part = hidden_back(d_two, ff_out_w, slope)
+    ff_in_grad = grad_up(middle_low, d_hidden)
+    d_hidden, ff_in_grad = lax.optimization_barrier((d_hidden, ff_in_grad))
+    ff_in_grad = reduce_stack(ff_in_grad)
+    back_one, d_one, sums_one = first_back(d_hidden, ff_in_w, back_two, unit_one, inverse_one, vec)
+    out_w_grad = grad_down(heads, d_one)
+    d_one, out_w_grad = lax.optimization_barrier((d_one, out_w_grad))
+    out_w_grad = reduce_stack(out_w_grad)
+    d_heads = heads_back(d_one, out_w)
     d_shared = spread_heads(d_heads[SEQ:], member)
-    d_qkv_own = attend_back(qkv[:SEQ], probs_own, d_heads[:SEQ])
+    d_qkv_own = attend_back(qkv, probs_own, d_heads)
     d_qkv_shared = attend_back(qkv_shared, probs_shared, d_shared)
     d_qkv = jnp.concatenate([d_qkv_own, collect_heads(d_qkv_shared, member)], 0)
-    qkv_grad = reduce_up(mm(x, d_qkv, TN))
-    column_sums = jnp.sum(d_qkv, 0, dtype=F32).reshape(-1, 3, HD)
-    qv_part = jnp.concatenate([column_sums[:, 0], column_sums[:, 2]], 1).reshape(-1)
-    input_grad = give_back(back_one + mm(d_qkv, qkv_w, NT), odd, col)
-
-    sums = lax.psum(
-        jnp.concatenate(
-            [
-                out_bias_part,
-                ln1_gain_part,
-                ln1_bias_part,
-                ff_out_bias_part,
-                ln2_gain_part,
-                ln2_bias_part,
-                ff_in_bias_part,
-                qv_part,
-            ]
-        ),
-        ("dp", "row", "col"),
-    )
+    qkv_grad = grad_up(x, d_qkv)
+    d_qkv, qkv_grad = lax.optimization_barrier((d_qkv, qkv_grad))
+    qkv_grad = reduce_stack(qkv_grad)
+    input_grad, column_sums = input_back(d_qkv, qkv_w, back_one)
+    input_grad = give_back(input_grad, odd, col)
+    column_sums = column_sums.reshape(-1, 3, HD)
+    qv_part = jnp.concatenate([column_sums[:, 0], column_sums[:, 2]], 1)
+
+    ff_out_grad = lax.psum(ff_out_grad, "dp")
+    ff_in_grad, ff_out_grad = lax.optimization_barrier((ff_in_grad, ff_out_grad))
+    ff_in_grad = lax.psum(ff_in_grad, "dp")
+    out_w_grad, ff_in_grad = lax.optimization_barrier((out_w_grad, ff_in_grad))
+    out_w_grad = lax.psum(out_w_grad, "dp")
+    qkv_grad, out_w_grad = lax.optimization_barrier((qkv_grad, out_w_grad))
+    qkv_grad = lax.psum(qkv_grad, "dp")
+
+    sums = jnp.concatenate(
+        [sums_one.reshape(-1), sums_two.reshape(-1), ff_in_bias_part.reshape(-1), qv_part.reshape(-1)]
+    )
+    sums = lax.psum(sums, ("dp", "row", "col"))
     halves = lax.dynamic_slice_in_dim(sums[: 6 * D].reshape(6, 2, D // 2), col, 1, 1)[:, 0]
     place = row * 2 + col
     ff_in_part = lax.dynamic_slice_in_dim(sums, 6 * D + place * 512, 512)
@@ -316,15 +629,15 @@
     return (
         layer_out,
         input_grad,
-        qkv_grad,
+        qkv_grad.astype(F32),
         qv_mine,
-        out_grad_w,
+        out_w_grad.astype(F32),
         halves[0],
         halves[1],
         halves[2],
-        ff_in_grad,
+        ff_in_grad.astype(F32),
         ff_in_part,
-        ff_out_grad,
+        ff_out_grad.astype(F32),
         halves[3],
         halves[4],
         halves[5],

time: 752 us -> 741 us (0.985)
  waiting for transfers between devices: 261 us -> 413 us
  matrix products: 124 us -> 0 us
  Pallas kernels: 32.3 us -> 142 us
  local copies, waits for them, and re-layouts: 159 us -> 51.7 us
  blocking collectives: 105 us -> 58.1 us
    dot_general x12 -> x0, matrix products: 124 us -> none  [mm(): return lax.dot_general(left, right, contract, preferred_element_type=F32)]
    pallas_call x0 -> x12, Pallas kernels: none -> 110 us  [the longest x2 18.4 us: grad_up(): dense(grad_up_kernel, 4, [whole(left), columns_of(right)], pair_of(out),...]
    psum x1 -> x4, waiting for transfers between devices: 49.5 us -> 143 us  [the longest x1 54.2 us: local(): ff_out_grad = lax.psum(ff_out_grad, 'dp')]
    reshape x9 -> x5, local copies, waits for them, and re-layouts: 89.4 us -> 0.38 us  [the longest x1 0.2 us: local(): qkv_w[:, D // 2:D // 2 + 15].astype(F32).reshape(8, 3, packed.shape[0])]
    all_gather x1 -> x0, blocking collectives: 52.2 us -> none  [local(): packed = lax.all_gather(packed, GRID, axis=0, tiled=False)]
    ppermute x2, waiting for transfers between devices: 0.01 us -> 39.5 us  [own_rows(): lax.ppermute(jnp.where(col == 0, second, first), 'col', [(0, 1), (1, 0)])]
    all_gather x4, waiting for transfers between devices: 58.8 us -> 91.1 us  [gather_weight(): return lax.all_gather(shard, GRID, axis=0, tiled=False)]
    transpose x4 -> x0, local copies, waits for them, and re-layouts: 27.5 us -> none  [the longest x2 16 us: reduce_up(): grad.astype(BF16).reshape(2, depth // 2, 4, width // 4)]
  transfers between devices with their start and end apart: 25 -> 28, of which waited for: 12 -> 16; matrix products, arithmetic and copies ran while one was open for 25% -> 5% of each run, Pallas kernels for 4% -> 16%
where the time goes in v2:
time: 741 us; the launch traced here: 727 us
  waiting for transfers between devices  413 us (56%)
  Pallas kernels  142 us (19%)
  blocking collectives  58.1 us (8%)
  local copies, waits for them, and re-layouts  51.7 us (7%)
  other arithmetic  29.7 us (4%)
  starting transfers between devices  16.3 us (2%)
  between operations  15.2 us (2%)
    reduce_scatter x4, waiting for transfers between devices, reduce_stack(): return lax.psum_scatter(stack, GRID, scatter_dimension=0, tiled=False)  129 us
    all_gather x4, waiting for transfers between devices, gather_weight(): return lax.all_gather(shard, GRID, axis=0, tiled=False)  91.1 us
    psum x1, blocking collectives, local(): sums = lax.psum(sums, ('dp', 'row', 'col'))  58.1 us
    psum x1, waiting for transfers between devices, local(): ff_out_grad = lax.psum(ff_out_grad, 'dp')  54.2 us
    ppermute x2, waiting for transfers between devices, own_rows(): lax.ppermute(jnp.where(col == 0, second, first), 'col', [(0, 1), (1, 0)])  39.5 us
    psum x1, waiting for transfers between devices, local(): out_w_grad = lax.psum(out_w_grad, 'dp')  37.7 us
    psum x1, waiting for transfers between devices, local(): qkv_grad = lax.psum(qkv_grad, 'dp')  37.1 us
    unnamed x84, local copies, waits for them, and re-layouts  35.9 us
  transfers between devices with their start and end apart: 28, of which 16 were waited for; matrix products, arithmetic and copies ran while one was open for 5% of the time, Pallas kernels for 16%

profile of v2, /device:TPU:0, one launch (start us, length us, event | category | flops | bytes accessed | tf_op | source)
XLA Modules:
  0.0 726.7 jit_solution(11003633255476164085)
XLA Ops:
  13.0 2.2 maximum_maximum_fusion
  19.9 2.9 collective-permute-start
  24.3 1.7 collective-permute-start.7
  28.1 19.3 %collective-permute-done = bf16[640,512]{1,0:T(8,128)(2,1)} collective-permute-done((bf16[640,512]{1,0:T(8,128)(2,1)}, bf16[640,512]{1,0:T(8,128)(2,1)}, u32[]{:S(2)}, u32[]{:S(2)}) %collective-permute-start) | collective-permute-done | bytes 655392 | tf_op jit(solution)/shard_map/ppermute | solution.py:123
  49.0 20.3 %collective-permute-done.7 = bf16[640,512]{1,0:T(8,128)(2,1)} collective-permute-done((bf16[640,512]{1,0:T(8,128)(2,1)}, bf16[640,512]{1,0:T(8,128)(2,1)}, u32[]{:S(2)}, u32[]{:S(2)}) %collective-permute-start.7) | collective-permute-done | bytes 655392 | tf_op jit(solution)/shard_map/ppermute | solution.py:123
  71.9 7.6 %all-gather.9.cloned.1.call-done = bf16[4224,768]{1,0:T(8,128)(2,1)} async-done(((bf16[528,768]{1,0:T(8,128)(2,1)}), bf16[4224,768]{1,0:T(8,128)(2,1)}) %all-gather.9.cloned.1.call-update) | async-done | bytes 6488080 | tf_op jit(solution)/shard_map/all_gather | solution.py:516
  81.1 6.6 project_qkv.1.qkv_ref
  87.9 1.7 collective-permute-start.3
  90.1 12.2 %attend.2 = (bf16[512,1024]{1,0:T(8,128)(2,1)S(1)}, bf16[16,512,512]{2,1,0:T(8,128)(2,1)S(1)}) custom-call(bf16[640,3072]{1,0:T(8,128)(2,1)S(1)} %project_qkv.1.qkv_ref, s32[512,1]{1,0:T(8,128)S(1)} %copy.31.column_ref, s32[1,512]{1,0:T(1,128)S(1)} %bitcast.54), custom_call_target="tpu_custom_call" | custom-call | flops 4294967296 | bytes 8388608 | tf_op jit(solution)/shard_map/attend/pallas_call | solution.py:52
  102.3 3.3 copy-done.27
  105.7 3.2 attend.3
  110.2 1.8 collective-permute-start.4
  112.6 2.0 collective-permute-done.4
  118.3 7.9 %first_norm.1 = (f32[640,1024]{1,0:T(8,128)}, f32[640,1]{1,0:T(8,128)S(1)}, bf16[640,1024]{1,0:T(8,128)(2,1)S(1)}) custom-call(bf16[640,1024]{1,0:T(8,128)(2,1)S(1)} %pad_maximum_fusion.2.heads_ref.left_ref, bf16[8,256,512]{2,1,0:T(8,128)(2,1)} %bitcast.55, bf16[640,1024]{1,0:T(8,128)(2,1)S(1)} %pad_maximum_fusion.1.x_ref.left_ref, f32[6,1024]{1,0:T(8,128)S(1)} %bitcast.46), custom_call_target="tpu_custom_call" | custom-call | flops 1342177280 | bytes 2097152 | tf_op jit(solution)/shard_map/first_norm/pallas_call | solution.py:303
  127.9 41.9 %all-gather.13.cloned.1.call-done = bf16[4096,1024]{1,0:T(8,128)(2,1)} async-done(((bf16[512,1024]{1,0:T(8,128)(2,1)}), bf16[4096,1024]{1,0:T(8,128)(2,1)}) %all-gather.13.cloned.1.call-update) | async-done | bytes 8388624 | tf_op jit(solution)/shard_map/all_gather | solution.py:516
  171.1 13.2 %project_hidden.1 = (bf16[640,4096]{1,0:T(8,128)(2,1)}, bf16[640,4096]{1,0:T(8,128)(2,1)}) custom-call(bf16[640,1024]{1,0:T(8,128)(2,1)S(1)} %copy-done.15, bf16[8,512,1024]{2,1,0:T(8,128)(2,1)} %bitcast.83, f32[1,4096]{1,0:T(1,128)S(1)} %bitcast.49), custom_call_target="tpu_custom_call" | custom-call | flops 10737418240 | bytes 16777216 | tf_op jit(solution)/shard_map/project_hidden/pallas_call | solution.py:234
  184.3 41.7 %all-gather.15.cloned.1.call-done = bf16[8192,512]{1,0:T(8,128)(2,1)} async-done(((bf16[1024,512]{1,0:T(8,128)(2,1)}), bf16[8192,512]{1,0:T(8,128)(2,1)}) %all-gather.15.cloned.1.call-update) | async-done | bytes 8388624 | tf_op jit(solution)/shard_map/all_gather | solution.py:516
  227.3 15.1 %second_norm.1 = (f32[640,1024]{1,0:T(8,128)S(1)}, f32[640,1024]{1,0:T(8,128)}, bf16[640,1024]{1,0:T(8,128)(2,1)S(1)}, f32[3,1024]{1,0:T(4,128)S(1)}) custom-call(bf16[640,4096]{1,0:T(8,128)(2,1)} %get-tuple-element.51.active_ref.left_ref, bf16[8,1024,512]{2,1,0:T(8,128)(2,1)} %bitcast.85, f32[640,1024]{1,0:T(8,128)} %get-tuple-element.52.unit_ref, ...), custom_call_target="tpu_custom_call" | custom-call | flops 5368709120 | bytes 8388608 | tf_op jit(solution)/shard_map/second_norm/pallas_call | solution.py:341
  242.4 10.3 %grad_down.2 = bf16[8,1024,512]{2,1,0:T(8,128)(2,1)} custom-call(bf16[640,4096]{1,0:T(8,128)(2,1)} %get-tuple-element.51.active_ref.left_ref, bf16[640,1024]{1,0:T(8,128)(2,1)S(1)} %get-tuple-element.56.right_ref.grad_ref), custom_call_target="tpu_custom_call" | custom-call | flops 5368709120 | bytes 8388608 | tf_op jit(solution)/shard_map/grad_down/pallas_call | solution.py:503
  255.1 11.6 %hidden_back.1 = (bf16[640,4096]{1,0:T(8,128)(2,1)}, f32[1,4096]{1,0:T(1,128)S(1)}) custom-call(bf16[640,1024]{1,0:T(8,128)(2,1)S(1)} %copy-done.24, bf16[8,1024,512]{2,1,0:T(8,128)(2,1)} %bitcast.86, bf16[640,4096]{1,0:T(8,128)(2,1)} %get-tuple-element.57.slope_ref), custom_call_target="tpu_custom_call" | custom-call | flops 5368709120 | bytes 8388608 | tf_op jit(solution)/shard_map/hidden_back/pallas_call | solution.py:439
  266.6 10.9 %grad_up.2 = bf16[8,512,1024]{2,1,0:T(8,128)(2,1)} custom-call(bf16[640,1024]{1,0:T(8,128)(2,1)S(1)} %copy-done.16, bf16[640,4096]{1,0:T(8,128)(2,1)} %get-tuple-element.59.right_ref.d_hidden_ref), custom_call_target="tpu_custom_call" | custom-call | flops 5368709120 | bytes 8388608 | tf_op jit(solution)/shard_map/grad_up/pallas_call | solution.py:481
  277.6 47.5 %reduce-scatter.11.cloned.1.call-done = bf16[1,1024,512]{2,1,0:T(8,128)(2,1)} async-done(((bf16[8,1024,512]{2,1,0:T(8,128)(2,1)}), bf16[1,1024,512]{2,1,0:T(8,128)(2,1)}) %reduce-scatter.11.cloned.1.call-update) | async-done | bytes 1048592 | tf_op jit(solution)/shard_map/reduce_scatter | solution.py:520
  326.2 13.6 %first_back.1 = (f32[640,1024]{1,0:T(8,128)S(1)}, bf16[640,1024]{1,0:T(8,128)(2,1)S(1)}, f32[3,1024]{1,0:T(4,128)S(1)}) custom-call(bf16[640,4096]{1,0:T(8,128)(2,1)} %get-tuple-element.59.right_ref.d_hidden_ref, bf16[8,512,1024]{2,1,0:T(8,128)(2,1)} %bitcast.84, f32[640,1024]{1,0:T(8,128)} %get-tuple-element.60.back_ref, ...), custom_call_target="tpu_custom_call" | custom-call | flops 5368709120 | bytes 8388608 | tf_op jit(solution)/shard_map/first_back/pallas_call | solution.py:377
  341.3 2.6 grad_down.3
  346.5 1.6 copy-done.13
  349.4 2.3 heads_back.1.grad_ref
  354.0 2.7 collective-permute-done.11
  356.7 2.8 collective-permute-done.9
  359.6 3.4 attend_back.3
  363.8 2.5 collective-permute-start.12
  366.3 3.7 copy-done.28
  370.0 13.4 %attend_back.2 = bf16[512,3072]{1,0:T(8,128)(2,1)S(1)} custom-call(bf16[640,3072]{1,0:T(8,128)(2,1)S(1)} %copy-done.12, bf16[16,512,512]{2,1,0:T(8,128)(2,1)S(1)} %copy-done.28, bf16[640,1024]{1,0:T(8,128)(2,1)S(1)} %heads_back.1.grad_ref), custom_call_target="tpu_custom_call" | custom-call | flops 10737418240 | bytes 8388608 | tf_op jit(solution)/shard_map/attend_back/pallas_call | solution.py:100
  383.4 1.7 copy-done.3
  385.1 21.0 %reduce-scatter.9.cloned.1.call-done = bf16[1,512,1024]{2,1,0:T(8,128)(2,1)} async-done(((bf16[8,512,1024]{2,1,0:T(8,128)(2,1)}), bf16[1,512,1024]{2,1,0:T(8,128)(2,1)}) %reduce-scatter.9.cloned.1.call-update) | async-done | bytes 1048592 | tf_op jit(solution)/shard_map/reduce_scatter | solution.py:520
  406.2 54.2 %all-reduce.5.cloned.1.call-done = bf16[1024,512]{1,0:T(8,128)(2,1)} async-done(((bf16[1024,512]{1,0:T(8,128)(2,1)}), bf16[1024,512]{1,0:T(8,128)(2,1)}) %all-reduce.5.cloned.1.call-update) | async-done | bytes 1048592 | tf_op jit(solution)/shard_map/psum | solution.py:613
  463.3 2.3 pad_maximum_fusion.right_ref.d_qkv_ref
  465.6 7.5 %grad_up.3 = bf16[8,512,768]{2,1,0:T(8,128)(2,1)} custom-call(bf16[640,1024]{1,0:T(8,128)(2,1)S(1)} %copy-done.6, bf16[640,3072]{1,0:T(8,128)(2,1)S(1)} %pad_maximum_fusion.right_ref.d_qkv_ref), custom_call_target="tpu_custom_call" | custom-call | flops 4026531840 | bytes 6291456 | tf_op jit(solution)/shard_map/grad_up/pallas_call | solution.py:481
  473.1 2.0 copy-done.2
  477.6 1.7 copy-done.22
  479.3 8.7 %input_back.1 = (f32[640,1024]{1,0:T(8,128)S(1)}, f32[1,3072]{1,0:T(1,128)S(1)}) custom-call(bf16[640,3072]{1,0:T(8,128)(2,1)} %copy-done.2, bf16[8,528,768]{2,1,0:T(8,128)(2,1)} %bitcast.68, f32[640,1024]{1,0:T(8,128)S(1)} %copy-done.22), custom_call_target="tpu_custom_call" | custom-call | flops 4026531840 | bytes 6291456 | tf_op jit(solution)/shard_map/input_back/pallas_call | solution.py:409
  492.3 58.1 %psum.39 = f32[12288]{0:T(1024)S(1)} all-reduce(f32[12288]{0:T(1024)S(1)} %pad_maximum_fusion.10), channel_id=1, replica_groups=mesh['dp'=4,'row'=4,'col'=2] {'dp','row','col'}, use_global_device_ids=true, to_apply=%region_8.9 | all-reduce | flops 12288 | bytes 98304 | tf_op jit(solution)/shard_map/psum | solution.py:624
  555.5 13.6 %all-reduce.7.cloned.1.call-done = bf16[512,1024]{1,0:T(8,128)(2,1)} async-done(((bf16[512,1024]{1,0:T(8,128)(2,1)}), bf16[512,1024]{1,0:T(8,128)(2,1)}) %all-reduce.7.cloned.1.call-update) | async-done | bytes 1048592 | tf_op jit(solution)/shard_map/psum | solution.py:615
  573.2 60.6 %reduce-scatter.5.cloned.1.call-done = bf16[1,512,768]{2,1,0:T(8,128)(2,1)} async-done(((bf16[8,512,768]{2,1,0:T(8,128)(2,1)}), bf16[1,512,768]{2,1,0:T(8,128)(2,1)}) %reduce-scatter.5.cloned.1.call-update) | async-done | bytes 786448 | tf_op jit(solution)/shard_map/reduce_scatter | solution.py:520
  633.8 37.7 %all-reduce.9.cloned.1.call-done = bf16[256,512]{1,0:T(8,128)(2,1)} async-done(((bf16[256,512]{1,0:T(8,128)(2,1)}), bf16[256,512]{1,0:T(8,128)(2,1)}) %all-reduce.9.cloned.1.call-update) | async-done | bytes 262160 | tf_op jit(solution)/shard_map/psum | solution.py:617
  671.6 4.5 maximum_select_fusion
  676.1 1.6 convert_element_type.38
  680.2 37.1 %all-reduce.11.cloned.1.call-done = bf16[512,768]{1,0:T(8,128)(2,1)} async-done(((bf16[512,768]{1,0:T(8,128)(2,1)}), bf16[512,768]{1,0:T(8,128)(2,1)}) %all-reduce.11.cloned.1.call-update) | async-done | bytes 786448 | tf_op jit(solution)/shard_map/psum | solution.py:619
  717.3 2.4 convert_element_type.35
  (212 shorter events, 63.8 us)
Async XLA Ops:
  7.2 72.3 %all-gather.9.cloned.1.call-start = ((), (), s32[]{:S(2)}) async-start(), calls=%async_computation.12 | async-start | bytes 7299072 | tf_op jit(solution)/shard_map/all_gather | solution.py:516
  15.2 103.1 %all-gather.11.cloned.1.call-start = ((), (), s32[]{:S(2)}) async-start(), calls=%async_computation.13 | async-start | bytes 2359296 | tf_op jit(solution)/shard_map/all_gather | solution.py:516
  16.0 153.9 %all-gather.13.cloned.1.call-start = ((), (), s32[]{:S(2)}) async-start(), calls=%async_computation.14 | async-start | bytes 9437184 | tf_op jit(solution)/shard_map/all_gather | solution.py:516
  16.7 209.3 %all-gather.15.cloned.1.call-start = ((), (), s32[]{:S(2)}) async-start(), calls=%async_computation.15 | async-start | bytes 9437184 | tf_op jit(solution)/shard_map/all_gather | solution.py:516
  17.3 307.8 %reduce-scatter.11.cloned.1.call-start = ((), (), s32[]{:S(2)}) async-start(), calls=%async_computation.7 | async-start | bytes 9437184 | tf_op jit(solution)/shard_map/reduce_scatter | solution.py:520
  19.9 2.9 copy-start.30
  19.9 2.9 slice-start.2
  19.9 2.9 slice-start.3
  19.9 27.5 %collective-permute-start = (bf16[640,512]{1,0:T(8,128)(2,1)}, bf16[640,512]{1,0:T(8,128)(2,1)}, u32[]{:S(2)}, u32[]{:S(2)}) collective-permute-start(bf16[640,512]{1,0:T(8,128)(2,1)} %broadcast_select_fusion.6), channel_id=1, source_target_pairs={{0,1},{1,0},{2,3},{3,2},{4,5},{5,4},{6,7},{7,6},{8,9},{9,8},{10,11... | collective-permute-start | bytes 1966088 | tf_op jit(solution)/shard_map/ppermute | solution.py:123
  24.3 44.9 %collective-permute-start.7 = (bf16[640,512]{1,0:T(8,128)(2,1)}, bf16[640,512]{1,0:T(8,128)(2,1)}, u32[]{:S(2)}, u32[]{:S(2)}) collective-permute-start(bf16[640,512]{1,0:T(8,128)(2,1)} %broadcast_select_fusion.2), channel_id=1, source_target_pairs={{0,1},{1,0},{2,3},{3,2},{4,5},{5,4},{6,7},{7,6},{8,9},{9,8},{10,11... | collective-permute-start | bytes 1966088 | tf_op jit(solution)/shard_map/ppermute | solution.py:123
  49.0 69.3 %copy-start.5 = (bf16[640,1024]{1,0:T(8,128)(2,1)}, bf16[640,1024]{1,0:T(8,128)(2,1)S(1)}, u32[]{:S(2)}) copy-start(bf16[640,1024]{1,0:T(8,128)(2,1)S(1)} %pad_maximum_fusion.1.x_ref.left_ref) | copy-start | bytes 3932164
  87.7 14.5 %copy-start.11 = (bf16[640,3072]{1,0:T(8,128)(2,1)}, bf16[640,3072]{1,0:T(8,128)(2,1)S(1)}, u32[]{:S(2)}) copy-start(bf16[640,3072]{1,0:T(8,128)(2,1)S(1)} %project_qkv.1.qkv_ref) | copy-start | bytes 11796484
  87.9 17.7 %collective-permute-start.3 = (bf16[128,768]{1,0:T(8,128)(2,1)S(1)}, bf16[128,768]{1,0:T(8,128)(2,1)S(1)}, u32[]{:S(2)}, u32[]{:S(2)}) collective-permute-start(bf16[128,768]{1,0:T(8,128)(2,1)S(1)} %get-tuple-element.103), channel_id=1, source_target_pairs={{0,3},{1,2},{2,1},{3,0},{4,7},{5,6},{6,5},{7,4},{8,11},{9,10},{10,... | collective-permute-start | bytes 589832 | tf_op jit(solution)/shard_map/ppermute | solution.py:147
  89.5 16.1 %collective-permute-start.2 = (bf16[128,768]{1,0:T(8,128)(2,1)S(1)}, bf16[128,768]{1,0:T(8,128)(2,1)S(1)}, u32[]{:S(2)}, u32[]{:S(2)}) collective-permute-start(bf16[128,768]{1,0:T(8,128)(2,1)S(1)} %get-tuple-element.104), channel_id=1, source_target_pairs={{0,2},{1,3},{2,0},{3,1},{4,6},{5,7},{6,4},{7,5},{8,10},{9,11},{10,... | collective-permute-start | bytes 589832 | tf_op jit(solution)/shard_map/ppermute | solution.py:147
  89.8 15.8 %collective-permute-start.1 = (bf16[128,768]{1,0:T(8,128)(2,1)S(1)}, bf16[128,768]{1,0:T(8,128)(2,1)S(1)}, u32[]{:S(2)}, u32[]{:S(2)}) collective-permute-start(bf16[128,768]{1,0:T(8,128)(2,1)S(1)} %get-tuple-element.105), channel_id=1, source_target_pairs={{0,1},{1,0},{2,3},{3,2},{4,5},{5,4},{6,7},{7,6},{8,9},{9,8},{10,11... | collective-permute-start | bytes 589832 | tf_op jit(solution)/shard_map/ppermute | solution.py:147
  102.3 3.3 copy-start.27
  105.6 3.3 copy-start.10
  110.2 4.3 collective-permute-start.4
  112.1 2.5 collective-permute-start.5
  112.2 3.9 collective-permute-start.6
  118.2 7.9 %copy-start.8 = (bf16[640,1024]{1,0:T(8,128)(2,1)}, bf16[640,1024]{1,0:T(8,128)(2,1)S(1)}, u32[]{:S(2)}) copy-start(bf16[640,1024]{1,0:T(8,128)(2,1)S(1)} %pad_maximum_fusion.2.heads_ref.left_ref) | copy-start | bytes 3932164
  253.7 152.5 %reduce-scatter.9.cloned.1.call-start = ((), (), s32[]{:S(2)}) async-start(), calls=%async_computation.6 | async-start | bytes 9437184 | tf_op jit(solution)/shard_map/reduce_scatter | solution.py:520
  255.1 11.6 %copy-start.16 = (bf16[640,1024]{1,0:T(8,128)(2,1)S(1)}, bf16[640,1024]{1,0:T(8,128)(2,1)}, u32[]{:S(2)}) copy-start(bf16[640,1024]{1,0:T(8,128)(2,1)} %copy-done.14) | copy-start | bytes 3932164
  277.6 182.8 %all-reduce.5.cloned.1.call-start = ((), (), s32[]{:S(2)}) async-start(), calls=%async_computation.8 | async-start | bytes 2097152 | tf_op jit(solution)/shard_map/psum | solution.py:613
  325.2 230.3 %reduce-scatter.7.cloned.1.call-start = ((), (), s32[]{:S(2)}) async-start(), calls=%async_computation.5 | async-start | bytes 2359296 | tf_op jit(solution)/shard_map/reduce_scatter | solution.py:520
  326.2 15.1 %copy-start.9 = (bf16[640,1024]{1,0:T(8,128)(2,1)S(1)}, bf16[640,1024]{1,0:T(8,128)(2,1)}, u32[]{:S(2)}) copy-start(bf16[640,1024]{1,0:T(8,128)(2,1)} %copy-done.8) | copy-start | bytes 3932164
  346.3 222.8 %all-reduce.7.cloned.1.call-start = ((), (), s32[]{:S(2)}) async-start(), calls=%async_computation.9 | async-start | bytes 2097152 | tf_op jit(solution)/shard_map/psum | solution.py:615
  349.4 10.1 %copy-start.26 = (bf16[4,512,512]{2,1,0:T(8,128)(2,1)S(1)}, bf16[4,512,512]{2,1,0:T(8,128)(2,1)}, u32[]{:S(2)}) copy-start(bf16[4,512,512]{2,1,0:T(8,128)(2,1)} %copy-done.25) | copy-start | bytes 6291460
  351.8 4.9 collective-permute-start.11
  353.0 3.6 collective-permute-start.10
  353.7 5.8 collective-permute-start.9
  359.6 6.8 copy-start.12
  363.8 96.6 %collective-permute-start.12 = (bf16[128,768]{1,0:T(8,128)(2,1)}, bf16[128,768]{1,0:T(8,128)(2,1)}, u32[]{:S(2)}, u32[]{:S(2)}) collective-permute-start(bf16[128,768]{1,0:T(8,128)(2,1)} %get-tuple-element.100), channel_id=1, source_target_pairs={{0,1},{1,0},{2,3},{3,2},{4,5},{5,4},{6,7},{7,6},{8,9},{9,8},{10,11... | collective-permute-start | bytes 589832 | tf_op jit(solution)/shard_map/ppermute | solution.py:157
  366.3 95.1 %collective-permute-start.13 = (bf16[128,768]{1,0:T(8,128)(2,1)}, bf16[128,768]{1,0:T(8,128)(2,1)}, u32[]{:S(2)}, u32[]{:S(2)}) collective-permute-start(bf16[128,768]{1,0:T(8,128)(2,1)} %get-tuple-element.99), channel_id=1, source_target_pairs={{0,2},{1,3},{2,0},{3,1},{4,6},{5,7},{6,4},{7,5},{8,10},{9,11},{10,... | collective-permute-start | bytes 589832 | tf_op jit(solution)/shard_map/ppermute | solution.py:157
  366.3 3.7 copy-start.28
  385.0 77.3 %collective-permute-start.14 = (bf16[128,768]{1,0:T(8,128)(2,1)}, bf16[128,768]{1,0:T(8,128)(2,1)}, u32[]{:S(2)}, u32[]{:S(2)}) collective-permute-start(bf16[128,768]{1,0:T(8,128)(2,1)} %get-tuple-element.98), channel_id=1, source_target_pairs={{0,3},{1,2},{2,1},{3,0},{4,7},{5,6},{6,5},{7,4},{8,11},{9,10},{10,... | collective-permute-start | bytes 589832 | tf_op jit(solution)/shard_map/ppermute | solution.py:157
  460.4 173.4 %reduce-scatter.5.cloned.1.call-start = ((), (), s32[]{:S(2)}) async-start(), calls=%async_computation.4 | async-start | bytes 7077888 | tf_op jit(solution)/shard_map/reduce_scatter | solution.py:520
  463.3 2.3 copy-start.6
  473.1 2.0 copy-start.2
  475.1 196.5 %all-reduce.9.cloned.1.call-start = ((), (), s32[]{:S(2)}) async-start(), calls=%async_computation.10 | async-start | bytes 524288 | tf_op jit(solution)/shard_map/psum | solution.py:617
  476.1 76.2 %collective-permute-start.8 = (bf16[640,512]{1,0:T(8,128)(2,1)}, bf16[640,512]{1,0:T(8,128)(2,1)S(1)}, u32[]{:S(2)}, u32[]{:S(2)}) collective-permute-start(bf16[640,512]{1,0:T(8,128)(2,1)} %select_convert_fusion.1), channel_id=1, source_target_pairs={{0,1},{1,0},{2,3},{3,2},{4,5},{5,4},{6,7},{7,6},{8,9},{9,8},{10,11... | collective-permute-start | bytes 1966088 | tf_op jit(solution)/shard_map/ppermute | solution.py:131
  477.6 1.7 copy-start.22
  490.5 78.6 %collective-permute-start.15 = (bf16[640,512]{1,0:T(8,128)(2,1)}, bf16[640,512]{1,0:T(8,128)(2,1)}, u32[]{:S(2)}, u32[]{:S(2)}) collective-permute-start(bf16[640,512]{1,0:T(8,128)(2,1)} %select_convert_fusion), channel_id=1, source_target_pairs={{0,1},{1,0},{2,3},{3,2},{4,5},{5,4},{6,7},{7,6},{8,9},{9,8},{10,11... | collective-permute-start | bytes 1966088 | tf_op jit(solution)/shard_map/ppermute | solution.py:131
  553.7 15.4 %copy-start.1 = (f32[640,1024]{1,0:T(8,128)S(1)}, f32[640,1024]{1,0:T(8,128)}, u32[]{:S(2)}) copy-start(f32[640,1024]{1,0:T(8,128)} %copy-done) | copy-start | bytes 7864324
  569.1 148.2 %all-reduce.11.cloned.1.call-start = ((), (), s32[]{:S(2)}) async-start(), calls=%async_computation.11 | async-start | bytes 1572864 | tf_op jit(solution)/shard_map/psum | solution.py:619
  571.4 100.1 %copy-start.31 = (f32[512,512]{1,0:T(8,128)S(1)}, f32[512,512]{1,0:T(8,128)}, u32[]{:S(2)}) copy-start(f32[512,512]{1,0:T(8,128)} %slice.262) | copy-start | bytes 3145732
  571.4 100.1 %copy-start.32 = (f32[512,512]{1,0:T(8,128)S(1)}, f32[512,512]{1,0:T(8,128)}, u32[]{:S(2)}) copy-start(f32[512,512]{1,0:T(8,128)} %slice.261) | copy-start | bytes 3145732
  671.6 4.6 copy-start.33
  (21 other events, 27.6 us)
Sparse Core Ops, SparseCore 0:
  15.3 64.1 all-gather.8
  81.4 32.0 all-gather.10
  115.4 54.3 all-gather.12
  171.6 54.3 all-gather.14
  253.8 71.2 reduce-scatter.10
  328.8 77.2 reduce-scatter.8
  408.5 51.7 all-reduce.4
  464.6 49.1 reduce-scatter.6
  516.2 52.8 all-reduce.6
  572.7 61.1 reduce-scatter.4
  636.2 35.3 all-reduce.8
  673.9 43.3 all-reduce.10

commit v3 on v2

v3 whole, which is shorter than its diff:
```python
import functools
import math

import jax
import jax.numpy as jnp
from jax import lax
from jax.experimental import pallas as pl
from jax.experimental.pallas import tpu as pltpu
from jax.sharding import PartitionSpec as P

D = 1024
HD = 64
SEQ = 512
QUARTER = SEQ // 4
GRID = ("row", "col")

EPSILON = 1e-06
NEGATIVE = -1e30
F32 = jnp.float32
BF16 = jnp.bfloat16
NN = (((1,), (0,)), ((), ()))
NT = (((1,), (1,)), ((), ()))
TN = (((0,), (0,)), ((), ()))
MIB = 1 << 20


def mm(left, right, contract):
    return lax.dot_general(left, right, contract, preferred_element_type=F32)


def attend_kernel(qkv_ref, column_ref, line_ref, heads_ref, probs_ref, mask):
    @pl.when(pl.program_id(0) == 0)
    def _():
        mask[...] = jnp.where(column_ref[...] == line_ref[...], 0.0, NEGATIVE)

    mixed = []
    for head in range(2):
        base = head * 3 * HD
        query = qkv_ref[:, base : base + HD] * jnp.asarray(1 / math.sqrt(HD), BF16)
        key = qkv_ref[:, base + HD : base + 2 * HD]
        value = qkv_ref[:, base + 2 * HD : base + 3 * HD]
        scores = mm(key, query, NT) + mask[...]
        powers = jnp.exp(scores - jnp.max(scores, 0, keepdims=True))
        total = jnp.sum(powers, 0, keepdims=True)
        probs = (powers * (1.0 / total)).astype(BF16)
        probs_ref[head] = probs
        mixed.append(mm(value, probs, TN))
    heads_ref[...] = jnp.concatenate(mixed, 0).T.astype(BF16)


def attend(qkv, labels):
    pairs = qkv.shape[1] // (6 * HD)
    return pl.pallas_call(
        attend_kernel,
        grid=(pairs,),
        in_specs=[
            pl.BlockSpec((SEQ, 6 * HD), lambda i: (0, i)),
            pl.BlockSpec((SEQ, 1), lambda i: (0, 0)),
            pl.BlockSpec((1, SEQ), lambda i: (0, 0)),
        ],
        out_specs=[
            pl.BlockSpec((SEQ, 2 * HD), lambda i: (0, i)),
            pl.BlockSpec((2, SEQ, SEQ), lambda i: (i, 0, 0)),
        ],
        out_shape=[
            jax.ShapeDtypeStruct((SEQ, pairs * 2 * HD), BF16),
            jax.ShapeDtypeStruct((pairs * 2, SEQ, SEQ), BF16),
        ],
        scratch_shapes=[pltpu.VMEM((SEQ, SEQ), F32)],
        compiler_params=pltpu.CompilerParams(vmem_limit_bytes=32 * MIB),
        cost_estimate=pl.CostEstimate(
            flops=pairs * 2 * 4 * SEQ * SEQ * 256, bytes_accessed=pairs * 2 * SEQ * SEQ * 2, transcendentals=pairs * 2 * SEQ * SEQ
        ),
        name="attend",
    )(qkv, labels[:, None], labels[None, :])


def attend_back_kernel(qkv_ref, probs_ref, grad_ref, out_ref):
    for head in range(2):
        base = head * 3 * HD
        scale = jnp.asarray(1 / math.sqrt(HD), BF16)
        query = qkv_ref[:, base : base + HD] * scale
        key = qkv_ref[:, base + HD : base + 2 * HD] * scale
        value = qkv_ref[:, base + 2 * HD : base + 3 * HD]
        grad = grad_ref[:, head * HD : (head + 1) * HD]
        probs = probs_ref[head]
        d_value = mm(probs, grad, NN)
        d_probs = mm(value, grad, NT)
        wide = probs.astype(F32)
        delta = jnp.sum(wide * d_probs, 0, keepdims=True)
        d_scores = (wide * (d_probs - delta)).astype(BF16)
        d_key = mm(d_scores, query, NN)
        d_query = mm(key, d_scores, TN).T
        out_ref[:, base : base + HD] = d_query.astype(BF16)
        out_ref[:, base + HD : base + 2 * HD] = d_key.astype(BF16)
        out_ref[:, base + 2 * HD : base + 3 * HD] = d_value.astype(BF16)


def attend_back(qkv, probs, grad):
    pairs = qkv.shape[1] // (6 * HD)
    return pl.pallas_call(
        attend_back_kernel,
        grid=(pairs,),
        in_specs=[
            pl.BlockSpec((SEQ, 6 * HD), lambda i: (0, i)),
            pl.BlockSpec((2, SEQ, SEQ), lambda i: (i, 0, 0)),
            pl.BlockSpec((SEQ, 2 * HD), lambda i: (0, i)),
        ],
        out_specs=pl.BlockSpec((SEQ, 6 * HD), lambda i: (0, i)),
        out_shape=jax.ShapeDtypeStruct((SEQ, qkv.shape[1]), BF16),
        compiler_params=pltpu.CompilerParams(vmem_limit_bytes=32 * MIB),
        cost_estimate=pl.CostEstimate(
            flops=pairs * 2 * 10 * SEQ * SEQ * 256, bytes_accessed=pairs * 2 * SEQ * SEQ * 2, transcendentals=0
        ),
        name="attend_back",
    )(qkv, probs, grad)


def swap_core(value):
    return lax.ppermute(value, "row", [(i, i ^ 1) for i in range(4)])


def swap_row(value):
    return lax.ppermute(value, "row", [(i, i ^ 2) for i in range(4)])


def swap_col(value):
    return lax.ppermute(value, "col", [(0, 1), (1, 0)])


def after(value, *others):
    return lax.optimization_barrier((value, *others))[0]


def add(*values):
    total = values[0].astype(F32)
    for value in values[1:]:
        total = total + value.astype(F32)
    return total.astype(BF16)


def own_rows(value, odd, col):
    rolled = jnp.where(odd, jnp.roll(value, -2 * QUARTER, 0), value)
    first = jnp.concatenate([rolled[:SEQ], rolled[2 * SEQ : 2 * SEQ + QUARTER]], 0)
    second = jnp.concatenate([rolled[SEQ : 2 * SEQ], rolled[2 * SEQ + QUARTER :]], 0)
    mine = jnp.where(col == 0, first, second)
    return jnp.concatenate([mine, swap_col(jnp.where(col == 0, second, first))], 1)


def give_back(mine, leaving, odd, col):
    other = swap_col(leaving).astype(F32)
    first = jnp.where(col == 0, mine, other)
    second = jnp.where(col == 0, other, mine)
    rolled = jnp.concatenate([first[:SEQ], second[:SEQ], first[SEQ:], second[SEQ:]], 0)
    return jnp.where(odd, jnp.roll(rolled, 2 * QUARTER, 0), rolled)


def swap(offset):
    return [(i, i ^ offset) for i in range(8)]


def spread_heads(value, member, row):
    width = value.shape[1] // 4
    pieces = []
    for offset in range(4):
        piece = lax.dynamic_slice_in_dim(value, ((member ^ offset) ^ row) * width, width, 1)
        pieces.append(piece if offset == 0 else lax.ppermute(piece, GRID, swap(offset)))
    return jnp.concatenate(pieces, 0)


def collect_heads(value, member, row):
    width = value.shape[1]
    whole = jnp.zeros((QUARTER, 4 * width), value.dtype)
    for offset in range(4):
        piece = value[offset * QUARTER : (offset + 1) * QUARTER]
        if offset:
            piece = lax.ppermute(piece, GRID, swap(offset))
        whole = lax.dynamic_update_slice_in_dim(whole, piece, ((member ^ offset) ^ row) * width, 1)
    return whole


class Shards:
    def __init__(self, shard, depth):
        half = depth // 2
        self.depth, self.width = depth, shard.shape[1]
        beside = swap_col(shard)
        across = swap_row(shard)
        top, bottom = swap_col(across[:half]), swap_row(beside[half:])
        self.first = (beside, across)
        near = [(0, 0, shard), (1, 0, beside), (4, 0, across), (5, 0, top), (5, half, bottom)]
        far = [(place + 2, start, swap_core(part)) for place, start, part in near]
        self.parts = near + far

    def riders(self):
        found = {}
        for place, start, part in self.parts:
            if start + part.shape[0] > self.depth:
                found[place] = part[self.depth - start :]
        return jnp.stack([found[place] for place in range(8)])


def dense(kernel, in_specs, out_specs, out_shape, scratch, flops, name, shards=None):
    if shards is None:
        body, extra_specs, extra_scratch = kernel, [], []
    else:
        places = [(place, start, min(part.shape[0], shards.depth - start)) for place, start, part in shards.parts]
        count = len(places)
        extra_specs = [pl.BlockSpec(memory_space=pl.ANY)] * count
        extra_scratch = [
            pltpu.VMEM((8, shards.depth, shards.width), BF16),
            pltpu.SemaphoreType.DMA((count,)),
        ]

        def body(*refs):
            step = pl.program_id(0)
            held, done = refs[-2:]
            copies = [
                pltpu.make_async_copy(
                    refs[k].at[pl.ds(0, rows)], held.at[place, pl.ds(start, rows)], done.at[k]
                )
                for k, (place, start, rows) in enumerate(places)
            ]
            for block in range(4):

                @pl.when(step == 0)
                def _():
                    for copy, (place, _, _) in zip(copies, places):
                        if place // 2 == block:
                            copy.start()

            for block in range(4):

                @pl.when(step == block)
                def _():
                    for copy, (place, _, _) in zip(copies, places):
                        if place // 2 == block:
                            copy.wait()

            kernel(held.at[pl.ds(2 * step, 2)], *refs[count:-2])

    return pl.pallas_call(
        body,
        grid=(4,),
        in_specs=extra_specs + in_specs,
        out_specs=out_specs,
        out_shape=out_shape,
        scratch_shapes=scratch + extra_scratch,
        compiler_params=pltpu.CompilerParams(vmem_limit_bytes=48 * MIB),
        cost_estimate=pl.CostEstimate(flops=flops, bytes_accessed=flops // 640, transcendentals=0),
        name=name,
    )


def whole(value):
    return pl.BlockSpec(value.shape, lambda i: (0,) * value.ndim)


def columns_of(value, parts=4):
    return pl.BlockSpec((value.shape[0], value.shape[1] // parts), lambda i: (0, i))


def shaped(shape, kind):
    return jax.ShapeDtypeStruct(shape, kind)


def halves_times(left_ref, weight_ref, start, width):
    half = left_ref.shape[1] // 2
    stop = start + width
    return mm(left_ref[:, :half], weight_ref[0, :, start:stop], NN) + mm(
        left_ref[:, half:], weight_ref[1, :, start:stop], NN
    )


def qkv_kernel(weight_ref, x_ref, bias_ref, out_ref):
    for start in range(0, out_ref.shape[1], 256):
        part = halves_times(x_ref, weight_ref, start, 256)
        out_ref[:, start : start + 256] = (part + bias_ref[:, start : start + 256]).astype(BF16)


def project_qkv(x, shards, bias):
    width = 4 * shards.width
    return dense(
        qkv_kernel,
        [whole(x), columns_of(bias)],
        pl.BlockSpec((x.shape[0], width // 4), lambda i: (0, i)),
        shaped((x.shape[0], width), BF16),
        [],
        2 * x.shape[0] * D * width,
        "project_qkv",
        shards,
    )(*[part for _, _, part in shards.parts], x, bias)


def hidden_kernel(weight_ref, x_ref, bias_ref, active_ref, slope_ref):
    for start in range(0, active_ref.shape[1], 256):
        stop = start + 256
        hidden = halves_times(x_ref, weight_ref, start, 256) + bias_ref[:, start:stop]
        share = 0.5 * (1.0 + lax.erf(hidden * math.sqrt(0.5)))
        bell = jnp.exp(hidden * hidden * -0.5) * (1 / math.sqrt(2 * math.pi))
        active_ref[:, start:stop] = (hidden * share).astype(BF16)
        slope_ref[:, start:stop] = (share + hidden * bell).astype(BF16)


def project_hidden(x, shards, bias):
    width = 4 * shards.width
    block = pl.BlockSpec((x.shape[0], width // 4), lambda i: (0, i))
    return dense(
        hidden_kernel,
        [whole(x), columns_of(bias)],
        [block, block],
        [shaped((x.shape[0], width), BF16)] * 2,
        [],
        4 * x.shape[0] * D * width,
        "project_hidden",
        shards,
    )(*[part for _, _, part in shards.parts], x, bias)


def add_product(left_ref, weight_ref, total, contract):
    step = pl.program_id(0)
    half = D // 2
    for col in range(2):
        part = mm(left_ref[...], weight_ref[col], contract)
        span = slice(col * half, (col + 1) * half)

        @pl.when(step == 0)
        def _():
            total[:, span] = part

        @pl.when(step > 0)
        def _():
            total[:, span] += part


ROWS = 16


def each_rows(count, body):
    @pl.loop(0, count // (2 * ROWS))
    def _(step):
        for part in range(2):
            body(pl.ds(pl.multiple_of((2 * step + part) * ROWS, ROWS), ROWS))


def add_rows(partial, place, value):
    partial[place] += value[:8] + value[8:]


def norm_parts(value):
    center = jnp.sum(value, 1, keepdims=True) * (1 / D)
    squares = jnp.sum(value * value, 1, keepdims=True) * (1 / D)
    inverse = lax.rsqrt(squares - center * center + EPSILON)
    return ((value - center) * inverse, inverse)


def norm_back(grad, unit, inverse, gain):
    scaled = grad * gain
    mean = jnp.sum(scaled, 1, keepdims=True) * (1 / D)
    paired = jnp.sum(scaled * unit, 1, keepdims=True) * (1 / D)
    return inverse * (scaled - mean - unit * paired)


def total_of(value):
    return jnp.sum(value, 0, keepdims=True)


def first_norm_kernel(weight_ref, heads_ref, x_ref, vec_ref, unit_ref, inverse_ref, low_ref, total):
    add_product(heads_ref, weight_ref, total, NN)

    @pl.when(pl.program_id(0) == 3)
    def _():
        def body(rows):
            value = x_ref[rows, :].astype(F32) + (total[rows, :] + vec_ref[0:1, :])
            unit, inverse = norm_parts(value)
            unit_ref[rows, :] = unit
            inverse_ref[rows, :] = inverse
            low_ref[rows, :] = (unit * vec_ref[1:2, :] + vec_ref[2:3, :]).astype(BF16)

        each_rows(x_ref.shape[0], body)


def first_norm(heads, shards, x, vec):
    rows = x.shape[0]
    outs = [shaped((rows, D), F32), shaped((rows, 1), F32), shaped((rows, D), BF16)]
    return dense(
        first_norm_kernel,
        [columns_of(heads), whole(x), whole(vec)],
        [whole(out) for out in outs],
        outs,
        [pltpu.VMEM((rows, D), F32)],
        2 * rows * D * D,
        "first_norm",
        shards,
    )(*[part for _, _, part in shards.parts], heads, x, vec)


def second_norm_kernel(
    weight_ref, active_ref, unit_ref, incoming_ref, vec_ref, out_ref, leave_ref, back_ref, low_ref, sums_ref, total, partial
):
    add_product(active_ref, weight_ref, total, NN)

    @pl.when(pl.program_id(0) == 3)
    def _():
        partial[...] = jnp.zeros_like(partial)
        half = D // 2

        def body(rows):
            middle = unit_ref[rows, :] * vec_ref[1:2, :] + vec_ref[2:3, :]
            unit, inverse = norm_parts(middle + (total[rows, :] + vec_ref[3:4, :]))
            out = unit * vec_ref[4:5, :] + vec_ref[5:6, :]
            out_ref[rows, :] = out[:, :half]
            leave_ref[rows, :] = out[:, half:].astype(BF16)
            grad = incoming_ref[rows, :].astype(F32)
            add_rows(partial, 1, grad * unit)
            add_rows(partial, 2, grad)
            back = norm_back(grad, unit, inverse, vec_ref[4:5, :])
            low = back.astype(BF16)
            back_ref[rows, :] = back
            low_ref[rows, :] = low
            add_rows(partial, 0, low.astype(F32))

        each_rows(unit_ref.shape[0], body)
        for place in range(3):
            sums_ref[place : place + 1, :] = total_of(partial[place])


def second_norm(active, shards, unit, incoming, vec):
    rows = unit.shape[0]
    outs = [
        shaped((rows, D // 2), F32),
        shaped((rows, D // 2), BF16),
        shaped((rows, D), F32),
        shaped((rows, D), BF16),
        shaped((3, D), F32),
    ]
    return dense(
        second_norm_kernel,
        [columns_of(active), whole(unit), whole(incoming), whole(vec)],
        [whole(out) for out in outs],
        outs,
        [pltpu.VMEM((rows, D), F32), pltpu.VMEM((3, 8, D), F32)],
        2 * rows * D * active.shape[1],
        "second_norm",
        shards,
    )(*[part for _, _, part in shards.parts], active, unit, incoming, vec)


def first_back_kernel(
    weight_ref, d_hidden_ref, back_ref, unit_ref, inverse_ref, vec_ref, out_ref, low_ref, sums_ref, total, partial
):
    add_product(d_hidden_ref, weight_ref, total, NT)

    @pl.when(pl.program_id(0) == 3)
    def _():
        partial[...] = jnp.zeros_like(partial)

        def body(rows):
            grad = back_ref[rows, :] + total[rows, :]
            unit = unit_ref[rows, :]
            add_rows(partial, 1, grad * unit)
            add_rows(partial, 2, grad)
            back = norm_back(grad, unit, inverse_ref[rows, :], vec_ref[1:2, :])
            low = back.astype(BF16)
            out_ref[rows, :] = back
            low_ref[rows, :] = low
            add_rows(partial, 0, low.astype(F32))

        each_rows(unit_ref.shape[0], body)
        for place in range(3):
            sums_ref[place : place + 1, :] = total_of(partial[place])


def first_back(d_hidden, shards, back, unit, inverse, vec):
    rows = unit.shape[0]
    outs = [shaped((rows, D), F32), shaped((rows, D), BF16), shaped((3, D), F32)]
    return dense(
        first_back_kernel,
        [columns_of(d_hidden), whole(back), whole(unit), whole(inverse), whole(vec)],
        [whole(out) for out in outs],
        outs,
        [pltpu.VMEM((rows, D), F32), pltpu.VMEM((3, 8, D), F32)],
        2 * rows * D * d_hidden.shape[1],
        "first_back",
        shards,
    )(*[part for _, _, part in shards.parts], d_hidden, back, unit, inverse, vec)


def input_back_kernel(weight_ref, d_qkv_ref, back_ref, out_ref, leave_ref, sums_ref, total):
    add_product(d_qkv_ref, weight_ref, total, NT)
    sums_ref[...] = total_of(d_qkv_ref[...].astype(F32))

    @pl.when(pl.program_id(0) == 3)
    def _():
        half = D // 2
        out_ref[...] = back_ref[:, :half] + total[:, :half]
        leave_ref[...] = (back_ref[:, half:] + total[:, half:]).astype(BF16)


def input_back(d_qkv, shards, back):
    rows, width = d_qkv.shape
    outs = [shaped((rows, D // 2), F32), shaped((rows, D // 2), BF16), shaped((1, width), F32)]
    return dense(
        input_back_kernel,
        [columns_of(d_qkv), whole(back)],
        [whole(outs[0]), whole(outs[1]), columns_of(outs[2])],
        outs,
        [pltpu.VMEM((rows, D), F32)],
        2 * rows * D * width,
        "input_back",
        shards,
    )(*[part for _, _, part in shards.parts], d_qkv, back)


def columns_back(grad_ref, weight_ref, start, stop):
    half = D // 2
    return mm(grad_ref[:, :half], weight_ref[0, start:stop, :], NT) + mm(
        grad_ref[:, half:], weight_ref[1, start:stop, :], NT
    )


def hidden_back_kernel(weight_ref, grad_ref, slope_ref, out_ref, sums_ref):
    for start in range(0, out_ref.shape[1], 256):
        span = slice(start, start + 256)
        part = columns_back(grad_ref, weight_ref, start, start + 256)
        low = (part * slope_ref[:, span].astype(F32)).astype(BF16)
        out_ref[:, span] = low
        sums_ref[:, span] = total_of(low.astype(F32))


def hidden_back(grad, shards, slope):
    outs = [shaped(slope.shape, BF16), shaped((1, slope.shape[1]), F32)]
    return dense(
        hidden_back_kernel,
        [whole(grad), columns_of(slope)],
        [columns_of(out) for out in outs],
        outs,
        [],
        2 * grad.shape[0] * D * slope.shape[1],
        "hidden_back",
        shards,
    )(*[part for _, _, part in shards.parts], grad, slope)


def heads_back_kernel(weight_ref, grad_ref, out_ref):
    out_ref[...] = columns_back(grad_ref, weight_ref, 0, weight_ref.shape[1]).astype(BF16)


def heads_back(grad, shards):
    return dense(
        heads_back_kernel,
        [whole(grad)],
        columns_of(grad),
        shaped(grad.shape, BF16),
        [],
        2 * grad.shape[0] * D * D,
        "heads_back",
        shards,
    )(*[part for _, _, part in shards.parts], grad)


def grad_up_kernel(left_ref, right_ref, keep_ref, leave_ref, turned):
    step = pl.program_id(0)
    half = D // 2

    @pl.when(step == 0)
    def _():
        turned[...] = left_ref[...].T

    for parity, out_ref in enumerate((keep_ref, leave_ref)):

        @pl.when(step % 2 == parity)
        def _():
            for col in range(2):
                out_ref[col] = mm(turned[col * half : (col + 1) * half, :], right_ref[...], NN).astype(BF16)


def two_blocks(out):
    return pl.BlockSpec((2, *out.shape[1:]), lambda i: (i // 2, 0, 0))


def grad_up(left, right):
    out = shaped((4, D // 2, right.shape[1] // 4), BF16)
    return dense(
        grad_up_kernel,
        [whole(left), columns_of(right)],
        [two_blocks(out)] * 2,
        [out] * 2,
        [pltpu.VMEM((D, left.shape[0]), BF16)],
        2 * left.shape[0] * D * right.shape[1],
        "grad_up",
    )(left, right)


def grad_down_kernel(left_ref, right_ref, keep_ref, leave_ref):
    step = pl.program_id(0)
    half = D // 2
    for parity, out_ref in enumerate((keep_ref, leave_ref)):

        @pl.when(step % 2 == parity)
        def _():
            turned = left_ref[...].T
            for col in range(2):
                out_ref[col] = mm(turned, right_ref[:, col * half : (col + 1) * half], NN).astype(BF16)


def grad_down(left, right):
    out = shaped((4, left.shape[1] // 4, D // 2), BF16)
    return dense(
        grad_down_kernel,
        [columns_of(left), whole(right)],
        [two_blocks(out)] * 2,
        [out] * 2,
        [],
        2 * left.shape[0] * D * left.shape[1],
        "grad_down",
    )(left, right)


def sum_devices(value, axis, size):
    if size & (size - 1):
        return lax.psum(value, axis)
    step = 1
    while step < size:
        value = value + lax.ppermute(value, axis, [(i, i ^ step) for i in range(size)])
        step *= 2
    return value


def sum_dp(value, size):
    return lax.psum(value, "dp")


def reduce_grid(keep, leaving):
    other = swap_core(leaving)
    half = keep.shape[1] // 2
    own, beside, across, corner = [(keep[k], other[k]) for k in range(4)]

    def upper(pair):
        return add(pair[0][:half], pair[1][:half])

    def lower(pair):
        return add(pair[0][half:], pair[1][half:])

    from_col = swap_col(jnp.concatenate([upper(corner), upper(beside)], 0))
    from_row = swap_row(jnp.concatenate([lower(corner), lower(across)], 0))
    last_col = swap_col(add(beside[0][half:], beside[1][half:], from_row[:half]))
    last_row = swap_row(add(across[0][:half], across[1][:half], from_col[:half]))
    return jnp.concatenate(
        [
            add(own[0][:half], own[1][:half], from_col[half:], last_row),
            add(own[0][half:], own[1][half:], from_row[half:], last_col),
        ],
        0,
    )


def in_three(value):
    high = lax.reduce_precision(value, 8, 7)
    rest = value - high
    mid = lax.reduce_precision(rest, 8, 7)
    return jnp.stack([high, mid, rest - mid]).astype(BF16)


def local(
    n_dp,
    tokens,
    segments,
    qkv_weight,
    qv_bias,
    out_weight,
    out_bias,
    ln1_gain,
    ln1_bias,
    ff_in_weight,
    ff_in_bias,
    ff_out_weight,
    ff_out_bias,
    ln2_gain,
    ln2_bias,
    out_grad,
):
    row, col = lax.axis_index("row"), lax.axis_index("col")
    odd = row % 2 == 1
    member = (row % 2) * 2 + col

    def in_order(mine, other):
        return jnp.where(col == 0, mine, other), jnp.where(col == 0, other, mine)

    packed = jnp.concatenate(
        [out_bias, ln1_gain, ln1_bias, ff_out_bias, ln2_gain, ln2_bias, ff_in_bias, qv_bias.reshape(-1)]
    )
    riders = in_three(packed).reshape(15, 768)
    riders = jnp.concatenate([qkv_weight, riders, jnp.zeros((1, 768), BF16)], 0)
    x = own_rows(tokens, odd, col)
    qkv_w = Shards(riders, D // 2)
    out_w = Shards(out_weight, D // 4)
    ff_in_w = Shards(after(ff_in_weight, *qkv_w.first), D // 2)
    incoming = own_rows(after(out_grad, *qkv_w.first), odd, col)
    ff_out_w = Shards(after(ff_out_weight, *ff_in_w.first), D)

    packed = qkv_w.riders()[:, :15].astype(F32).reshape(8, 3, packed.shape[0])
    packed = (packed[:, 0] + packed[:, 1]) + packed[:, 2]
    vec = packed[:2, : 6 * 512].reshape(2, 6, 512).transpose(1, 0, 2).reshape(6, D)
    pairs = packed[:, 6 * 512 :].reshape(4, 2, 768)
    first, second = in_order(pairs[:, 0], pairs[:, 1])
    ff_in_b = jnp.concatenate([first[:, :512], second[:, :512]], 1).reshape(1, -1)
    qv_b = jnp.concatenate([first[:, 512:], second[:, 512:]], 1).reshape(-1, 2 * HD)
    hollow = jnp.zeros((qv_b.shape[0], HD), F32)
    qkv_b = jnp.concatenate([qv_b[:, :HD], hollow, qv_b[:, HD:]], 1).reshape(1, -1)

    group = (row // 2) * 5
    labels = lax.dynamic_slice_in_dim(segments, (group + (row % 2) * 3 + col) * SEQ, SEQ)
    shared = lax.dynamic_slice_in_dim(segments, (group + 2) * SEQ, SEQ)
    shared = jnp.concatenate(
        [lax.dynamic_slice_in_dim(shared, (member ^ offset) * QUARTER, QUARTER) for offset in range(4)]
    )

    qkv = project_qkv(x, qkv_w, qkv_b)
    qkv_shared = spread_heads(qkv[SEQ:], member, row)
    heads_own, probs_own = attend(qkv, labels)
    heads_shared, probs_shared = attend(qkv_shared, shared)
    heads = jnp.concatenate([heads_own, collect_heads(heads_shared, member, row)], 0)
    unit_one, inverse_one, middle_low = first_norm(heads, out_w, x, vec)
    active, slope = project_hidden(middle_low, ff_in_w, ff_in_b)
    out_mine, out_leave, back_two, d_two, sums_two = second_norm(active, ff_out_w, unit_one, incoming, vec)

    ff_out_keep, ff_out_leave = grad_down(active, d_two)
    d_two, out_leave, ff_out_leave = lax.optimization_barrier((d_two, out_leave, ff_out_leave))
    ff_out_grad = reduce_grid(ff_out_keep, ff_out_leave)
    ff_out_grad = sum_dp(ff_out_grad, n_dp)
    d_hidden, ff_in_bias_part = hidden_back(d_two, ff_out_w, slope)
    ff_in_keep, ff_in_leave = grad_up(middle_low, d_hidden)
    d_hidden, ff_in_leave = lax.optimization_barrier((d_hidden, ff_in_leave))
    ff_in_grad = reduce_grid(ff_in_keep, ff_in_leave)
    layer_out = give_back(out_mine, out_leave, odd, col)
    back_one, d_one, sums_one = first_back(d_hidden, ff_in_w, back_two, unit_one, inverse_one, vec)
    d_heads = heads_back(d_one, out_w)
    d_shared = spread_heads(d_heads[SEQ:], member, row)
    d_qkv_own = attend_back(qkv, probs_own, d_heads)
    d_qkv_shared = attend_back(qkv_shared, probs_shared, d_shared)
    d_qkv = jnp.concatenate([d_qkv_own, collect_heads(d_qkv_shared, member, row)], 0)
    qkv_keep, qkv_leave = grad_up(x, d_qkv)
    d_qkv, d_one, qkv_leave = lax.optimization_barrier((d_qkv, d_one, qkv_leave))
    qkv_grad = reduce_grid(qkv_keep, qkv_leave)
    out_keep, out_leave = grad_down(heads, d_one)
    d_qkv, out_leave = lax.optimization_barrier((d_qkv, out_leave))
    out_w_grad = reduce_grid(out_keep, out_leave)
    in_mine, in_leave, column_sums = input_back(d_qkv, qkv_w, back_one)
    input_grad = give_back(in_mine, in_leave, odd, col)

    ff_in_grad = sum_dp(after(ff_in_grad, ff_out_grad), n_dp)
    qkv_grad = sum_dp(after(qkv_grad, ff_in_grad), n_dp)
    out_w_grad = sum_dp(after(out_w_grad, qkv_grad), n_dp)

    def across_grid(value):
        return sum_devices(sum_devices(value, "row", 4), "col", 2)

    def ordered(value):
        blocks = value.reshape(4, -1)
        return jnp.stack([lax.dynamic_index_in_dim(blocks, row ^ place, 0, False) for place in range(4)])

    place = row * 2 + col
    halves = jnp.concatenate([sums_one, sums_two], 0)
    halves = jnp.concatenate(in_order(halves[:, : D // 2], halves[:, D // 2 :]), 1)
    early = across_grid(jnp.concatenate([halves.reshape(-1), ordered(ff_in_bias_part).reshape(-1)]))
    halves = lax.dynamic_slice_in_dim(early[: 6 * D].reshape(6, 2, D // 2), col, 1, 1)[:, 0]
    early = jnp.concatenate([halves.reshape(-1), lax.dynamic_slice_in_dim(early, 6 * D + place * 512, 512)])
    early = sum_devices(early, "dp", n_dp)
    column_sums = ordered(column_sums).reshape(-1, 3, HD)
    late = across_grid(jnp.concatenate([column_sums[:, 0], column_sums[:, 2]], 1).reshape(-1))
    late = sum_devices(lax.dynamic_slice_in_dim(late, place * 256, 256), "dp", n_dp)
    halves = early[: 6 * 512].reshape(6, 512)
    return (
        layer_out,
        input_grad,
        qkv_grad.astype(F32),
        late.reshape(2, 2 * HD),
        out_w_grad.astype(F32),
        halves[0],
        halves[1],
        halves[2],
        ff_in_grad.astype(F32),
        early[6 * 512 :],
        ff_out_grad.astype(F32),
        halves[3],
        halves[4],
        halves[5],
    )


def solution(mesh):
    in_specs = (
        P(("dp", "row"), "col"),
        P("dp"),
        P("col", "row"),
        P(("row", "col"), None),
        P("row", "col"),
        P("col"),
        P("col"),
        P("col"),
        P("col", "row"),
        P(("row", "col")),
        P("row", "col"),
        P("col"),
        P("col"),
        P("col"),
        P(("dp", "row"), "col"),
    )
    out_specs = (
        P(("dp", "row"), "col"),
        P(("dp", "row"), "col"),
        P("col", "row"),
        P(("row", "col"), None),
        P("row", "col"),
        P("col"),
        P("col"),
        P("col"),
        P("col", "row"),
        P(("row", "col")),
        P("row", "col"),
        P("col"),
        P("col"),
        P("col"),
    )
    step = functools.partial(local, mesh.shape["dp"])
    return jax.shard_map(step, mesh=mesh, in_specs=in_specs, out_specs=out_specs, check_vma=False)
```

time: 741 us -> 703 us (0.949); the launches traced: 727 us -> 697 us
  waiting for transfers between devices: 413 us -> 325 us
  blocking collectives: 58.1 us -> 0 us
  starting transfers between devices: 16.3 us -> 58.8 us
  other arithmetic: 29.7 us -> 71 us
  Pallas kernels: 142 us -> 160 us
  local copies, waits for them, and re-layouts: 51.7 us -> 65.8 us
    reduce_scatter x4 -> x0, waiting for transfers between devices: 129 us -> none  [reduce_stack(): return lax.psum_scatter(stack, GRID, scatter_dimension=0, tiled=False)]
    ppermute x4 -> x70, waiting for transfers between devices: 39.5 us -> 139 us  [the longest x20 77.6 us: swap_col(): return lax.ppermute(value, 'col', [(0, 1), (1, 0)])]
    all_gather x4 -> x0, waiting for transfers between devices: 91.1 us -> none  [gather_weight(): return lax.all_gather(shard, GRID, axis=0, tiled=False)]
    psum x1 -> x0, blocking collectives: 58.1 us -> none  [local(): sums = lax.psum(sums, ('dp', 'row', 'col'))]
    ppermute x4 -> x70, starting transfers between devices: 6.44 us -> 50.8 us  [the longest x20 23 us: swap_col(): return lax.ppermute(value, 'col', [(0, 1), (1, 0)])]
    ppermute x6, waiting for transfers between devices: 3.46 us -> 33.8 us  [collect_heads(): piece = lax.ppermute(piece, GRID, swap(offset))]
    convert_element_type x2 -> x16, other arithmetic: 1.91 us -> 28.6 us  [add(): return total.astype(BF16)]
    pallas_call x12, Pallas kernels: 110 us -> 128 us  [the longest x2 19.3 us: grad_up(): dense(grad_up_kernel, [whole(left), columns_of(right)], [two_blocks(out)]...]
  transfers between devices with their start and end apart: 28 -> 86, of which waited for: 16 -> 32; matrix products, arithmetic and copies ran while one was open for 5% -> 13% of each run, Pallas kernels for 16% -> 13%
where the time goes in v3:
time: 703 us; the launch traced here: 697 us
  waiting for transfers between devices  325 us (46%)
  Pallas kernels  160 us (23%)
  other arithmetic  71 us (10%)
  local copies, waits for them, and re-layouts  65.8 us (9%)
  starting transfers between devices  58.8 us (8%)
  between operations  15.5 us (2%)
    psum x4, waiting for transfers between devices, sum_dp(): return lax.psum(value, 'dp')  133 us
    ppermute x20, waiting for transfers between devices, swap_col(): return lax.ppermute(value, 'col', [(0, 1), (1, 0)])  77.6 us
    ppermute x16, waiting for transfers between devices, swap_row(): return lax.ppermute(value, 'row', [(i, i ^ 2) for i in range(4)])  41.7 us
    unnamed x177, local copies, waits for them, and re-layouts  41.7 us
    ppermute x6, waiting for transfers between devices, collect_heads(): piece = lax.ppermute(piece, GRID, swap(offset))  33.8 us
    convert_element_type x16, other arithmetic, add(): return total.astype(BF16)  28.6 us
    ppermute x20, starting transfers between devices, swap_col(): return lax.ppermute(value, 'col', [(0, 1), (1, 0)])  23 us
    pallas_call x2, Pallas kernels, grad_up(): dense(grad_up_kernel, [whole(left), columns_of(right)], [two_blocks(out)]...  19.3 us
  transfers between devices with their start and end apart: 86, of which 32 were waited for; matrix products, arithmetic and copies ran while one was open for 13% of the time, Pallas kernels for 13%

profile of v3, /device:TPU:0, one launch (start us, length us, event | category | flops | bytes accessed | tf_op | source)
XLA Modules:
  0.0 696.8 jit_solution(11768664164273024115)
XLA Ops:
  14.4 3.0 collective-permute-start
  23.1 2.5 broadcast_select_fusion.3
  28.2 14.4 %collective-permute-done.21.refs_2_ = bf16[256,512]{1,0:T(8,128)(2,1)S(1)} collective-permute-done((bf16[256,512]{1,0:T(8,128)(2,1)S(1)}, bf16[256,512]{1,0:T(8,128)(2,1)S(1)}, u32[]{:S(2)}, u32[]{:S(2)}) %collective-permute-start.21) | collective-permute-done | bytes 262176 | tf_op jit(solution)/shard_map/ppermute | solution.py:124
  43.3 11.9 %collective-permute-done.20.refs_1_ = bf16[256,512]{1,0:T(8,128)(2,1)S(1)} collective-permute-done((bf16[256,512]{1,0:T(8,128)(2,1)S(1)}, bf16[256,512]{1,0:T(8,128)(2,1)S(1)}, u32[]{:S(2)}, u32[]{:S(2)}) %collective-permute-start.20) | collective-permute-done | bytes 262176 | tf_op jit(solution)/shard_map/ppermute | solution.py:128
  57.6 2.5 pad_maximum_fusion.1.refs_10_.refs_11_.left_ref
  65.2 6.8 collective-permute-done.30.refs_4_
  83.8 2.9 collective-permute-done.29.refs_3_
  95.9 8.2 %project_qkv.1.qkv_ref = bf16[640,3072]{1,0:T(8,128)(2,1)} custom-call(bf16[528,768]{1,0:T(8,128)(2,1)S(1)} %maximum_maximum_fusion.refs_0_, bf16[528,768]{1,0:T(8,128)(2,1)S(1)} %copy-done.13, bf16[528,768]{1,0:T(8,128)(2,1)S(1)} %copy-done.16, bf16[256,768]{1,0:T(8,128)(2,1)} %collective-permute-done.29.refs_3_, bf16[272,768]{1,0:T(8,128)(2,1)S(1)} %copy-done.25, ...), custom_call_target="tpu_custom_call" | custom-call | flops 4026531840 | bytes 6291456 | tf_op jit(solution)/shard_map/project_qkv/pallas_call | solution.py:282
  111.6 15.0 %collective-permute-done.39 = bf16[128,768]{1,0:T(8,128)(2,1)S(1)} collective-permute-done((bf16[128,768]{1,0:T(8,128)(2,1)}, bf16[128,768]{1,0:T(8,128)(2,1)S(1)}, u32[]{:S(2)}, u32[]{:S(2)}) %collective-permute-start.39) | collective-permute-done | bytes 196640 | tf_op jit(solution)/shard_map/ppermute | solution.py:167
  127.5 4.2 collective-permute-done.37
  133.4 3.2 attend.3
  140.8 25.5 %collective-permute-done.40 = bf16[128,256]{1,0:T(8,128)(2,1)S(1)} collective-permute-done((bf16[128,256]{1,0:T(8,128)(2,1)S(1)}, bf16[128,256]{1,0:T(8,128)(2,1)S(1)}, u32[]{:S(2)}, u32[]{:S(2)}) %collective-permute-start.40) | collective-permute-done | bytes 65568 | tf_op jit(solution)/shard_map/ppermute | solution.py:177
  172.5 12.2 %attend.2 = (bf16[512,1024]{1,0:T(8,128)(2,1)S(1)}, bf16[16,512,512]{2,1,0:T(8,128)(2,1)S(1)}) custom-call(bf16[640,3072]{1,0:T(8,128)(2,1)S(1)} %copy-done.18, s32[512,1]{1,0:T(8,128)S(1)} %copy.35.column_ref, s32[1,512]{1,0:T(1,128)S(1)} %bitcast.189), custom_call_target="tpu_custom_call" | custom-call | flops 4294967296 | bytes 8388608 | tf_op jit(solution)/shard_map/attend/pallas_call | solution.py:53
  184.7 3.3 copy-done.49
  198.1 9.8 %first_norm.1 = (f32[640,1024]{1,0:T(8,128)}, f32[640,1]{1,0:T(8,128)S(1)}, bf16[640,1024]{1,0:T(8,128)(2,1)S(1)}) custom-call(bf16[256,512]{1,0:T(8,128)(2,1)S(1)} %copy-done.37, bf16[256,512]{1,0:T(8,128)(2,1)S(1)} %copy-done.23, bf16[256,512]{1,0:T(8,128)(2,1)S(1)} %copy-done.21, bf16[128,512]{1,0:T(8,128)(2,1)S(1)} %collective-permute-done.22.refs_3_, ...), custom_call_target="tpu_custom_call" | custom-call | flops 1342177280 | bytes 2097152 | tf_op jit(solution)/shard_map/first_norm/pallas_call | solution.py:385
  209.6 14.0 %project_hidden.1 = (bf16[640,4096]{1,0:T(8,128)(2,1)}, bf16[640,4096]{1,0:T(8,128)(2,1)}) custom-call(bf16[512,1024]{1,0:T(8,128)(2,1)} %refs_0_.6, bf16[512,1024]{1,0:T(8,128)(2,1)S(1)} %collective-permute-done.2.refs_1_, bf16[512,1024]{1,0:T(8,128)(2,1)S(1)} %collective-permute-done.3.refs_2_, bf16[256,1024]{1,0:T(8,128)(2,1)} %collective-permute-done.13.refs_3_, ...), custom_call_target="tpu_custom_call" | custom-call | flops 10737418240 | bytes 16777216 | tf_op jit(solution)/shard_map/project_hidden/pallas_call | solution.py:307
  225.2 19.0 %second_norm.1 = (f32[640,512]{1,0:T(8,128)}, bf16[640,512]{1,0:T(8,128)(2,1)}, f32[640,1024]{1,0:T(8,128)}, bf16[640,1024]{1,0:T(8,128)(2,1)}, f32[3,1024]{1,0:T(4,128)S(1)}) custom-call(bf16[1024,512]{1,0:T(8,128)(2,1)S(1)} %copy-done.35, bf16[1024,512]{1,0:T(8,128)(2,1)} %collective-permute-done.4.refs_1_, ...), custom_call_target="tpu_custom_call" | custom-call | flops 5368709120 | bytes 8388608 | tf_op jit(solution)/shard_map/second_norm/pallas_call | solution.py:436
  245.5 10.6 %grad_down.2 = (bf16[4,1024,512]{2,1,0:T(8,128)(2,1)S(1)}, bf16[4,1024,512]{2,1,0:T(8,128)(2,1)}) custom-call(bf16[640,4096]{1,0:T(8,128)(2,1)} %get-tuple-element.65.refs_10_.left_ref, bf16[640,1024]{1,0:T(8,128)(2,1)S(1)} %copy-done.46), custom_call_target="tpu_custom_call" | custom-call | flops 5368709120 | bytes 8388608 | tf_op jit(solution)/shard_map/grad_down/pallas_call | solution.py:608
  258.1 11.2 %hidden_back.1 = (bf16[640,4096]{1,0:T(8,128)(2,1)}, f32[1,4096]{1,0:T(1,128)S(1)}) custom-call(bf16[1024,512]{1,0:T(8,128)(2,1)S(1)} %copy-done.35, bf16[1024,512]{1,0:T(8,128)(2,1)} %collective-permute-done.4.refs_1_, bf16[1024,512]{1,0:T(8,128)(2,1)} %collective-permute-done.5.refs_2_, bf16[512,512]{1,0:T(8,128)(2,1)S(1)} %collective-permute-done.6.refs_3_, ...), custom_call_target="tpu_custom_call" | custom-call | flops 5368709120 | bytes 8388608 | tf_op jit(solution)/shard_map/hidden_back/pallas_call | solution.py:532
  269.4 10.6 %grad_up.2 = (bf16[4,512,1024]{2,1,0:T(8,128)(2,1)S(1)}, bf16[4,512,1024]{2,1,0:T(8,128)(2,1)}) custom-call(bf16[640,1024]{1,0:T(8,128)(2,1)S(1)} %copy-done.43, bf16[640,4096]{1,0:T(8,128)(2,1)} %get-tuple-element.78.right_ref.refs_10_), custom_call_target="tpu_custom_call" | custom-call | flops 5368709120 | bytes 8388608 | tf_op jit(solution)/shard_map/grad_up/pallas_call | solution.py:583
  281.9 17.3 %first_back.1 = (f32[640,1024]{1,0:T(8,128)}, bf16[640,1024]{1,0:T(8,128)(2,1)}, f32[3,1024]{1,0:T(4,128)S(1)}) custom-call(bf16[512,1024]{1,0:T(8,128)(2,1)} %refs_0_.6, bf16[512,1024]{1,0:T(8,128)(2,1)S(1)} %collective-permute-done.2.refs_1_, bf16[512,1024]{1,0:T(8,128)(2,1)S(1)} %collective-permute-done.3.refs_2_, ...), custom_call_target="tpu_custom_call" | custom-call | flops 5368709120 | bytes 8388608 | tf_op jit(solution)/shard_map/first_back/pallas_call | solution.py:476
  300.5 3.0 heads_back.1.grad_ref
  306.4 3.4 copy-done.50
  309.8 13.4 %attend_back.2 = bf16[512,3072]{1,0:T(8,128)(2,1)S(1)} custom-call(bf16[640,3072]{1,0:T(8,128)(2,1)S(1)} %copy-done.19, bf16[16,512,512]{2,1,0:T(8,128)(2,1)S(1)} %copy-done.50, bf16[640,1024]{1,0:T(8,128)(2,1)S(1)} %heads_back.1.grad_ref), custom_call_target="tpu_custom_call" | custom-call | flops 10737418240 | bytes 8388608 | tf_op jit(solution)/shard_map/attend_back/pallas_call | solution.py:101
  328.7 3.7 attend_back.3
  335.0 5.4 collective-permute-done.48
  340.4 2.6 collective-permute-done.50
  345.3 8.8 %grad_up.3 = (bf16[4,512,768]{2,1,0:T(8,128)(2,1)S(1)}, bf16[4,512,768]{2,1,0:T(8,128)(2,1)}) custom-call(bf16[640,1024]{1,0:T(8,128)(2,1)S(1)} %copy-done.4, bf16[640,3072]{1,0:T(8,128)(2,1)} %pad_maximum_fusion.right_ref.refs_10_), custom_call_target="tpu_custom_call" | custom-call | flops 4026531840 | bytes 6291456 | tf_op jit(solution)/shard_map/grad_up/pallas_call | solution.py:583
  354.7 5.2 collective-permute-done.77
  360.4 3.5 collective-permute-done.78
  364.4 3.5 collective-permute-done.79
  370.7 3.6 grad_down.3
  375.3 11.8 %input_back.1 = (f32[640,512]{1,0:T(8,128)}, bf16[640,512]{1,0:T(8,128)(2,1)}, f32[1,3072]{1,0:T(1,128)S(1)}) custom-call(bf16[528,768]{1,0:T(8,128)(2,1)S(1)} %copy-done.9, bf16[528,768]{1,0:T(8,128)(2,1)S(1)} %copy-done.14, bf16[528,768]{1,0:T(8,128)(2,1)S(1)} %copy-done.17, bf16[256,768]{1,0:T(8,128)(2,1)} %collective-permute-done.29.refs_3_, ...), custom_call_target="tpu_custom_call" | custom-call | flops 4026531840 | bytes 6291456 | tf_op jit(solution)/shard_map/input_back/pallas_call | solution.py:502
  391.9 2.6 collective-permute-start.81
  403.3 2.9 fusion.22
  406.9 2.5 fusion.18
  414.1 18.4 %collective-permute-done.63 = bf16[1024,512]{1,0:T(8,128)(2,1)S(1)} collective-permute-done((bf16[1024,512]{1,0:T(8,128)(2,1)S(1)}, bf16[1024,512]{1,0:T(8,128)(2,1)S(1)}, u32[]{:S(2)}, u32[]{:S(2)}) %collective-permute-start.63) | collective-permute-done | bytes 1048608 | tf_op jit(solution)/shard_map/ppermute | solution.py:128
  437.4 17.6 %collective-permute-done.58 = bf16[512,1024]{1,0:T(8,128)(2,1)S(1)} collective-permute-done((bf16[512,1024]{1,0:T(8,128)(2,1)S(1)}, bf16[512,1024]{1,0:T(8,128)(2,1)S(1)}, u32[]{:S(2)}, u32[]{:S(2)}) %collective-permute-start.58) | collective-permute-done | bytes 1048608 | tf_op jit(solution)/shard_map/ppermute | solution.py:128
  456.9 13.7 %collective-permute-done.64 = bf16[512,512]{1,0:T(8,128)(2,1)S(1)} collective-permute-done((bf16[512,512]{1,0:T(8,128)(2,1)S(1)}, bf16[512,512]{1,0:T(8,128)(2,1)S(1)}, u32[]{:S(2)}, u32[]{:S(2)}) %collective-permute-start.64) | collective-permute-done | bytes 524320 | tf_op jit(solution)/shard_map/ppermute | solution.py:124
  476.2 6.6 collective-permute-done.59
  483.3 2.9 fusion.11
  486.2 10.9 %collective-permute-done.66 = bf16[512,512]{1,0:T(8,128)(2,1)S(1)} collective-permute-done((bf16[512,512]{1,0:T(8,128)(2,1)S(1)}, bf16[512,512]{1,0:T(8,128)(2,1)S(1)}, u32[]{:S(2)}, u32[]{:S(2)}) %collective-permute-start.66) | collective-permute-done | bytes 524320 | tf_op jit(solution)/shard_map/ppermute | solution.py:128
  509.2 13.2 %collective-permute-done.61 = bf16[256,1024]{1,0:T(8,128)(2,1)S(1)} collective-permute-done((bf16[256,1024]{1,0:T(8,128)(2,1)}, bf16[256,1024]{1,0:T(8,128)(2,1)S(1)}, u32[]{:S(2)}, u32[]{:S(2)}) %collective-permute-start.61) | collective-permute-done | bytes 524320 | tf_op jit(solution)/shard_map/ppermute | solution.py:128
  525.0 26.1 %all-reduce.6.cloned.1.call-done = bf16[1024,512]{1,0:T(8,128)(2,1)} async-done(((bf16[1024,512]{1,0:T(8,128)(2,1)}), bf16[1024,512]{1,0:T(8,128)(2,1)}) %all-reduce.6.cloned.1.call-update) | async-done | bytes 1048592 | tf_op jit(solution)/shard_map/psum | solution.py:630
  551.1 4.4 convert_select_fusion.1
  566.0 39.4 %all-reduce.8.cloned.1.call-done = bf16[512,1024]{1,0:T(8,128)(2,1)} async-done(((bf16[512,1024]{1,0:T(8,128)(2,1)}), bf16[512,1024]{1,0:T(8,128)(2,1)}) %all-reduce.8.cloned.1.call-update) | async-done | bytes 1048592 | tf_op jit(solution)/shard_map/psum | solution.py:630
  614.2 36.6 %all-reduce.10.cloned.1.call-done = bf16[512,768]{1,0:T(8,128)(2,1)} async-done(((bf16[512,768]{1,0:T(8,128)(2,1)}), bf16[512,768]{1,0:T(8,128)(2,1)}) %all-reduce.10.cloned.1.call-update) | async-done | bytes 786448 | tf_op jit(solution)/shard_map/psum | solution.py:630
  657.1 31.1 %all-reduce.12.cloned.1.call-done = bf16[256,512]{1,0:T(8,128)(2,1)} async-done(((bf16[256,512]{1,0:T(8,128)(2,1)}), bf16[256,512]{1,0:T(8,128)(2,1)}) %all-reduce.12.cloned.1.call-update) | async-done | bytes 262160 | tf_op jit(solution)/shard_map/psum | solution.py:630
  (473 shorter events, 176.5 us)
Async XLA Ops:
  7.2 543.9 %all-reduce.6.cloned.1.call-start = ((), (), s32[]{:S(2)}) async-start(), calls=%async_computation | async-start | bytes 2097152 | tf_op jit(solution)/shard_map/psum | solution.py:630
  14.4 45.7 %collective-permute-start = (bf16[528,768]{1,0:T(8,128)(2,1)S(1)}, bf16[528,768]{1,0:T(8,128)(2,1)S(1)}, u32[]{:S(2)}, u32[]{:S(2)}) collective-permute-start(bf16[528,768]{1,0:T(8,128)(2,1)S(1)} %maximum_maximum_fusion.refs_0_), channel_id=1, source_target_pairs={{0,1},{1,0},{2,3},{3,2},{4,5},{5,4},{6,7},{7,6},{8,9},{9,8},{10,11... | collective-permute-start | bytes 2433032 | tf_op jit(solution)/shard_map/ppermute | solution.py:128
  17.4 42.7 %collective-permute-start.1 = (bf16[528,768]{1,0:T(8,128)(2,1)S(1)}, bf16[528,768]{1,0:T(8,128)(2,1)S(1)}, u32[]{:S(2)}, u32[]{:S(2)}) collective-permute-start(bf16[528,768]{1,0:T(8,128)(2,1)S(1)} %maximum_maximum_fusion.refs_0_), channel_id=1, source_target_pairs={{0,4},{2,6},{4,0},{6,2},{1,5},{3,7},{5,1},{7,3},{8,12},{10,14},{12... | collective-permute-start | bytes 2433032 | tf_op jit(solution)/shard_map/ppermute | solution.py:124
  25.5 30.3 %collective-permute-start.36 = (bf16[640,512]{1,0:T(8,128)(2,1)}, bf16[640,512]{1,0:T(8,128)(2,1)}, u32[]{:S(2)}, u32[]{:S(2)}) collective-permute-start(bf16[640,512]{1,0:T(8,128)(2,1)} %get-tuple-element.141), channel_id=1, source_target_pairs={{0,1},{1,0},{2,3},{3,2},{4,5},{5,4},{6,7},{7,6},{8,9},{9,8},{10,11... | collective-permute-start | bytes 1966088 | tf_op jit(solution)/shard_map/ppermute | solution.py:128
  26.1 29.0 %collective-permute-start.20 = (bf16[256,512]{1,0:T(8,128)(2,1)S(1)}, bf16[256,512]{1,0:T(8,128)(2,1)S(1)}, u32[]{:S(2)}, u32[]{:S(2)}) collective-permute-start(bf16[256,512]{1,0:T(8,128)(2,1)S(1)} %copy-done.36), channel_id=1, source_target_pairs={{0,1},{1,0},{2,3},{3,2},{4,5},{5,4},{6,7},{7,6},{8,9},{9,8},{10,11... | collective-permute-start | bytes 786440 | tf_op jit(solution)/shard_map/ppermute | solution.py:128
  55.2 27.6 %collective-permute-start.24 = (bf16[256,512]{1,0:T(8,128)(2,1)S(1)}, bf16[256,512]{1,0:T(8,128)(2,1)}, u32[]{:S(2)}, u32[]{:S(2)}) collective-permute-start(bf16[256,512]{1,0:T(8,128)(2,1)S(1)} %copy-done.36), channel_id=1, source_target_pairs={{0,2},{2,0},{4,6},{6,4},{1,3},{3,1},{5,7},{7,5},{8,10},{10,8},{12,... | collective-permute-start | bytes 786440 | tf_op jit(solution)/shard_map/ppermute | solution.py:120
  55.8 27.4 %collective-permute-start.22 = (bf16[128,512]{1,0:T(8,128)(2,1)}, bf16[128,512]{1,0:T(8,128)(2,1)S(1)}, u32[]{:S(2)}, u32[]{:S(2)}) collective-permute-start(bf16[128,512]{1,0:T(8,128)(2,1)} %slice.806), channel_id=1, source_target_pairs={{0,1},{1,0},{2,3},{3,2},{4,5},{5,4},{6,7},{7,6},{8,9},{9,8},{10,11... | collective-permute-start | bytes 393224 | tf_op jit(solution)/shard_map/ppermute | solution.py:128
  75.3 33.9 %collective-permute-start.2 = (bf16[512,1024]{1,0:T(8,128)(2,1)}, bf16[512,1024]{1,0:T(8,128)(2,1)S(1)}, u32[]{:S(2)}, u32[]{:S(2)}) collective-permute-start(bf16[512,1024]{1,0:T(8,128)(2,1)} %refs_0_.6), channel_id=1, source_target_pairs={{0,1},{1,0},{2,3},{3,2},{4,5},{5,4},{6,7},{7,6},{8,9},{9,8},{10,11... | collective-permute-start | bytes 3145736 | tf_op jit(solution)/shard_map/ppermute | solution.py:128
  82.7 26.4 %collective-permute-start.3 = (bf16[512,1024]{1,0:T(8,128)(2,1)}, bf16[512,1024]{1,0:T(8,128)(2,1)S(1)}, u32[]{:S(2)}, u32[]{:S(2)}) collective-permute-start(bf16[512,1024]{1,0:T(8,128)(2,1)} %refs_0_.6), channel_id=1, source_target_pairs={{0,4},{2,6},{4,0},{6,2},{1,5},{3,7},{5,1},{7,3},{8,12},{10,14},{12... | collective-permute-start | bytes 3145736 | tf_op jit(solution)/shard_map/ppermute | solution.py:124
  87.5 51.8 %collective-permute-start.15 = (bf16[512,1024]{1,0:T(8,128)(2,1)}, bf16[512,1024]{1,0:T(8,128)(2,1)}, u32[]{:S(2)}, u32[]{:S(2)}) collective-permute-start(bf16[512,1024]{1,0:T(8,128)(2,1)} %refs_0_.6), channel_id=1, source_target_pairs={{0,2},{2,0},{4,6},{6,4},{1,3},{3,1},{5,7},{7,5},{8,10},{10,8},{12,... | collective-permute-start | bytes 3145736 | tf_op jit(solution)/shard_map/ppermute | solution.py:120
  88.8 44.5 %collective-permute-start.43 = (bf16[640,512]{1,0:T(8,128)(2,1)}, bf16[640,512]{1,0:T(8,128)(2,1)}, u32[]{:S(2)}, u32[]{:S(2)}) collective-permute-start(bf16[640,512]{1,0:T(8,128)(2,1)} %get-tuple-element.135), channel_id=1, source_target_pairs={{0,1},{1,0},{2,3},{3,2},{4,5},{5,4},{6,7},{7,6},{8,9},{9,8},{10,11... | collective-permute-start | bytes 1966088 | tf_op jit(solution)/shard_map/ppermute | solution.py:128
  106.2 20.4 %collective-permute-start.39 = (bf16[128,768]{1,0:T(8,128)(2,1)}, bf16[128,768]{1,0:T(8,128)(2,1)S(1)}, u32[]{:S(2)}, u32[]{:S(2)}) collective-permute-start(bf16[128,768]{1,0:T(8,128)(2,1)} %get-tuple-element.151), channel_id=1, source_target_pairs={{0,3},{1,2},{2,1},{3,0},{4,7},{5,6},{6,5},{7,4},{8,11},{9,10},{10,... | collective-permute-start | bytes 589832 | tf_op jit(solution)/shard_map/ppermute | solution.py:167
  109.1 22.6 %collective-permute-start.37 = (bf16[128,768]{1,0:T(8,128)(2,1)}, bf16[128,768]{1,0:T(8,128)(2,1)}, u32[]{:S(2)}, u32[]{:S(2)}) collective-permute-start(bf16[128,768]{1,0:T(8,128)(2,1)} %get-tuple-element.153), channel_id=1, source_target_pairs={{0,1},{1,0},{2,3},{3,2},{4,5},{5,4},{6,7},{7,6},{8,9},{9,8},{10,11... | collective-permute-start | bytes 589832 | tf_op jit(solution)/shard_map/ppermute | solution.py:167
  126.6 61.8 %collective-permute-start.4 = (bf16[1024,512]{1,0:T(8,128)(2,1)}, bf16[1024,512]{1,0:T(8,128)(2,1)}, u32[]{:S(2)}, u32[]{:S(2)}) collective-permute-start(bf16[1024,512]{1,0:T(8,128)(2,1)} %refs_0_.5), channel_id=1, source_target_pairs={{0,1},{1,0},{2,3},{3,2},{4,5},{5,4},{6,7},{7,6},{8,9},{9,8},{10,11... | collective-permute-start | bytes 3145736 | tf_op jit(solution)/shard_map/ppermute | solution.py:128
  127.1 61.4 %collective-permute-start.5 = (bf16[1024,512]{1,0:T(8,128)(2,1)}, bf16[1024,512]{1,0:T(8,128)(2,1)}, u32[]{:S(2)}, u32[]{:S(2)}) collective-permute-start(bf16[1024,512]{1,0:T(8,128)(2,1)} %refs_0_.5), channel_id=1, source_target_pairs={{0,4},{2,6},{4,0},{6,2},{1,5},{3,7},{5,1},{7,3},{8,12},{10,14},{12... | collective-permute-start | bytes 3145736 | tf_op jit(solution)/shard_map/ppermute | solution.py:124
  131.7 36.4 %collective-permute-start.13 = (bf16[256,1024]{1,0:T(8,128)(2,1)}, bf16[256,1024]{1,0:T(8,128)(2,1)}, u32[]{:S(2)}, u32[]{:S(2)}) collective-permute-start(bf16[256,1024]{1,0:T(8,128)(2,1)} %slice.804), channel_id=1, source_target_pairs={{0,1},{1,0},{2,3},{3,2},{4,5},{5,4},{6,7},{7,6},{8,9},{9,8},{10,11... | collective-permute-start | bytes 1572872 | tf_op jit(solution)/shard_map/ppermute | solution.py:128
  133.3 60.7 %collective-permute-start.16 = (bf16[512,1024]{1,0:T(8,128)(2,1)S(1)}, bf16[512,1024]{1,0:T(8,128)(2,1)}, u32[]{:S(2)}, u32[]{:S(2)}) collective-permute-start(bf16[512,1024]{1,0:T(8,128)(2,1)S(1)} %collective-permute-done.2.refs_1_), channel_id=1, source_target_pairs={{0,2},{2,0},{4,6},{6,4},{1,3},{3,1},{5,7},{7,5},{8,10},{10,8},{12,... | collective-permute-start | bytes 3145736 | tf_op jit(solution)/shard_map/ppermute | solution.py:120
  139.3 27.0 %collective-permute-start.40 = (bf16[128,256]{1,0:T(8,128)(2,1)S(1)}, bf16[128,256]{1,0:T(8,128)(2,1)S(1)}, u32[]{:S(2)}, u32[]{:S(2)}) collective-permute-start(bf16[128,256]{1,0:T(8,128)(2,1)S(1)} %get-tuple-element.160), channel_id=1, source_target_pairs={{0,1},{1,0},{2,3},{3,2},{4,5},{5,4},{6,7},{7,6},{8,9},{9,8},{10,11... | collective-permute-start | bytes 196616 | tf_op jit(solution)/shard_map/ppermute | solution.py:177
  167.6 20.5 %collective-permute-start.14 = (bf16[256,1024]{1,0:T(8,128)(2,1)S(1)}, bf16[256,1024]{1,0:T(8,128)(2,1)}, u32[]{:S(2)}, u32[]{:S(2)}) collective-permute-start(bf16[256,1024]{1,0:T(8,128)(2,1)S(1)} %slice.805), channel_id=1, source_target_pairs={{0,4},{2,6},{4,0},{6,2},{1,5},{3,7},{5,1},{7,3},{8,12},{10,14},{12... | collective-permute-start | bytes 1572872 | tf_op jit(solution)/shard_map/ppermute | solution.py:124
  168.1 29.4 %collective-permute-start.17 = (bf16[512,1024]{1,0:T(8,128)(2,1)S(1)}, bf16[512,1024]{1,0:T(8,128)(2,1)}, u32[]{:S(2)}, u32[]{:S(2)}) collective-permute-start(bf16[512,1024]{1,0:T(8,128)(2,1)S(1)} %collective-permute-done.3.refs_2_), channel_id=1, source_target_pairs={{0,2},{2,0},{4,6},{6,4},{1,3},{3,1},{5,7},{7,5},{8,10},{10,8},{12,... | collective-permute-start | bytes 3145736 | tf_op jit(solution)/shard_map/ppermute | solution.py:120
  197.4 26.2 %collective-permute-start.8 = (bf16[1024,512]{1,0:T(8,128)(2,1)S(1)}, bf16[1024,512]{1,0:T(8,128)(2,1)S(1)}, u32[]{:S(2)}, u32[]{:S(2)}) collective-permute-start(bf16[1024,512]{1,0:T(8,128)(2,1)S(1)} %copy-done.35), channel_id=1, source_target_pairs={{0,2},{2,0},{4,6},{6,4},{1,3},{3,1},{5,7},{7,5},{8,10},{10,8},{12,... | collective-permute-start | bytes 3145736 | tf_op jit(solution)/shard_map/ppermute | solution.py:120
  197.5 26.1 %collective-permute-start.9 = (bf16[1024,512]{1,0:T(8,128)(2,1)}, bf16[1024,512]{1,0:T(8,128)(2,1)S(1)}, u32[]{:S(2)}, u32[]{:S(2)}) collective-permute-start(bf16[1024,512]{1,0:T(8,128)(2,1)} %collective-permute-done.4.refs_1_), channel_id=1, source_target_pairs={{0,2},{2,0},{4,6},{6,4},{1,3},{3,1},{5,7},{7,5},{8,10},{10,8},{12,... | collective-permute-start | bytes 3145736 | tf_op jit(solution)/shard_map/ppermute | solution.py:120
  198.0 25.6 %collective-permute-start.10 = (bf16[1024,512]{1,0:T(8,128)(2,1)}, bf16[1024,512]{1,0:T(8,128)(2,1)S(1)}, u32[]{:S(2)}, u32[]{:S(2)}) collective-permute-start(bf16[1024,512]{1,0:T(8,128)(2,1)} %collective-permute-done.5.refs_2_), channel_id=1, source_target_pairs={{0,2},{2,0},{4,6},{6,4},{1,3},{3,1},{5,7},{7,5},{8,10},{10,8},{12,... | collective-permute-start | bytes 3145736 | tf_op jit(solution)/shard_map/ppermute | solution.py:120
  304.2 20.8 %collective-permute-start.47 = (bf16[128,256]{1,0:T(8,128)(2,1)}, bf16[128,256]{1,0:T(8,128)(2,1)S(1)}, u32[]{:S(2)}, u32[]{:S(2)}) collective-permute-start(bf16[128,256]{1,0:T(8,128)(2,1)} %get-tuple-element.155), channel_id=1, source_target_pairs={{0,3},{1,2},{2,1},{3,0},{4,7},{5,6},{6,5},{7,4},{8,11},{9,10},{10,... | collective-permute-start | bytes 196616 | tf_op jit(solution)/shard_map/ppermute | solution.py:167
  304.8 20.3 %collective-permute-start.46 = (bf16[128,256]{1,0:T(8,128)(2,1)S(1)}, bf16[128,256]{1,0:T(8,128)(2,1)}, u32[]{:S(2)}, u32[]{:S(2)}) collective-permute-start(bf16[128,256]{1,0:T(8,128)(2,1)S(1)} %get-tuple-element.156), channel_id=1, source_target_pairs={{0,2},{1,3},{2,0},{3,1},{4,6},{5,7},{6,4},{7,5},{8,10},{9,11},{10,... | collective-permute-start | bytes 196616 | tf_op jit(solution)/shard_map/ppermute | solution.py:167
  323.2 83.7 %collective-permute-start.57 = (bf16[4,512,1024]{2,1,0:T(8,128)(2,1)}, bf16[4,512,1024]{2,1,0:T(8,128)(2,1)}, u32[]{:S(2)}, u32[]{:S(2)}) collective-permute-start(bf16[4,512,1024]{2,1,0:T(8,128)(2,1)} %get-tuple-element.94), channel_id=1, source_target_pairs={{0,2},{2,0},{4,6},{6,4},{1,3},{3,1},{5,7},{7,5},{8,10},{10,8},{12,... | collective-permute-start | bytes 12582920 | tf_op jit(solution)/shard_map/ppermute | solution.py:120
  323.4 79.9 %collective-permute-start.62 = (bf16[4,1024,512]{2,1,0:T(8,128)(2,1)}, bf16[4,1024,512]{2,1,0:T(8,128)(2,1)}, u32[]{:S(2)}, u32[]{:S(2)}) collective-permute-start(bf16[4,1024,512]{2,1,0:T(8,128)(2,1)} %get-tuple-element.96), channel_id=1, source_target_pairs={{0,2},{2,0},{4,6},{6,4},{1,3},{3,1},{5,7},{7,5},{8,10},{10,8},{12,... | collective-permute-start | bytes 12582920 | tf_op jit(solution)/shard_map/ppermute | solution.py:120
  354.1 57.0 %collective-permute-start.52 = (bf16[4,512,768]{2,1,0:T(8,128)(2,1)}, bf16[4,512,768]{2,1,0:T(8,128)(2,1)}, u32[]{:S(2)}, u32[]{:S(2)}) collective-permute-start(bf16[4,512,768]{2,1,0:T(8,128)(2,1)} %get-tuple-element.92), channel_id=1, source_target_pairs={{0,2},{2,0},{4,6},{6,4},{1,3},{3,1},{5,7},{7,5},{8,10},{10,8},{12,... | collective-permute-start | bytes 9437192 | tf_op jit(solution)/shard_map/ppermute | solution.py:120
  401.8 32.5 %collective-permute-start.71 = (f32[256]{0:T(256)S(1)}, f32[256]{0:T(256)S(1)}, u32[]{:S(2)}, u32[]{:S(2)}) collective-permute-start(f32[256]{0:T(256)S(1)} %add.472), channel_id=1, source_target_pairs={{0,16},{8,24},{16,0},{24,8},{1,17},{9,25},{17,1},{25,9},{2,18},{10... | collective-permute-start | bytes 3080 | tf_op jit(solution)/shard_map/ppermute | solution.py:624
  406.3 26.2 %collective-permute-start.63 = (bf16[1024,512]{1,0:T(8,128)(2,1)S(1)}, bf16[1024,512]{1,0:T(8,128)(2,1)S(1)}, u32[]{:S(2)}, u32[]{:S(2)}) collective-permute-start(bf16[1024,512]{1,0:T(8,128)(2,1)S(1)} %pad_maximum_fusion.7), channel_id=1, source_target_pairs={{0,1},{1,0},{2,3},{3,2},{4,5},{5,4},{6,7},{7,6},{8,9},{9,8},{10,11... | collective-permute-start | bytes 3145736 | tf_op jit(solution)/shard_map/ppermute | solution.py:128
  409.5 45.5 %collective-permute-start.58 = (bf16[512,1024]{1,0:T(8,128)(2,1)S(1)}, bf16[512,1024]{1,0:T(8,128)(2,1)S(1)}, u32[]{:S(2)}, u32[]{:S(2)}) collective-permute-start(bf16[512,1024]{1,0:T(8,128)(2,1)S(1)} %pad_maximum_fusion.4), channel_id=1, source_target_pairs={{0,1},{1,0},{2,3},{3,2},{4,5},{5,4},{6,7},{7,6},{8,9},{9,8},{10,11... | collective-permute-start | bytes 3145736 | tf_op jit(solution)/shard_map/ppermute | solution.py:128
  412.9 60.0 %collective-permute-start.53 = (bf16[512,768]{1,0:T(8,128)(2,1)S(1)}, bf16[512,768]{1,0:T(8,128)(2,1)S(1)}, u32[]{:S(2)}, u32[]{:S(2)}) collective-permute-start(bf16[512,768]{1,0:T(8,128)(2,1)S(1)} %pad_maximum_fusion.11), channel_id=1, source_target_pairs={{0,1},{1,0},{2,3},{3,2},{4,5},{5,4},{6,7},{7,6},{8,9},{9,8},{10,11... | collective-permute-start | bytes 2359304 | tf_op jit(solution)/shard_map/ppermute | solution.py:128
  413.5 43.3 %collective-permute-start.65 = (bf16[1024,512]{1,0:T(8,128)(2,1)S(1)}, bf16[1024,512]{1,0:T(8,128)(2,1)S(1)}, u32[]{:S(2)}, u32[]{:S(2)}) collective-permute-start(bf16[1024,512]{1,0:T(8,128)(2,1)S(1)} %pad_maximum_fusion.8), channel_id=1, source_target_pairs={{0,4},{2,6},{4,0},{6,2},{1,5},{3,7},{5,1},{7,3},{8,12},{10,14},{12... | collective-permute-start | bytes 3145736 | tf_op jit(solution)/shard_map/ppermute | solution.py:124
  432.5 43.1 %collective-permute-start.60 = (bf16[512,1024]{1,0:T(8,128)(2,1)S(1)}, bf16[512,1024]{1,0:T(8,128)(2,1)S(1)}, u32[]{:S(2)}, u32[]{:S(2)}) collective-permute-start(bf16[512,1024]{1,0:T(8,128)(2,1)S(1)} %pad_maximum_fusion.5), channel_id=1, source_target_pairs={{0,4},{2,6},{4,0},{6,2},{1,5},{3,7},{5,1},{7,3},{8,12},{10,14},{12... | collective-permute-start | bytes 3145736 | tf_op jit(solution)/shard_map/ppermute | solution.py:124
  434.2 36.3 %collective-permute-start.64 = (bf16[512,512]{1,0:T(8,128)(2,1)S(1)}, bf16[512,512]{1,0:T(8,128)(2,1)S(1)}, u32[]{:S(2)}, u32[]{:S(2)}) collective-permute-start(bf16[512,512]{1,0:T(8,128)(2,1)S(1)} %fusion.3), channel_id=1, source_target_pairs={{0,4},{2,6},{4,0},{6,2},{1,5},{3,7},{5,1},{7,3},{8,12},{10,14},{12... | collective-permute-start | bytes 1572872 | tf_op jit(solution)/shard_map/ppermute | solution.py:124
  455.0 96.2 %collective-permute-start.44 = (bf16[640,512]{1,0:T(8,128)(2,1)}, bf16[640,512]{1,0:T(8,128)(2,1)}, u32[]{:S(2)}, u32[]{:S(2)}) collective-permute-start(bf16[640,512]{1,0:T(8,128)(2,1)} %get-tuple-element.72), channel_id=1, source_target_pairs={{0,1},{1,0},{2,3},{3,2},{4,5},{5,4},{6,7},{7,6},{8,9},{9,8},{10,11... | collective-permute-start | bytes 1966088 | tf_op jit(solution)/shard_map/ppermute | solution.py:128
  456.8 43.2 %collective-permute-start.72 = (bf16[4,256,512]{2,1,0:T(8,128)(2,1)}, bf16[4,256,512]{2,1,0:T(8,128)(2,1)}, u32[]{:S(2)}, u32[]{:S(2)}) collective-permute-start(bf16[4,256,512]{2,1,0:T(8,128)(2,1)} %get-tuple-element.101), channel_id=1, source_target_pairs={{0,2},{2,0},{4,6},{6,4},{1,3},{3,1},{5,7},{7,5},{8,10},{10,8},{12,... | collective-permute-start | bytes 3145736 | tf_op jit(solution)/shard_map/ppermute | solution.py:120
  472.8 24.2 %collective-permute-start.66 = (bf16[512,512]{1,0:T(8,128)(2,1)S(1)}, bf16[512,512]{1,0:T(8,128)(2,1)S(1)}, u32[]{:S(2)}, u32[]{:S(2)}) collective-permute-start(bf16[512,512]{1,0:T(8,128)(2,1)S(1)} %get-tuple-element.107), channel_id=1, source_target_pairs={{0,1},{1,0},{2,3},{3,2},{4,5},{5,4},{6,7},{7,6},{8,9},{9,8},{10,11... | collective-permute-start | bytes 1572872 | tf_op jit(solution)/shard_map/ppermute | solution.py:128
  475.6 75.5 %collective-permute-start.51 = (bf16[640,512]{1,0:T(8,128)(2,1)}, bf16[640,512]{1,0:T(8,128)(2,1)}, u32[]{:S(2)}, u32[]{:S(2)}) collective-permute-start(bf16[640,512]{1,0:T(8,128)(2,1)} %get-tuple-element.90), channel_id=1, source_target_pairs={{0,1},{1,0},{2,3},{3,2},{4,5},{5,4},{6,7},{7,6},{8,9},{9,8},{10,11... | collective-permute-start | bytes 1966088 | tf_op jit(solution)/shard_map/ppermute | solution.py:128
  482.8 20.7 %collective-permute-start.55 = (bf16[512,768]{1,0:T(8,128)(2,1)}, bf16[512,768]{1,0:T(8,128)(2,1)}, u32[]{:S(2)}, u32[]{:S(2)}) collective-permute-start(bf16[512,768]{1,0:T(8,128)(2,1)} %pad_maximum_fusion.12), channel_id=1, source_target_pairs={{0,4},{2,6},{4,0},{6,2},{1,5},{3,7},{5,1},{7,3},{8,12},{10,14},{12... | collective-permute-start | bytes 2359304 | tf_op jit(solution)/shard_map/ppermute | solution.py:124
  500.0 105.4 %all-reduce.8.cloned.1.call-start = ((), (), s32[]{:S(2)}) async-start(), calls=%async_computation.1 | async-start | bytes 2097152 | tf_op jit(solution)/shard_map/psum | solution.py:630
  500.0 22.3 %collective-permute-start.61 = (bf16[256,1024]{1,0:T(8,128)(2,1)}, bf16[256,1024]{1,0:T(8,128)(2,1)S(1)}, u32[]{:S(2)}, u32[]{:S(2)}) collective-permute-start(bf16[256,1024]{1,0:T(8,128)(2,1)} %get-tuple-element.113), channel_id=1, source_target_pairs={{0,1},{1,0},{2,3},{3,2},{4,5},{5,4},{6,7},{7,6},{8,9},{9,8},{10,11... | collective-permute-start | bytes 1572872 | tf_op jit(solution)/shard_map/ppermute | solution.py:128
  503.5 57.8 %collective-permute-start.73 = (bf16[256,512]{1,0:T(8,128)(2,1)}, bf16[256,512]{1,0:T(8,128)(2,1)}, u32[]{:S(2)}, u32[]{:S(2)}) collective-permute-start(bf16[256,512]{1,0:T(8,128)(2,1)} %pad_maximum_fusion.19), channel_id=1, source_target_pairs={{0,1},{1,0},{2,3},{3,2},{4,5},{5,4},{6,7},{7,6},{8,9},{9,8},{10,11... | collective-permute-start | bytes 786440 | tf_op jit(solution)/shard_map/ppermute | solution.py:128
  507.6 55.9 %collective-permute-start.56 = (bf16[256,768]{1,0:T(8,128)(2,1)}, bf16[256,768]{1,0:T(8,128)(2,1)}, u32[]{:S(2)}, u32[]{:S(2)}) collective-permute-start(bf16[256,768]{1,0:T(8,128)(2,1)} %get-tuple-element.119), channel_id=1, source_target_pairs={{0,1},{1,0},{2,3},{3,2},{4,5},{5,4},{6,7},{7,6},{8,9},{9,8},{10,11... | collective-permute-start | bytes 1179656 | tf_op jit(solution)/shard_map/ppermute | solution.py:128
  551.1 99.7 %all-reduce.10.cloned.1.call-start = ((), (), s32[]{:S(2)}) async-start(), calls=%async_computation.2 | async-start | bytes 1572864 | tf_op jit(solution)/shard_map/psum | solution.py:630
  559.8 45.6 %collective-permute-start.75 = (bf16[256,512]{1,0:T(8,128)(2,1)}, bf16[256,512]{1,0:T(8,128)(2,1)}, u32[]{:S(2)}, u32[]{:S(2)}) collective-permute-start(bf16[256,512]{1,0:T(8,128)(2,1)} %pad_maximum_fusion.20), channel_id=1, source_target_pairs={{0,4},{2,6},{4,0},{6,2},{1,5},{3,7},{5,1},{7,3},{8,12},{10,14},{12... | collective-permute-start | bytes 786440 | tf_op jit(solution)/shard_map/ppermute | solution.py:124
  563.0 42.4 %collective-permute-start.74 = (bf16[128,512]{1,0:T(8,128)(2,1)}, bf16[128,512]{1,0:T(8,128)(2,1)}, u32[]{:S(2)}, u32[]{:S(2)}) collective-permute-start(bf16[128,512]{1,0:T(8,128)(2,1)} %fusion.33), channel_id=1, source_target_pairs={{0,4},{2,6},{4,0},{6,2},{1,5},{3,7},{5,1},{7,3},{8,12},{10,14},{12... | collective-permute-start | bytes 393224 | tf_op jit(solution)/shard_map/ppermute | solution.py:124
  605.4 82.8 %all-reduce.12.cloned.1.call-start = ((), (), s32[]{:S(2)}) async-start(), calls=%async_computation.3 | async-start | bytes 524288 | tf_op jit(solution)/shard_map/psum | solution.py:630
  (122 other events, 1040.8 us)
Sparse Core Ops, SparseCore 0:
  500.1 50.9 all-reduce.5
  554.1 51.1 all-reduce.7
  607.7 43.0 all-reduce.9
  653.6 34.6 all-reduce.11

commit v4 on v3

--- a/solution.py
+++ b/solution.py
@@ -22,6 +22,14 @@
 NT = (((1,), (1,)), ((), ()))
 TN = (((0,), (0,)), ((), ()))
 MIB = 1 << 20
+
+
+LIGHT = ("project_hidden", "first_back", "heads_back")
+
+
+def cost_of(name):
+    scale = 1e-6 if name in LIGHT else 1
+    return pl.CostEstimate(flops=int(1e13 * scale), bytes_accessed=int(1e9 * scale), transcendentals=0)
 
 
 def mm(left, right, contract):
@@ -68,9 +76,7 @@
         ],
         scratch_shapes=[pltpu.VMEM((SEQ, SEQ), F32)],
         compiler_params=pltpu.CompilerParams(vmem_limit_bytes=32 * MIB),
-        cost_estimate=pl.CostEstimate(
-            flops=pairs * 2 * 4 * SEQ * SEQ * 256, bytes_accessed=pairs * 2 * SEQ * SEQ * 2, transcendentals=pairs * 2 * SEQ * SEQ
-        ),
+        cost_estimate=cost_of("attend"),
         name="attend",
     )(qkv, labels[:, None], labels[None, :])
 
@@ -109,9 +115,7 @@
         out_specs=pl.BlockSpec((SEQ, 6 * HD), lambda i: (0, i)),
         out_shape=jax.ShapeDtypeStruct((SEQ, qkv.shape[1]), BF16),
         compiler_params=pltpu.CompilerParams(vmem_limit_bytes=32 * MIB),
-        cost_estimate=pl.CostEstimate(
-            flops=pairs * 2 * 10 * SEQ * SEQ * 256, bytes_accessed=pairs * 2 * SEQ * SEQ * 2, transcendentals=0
-        ),
+        cost_estimate=cost_of("attend_back"),
         name="attend_back",
     )(qkv, probs, grad)
 
@@ -130,6 +134,10 @@
 
 def after(value, *others):
     return lax.optimization_barrier((value, *others))[0]
+
+
+def after_all(values, *others):
+    return lax.optimization_barrier((*values, *others))[: len(values)]
 
 
 def add(*values):
@@ -147,8 +155,8 @@
     return jnp.concatenate([mine, swap_col(jnp.where(col == 0, second, first))], 1)
 
 
-def give_back(mine, leaving, odd, col):
-    other = swap_col(leaving).astype(F32)
+def give_back(mine, leaving, odd, col, *ties):
+    other = after(swap_col(leaving), *ties).astype(F32)
     first = jnp.where(col == 0, mine, other)
     second = jnp.where(col == 0, other, mine)
     rolled = jnp.concatenate([first[:SEQ], second[:SEQ], first[SEQ:], second[SEQ:]], 0)
@@ -168,26 +176,24 @@
     return jnp.concatenate(pieces, 0)
 
 
-def collect_heads(value, member, row):
-    width = value.shape[1]
-    whole = jnp.zeros((QUARTER, 4 * width), value.dtype)
-    for offset in range(4):
-        piece = value[offset * QUARTER : (offset + 1) * QUARTER]
-        if offset:
-            piece = lax.ppermute(piece, GRID, swap(offset))
+def send_heads(value):
+    pieces = [value[offset * QUARTER : (offset + 1) * QUARTER] for offset in range(4)]
+    return [piece if offset == 0 else lax.ppermute(piece, GRID, swap(offset)) for offset, piece in enumerate(pieces)]
+
+
+def join_heads(pieces, member, row):
+    width = pieces[0].shape[1]
+    whole = jnp.zeros((QUARTER, 4 * width), pieces[0].dtype)
+    for offset, piece in enumerate(pieces):
         whole = lax.dynamic_update_slice_in_dim(whole, piece, ((member ^ offset) ^ row) * width, 1)
     return whole
 
 
 class Shards:
-    def __init__(self, shard, depth):
-        half = depth // 2
+    def __init__(self, depth, shard, beside, across, *corners):
         self.depth, self.width = depth, shard.shape[1]
-        beside = swap_col(shard)
-        across = swap_row(shard)
-        top, bottom = swap_col(across[:half]), swap_row(beside[half:])
-        self.first = (beside, across)
-        near = [(0, 0, shard), (1, 0, beside), (4, 0, across), (5, 0, top), (5, half, bottom)]
+        near = [(0, 0, shard), (1, 0, beside), (4, 0, across)]
+        near += [(5, index * depth // 2, corner) for index, corner in enumerate(corners)]
         far = [(place + 2, start, swap_core(part)) for place, start, part in near]
         self.parts = near + far
 
@@ -246,7 +252,7 @@
         out_shape=out_shape,
         scratch_shapes=scratch + extra_scratch,
         compiler_params=pltpu.CompilerParams(vmem_limit_bytes=48 * MIB),
-        cost_estimate=pl.CostEstimate(flops=flops, bytes_accessed=flops // 640, transcendentals=0),
+        cost_estimate=cost_of(name),
         name=name,
     )
 
@@ -626,32 +632,87 @@
     return value
 
 
-def sum_dp(value, size):
-    return lax.psum(value, "dp")
-
-
-def reduce_grid(keep, leaving):
-    other = swap_core(leaving)
-    half = keep.shape[1] // 2
-    own, beside, across, corner = [(keep[k], other[k]) for k in range(4)]
-
-    def upper(pair):
-        return add(pair[0][:half], pair[1][:half])
-
-    def lower(pair):
-        return add(pair[0][half:], pair[1][half:])
-
-    from_col = swap_col(jnp.concatenate([upper(corner), upper(beside)], 0))
-    from_row = swap_row(jnp.concatenate([lower(corner), lower(across)], 0))
-    last_col = swap_col(add(beside[0][half:], beside[1][half:], from_row[:half]))
-    last_row = swap_row(add(across[0][:half], across[1][:half], from_col[:half]))
-    return jnp.concatenate(
-        [
-            add(own[0][:half], own[1][:half], from_col[half:], last_row),
-            add(own[0][half:], own[1][half:], from_row[half:], last_col),
-        ],
-        0,
-    )
+class PairSum:
+    def __init__(self, value, size):
+        self.whole = None
+        if size & (size - 1):
+            self.whole = lax.psum(value, "dp")
+        self.value, self.other = value, None
+        place = lax.axis_index("dp")
+        levels = [1 << k for k in range(size.bit_length() - 1)]
+        pairs = [([(i, i ^ step) for i in range(size)], (place // step) % 2 == 1) for step in levels]
+        self.plan = [(True, *pair) for pair in pairs] + [(False, *pair) for pair in reversed(pairs)]
+        self.upper = self.down = None
+        if self.whole is not None:
+            self.plan = []
+
+    def step(self, last):
+        self.take(last)
+        if not self.plan:
+            return self.value
+        self.down, pairs, self.upper = self.plan.pop(0)
+        if self.down:
+            half = self.value.shape[0] // 2
+            top, bottom = self.value[:half], self.value[half:]
+            self.value = jnp.where(self.upper, bottom, top)
+            leaving = jnp.where(self.upper, top, bottom)
+        else:
+            leaving = self.value
+        leaving = after(leaving, last)
+        self.other = lax.ppermute(leaving, "dp", pairs)
+        return leaving
+
+    def take(self, last):
+        if self.other is None:
+            return
+        other = after(self.other, last)
+        if self.down:
+            self.value = add(self.value, other)
+        else:
+            parts = jnp.where(self.upper, other, self.value), jnp.where(self.upper, self.value, other)
+            self.value = jnp.concatenate(parts, 0)
+        self.other = None
+
+    def result(self):
+        return self.value if self.whole is None else self.whole
+
+
+class GridSum:
+    def __init__(self, keep, leaving):
+        self.keep, self.other = keep, swap_core(leaving)
+        self.half = keep.shape[1] // 2
+        self.kernel = leaving
+
+    def upper(self, place, *more):
+        return add(self.keep[place, : self.half], self.other[place, : self.half], *more)
+
+    def lower(self, place, *more):
+        return add(self.keep[place, self.half :], self.other[place, self.half :], *more)
+
+    def send(self, *ties):
+        if ties:
+            self.other = after(self.other, *ties)
+        col = jnp.concatenate([self.upper(3), self.upper(1)], 0)
+        row = jnp.concatenate([self.lower(3), self.lower(2)], 0)
+        self.sent = lax.optimization_barrier((col, row))
+        self.from_col, self.from_row = swap_col(self.sent[0]), swap_row(self.sent[1])
+        return self.sent
+
+    def send_last(self, *ties):
+        if ties:
+            self.from_row, self.from_col = lax.optimization_barrier((self.from_row, self.from_col, *ties))[:2]
+        col = self.lower(1, self.from_row[: self.half])
+        row = self.upper(2, self.from_col[: self.half])
+        self.last = lax.optimization_barrier((col, row))
+        self.last_col, self.last_row = swap_col(self.last[0]), swap_row(self.last[1])
+        return self.last
+
+    def result(self, *ties):
+        from_col, last_row = self.from_col, self.last_row
+        if ties:
+            from_col, last_row = lax.optimization_barrier((from_col, last_row, *ties))[:2]
+        upper = self.upper(0, from_col[self.half :], last_row)
+        return jnp.concatenate([upper, self.lower(0, self.from_row[self.half :], self.last_col)], 0)
 
 
 def in_three(value):
@@ -691,12 +752,14 @@
     )
     riders = in_three(packed).reshape(15, 768)
     riders = jnp.concatenate([qkv_weight, riders, jnp.zeros((1, 768), BF16)], 0)
-    x = own_rows(tokens, odd, col)
-    qkv_w = Shards(riders, D // 2)
-    out_w = Shards(out_weight, D // 4)
-    ff_in_w = Shards(after(ff_in_weight, *qkv_w.first), D // 2)
-    incoming = own_rows(after(out_grad, *qkv_w.first), odd, col)
-    ff_out_w = Shards(after(ff_out_weight, *ff_in_w.first), D)
+    qkv_beside, qkv_across = swap_col(riders), swap_row(riders)
+    x = own_rows(after(tokens, qkv_beside), odd, col)
+    qkv_corner = swap_row(qkv_beside)
+    qkv_w = Shards(D // 2, riders, qkv_beside, qkv_across, qkv_corner)
+    out_beside = swap_col(after(out_weight, x))
+    out_across = swap_row(after(out_weight, qkv_corner))
+    incoming = own_rows(after(out_grad, out_beside), odd, col)
+    ff_in_across = swap_row(after(ff_in_weight, out_across))
 
     packed = qkv_w.riders()[:, :15].astype(F32).reshape(8, 3, packed.shape[0])
     packed = (packed[:, 0] + packed[:, 1]) + packed[:, 2]
@@ -717,40 +780,74 @@
 
     qkv = project_qkv(x, qkv_w, qkv_b)
     qkv_shared = spread_heads(qkv[SEQ:], member, row)
-    heads_own, probs_own = attend(qkv, labels)
-    heads_shared, probs_shared = attend(qkv_shared, shared)
-    heads = jnp.concatenate([heads_own, collect_heads(heads_shared, member, row)], 0)
-    unit_one, inverse_one, middle_low = first_norm(heads, out_w, x, vec)
+    heads_shared, probs_shared = attend(after(qkv_shared, incoming), shared)
+    pieces = send_heads(heads_shared)
+    ff_in_beside = swap_col(after(ff_in_weight, heads_shared))
+    half = out_weight.shape[0] // 2
+    out_corners = swap_col(out_across[:half]), swap_row(out_beside[half:])
+    out_w = Shards(D // 4, out_weight, out_beside, out_across, *out_corners)
+    heads_own, probs_own = attend(after(qkv, heads_shared, *[part for _, _, part in out_w.parts]), labels)
+    pieces = after_all(pieces, heads_own)
+    heads = jnp.concatenate([heads_own, join_heads(pieces, member, row)], 0)
+    ff_in_beside, ff_in_across, ff_out_weight = after_all((ff_in_beside, ff_in_across, ff_out_weight), heads)
+    half = ff_in_weight.shape[0] // 2
+    ff_in_corners = swap_col(ff_in_across[:half]), swap_row(ff_in_beside[half:])
+    ff_in_w = Shards(D // 2, ff_in_weight, ff_in_beside, ff_in_across, *ff_in_corners)
+    ff_out_beside, ff_out_across = swap_col(ff_out_weight), swap_row(ff_out_weight)
+    unit_one, inverse_one, middle_low = first_norm(after(heads, ff_in_beside, ff_in_across), out_w, x, vec)
     active, slope = project_hidden(middle_low, ff_in_w, ff_in_b)
+    ff_out_beside, ff_out_across = after_all((ff_out_beside, ff_out_across), active)
+    half = ff_out_weight.shape[0] // 2
+    ff_out_corners = swap_col(ff_out_across[:half]), swap_row(ff_out_beside[half:])
+    ff_out_w = Shards(D, ff_out_weight, ff_out_beside, ff_out_across, *ff_out_corners)
     out_mine, out_leave, back_two, d_two, sums_two = second_norm(active, ff_out_w, unit_one, incoming, vec)
 
-    ff_out_keep, ff_out_leave = grad_down(active, d_two)
-    d_two, out_leave, ff_out_leave = lax.optimization_barrier((d_two, out_leave, ff_out_leave))
-    ff_out_grad = reduce_grid(ff_out_keep, ff_out_leave)
-    ff_out_grad = sum_dp(ff_out_grad, n_dp)
-    d_hidden, ff_in_bias_part = hidden_back(d_two, ff_out_w, slope)
-    ff_in_keep, ff_in_leave = grad_up(middle_low, d_hidden)
-    d_hidden, ff_in_leave = lax.optimization_barrier((d_hidden, ff_in_leave))
-    ff_in_grad = reduce_grid(ff_in_keep, ff_in_leave)
-    layer_out = give_back(out_mine, out_leave, odd, col)
-    back_one, d_one, sums_one = first_back(d_hidden, ff_in_w, back_two, unit_one, inverse_one, vec)
+    ff_out = GridSum(*grad_down(active, d_two))
+    d_hidden, ff_in_bias_part = hidden_back(after(d_two, ff_out.kernel), ff_out_w, slope)
+    layer_out = give_back(out_mine, out_leave, odd, col, d_hidden)
+    ff_out.send(d_hidden, layer_out)
+    ff_in = GridSum(*grad_up(after(middle_low, *ff_out.sent), d_hidden))
+    back_one, d_one, sums_one = first_back(
+        after(d_hidden, ff_in.kernel), ff_in_w, back_two, unit_one, inverse_one, vec
+    )
     d_heads = heads_back(d_one, out_w)
     d_shared = spread_heads(d_heads[SEQ:], member, row)
-    d_qkv_own = attend_back(qkv, probs_own, d_heads)
-    d_qkv_shared = attend_back(qkv_shared, probs_shared, d_shared)
-    d_qkv = jnp.concatenate([d_qkv_own, collect_heads(d_qkv_shared, member, row)], 0)
-    qkv_keep, qkv_leave = grad_up(x, d_qkv)
-    d_qkv, d_one, qkv_leave = lax.optimization_barrier((d_qkv, d_one, qkv_leave))
-    qkv_grad = reduce_grid(qkv_keep, qkv_leave)
-    out_keep, out_leave = grad_down(heads, d_one)
-    d_qkv, out_leave = lax.optimization_barrier((d_qkv, out_leave))
-    out_w_grad = reduce_grid(out_keep, out_leave)
-    in_mine, in_leave, column_sums = input_back(d_qkv, qkv_w, back_one)
-    input_grad = give_back(in_mine, in_leave, odd, col)
-
-    ff_in_grad = sum_dp(after(ff_in_grad, ff_out_grad), n_dp)
-    qkv_grad = sum_dp(after(qkv_grad, ff_in_grad), n_dp)
-    out_w_grad = sum_dp(after(out_w_grad, qkv_grad), n_dp)
+    ff_out.send_last(d_heads)
+    d_qkv_shared = attend_back(qkv_shared, probs_shared, after(d_shared, *ff_out.last))
+    pieces = send_heads(d_qkv_shared)
+    ff_in.send(d_qkv_shared)
+    d_qkv_own = attend_back(qkv, probs_own, after(d_heads, *ff_in.sent))
+    d_qkv = jnp.concatenate([d_qkv_own, join_heads(after_all(pieces, d_qkv_own), member, row)], 0)
+    qkv_sum = GridSum(*grad_up(x, d_qkv))
+    ff_out_pairs = PairSum(ff_out.result(qkv_sum.kernel), n_dp)
+    event = ff_out_pairs.step(qkv_sum.kernel)
+    ff_in.send_last(event)
+    out_sum = GridSum(*grad_down(heads, after(d_one, *ff_in.last)))
+    event = ff_out_pairs.step(out_sum.kernel)
+    qkv_sum.send(event)
+    in_mine, in_leave, column_sums = input_back(after(d_qkv, *qkv_sum.sent), qkv_w, back_one)
+    ff_in_pairs = PairSum(ff_in.result(in_leave), n_dp)
+    event = ff_in_pairs.step(in_leave)
+    event = ff_out_pairs.step(event)
+    out_sum.send(event)
+    qkv_sum.send_last(*out_sum.sent)
+    event = ff_in_pairs.step(qkv_sum.last[0])
+    event = ff_out_pairs.step(event)
+    out_sum.send_last(event)
+    input_grad = give_back(*after_all((in_mine, in_leave), *out_sum.last), odd, col)
+    event = ff_in_pairs.step(out_sum.last[0])
+    event = ff_out_pairs.step(event)
+    qkv_pairs = PairSum(qkv_sum.result(event), n_dp)
+    event = qkv_pairs.step(event)
+    out_pairs = PairSum(out_sum.result(event), n_dp)
+    sums_start = event = out_pairs.step(event)
+    every = [ff_out_pairs, ff_in_pairs, qkv_pairs, out_pairs]
+    while any(pairs.plan for pairs in every):
+        for pairs in every:
+            event = pairs.step(event)
+    for pairs in every:
+        pairs.take(event)
+    ff_out_grad, ff_in_grad, qkv_grad, out_w_grad = [pairs.result() for pairs in every]
 
     def across_grid(value):
         return sum_devices(sum_devices(value, "row", 4), "col", 2)
@@ -762,25 +859,36 @@
     place = row * 2 + col
     halves = jnp.concatenate([sums_one, sums_two], 0)
     halves = jnp.concatenate(in_order(halves[:, : D // 2], halves[:, D // 2 :]), 1)
-    early = across_grid(jnp.concatenate([halves.reshape(-1), ordered(ff_in_bias_part).reshape(-1)]))
+    column_sums = ordered(column_sums).reshape(-1, 3, HD)
+    early = jnp.concatenate(
+        [
+            halves.reshape(-1),
+            ordered(ff_in_bias_part).reshape(-1),
+            jnp.concatenate([column_sums[:, 0], column_sums[:, 2]], 1).reshape(-1),
+        ]
+    )
+    early = across_grid(after(early, sums_start))
     halves = lax.dynamic_slice_in_dim(early[: 6 * D].reshape(6, 2, D // 2), col, 1, 1)[:, 0]
-    early = jnp.concatenate([halves.reshape(-1), lax.dynamic_slice_in_dim(early, 6 * D + place * 512, 512)])
+    early = jnp.concatenate(
+        [
+            halves.reshape(-1),
+            lax.dynamic_slice_in_dim(early, 6 * D + place * 512, 512),
+            lax.dynamic_slice_in_dim(early, 10 * D + place * 256, 256),
+        ]
+    )
     early = sum_devices(early, "dp", n_dp)
-    column_sums = ordered(column_sums).reshape(-1, 3, HD)
-    late = across_grid(jnp.concatenate([column_sums[:, 0], column_sums[:, 2]], 1).reshape(-1))
-    late = sum_devices(lax.dynamic_slice_in_dim(late, place * 256, 256), "dp", n_dp)
     halves = early[: 6 * 512].reshape(6, 512)
     return (
         layer_out,
         input_grad,
         qkv_grad.astype(F32),
-        late.reshape(2, 2 * HD),
+        early[7 * 512 :].reshape(2, 2 * HD),
         out_w_grad.astype(F32),
         halves[0],
         halves[1],
         halves[2],
         ff_in_grad.astype(F32),
-        early[6 * 512 :],
+        early[6 * 512 : 7 * 512],
         ff_out_grad.astype(F32),
         halves[3],
         halves[4],

time: 703 us -> 522 us (0.74)
  waiting for transfers between devices: 325 us -> 139 us
  starting transfers between devices: 58.8 us -> 76.3 us
  between operations: 15.5 us -> 2.63 us
    psum x4 -> x0, waiting for transfers between devices: 133 us -> none  [sum_dp(): return lax.psum(value, 'dp')]
    ppermute x16, waiting for transfers between devices: 41.7 us -> 12.8 us  [swap_row(): return lax.ppermute(value, 'row', [(i, i ^ 2) for i in range(4)])]
    ppermute x6 -> x22, starting transfers between devices: 4.19 us -> 22.3 us  [the longest x16 18 us: step(): self.other = lax.ppermute(leaving, 'dp', pairs)]
    select_n x0 -> x16, other arithmetic: none -> 16.9 us  [the longest x8 14.2 us: step(): leaving = jnp.where(self.upper, top, bottom)]
    ppermute x6, waiting for transfers between devices: 19.2 us -> 2.49 us  [spread_heads(): lax.ppermute(piece, GRID, swap(offset))]
    ppermute x20 -> x19, waiting for transfers between devices: 77.6 us -> 65.6 us  [swap_col(): return lax.ppermute(value, 'col', [(0, 1), (1, 0)])]
    ppermute x6 -> x22, waiting for transfers between devices: 33.8 us -> 42.9 us  [the longest x16 42.9 us: step(): self.other = lax.ppermute(leaving, 'dp', pairs)]
    unnamed x177 -> x147, local copies, waits for them, and re-layouts: 41.7 us -> 32.6 us
  transfers between devices with their start and end apart: 86 -> 91, of which waited for: 32 -> 32; matrix products, arithmetic and copies ran while one was open for 13% -> 19% of each run, Pallas kernels for 13% -> 26%
where the time goes in v4:
time: 522 us; the launch traced here: 516 us
  Pallas kernels  161 us (31%)
  waiting for transfers between devices  139 us (27%)
  other arithmetic  76.4 us (15%)
  starting transfers between devices  76.3 us (15%)
  local copies, waits for them, and re-layouts  60.8 us (12%)
    ppermute x19, waiting for transfers between devices, swap_col(): return lax.ppermute(value, 'col', [(0, 1), (1, 0)])  65.6 us
    ppermute x16, waiting for transfers between devices, step(): self.other = lax.ppermute(leaving, 'dp', pairs)  42.9 us
    unnamed x147, local copies, waits for them, and re-layouts  32.6 us
    convert_element_type x16, other arithmetic, add(): return total.astype(BF16)  25.2 us
    ppermute x19, starting transfers between devices, swap_col(): return lax.ppermute(value, 'col', [(0, 1), (1, 0)])  23.9 us
    pallas_call x2, Pallas kernels, grad_up(): dense(grad_up_kernel, [whole(left), columns_of(right)], [two_blocks(out)]...  19.3 us
    pallas_call x1, Pallas kernels, second_norm(): dense(second_norm_kernel, [columns_of(active), whole(unit), whole(incomin...  19.2 us
    ppermute x16, starting transfers between devices, swap_row(): return lax.ppermute(value, 'row', [(i, i ^ 2) for i in range(4)])  18.6 us
  transfers between devices with their start and end apart: 91, of which 32 were waited for; matrix products, arithmetic and copies ran while one was open for 19% of the time, Pallas kernels for 26%

profile of v4, /device:TPU:0, one launch (start us, length us, event | category | flops | bytes accessed | tf_op | source)
XLA Modules:
  0.0 516.3 jit_solution(6820676073248571493)
XLA Ops:
  7.8 3.0 collective-permute-start
  12.4 16.5 %collective-permute-done.refs_1_ = bf16[528,768]{1,0:T(8,128)(2,1)S(1)} collective-permute-done((bf16[528,768]{1,0:T(8,128)(2,1)S(1)}, bf16[528,768]{1,0:T(8,128)(2,1)S(1)}, u32[]{:S(2)}, u32[]{:S(2)}) %collective-permute-start) | collective-permute-done | bytes 811040 | tf_op jit(solution)/shard_map/ppermute | solution.py:132
  34.7 10.9 %collective-permute-done.7 = bf16[640,512]{1,0:T(8,128)(2,1)S(1)} collective-permute-done((bf16[640,512]{1,0:T(8,128)(2,1)S(1)}, bf16[640,512]{1,0:T(8,128)(2,1)S(1)}, u32[]{:S(2)}, u32[]{:S(2)}) %collective-permute-start.7) | collective-permute-done | bytes 655392 | tf_op jit(solution)/shard_map/ppermute | solution.py:132
  48.2 3.7 collective-permute-done.2.refs_3_
  68.9 8.0 %project_qkv.1.qkv_ref = bf16[640,3072]{1,0:T(8,128)(2,1)} custom-call(bf16[528,768]{1,0:T(8,128)(2,1)S(1)} %maximum_maximum_fusion.refs_0_, bf16[528,768]{1,0:T(8,128)(2,1)S(1)} %collective-permute-done.refs_1_, bf16[528,768]{1,0:T(8,128)(2,1)S(1)} %collective-permute-done.1.refs_2_, bf16[528,768]{1,0:T(8,128)(2,1)S(1)} %copy-done.30, ...), custom_call_target="tpu_custom_call" | custom-call | flops 9999999827968 | bytes 1000000000 | tf_op jit(solution)/shard_map/project_qkv/pallas_call | solution.py:288
  88.2 4.3 collective-permute-done.16.refs_3_
  93.6 3.2 attend.2
  103.0 12.2 %attend.3 = (bf16[512,1024]{1,0:T(8,128)(2,1)S(1)}, bf16[16,512,512]{2,1,0:T(8,128)(2,1)S(1)}) custom-call(bf16[640,3072]{1,0:T(8,128)(2,1)S(1)} %copy-done.18, s32[512,1]{1,0:T(8,128)S(1)} %copy.36.column_ref, s32[1,512]{1,0:T(1,128)S(1)} %bitcast.196), custom_call_target="tpu_custom_call" | custom-call | flops 9999999827968 | bytes 1000000000 | tf_op jit(solution)/shard_map/attend/pallas_call | solution.py:61
  115.2 3.3 copy-done.34
  121.3 3.0 collective-permute-done.15.refs_2_
  124.2 3.8 collective-permute-done.13.refs_1_
  133.1 9.4 %collective-permute-done.28.refs_3_ = bf16[256,1024]{1,0:T(8,128)(2,1)S(1)} collective-permute-done((bf16[256,1024]{1,0:T(8,128)(2,1)S(1)}, bf16[256,1024]{1,0:T(8,128)(2,1)S(1)}, u32[]{:S(2)}, u32[]{:S(2)}) %collective-permute-start.28) | collective-permute-done | bytes 524320 | tf_op jit(solution)/shard_map/ppermute | solution.py:132
  146.9 10.3 %first_norm.1 = (f32[640,1024]{1,0:T(8,128)}, f32[640,1]{1,0:T(8,128)S(1)}, bf16[640,1024]{1,0:T(8,128)(2,1)S(1)}) custom-call(bf16[256,512]{1,0:T(8,128)(2,1)} %refs_0_.9, bf16[256,512]{1,0:T(8,128)(2,1)} %collective-permute-done.11.refs_1_, bf16[256,512]{1,0:T(8,128)(2,1)} %collective-permute-done.14.refs_2_, ...), custom_call_target="tpu_custom_call" | custom-call | flops 9999999827968 | bytes 1000000000 | tf_op jit(solution)/shard_map/first_norm/pallas_call | solution.py:391
  158.7 14.3 %project_hidden.1 = (bf16[640,4096]{1,0:T(8,128)(2,1)}, bf16[640,4096]{1,0:T(8,128)(2,1)}) custom-call(bf16[512,1024]{1,0:T(8,128)(2,1)} %refs_0_.8, bf16[512,1024]{1,0:T(8,128)(2,1)} %collective-permute-done.13.refs_1_, bf16[512,1024]{1,0:T(8,128)(2,1)} %collective-permute-done.15.refs_2_, bf16[256,1024]{1,0:T(8,128)(2,1)S(1)} %collective-permute-done.28.refs_3_, ...), custom_call_target="tpu_custom_call" | custom-call | flops 10000000 | bytes 1000 | tf_op jit(solution)/shard_map/project_hidden/pallas_call | solution.py:313
  177.2 10.8 %collective-permute-done.35.refs_3_ = bf16[512,512]{1,0:T(8,128)(2,1)S(1)} collective-permute-done((bf16[512,512]{1,0:T(8,128)(2,1)S(1)}, bf16[512,512]{1,0:T(8,128)(2,1)S(1)}, u32[]{:S(2)}, u32[]{:S(2)}) %collective-permute-start.35) | collective-permute-done | bytes 524320 | tf_op jit(solution)/shard_map/ppermute | solution.py:132
  192.2 19.2 %second_norm.1 = (f32[640,512]{1,0:T(8,128)}, bf16[640,512]{1,0:T(8,128)(2,1)}, f32[640,1024]{1,0:T(8,128)}, bf16[640,1024]{1,0:T(8,128)(2,1)}, f32[3,1024]{1,0:T(4,128)S(1)}) custom-call(bf16[1024,512]{1,0:T(8,128)(2,1)} %refs_0_.7, bf16[1024,512]{1,0:T(8,128)(2,1)} %collective-permute-done.26.refs_1_, bf16[1024,512]{1,0:T(8,128)(2,1)} %collective-permute-done.27.refs_2_, ...), custom_call_target="tpu_custom_call" | custom-call | flops 9999999827968 | bytes 1000000000 | tf_op jit(solution)/shard_map/second_norm/pallas_call | solution.py:442
  212.7 10.4 %grad_down.2 = (bf16[4,1024,512]{2,1,0:T(8,128)(2,1)S(1)}, bf16[4,1024,512]{2,1,0:T(8,128)(2,1)}) custom-call(bf16[640,4096]{1,0:T(8,128)(2,1)} %get-tuple-element.164.refs_10_.left_ref, bf16[640,1024]{1,0:T(8,128)(2,1)S(1)} %copy-done.38), custom_call_target="tpu_custom_call" | custom-call | flops 9999999827968 | bytes 1000000000 | tf_op jit(solution)/shard_map/grad_down/pallas_call | solution.py:614
  226.5 11.4 %hidden_back.1 = (bf16[640,4096]{1,0:T(8,128)(2,1)}, f32[1,4096]{1,0:T(1,128)S(1)}) custom-call(bf16[1024,512]{1,0:T(8,128)(2,1)} %refs_0_.7, bf16[1024,512]{1,0:T(8,128)(2,1)} %collective-permute-done.26.refs_1_, bf16[1024,512]{1,0:T(8,128)(2,1)} %collective-permute-done.27.refs_2_, bf16[512,512]{1,0:T(8,128)(2,1)S(1)} %collective-permute-done.35.refs_3_, ...), custom_call_target="tpu_custom_call" | custom-call | flops 9999999827968 | bytes 1000000000 | tf_op jit(solution)/shard_map/hidden_back/pallas_call | solution.py:538
  239.7 2.9 collective-permute-done.42
  253.0 10.6 %grad_up.2 = (bf16[4,512,1024]{2,1,0:T(8,128)(2,1)S(1)}, bf16[4,512,1024]{2,1,0:T(8,128)(2,1)}) custom-call(bf16[640,1024]{1,0:T(8,128)(2,1)S(1)} %copy-done.8, bf16[640,4096]{1,0:T(8,128)(2,1)} %get-tuple-element.183.right_ref.refs_10_), custom_call_target="tpu_custom_call" | custom-call | flops 9999999827968 | bytes 1000000000 | tf_op jit(solution)/shard_map/grad_up/pallas_call | solution.py:589
  265.5 17.6 %first_back.1 = (f32[640,1024]{1,0:T(8,128)}, bf16[640,1024]{1,0:T(8,128)(2,1)}, f32[3,1024]{1,0:T(4,128)S(1)}) custom-call(bf16[512,1024]{1,0:T(8,128)(2,1)} %refs_0_.8, bf16[512,1024]{1,0:T(8,128)(2,1)} %collective-permute-done.13.refs_1_, bf16[512,1024]{1,0:T(8,128)(2,1)} %collective-permute-done.15.refs_2_, ...), custom_call_target="tpu_custom_call" | custom-call | flops 10000000 | bytes 1000 | tf_op jit(solution)/shard_map/first_back/pallas_call | solution.py:482
  284.4 3.4 heads_back.1.grad_ref
  294.4 3.4 fusion.10
  300.2 3.6 attend_back.2
  306.8 3.3 fusion.24
  312.2 3.4 copy-done.35
  315.6 13.4 %attend_back.3 = bf16[512,3072]{1,0:T(8,128)(2,1)S(1)} custom-call(bf16[640,3072]{1,0:T(8,128)(2,1)S(1)} %copy-done.19, bf16[16,512,512]{2,1,0:T(8,128)(2,1)S(1)} %copy-done.35, bf16[640,1024]{1,0:T(8,128)(2,1)S(1)} %copy-done.6), custom_call_target="tpu_custom_call" | custom-call | flops 9999999827968 | bytes 1000000000 | tf_op jit(solution)/shard_map/attend_back/pallas_call | solution.py:107
  335.9 8.8 %grad_up.3 = (bf16[4,512,768]{2,1,0:T(8,128)(2,1)S(1)}, bf16[4,512,768]{2,1,0:T(8,128)(2,1)}) custom-call(bf16[640,1024]{1,0:T(8,128)(2,1)S(1)} %copy-done.11, bf16[640,3072]{1,0:T(8,128)(2,1)} %pad_maximum_fusion.right_ref.refs_8_), custom_call_target="tpu_custom_call" | custom-call | flops 9999999827968 | bytes 1000000000 | tf_op jit(solution)/shard_map/grad_up/pallas_call | solution.py:589
  344.6 4.8 broadcast_select_fusion.9
  351.2 3.3 collective-permute-done.57
  354.8 3.5 fusion.4
  361.0 3.6 grad_down.3
  367.0 2.6 collective-permute-start.60
  373.9 11.5 %input_back.1 = (f32[640,512]{1,0:T(8,128)}, bf16[640,512]{1,0:T(8,128)(2,1)}, f32[1,3072]{1,0:T(1,128)S(1)}) custom-call(bf16[528,768]{1,0:T(8,128)(2,1)S(1)} %copy-done.15, bf16[528,768]{1,0:T(8,128)(2,1)S(1)} %copy-done.21, bf16[528,768]{1,0:T(8,128)(2,1)S(1)} %copy-done.25, bf16[528,768]{1,0:T(8,128)(2,1)S(1)} %copy-done.31, ...), custom_call_target="tpu_custom_call" | custom-call | flops 9999999827968 | bytes 1000000000 | tf_op jit(solution)/shard_map/input_back/pallas_call | solution.py:508
  386.3 3.9 broadcast_select_fusion.6
  399.7 6.6 %collective-permute-done.68 = bf16[512,768]{1,0:T(8,128)(2,1)} collective-permute-done((bf16[512,768]{1,0:T(8,128)(2,1)}, bf16[512,768]{1,0:T(8,128)(2,1)}, u32[]{:S(2)}, u32[]{:S(2)}) %collective-permute-start.68) | collective-permute-done | bytes 786464 | tf_op jit(solution)/shard_map/ppermute | solution.py:132
  419.1 3.7 collective-permute-done.73
  425.2 4.4 collective-permute-done.72
  433.1 2.7 broadcast_select_fusion.12
  437.7 3.5 collective-permute-start.82
  441.3 5.2 %collective-permute-done.75 = bf16[128,1024]{1,0:T(8,128)(2,1)} collective-permute-done((bf16[128,1024]{1,0:T(8,128)(2,1)}, bf16[128,1024]{1,0:T(8,128)(2,1)}, u32[]{:S(2)}, u32[]{:S(2)}) %collective-permute-start.75) | collective-permute-done | bytes 262176 | tf_op jit(solution)/shard_map/ppermute | solution.py:662
  451.4 2.3 collective-permute-start.87
  462.5 6.6 %collective-permute-done.88 = f32[3840]{0:T(1024)S(1)} collective-permute-done((f32[3840]{0:T(1024)S(1)}, f32[3840]{0:T(1024)S(1)}, u32[]{:S(2)}, u32[]{:S(2)}) %collective-permute-start.88) | collective-permute-done | bytes 15392 | tf_op jit(solution)/shard_map/ppermute | solution.py:630
  471.1 2.8 collective-permute-done.89
  476.8 2.9 collective-permute-start.83
  481.5 5.8 %collective-permute-done.76 = bf16[128,768]{1,0:T(8,128)(2,1)S(1)} collective-permute-done((bf16[128,768]{1,0:T(8,128)(2,1)S(1)}, bf16[128,768]{1,0:T(8,128)(2,1)S(1)}, u32[]{:S(2)}, u32[]{:S(2)}) %collective-permute-start.76) | collective-permute-done | bytes 196640 | tf_op jit(solution)/shard_map/ppermute | solution.py:662
  490.4 9.2 %collective-permute-done.78 = bf16[128,768]{1,0:T(8,128)(2,1)S(1)} collective-permute-done((bf16[128,768]{1,0:T(8,128)(2,1)S(1)}, bf16[128,768]{1,0:T(8,128)(2,1)S(1)}, u32[]{:S(2)}, u32[]{:S(2)}) %collective-permute-start.78) | collective-permute-done | bytes 196640 | tf_op jit(solution)/shard_map/ppermute | solution.py:662
  502.5 11.1 %collective-permute-done.90 = bf16[128,512]{1,0:T(8,128)(2,1)S(1)} collective-permute-done((bf16[128,512]{1,0:T(8,128)(2,1)S(1)}, bf16[128,512]{1,0:T(8,128)(2,1)S(1)}, u32[]{:S(2)}, u32[]{:S(2)}) %collective-permute-start.90) | collective-permute-done | bytes 131104 | tf_op jit(solution)/shard_map/ppermute | solution.py:662
  (463 shorter events, 185.8 us)
Async XLA Ops:
  7.8 21.1 %collective-permute-start = (bf16[528,768]{1,0:T(8,128)(2,1)S(1)}, bf16[528,768]{1,0:T(8,128)(2,1)S(1)}, u32[]{:S(2)}, u32[]{:S(2)}) collective-permute-start(bf16[528,768]{1,0:T(8,128)(2,1)S(1)} %maximum_maximum_fusion.refs_0_), channel_id=1, source_target_pairs={{0,1},{1,0},{2,3},{3,2},{4,5},{5,4},{6,7},{7,6},{8,9},{9,8},{10,11... | collective-permute-start | bytes 2433032 | tf_op jit(solution)/shard_map/ppermute | solution.py:132
  10.8 23.9 %collective-permute-start.3 = (bf16[528,768]{1,0:T(8,128)(2,1)S(1)}, bf16[528,768]{1,0:T(8,128)(2,1)S(1)}, u32[]{:S(2)}, u32[]{:S(2)}) collective-permute-start(bf16[528,768]{1,0:T(8,128)(2,1)S(1)} %maximum_maximum_fusion.refs_0_), channel_id=1, source_target_pairs={{0,2},{2,0},{4,6},{6,4},{1,3},{3,1},{5,7},{7,5},{8,10},{10,8},{12,... | collective-permute-start | bytes 2433032 | tf_op jit(solution)/shard_map/ppermute | solution.py:124
  10.8 23.6 %collective-permute-start.1 = (bf16[528,768]{1,0:T(8,128)(2,1)S(1)}, bf16[528,768]{1,0:T(8,128)(2,1)S(1)}, u32[]{:S(2)}, u32[]{:S(2)}) collective-permute-start(bf16[528,768]{1,0:T(8,128)(2,1)S(1)} %maximum_maximum_fusion.refs_0_), channel_id=1, source_target_pairs={{0,4},{2,6},{4,0},{6,2},{1,5},{3,7},{5,1},{7,3},{8,12},{10,14},{12... | collective-permute-start | bytes 2433032 | tf_op jit(solution)/shard_map/ppermute | solution.py:128
  29.6 16.0 %collective-permute-start.7 = (bf16[640,512]{1,0:T(8,128)(2,1)S(1)}, bf16[640,512]{1,0:T(8,128)(2,1)S(1)}, u32[]{:S(2)}, u32[]{:S(2)}) collective-permute-start(bf16[640,512]{1,0:T(8,128)(2,1)S(1)} %get-tuple-element.323), channel_id=1, source_target_pairs={{0,1},{1,0},{2,3},{3,2},{4,5},{5,4},{6,7},{7,6},{8,9},{9,8},{10,11... | collective-permute-start | bytes 1966088 | tf_op jit(solution)/shard_map/ppermute | solution.py:132
  31.4 22.0 %collective-permute-start.4 = (bf16[528,768]{1,0:T(8,128)(2,1)S(1)}, bf16[528,768]{1,0:T(8,128)(2,1)S(1)}, u32[]{:S(2)}, u32[]{:S(2)}) collective-permute-start(bf16[528,768]{1,0:T(8,128)(2,1)S(1)} %collective-permute-done.refs_1_), channel_id=1, source_target_pairs={{0,2},{2,0},{4,6},{6,4},{1,3},{3,1},{5,7},{7,5},{8,10},{10,8},{12,... | collective-permute-start | bytes 2433032 | tf_op jit(solution)/shard_map/ppermute | solution.py:124
  31.4 20.5 %collective-permute-start.2 = (bf16[528,768]{1,0:T(8,128)(2,1)S(1)}, bf16[528,768]{1,0:T(8,128)(2,1)S(1)}, u32[]{:S(2)}, u32[]{:S(2)}) collective-permute-start(bf16[528,768]{1,0:T(8,128)(2,1)S(1)} %collective-permute-done.refs_1_), channel_id=1, source_target_pairs={{0,4},{2,6},{4,0},{6,2},{1,5},{3,7},{5,1},{7,3},{8,12},{10,14},{12... | collective-permute-start | bytes 2433032 | tf_op jit(solution)/shard_map/ppermute | solution.py:128
  34.4 20.8 %collective-permute-start.5 = (bf16[528,768]{1,0:T(8,128)(2,1)S(1)}, bf16[528,768]{1,0:T(8,128)(2,1)S(1)}, u32[]{:S(2)}, u32[]{:S(2)}) collective-permute-start(bf16[528,768]{1,0:T(8,128)(2,1)S(1)} %collective-permute-done.1.refs_2_), channel_id=1, source_target_pairs={{0,2},{2,0},{4,6},{6,4},{1,3},{3,1},{5,7},{7,5},{8,10},{10,8},{12,... | collective-permute-start | bytes 2433032 | tf_op jit(solution)/shard_map/ppermute | solution.py:124
  51.9 30.2 %collective-permute-start.14 = (bf16[256,512]{1,0:T(8,128)(2,1)}, bf16[256,512]{1,0:T(8,128)(2,1)}, u32[]{:S(2)}, u32[]{:S(2)}) collective-permute-start(bf16[256,512]{1,0:T(8,128)(2,1)} %refs_0_.9), channel_id=1, source_target_pairs={{0,4},{2,6},{4,0},{6,2},{1,5},{3,7},{5,1},{7,3},{8,12},{10,14},{12... | collective-permute-start | bytes 786440 | tf_op jit(solution)/shard_map/ppermute | solution.py:128
  58.0 25.4 %collective-permute-start.12 = (bf16[640,512]{1,0:T(8,128)(2,1)}, bf16[640,512]{1,0:T(8,128)(2,1)}, u32[]{:S(2)}, u32[]{:S(2)}) collective-permute-start(bf16[640,512]{1,0:T(8,128)(2,1)} %get-tuple-element.317), channel_id=1, source_target_pairs={{0,1},{1,0},{2,3},{3,2},{4,5},{5,4},{6,7},{7,6},{8,9},{9,8},{10,11... | collective-permute-start | bytes 1966088 | tf_op jit(solution)/shard_map/ppermute | solution.py:132
  98.8 25.4 %collective-permute-start.15 = (bf16[512,1024]{1,0:T(8,128)(2,1)}, bf16[512,1024]{1,0:T(8,128)(2,1)}, u32[]{:S(2)}, u32[]{:S(2)}) collective-permute-start(bf16[512,1024]{1,0:T(8,128)(2,1)} %refs_0_.8), channel_id=1, source_target_pairs={{0,4},{2,6},{4,0},{6,2},{1,5},{3,7},{5,1},{7,3},{8,12},{10,14},{12... | collective-permute-start | bytes 3145736 | tf_op jit(solution)/shard_map/ppermute | solution.py:128
  99.1 19.4 %collective-permute-start.23 = (bf16[128,256]{1,0:T(8,128)(2,1)}, bf16[128,256]{1,0:T(8,128)(2,1)}, u32[]{:S(2)}, u32[]{:S(2)}) collective-permute-start(bf16[128,256]{1,0:T(8,128)(2,1)} %get-tuple-element.360), channel_id=1, source_target_pairs={{0,1},{1,0},{2,3},{3,2},{4,5},{5,4},{6,7},{7,6},{8,9},{9,8},{10,11... | collective-permute-start | bytes 196616 | tf_op jit(solution)/shard_map/ppermute | solution.py:181
  100.9 17.7 %collective-permute-start.24 = (bf16[128,256]{1,0:T(8,128)(2,1)}, bf16[128,256]{1,0:T(8,128)(2,1)}, u32[]{:S(2)}, u32[]{:S(2)}) collective-permute-start(bf16[128,256]{1,0:T(8,128)(2,1)} %get-tuple-element.359), channel_id=1, source_target_pairs={{0,2},{1,3},{2,0},{3,1},{4,6},{5,7},{6,4},{7,5},{8,10},{9,11},{10,... | collective-permute-start | bytes 196616 | tf_op jit(solution)/shard_map/ppermute | solution.py:181
  100.9 17.7 %collective-permute-start.25 = (bf16[128,256]{1,0:T(8,128)(2,1)}, bf16[128,256]{1,0:T(8,128)(2,1)}, u32[]{:S(2)}, u32[]{:S(2)}) collective-permute-start(bf16[128,256]{1,0:T(8,128)(2,1)} %get-tuple-element.358), channel_id=1, source_target_pairs={{0,3},{1,2},{2,1},{3,0},{4,7},{5,6},{6,5},{7,4},{8,11},{9,10},{10,... | collective-permute-start | bytes 196616 | tf_op jit(solution)/shard_map/ppermute | solution.py:181
  101.3 26.7 %collective-permute-start.13 = (bf16[512,1024]{1,0:T(8,128)(2,1)}, bf16[512,1024]{1,0:T(8,128)(2,1)}, u32[]{:S(2)}, u32[]{:S(2)}) collective-permute-start(bf16[512,1024]{1,0:T(8,128)(2,1)} %refs_0_.8), channel_id=1, source_target_pairs={{0,1},{1,0},{2,3},{3,2},{4,5},{5,4},{6,7},{7,6},{8,9},{9,8},{10,11... | collective-permute-start | bytes 3145736 | tf_op jit(solution)/shard_map/ppermute | solution.py:132
  118.6 25.6 %collective-permute-start.30 = (bf16[512,1024]{1,0:T(8,128)(2,1)}, bf16[512,1024]{1,0:T(8,128)(2,1)}, u32[]{:S(2)}, u32[]{:S(2)}) collective-permute-start(bf16[512,1024]{1,0:T(8,128)(2,1)} %refs_0_.8), channel_id=1, source_target_pairs={{0,2},{2,0},{4,6},{6,4},{1,3},{3,1},{5,7},{7,5},{8,10},{10,8},{12,... | collective-permute-start | bytes 3145736 | tf_op jit(solution)/shard_map/ppermute | solution.py:124
  144.2 28.9 %collective-permute-start.26 = (bf16[1024,512]{1,0:T(8,128)(2,1)}, bf16[1024,512]{1,0:T(8,128)(2,1)}, u32[]{:S(2)}, u32[]{:S(2)}) collective-permute-start(bf16[1024,512]{1,0:T(8,128)(2,1)} %refs_0_.7), channel_id=1, source_target_pairs={{0,1},{1,0},{2,3},{3,2},{4,5},{5,4},{6,7},{7,6},{8,9},{9,8},{10,11... | collective-permute-start | bytes 3145736 | tf_op jit(solution)/shard_map/ppermute | solution.py:132
  145.2 27.9 %collective-permute-start.27 = (bf16[1024,512]{1,0:T(8,128)(2,1)}, bf16[1024,512]{1,0:T(8,128)(2,1)}, u32[]{:S(2)}, u32[]{:S(2)}) collective-permute-start(bf16[1024,512]{1,0:T(8,128)(2,1)} %refs_0_.7), channel_id=1, source_target_pairs={{0,4},{2,6},{4,0},{6,2},{1,5},{3,7},{5,1},{7,3},{8,12},{10,14},{12... | collective-permute-start | bytes 3145736 | tf_op jit(solution)/shard_map/ppermute | solution.py:128
  158.2 31.7 %collective-permute-start.37 = (bf16[1024,512]{1,0:T(8,128)(2,1)}, bf16[1024,512]{1,0:T(8,128)(2,1)}, u32[]{:S(2)}, u32[]{:S(2)}) collective-permute-start(bf16[1024,512]{1,0:T(8,128)(2,1)} %refs_0_.7), channel_id=1, source_target_pairs={{0,2},{2,0},{4,6},{6,4},{1,3},{3,1},{5,7},{7,5},{8,10},{10,8},{12,... | collective-permute-start | bytes 3145736 | tf_op jit(solution)/shard_map/ppermute | solution.py:124
  225.2 21.4 %collective-permute-start.43 = (bf16[4,1024,512]{2,1,0:T(8,128)(2,1)}, bf16[4,1024,512]{2,1,0:T(8,128)(2,1)}, u32[]{:S(2)}, u32[]{:S(2)}) collective-permute-start(bf16[4,1024,512]{2,1,0:T(8,128)(2,1)} %get-tuple-element.171), channel_id=1, source_target_pairs={{0,2},{2,0},{4,6},{6,4},{1,3},{3,1},{5,7},{7,5},{8,10},{10,8},{12,... | collective-permute-start | bytes 12582920 | tf_op jit(solution)/shard_map/ppermute | solution.py:124
  225.3 17.3 %collective-permute-start.42 = (bf16[640,512]{1,0:T(8,128)(2,1)}, bf16[640,512]{1,0:T(8,128)(2,1)}, u32[]{:S(2)}, u32[]{:S(2)}) collective-permute-start(bf16[640,512]{1,0:T(8,128)(2,1)} %get-tuple-element.169), channel_id=1, source_target_pairs={{0,1},{1,0},{2,3},{3,2},{4,5},{5,4},{6,7},{7,6},{8,9},{9,8},{10,11... | collective-permute-start | bytes 1966088 | tf_op jit(solution)/shard_map/ppermute | solution.py:132
  251.5 42.9 %collective-permute-start.48 = (bf16[1024,512]{1,0:T(8,128)(2,1)}, bf16[1024,512]{1,0:T(8,128)(2,1)}, u32[]{:S(2)}, u32[]{:S(2)}) collective-permute-start(bf16[1024,512]{1,0:T(8,128)(2,1)} %get-tuple-element.180), channel_id=1, source_target_pairs={{0,4},{2,6},{4,0},{6,2},{1,5},{3,7},{5,1},{7,3},{8,12},{10,14},{12... | collective-permute-start | bytes 3145736 | tf_op jit(solution)/shard_map/ppermute | solution.py:128
  252.0 42.4 %collective-permute-start.49 = (bf16[1024,512]{1,0:T(8,128)(2,1)}, bf16[1024,512]{1,0:T(8,128)(2,1)}, u32[]{:S(2)}, u32[]{:S(2)}) collective-permute-start(bf16[1024,512]{1,0:T(8,128)(2,1)} %get-tuple-element.179), channel_id=1, source_target_pairs={{0,1},{1,0},{2,3},{3,2},{4,5},{5,4},{6,7},{7,6},{8,9},{9,8},{10,11... | collective-permute-start | bytes 3145736 | tf_op jit(solution)/shard_map/ppermute | solution.py:132
  297.8 46.9 %collective-permute-start.55 = (bf16[512,512]{1,0:T(8,128)(2,1)}, bf16[512,512]{1,0:T(8,128)(2,1)}, u32[]{:S(2)}, u32[]{:S(2)}) collective-permute-start(bf16[512,512]{1,0:T(8,128)(2,1)} %get-tuple-element.192), channel_id=1, source_target_pairs={{0,4},{2,6},{4,0},{6,2},{1,5},{3,7},{5,1},{7,3},{8,12},{10,14},{12... | collective-permute-start | bytes 1572872 | tf_op jit(solution)/shard_map/ppermute | solution.py:128
  299.4 45.2 %collective-permute-start.54 = (bf16[512,512]{1,0:T(8,128)(2,1)}, bf16[512,512]{1,0:T(8,128)(2,1)}, u32[]{:S(2)}, u32[]{:S(2)}) collective-permute-start(bf16[512,512]{1,0:T(8,128)(2,1)} %get-tuple-element.191), channel_id=1, source_target_pairs={{0,1},{1,0},{2,3},{3,2},{4,5},{5,4},{6,7},{7,6},{8,9},{9,8},{10,11... | collective-permute-start | bytes 1572872 | tf_op jit(solution)/shard_map/ppermute | solution.py:132
  304.7 24.3 %collective-permute-start.50 = (bf16[128,768]{1,0:T(8,128)(2,1)}, bf16[128,768]{1,0:T(8,128)(2,1)}, u32[]{:S(2)}, u32[]{:S(2)}) collective-permute-start(bf16[128,768]{1,0:T(8,128)(2,1)} %get-tuple-element.340), channel_id=1, source_target_pairs={{0,1},{1,0},{2,3},{3,2},{4,5},{5,4},{6,7},{7,6},{8,9},{9,8},{10,11... | collective-permute-start | bytes 589832 | tf_op jit(solution)/shard_map/ppermute | solution.py:181
  305.9 23.8 %collective-permute-start.51 = (bf16[128,768]{1,0:T(8,128)(2,1)}, bf16[128,768]{1,0:T(8,128)(2,1)}, u32[]{:S(2)}, u32[]{:S(2)}) collective-permute-start(bf16[128,768]{1,0:T(8,128)(2,1)} %get-tuple-element.339), channel_id=1, source_target_pairs={{0,2},{1,3},{2,0},{3,1},{4,6},{5,7},{6,4},{7,5},{8,10},{9,11},{10,... | collective-permute-start | bytes 589832 | tf_op jit(solution)/shard_map/ppermute | solution.py:181
  305.9 24.8 %collective-permute-start.52 = (bf16[128,768]{1,0:T(8,128)(2,1)}, bf16[128,768]{1,0:T(8,128)(2,1)}, u32[]{:S(2)}, u32[]{:S(2)}) collective-permute-start(bf16[128,768]{1,0:T(8,128)(2,1)} %get-tuple-element.338), channel_id=1, source_target_pairs={{0,3},{1,2},{2,1},{3,0},{4,7},{5,6},{6,5},{7,4},{8,11},{9,10},{10,... | collective-permute-start | bytes 589832 | tf_op jit(solution)/shard_map/ppermute | solution.py:181
  329.0 25.4 %collective-permute-start.57 = (bf16[512,1024]{1,0:T(8,128)(2,1)}, bf16[512,1024]{1,0:T(8,128)(2,1)}, u32[]{:S(2)}, u32[]{:S(2)}) collective-permute-start(bf16[512,1024]{1,0:T(8,128)(2,1)} %pad_maximum_fusion.7), channel_id=1, source_target_pairs={{0,4},{2,6},{4,0},{6,2},{1,5},{3,7},{5,1},{7,3},{8,12},{10,14},{12... | collective-permute-start | bytes 3145736 | tf_op jit(solution)/shard_map/ppermute | solution.py:128
  329.7 25.1 %collective-permute-start.58 = (bf16[512,1024]{1,0:T(8,128)(2,1)}, bf16[512,1024]{1,0:T(8,128)(2,1)}, u32[]{:S(2)}, u32[]{:S(2)}) collective-permute-start(bf16[512,1024]{1,0:T(8,128)(2,1)} %pad_maximum_fusion.6), channel_id=1, source_target_pairs={{0,1},{1,0},{2,3},{3,2},{4,5},{5,4},{6,7},{7,6},{8,9},{9,8},{10,11... | collective-permute-start | bytes 3145736 | tf_op jit(solution)/shard_map/ppermute | solution.py:132
  344.6 25.0 %collective-permute-start.53 = (bf16[4,512,768]{2,1,0:T(8,128)(2,1)}, bf16[4,512,768]{2,1,0:T(8,128)(2,1)}, u32[]{:S(2)}, u32[]{:S(2)}) collective-permute-start(bf16[4,512,768]{2,1,0:T(8,128)(2,1)} %get-tuple-element.203), channel_id=1, source_target_pairs={{0,2},{2,0},{4,6},{6,4},{1,3},{3,1},{5,7},{7,5},{8,10},{10,8},{12,... | collective-permute-start | bytes 9437192 | tf_op jit(solution)/shard_map/ppermute | solution.py:124
  358.3 27.2 %collective-permute-start.61 = (bf16[256,1024]{1,0:T(8,128)(2,1)}, bf16[256,1024]{1,0:T(8,128)(2,1)}, u32[]{:S(2)}, u32[]{:S(2)}) collective-permute-start(bf16[256,1024]{1,0:T(8,128)(2,1)} %get-tuple-element.210), channel_id=1, source_target_pairs={{0,4},{2,6},{4,0},{6,2},{1,5},{3,7},{5,1},{7,3},{8,12},{10,14},{12... | collective-permute-start | bytes 1572872 | tf_op jit(solution)/shard_map/ppermute | solution.py:128
  359.7 26.6 %collective-permute-start.62 = (bf16[256,1024]{1,0:T(8,128)(2,1)}, bf16[256,1024]{1,0:T(8,128)(2,1)}, u32[]{:S(2)}, u32[]{:S(2)}) collective-permute-start(bf16[256,1024]{1,0:T(8,128)(2,1)} %get-tuple-element.209), channel_id=1, source_target_pairs={{0,1},{1,0},{2,3},{3,2},{4,5},{5,4},{6,7},{7,6},{8,9},{9,8},{10,11... | collective-permute-start | bytes 1572872 | tf_op jit(solution)/shard_map/ppermute | solution.py:132
  364.5 28.7 %collective-permute-start.59 = (bf16[4,256,512]{2,1,0:T(8,128)(2,1)}, bf16[4,256,512]{2,1,0:T(8,128)(2,1)}, u32[]{:S(2)}, u32[]{:S(2)}) collective-permute-start(bf16[4,256,512]{2,1,0:T(8,128)(2,1)} %get-tuple-element.212), channel_id=1, source_target_pairs={{0,2},{2,0},{4,6},{6,4},{1,3},{3,1},{5,7},{7,5},{8,10},{10,8},{12,... | collective-permute-start | bytes 3145736 | tf_op jit(solution)/shard_map/ppermute | solution.py:124
  367.0 24.8 %collective-permute-start.60 = (bf16[256,512]{1,0:T(8,128)(2,1)}, bf16[256,512]{1,0:T(8,128)(2,1)}, u32[]{:S(2)}, u32[]{:S(2)}) collective-permute-start(bf16[256,512]{1,0:T(8,128)(2,1)} %broadcast_select_fusion.18), channel_id=1, source_target_pairs={{0,16},{8,24},{16,0},{24,8},{1,17},{9,25},{17,1},{25,9},{2,18},{10... | collective-permute-start | bytes 786440 | tf_op jit(solution)/shard_map/ppermute | solution.py:662
  373.4 25.0 %collective-permute-start.67 = (bf16[512,768]{1,0:T(8,128)(2,1)}, bf16[512,768]{1,0:T(8,128)(2,1)}, u32[]{:S(2)}, u32[]{:S(2)}) collective-permute-start(bf16[512,768]{1,0:T(8,128)(2,1)} %pad_maximum_fusion.12), channel_id=1, source_target_pairs={{0,4},{2,6},{4,0},{6,2},{1,5},{3,7},{5,1},{7,3},{8,12},{10,14},{12... | collective-permute-start | bytes 2359304 | tf_op jit(solution)/shard_map/ppermute | solution.py:128
  385.5 20.8 %collective-permute-start.68 = (bf16[512,768]{1,0:T(8,128)(2,1)}, bf16[512,768]{1,0:T(8,128)(2,1)}, u32[]{:S(2)}, u32[]{:S(2)}) collective-permute-start(bf16[512,768]{1,0:T(8,128)(2,1)} %pad_maximum_fusion.11), channel_id=1, source_target_pairs={{0,1},{1,0},{2,3},{3,2},{4,5},{5,4},{6,7},{7,6},{8,9},{9,8},{10,11... | collective-permute-start | bytes 2359304 | tf_op jit(solution)/shard_map/ppermute | solution.py:132
  390.2 19.0 %collective-permute-start.66 = (bf16[256,1024]{1,0:T(8,128)(2,1)}, bf16[256,1024]{1,0:T(8,128)(2,1)}, u32[]{:S(2)}, u32[]{:S(2)}) collective-permute-start(bf16[256,1024]{1,0:T(8,128)(2,1)} %get-tuple-element.225), channel_id=1, source_target_pairs={{0,8},{8,0},{16,24},{24,16},{1,9},{9,1},{17,25},{25,17},{2,10},{10... | collective-permute-start | bytes 1572872 | tf_op jit(solution)/shard_map/ppermute | solution.py:662
  392.9 17.8 %collective-permute-start.65 = (bf16[256,512]{1,0:T(8,128)(2,1)S(1)}, bf16[256,512]{1,0:T(8,128)(2,1)}, u32[]{:S(2)}, u32[]{:S(2)}) collective-permute-start(bf16[256,512]{1,0:T(8,128)(2,1)S(1)} %add_convert_fusion.16), channel_id=1, source_target_pairs={{0,16},{8,24},{16,0},{24,8},{1,17},{9,25},{17,1},{25,9},{2,18},{10... | collective-permute-start | bytes 786440 | tf_op jit(solution)/shard_map/ppermute | solution.py:662
  395.9 19.7 %collective-permute-start.63 = (bf16[256,512]{1,0:T(8,128)(2,1)}, bf16[256,512]{1,0:T(8,128)(2,1)}, u32[]{:S(2)}, u32[]{:S(2)}) collective-permute-start(bf16[256,512]{1,0:T(8,128)(2,1)} %pad_maximum_fusion.22), channel_id=1, source_target_pairs={{0,4},{2,6},{4,0},{6,2},{1,5},{3,7},{5,1},{7,3},{8,12},{10,14},{12... | collective-permute-start | bytes 786440 | tf_op jit(solution)/shard_map/ppermute | solution.py:128
  398.4 17.2 %collective-permute-start.64 = (bf16[256,512]{1,0:T(8,128)(2,1)}, bf16[256,512]{1,0:T(8,128)(2,1)S(1)}, u32[]{:S(2)}, u32[]{:S(2)}) collective-permute-start(bf16[256,512]{1,0:T(8,128)(2,1)} %pad_maximum_fusion.21), channel_id=1, source_target_pairs={{0,1},{1,0},{2,3},{3,2},{4,5},{5,4},{6,7},{7,6},{8,9},{9,8},{10,11... | collective-permute-start | bytes 786440 | tf_op jit(solution)/shard_map/ppermute | solution.py:132
  411.7 17.9 %collective-permute-start.72 = (bf16[512,512]{1,0:T(8,128)(2,1)S(1)}, bf16[512,512]{1,0:T(8,128)(2,1)S(1)}, u32[]{:S(2)}, u32[]{:S(2)}) collective-permute-start(bf16[512,512]{1,0:T(8,128)(2,1)S(1)} %pad_maximum_fusion.17), channel_id=1, source_target_pairs={{0,8},{8,0},{16,24},{24,16},{1,9},{9,1},{17,25},{25,17},{2,10},{10... | collective-permute-start | bytes 1572872 | tf_op jit(solution)/shard_map/ppermute | solution.py:662
  414.4 18.7 %collective-permute-start.70 = (bf16[256,768]{1,0:T(8,128)(2,1)S(1)}, bf16[256,768]{1,0:T(8,128)(2,1)S(1)}, u32[]{:S(2)}, u32[]{:S(2)}) collective-permute-start(bf16[256,768]{1,0:T(8,128)(2,1)S(1)} %get-tuple-element.233), channel_id=1, source_target_pairs={{0,1},{1,0},{2,3},{3,2},{4,5},{5,4},{6,7},{7,6},{8,9},{9,8},{10,11... | collective-permute-start | bytes 1179656 | tf_op jit(solution)/shard_map/ppermute | solution.py:132
  416.8 19.0 %collective-permute-start.81 = (bf16[128,512]{1,0:T(8,128)(2,1)S(1)}, bf16[128,512]{1,0:T(8,128)(2,1)S(1)}, u32[]{:S(2)}, u32[]{:S(2)}) collective-permute-start(bf16[128,512]{1,0:T(8,128)(2,1)S(1)} %get-tuple-element.241), channel_id=1, source_target_pairs={{0,4},{2,6},{4,0},{6,2},{1,5},{3,7},{5,1},{7,3},{8,12},{10,14},{12... | collective-permute-start | bytes 393224 | tf_op jit(solution)/shard_map/ppermute | solution.py:128
  418.3 17.4 %collective-permute-start.80 = (bf16[128,512]{1,0:T(8,128)(2,1)S(1)}, bf16[128,512]{1,0:T(8,128)(2,1)S(1)}, u32[]{:S(2)}, u32[]{:S(2)}) collective-permute-start(bf16[128,512]{1,0:T(8,128)(2,1)S(1)} %get-tuple-element.240), channel_id=1, source_target_pairs={{0,1},{1,0},{2,3},{3,2},{4,5},{5,4},{6,7},{7,6},{8,9},{9,8},{10,11... | collective-permute-start | bytes 393224 | tf_op jit(solution)/shard_map/ppermute | solution.py:132
  429.6 24.3 %collective-permute-start.69 = (bf16[640,512]{1,0:T(8,128)(2,1)}, bf16[640,512]{1,0:T(8,128)(2,1)}, u32[]{:S(2)}, u32[]{:S(2)}) collective-permute-start(bf16[640,512]{1,0:T(8,128)(2,1)} %get-tuple-element.243), channel_id=1, source_target_pairs={{0,1},{1,0},{2,3},{3,2},{4,5},{5,4},{6,7},{7,6},{8,9},{9,8},{10,11... | collective-permute-start | bytes 1966088 | tf_op jit(solution)/shard_map/ppermute | solution.py:132
  437.7 38.1 %collective-permute-start.82 = (bf16[128,512]{1,0:T(8,128)(2,1)}, bf16[128,512]{1,0:T(8,128)(2,1)}, u32[]{:S(2)}, u32[]{:S(2)}) collective-permute-start(bf16[128,512]{1,0:T(8,128)(2,1)} %get-tuple-element.262), channel_id=1, source_target_pairs={{0,8},{8,0},{16,24},{24,16},{1,9},{9,1},{17,25},{25,17},{2,10},{10... | collective-permute-start | bytes 393224 | tf_op jit(solution)/shard_map/ppermute | solution.py:662
  441.2 33.2 %collective-permute-start.74 = (bf16[256,768]{1,0:T(8,128)(2,1)}, bf16[256,768]{1,0:T(8,128)(2,1)}, u32[]{:S(2)}, u32[]{:S(2)}) collective-permute-start(bf16[256,768]{1,0:T(8,128)(2,1)} %get-tuple-element.250), channel_id=1, source_target_pairs={{0,8},{8,0},{16,24},{24,16},{1,9},{9,1},{17,25},{25,17},{2,10},{10... | collective-permute-start | bytes 1179656 | tf_op jit(solution)/shard_map/ppermute | solution.py:662
  453.8 25.9 %collective-permute-start.77 = (bf16[256,1024]{1,0:T(8,128)(2,1)S(1)}, bf16[256,1024]{1,0:T(8,128)(2,1)S(1)}, u32[]{:S(2)}, u32[]{:S(2)}) collective-permute-start(bf16[256,1024]{1,0:T(8,128)(2,1)S(1)} %pad_maximum_fusion.18), channel_id=1, source_target_pairs={{0,8},{8,0},{16,24},{24,16},{1,9},{9,1},{17,25},{25,17},{2,10},{10... | collective-permute-start | bytes 1572872 | tf_op jit(solution)/shard_map/ppermute | solution.py:662
  (113 other events, 1020.1 us)

commit v5 on v4

--- a/solution.py
+++ b/solution.py
@@ -75,7 +75,7 @@
             jax.ShapeDtypeStruct((pairs * 2, SEQ, SEQ), BF16),
         ],
         scratch_shapes=[pltpu.VMEM((SEQ, SEQ), F32)],
-        compiler_params=pltpu.CompilerParams(vmem_limit_bytes=32 * MIB),
+        compiler_params=pltpu.CompilerParams(vmem_limit_bytes=(56 if pairs > 2 else 32) * MIB),
         cost_estimate=cost_of("attend"),
         name="attend",
     )(qkv, labels[:, None], labels[None, :])
@@ -114,7 +114,7 @@
         ],
         out_specs=pl.BlockSpec((SEQ, 6 * HD), lambda i: (0, i)),
         out_shape=jax.ShapeDtypeStruct((SEQ, qkv.shape[1]), BF16),
-        compiler_params=pltpu.CompilerParams(vmem_limit_bytes=32 * MIB),
+        compiler_params=pltpu.CompilerParams(vmem_limit_bytes=(56 if pairs > 2 else 32) * MIB),
         cost_estimate=cost_of("attend_back"),
         name="attend_back",
     )(qkv, probs, grad)
@@ -155,8 +155,8 @@
     return jnp.concatenate([mine, swap_col(jnp.where(col == 0, second, first))], 1)
 
 
-def give_back(mine, leaving, odd, col, *ties):
-    other = after(swap_col(leaving), *ties).astype(F32)
+def give_back(mine, other, odd, col):
+    other = other.astype(F32)
     first = jnp.where(col == 0, mine, other)
     second = jnp.where(col == 0, other, mine)
     rolled = jnp.concatenate([first[:SEQ], second[:SEQ], first[SEQ:], second[SEQ:]], 0)
@@ -190,19 +190,17 @@
 
 
 class Shards:
-    def __init__(self, depth, shard, beside, across, *corners):
+    def __init__(self, depth, shard, beside, across, *corners, near_only=False):
         self.depth, self.width = depth, shard.shape[1]
         near = [(0, 0, shard), (1, 0, beside), (4, 0, across)]
         near += [(5, index * depth // 2, corner) for index, corner in enumerate(corners)]
-        far = [(place + 2, start, swap_core(part)) for place, start, part in near]
-        self.parts = near + far
-
-    def riders(self):
-        found = {}
-        for place, start, part in self.parts:
-            if start + part.shape[0] > self.depth:
-                found[place] = part[self.depth - start :]
-        return jnp.stack([found[place] for place in range(8)])
+        self.parts = near
+        if not near_only:
+            self.pass_on(near)
+
+    def pass_on(self, near, *ties):
+        far = [(place + 2, start, swap_core(after(part, *ties) if ties else part)) for place, start, part in near]
+        self.parts = self.parts + far
 
 
 def dense(kernel, in_specs, out_specs, out_shape, scratch, flops, name, shards=None):
@@ -622,16 +620,6 @@
     )(left, right)
 
 
-def sum_devices(value, axis, size):
-    if size & (size - 1):
-        return lax.psum(value, axis)
-    step = 1
-    while step < size:
-        value = value + lax.ppermute(value, axis, [(i, i ^ step) for i in range(size)])
-        step *= 2
-    return value
-
-
 class PairSum:
     def __init__(self, value, size):
         self.whole = None
@@ -715,11 +703,35 @@
         return jnp.concatenate([upper, self.lower(0, self.from_row[self.half :], self.last_col)], 0)
 
 
-def in_three(value):
-    high = lax.reduce_precision(value, 8, 7)
-    rest = value - high
-    mid = lax.reduce_precision(rest, 8, 7)
-    return jnp.stack([high, mid, rest - mid]).astype(BF16)
+class VectorSum:
+    def __init__(self, value, then, size):
+        self.value, self.then, self.other = value, then, None
+        self.size = size
+        levels = [1 << k for k in range(size.bit_length() - 1)] if size & (size - 1) == 0 else []
+        self.plan = [swap_core, swap_row, swap_col, None]
+        self.plan += [functools.partial(lax.ppermute, axis_name="dp", perm=[(i, i ^ k) for i in range(size)]) for k in levels]
+
+    def step(self, last):
+        self.take(last)
+        if not self.plan:
+            return last
+        move = self.plan.pop(0)
+        if move is None:
+            self.value = self.then(self.value)
+            if not self.plan:
+                return last
+            move = self.plan.pop(0)
+        leaving = after(self.value, last)
+        self.other = move(leaving)
+        return leaving
+
+    def take(self, last):
+        if self.other is not None:
+            self.value = self.value + after(self.other, last)
+            self.other = None
+
+    def result(self):
+        return lax.psum(self.value, "dp") if self.size & (self.size - 1) else self.value
 
 
 def local(
@@ -750,19 +762,19 @@
     packed = jnp.concatenate(
         [out_bias, ln1_gain, ln1_bias, ff_out_bias, ln2_gain, ln2_bias, ff_in_bias, qv_bias.reshape(-1)]
     )
-    riders = in_three(packed).reshape(15, 768)
-    riders = jnp.concatenate([qkv_weight, riders, jnp.zeros((1, 768), BF16)], 0)
-    qkv_beside, qkv_across = swap_col(riders), swap_row(riders)
-    x = own_rows(after(tokens, qkv_beside), odd, col)
+    beside, across = swap_col(packed), swap_row(packed)
+    near = [packed, beside, across, swap_row(beside)]
+    far = [swap_core(value) for value in near]
+    packed = jnp.stack([near[0], near[1], far[0], far[1], near[2], near[3], far[2], far[3]])
+    qkv_beside, qkv_across = swap_col(qkv_weight), swap_row(qkv_weight)
+    x = own_rows(after(tokens, qkv_beside, qkv_across), odd, col)
     qkv_corner = swap_row(qkv_beside)
-    qkv_w = Shards(D // 2, riders, qkv_beside, qkv_across, qkv_corner)
+    qkv_w = Shards(D // 2, qkv_weight, qkv_beside, qkv_across, qkv_corner)
     out_beside = swap_col(after(out_weight, x))
     out_across = swap_row(after(out_weight, qkv_corner))
     incoming = own_rows(after(out_grad, out_beside), odd, col)
     ff_in_across = swap_row(after(ff_in_weight, out_across))
 
-    packed = qkv_w.riders()[:, :15].astype(F32).reshape(8, 3, packed.shape[0])
-    packed = (packed[:, 0] + packed[:, 1]) + packed[:, 2]
     vec = packed[:2, : 6 * 512].reshape(2, 6, 512).transpose(1, 0, 2).reshape(6, D)
     pairs = packed[:, 6 * 512 :].reshape(4, 2, 768)
     first, second = in_order(pairs[:, 0], pairs[:, 1])
@@ -792,9 +804,12 @@
     ff_in_beside, ff_in_across, ff_out_weight = after_all((ff_in_beside, ff_in_across, ff_out_weight), heads)
     half = ff_in_weight.shape[0] // 2
     ff_in_corners = swap_col(ff_in_across[:half]), swap_row(ff_in_beside[half:])
-    ff_in_w = Shards(D // 2, ff_in_weight, ff_in_beside, ff_in_across, *ff_in_corners)
+    ff_in_w = Shards(D // 2, ff_in_weight, ff_in_beside, ff_in_across, *ff_in_corners, near_only=True)
+    ff_in_near = ff_in_w.parts
+    ff_in_w.pass_on(ff_in_near[:3])
     ff_out_beside, ff_out_across = swap_col(ff_out_weight), swap_row(ff_out_weight)
     unit_one, inverse_one, middle_low = first_norm(after(heads, ff_in_beside, ff_in_across), out_w, x, vec)
+    ff_in_w.pass_on(ff_in_near[3:], unit_one)
     active, slope = project_hidden(middle_low, ff_in_w, ff_in_b)
     ff_out_beside, ff_out_across = after_all((ff_out_beside, ff_out_across), active)
     half = ff_out_weight.shape[0] // 2
@@ -804,8 +819,8 @@
 
     ff_out = GridSum(*grad_down(active, d_two))
     d_hidden, ff_in_bias_part = hidden_back(after(d_two, ff_out.kernel), ff_out_w, slope)
-    layer_out = give_back(out_mine, out_leave, odd, col, d_hidden)
-    ff_out.send(d_hidden, layer_out)
+    out_other = after(swap_col(out_leave), d_hidden)
+    ff_out.send(d_hidden, out_other)
     ff_in = GridSum(*grad_up(after(middle_low, *ff_out.sent), d_hidden))
     back_one, d_one, sums_one = first_back(
         after(d_hidden, ff_in.kernel), ff_in_w, back_two, unit_one, inverse_one, vec
@@ -817,66 +832,64 @@
     pieces = send_heads(d_qkv_shared)
     ff_in.send(d_qkv_shared)
     d_qkv_own = attend_back(qkv, probs_own, after(d_heads, *ff_in.sent))
-    d_qkv = jnp.concatenate([d_qkv_own, join_heads(after_all(pieces, d_qkv_own), member, row)], 0)
+    ff_out_pairs = PairSum(ff_out.result(d_qkv_own), n_dp)
+    event = ff_out_pairs.step(d_qkv_own)
+    pieces = after_all(pieces, d_qkv_own, event)
+    d_qkv = jnp.concatenate([d_qkv_own, join_heads(pieces, member, row)], 0)
     qkv_sum = GridSum(*grad_up(x, d_qkv))
-    ff_out_pairs = PairSum(ff_out.result(qkv_sum.kernel), n_dp)
     event = ff_out_pairs.step(qkv_sum.kernel)
     ff_in.send_last(event)
     out_sum = GridSum(*grad_down(heads, after(d_one, *ff_in.last)))
     event = ff_out_pairs.step(out_sum.kernel)
+    ff_in_pairs = PairSum(ff_in.result(event), n_dp)
+    event = ff_in_pairs.step(event)
     qkv_sum.send(event)
     in_mine, in_leave, column_sums = input_back(after(d_qkv, *qkv_sum.sent), qkv_w, back_one)
-    ff_in_pairs = PairSum(ff_in.result(in_leave), n_dp)
-    event = ff_in_pairs.step(in_leave)
-    event = ff_out_pairs.step(event)
+    def ordered(value):
+        blocks = value.reshape(4, -1)
+        return jnp.stack([lax.dynamic_index_in_dim(blocks, row ^ place, 0, False) for place in range(4)])
+
+    place = row * 2 + col
+
+    def own_part(value):
+        halves = lax.dynamic_slice_in_dim(value[: 6 * D].reshape(6, 2, D // 2), col, 1, 1)[:, 0]
+        ff_in_part = lax.dynamic_slice_in_dim(value, 6 * D + place * 512, 512)
+        qv_part = lax.dynamic_slice_in_dim(value, 10 * D + place * 256, 256)
+        return jnp.concatenate([halves.reshape(-1), ff_in_part, qv_part])
+
+    halves = jnp.concatenate([sums_one, sums_two], 0)
+    halves = jnp.concatenate(in_order(halves[:, : D // 2], halves[:, D // 2 :]), 1)
+    column_sums = ordered(column_sums).reshape(-1, 3, HD)
+    qv_sums = jnp.concatenate([column_sums[:, 0], column_sums[:, 2]], 1)
+    sums = jnp.concatenate([halves.reshape(-1), ordered(ff_in_bias_part).reshape(-1), qv_sums.reshape(-1)])
+    sums = VectorSum(sums, own_part, n_dp)
+    qkv_sum.send_last(in_leave)
+    event = ff_out_pairs.step(qkv_sum.last[0])
+    event = ff_in_pairs.step(event)
+    event = sums.step(event)
     out_sum.send(event)
-    qkv_sum.send_last(*out_sum.sent)
-    event = ff_in_pairs.step(qkv_sum.last[0])
-    event = ff_out_pairs.step(event)
+    qkv_pairs = PairSum(qkv_sum.result(*out_sum.sent), n_dp)
+    event = qkv_pairs.step(out_sum.sent[0])
+    event = ff_in_pairs.step(event)
+    event = sums.step(event)
     out_sum.send_last(event)
-    input_grad = give_back(*after_all((in_mine, in_leave), *out_sum.last), odd, col)
-    event = ff_in_pairs.step(out_sum.last[0])
-    event = ff_out_pairs.step(event)
-    qkv_pairs = PairSum(qkv_sum.result(event), n_dp)
-    event = qkv_pairs.step(event)
+    event = qkv_pairs.step(out_sum.last[0])
+    event = sums.step(event)
+    in_other = swap_col(after(in_leave, event))
+    event = ff_in_pairs.step(event)
     out_pairs = PairSum(out_sum.result(event), n_dp)
-    sums_start = event = out_pairs.step(event)
-    every = [ff_out_pairs, ff_in_pairs, qkv_pairs, out_pairs]
+    event = out_pairs.step(event)
+    event = sums.step(event)
+
+    every = [ff_out_pairs, ff_in_pairs, qkv_pairs, sums, out_pairs]
     while any(pairs.plan for pairs in every):
         for pairs in every:
             event = pairs.step(event)
+    input_grad = give_back(in_mine, after(in_other, event), odd, col)
+    layer_out = give_back(out_mine, after(out_other, event), odd, col)
     for pairs in every:
         pairs.take(event)
-    ff_out_grad, ff_in_grad, qkv_grad, out_w_grad = [pairs.result() for pairs in every]
-
-    def across_grid(value):
-        return sum_devices(sum_devices(value, "row", 4), "col", 2)
-
-    def ordered(value):
-        blocks = value.reshape(4, -1)
-        return jnp.stack([lax.dynamic_index_in_dim(blocks, row ^ place, 0, False) for place in range(4)])
-
-    place = row * 2 + col
-    halves = jnp.concatenate([sums_one, sums_two], 0)
-    halves = jnp.concatenate(in_order(halves[:, : D // 2], halves[:, D // 2 :]), 1)
-    column_sums = ordered(column_sums).reshape(-1, 3, HD)
-    early = jnp.concatenate(
-        [
-            halves.reshape(-1),
-            ordered(ff_in_bias_part).reshape(-1),
-            jnp.concatenate([column_sums[:, 0], column_sums[:, 2]], 1).reshape(-1),
-        ]
-    )
-    early = across_grid(after(early, sums_start))
-    halves = lax.dynamic_slice_in_dim(early[: 6 * D].reshape(6, 2, D // 2), col, 1, 1)[:, 0]
-    early = jnp.concatenate(
-        [
-            halves.reshape(-1),
-            lax.dynamic_slice_in_dim(early, 6 * D + place * 512, 512),
-            lax.dynamic_slice_in_dim(early, 10 * D + place * 256, 256),
-        ]
-    )
-    early = sum_devices(early, "dp", n_dp)
+    ff_out_grad, ff_in_grad, qkv_grad, early, out_w_grad = [pairs.result() for pairs in every]
     halves = early[: 6 * 512].reshape(6, 512)
     return (
         layer_out,

time: 522 us -> 499 us (0.956)
  local copies, waits for them, and re-layouts: 60.8 us -> 49 us
  waiting for transfers between devices: 139 us -> 129 us
    ppermute x16 -> x19, waiting for transfers between devices: 12.8 us -> 31 us  [swap_row(): return lax.ppermute(value, 'row', [(i, i ^ 2) for i in range(4)])]
    ppermute x19 -> x21, waiting for transfers between devices: 65.6 us -> 48.1 us  [swap_col(): return lax.ppermute(value, 'col', [(0, 1), (1, 0)])]
    ppermute x5 -> x2, waiting for transfers between devices: 12.7 us -> 0.01 us  [step(): self.other = move(leaving)]
    unnamed x147 -> x144, local copies, waits for them, and re-layouts: 32.6 us -> 20.9 us
    another operation x1 -> x9, local copies, waits for them, and re-layouts: 0.01 us -> 5.89 us  [local(): jnp.stack([near[0], near[1], far[0], far[1], near[2], near[3], far[2], fa...]
    ppermute x16 -> x19, starting transfers between devices: 18.6 us -> 21.2 us  [swap_row(): return lax.ppermute(value, 'row', [(i, i ^ 2) for i in range(4)])]
    ppermute x19 -> x21, starting transfers between devices: 23.9 us -> 22.5 us  [swap_col(): return lax.ppermute(value, 'col', [(0, 1), (1, 0)])]
  transfers between devices with their start and end apart: 91 -> 98, of which waited for: 32 -> 30; matrix products, arithmetic and copies ran while one was open for 19% -> 20% of each run, Pallas kernels for 26% -> 27%
where the time goes in v5:
time: 499 us; the launch traced here: 493 us
  Pallas kernels  162 us (32%)
  waiting for transfers between devices  129 us (26%)
  starting transfers between devices  77.2 us (15%)
  other arithmetic  73.5 us (15%)
  local copies, waits for them, and re-layouts  49 us (10%)
    ppermute x21, waiting for transfers between devices, swap_col(): return lax.ppermute(value, 'col', [(0, 1), (1, 0)])  48.1 us
    ppermute x16, waiting for transfers between devices, step(): self.other = lax.ppermute(leaving, 'dp', pairs)  42.1 us
    ppermute x19, waiting for transfers between devices, swap_row(): return lax.ppermute(value, 'row', [(i, i ^ 2) for i in range(4)])  31 us
    convert_element_type x16, other arithmetic, add(): return total.astype(BF16)  24.6 us
    ppermute x21, starting transfers between devices, swap_col(): return lax.ppermute(value, 'col', [(0, 1), (1, 0)])  22.5 us
    ppermute x19, starting transfers between devices, swap_row(): return lax.ppermute(value, 'row', [(i, i ^ 2) for i in range(4)])  21.2 us
    unnamed x144, local copies, waits for them, and re-layouts  20.9 us
    pallas_call x2, Pallas kernels, grad_up(): dense(grad_up_kernel, [whole(left), columns_of(right)], [two_blocks(out)]...  19.5 us
  transfers between devices with their start and end apart: 98, of which 30 were waited for; matrix products, arithmetic and copies ran while one was open for 20% of the time, Pallas kernels for 27%

profile of v5, /device:TPU:0, one launch (start us, length us, event | category | flops | bytes accessed | tf_op | source)
XLA Modules:
  0.0 493.2 jit_solution(7034711333533510537)
XLA Ops:
  0.7 3.0 collective-permute-start
  11.3 10.5 %collective-permute-done.8 = f32[3840]{0:T(1024)S(1)} collective-permute-done((f32[3840]{0:T(1024)S(1)}, f32[3840]{0:T(1024)S(1)}, u32[]{:S(2)}, u32[]{:S(2)}) %collective-permute-start.8) | collective-permute-done | bytes 15392 | tf_op jit(solution)/shard_map/ppermute | solution.py:132
  41.6 3.3 collective-permute-done.7
  44.9 2.5 pad_maximum_fusion.1.refs_8_.refs_11_.left_ref
  49.9 9.0 %collective-permute-done.2.refs_3_ = bf16[512,768]{1,0:T(8,128)(2,1)} collective-permute-done((bf16[512,768]{1,0:T(8,128)(2,1)S(1)}, bf16[512,768]{1,0:T(8,128)(2,1)}, u32[]{:S(2)}, u32[]{:S(2)}) %collective-permute-start.2) | collective-permute-done | bytes 786464 | tf_op jit(solution)/shard_map/ppermute | solution.py:128
  64.0 8.0 %project_qkv.1.qkv_ref = bf16[640,3072]{1,0:T(8,128)(2,1)} custom-call(bf16[512,768]{1,0:T(8,128)(2,1)S(1)} %copy-done.23, bf16[512,768]{1,0:T(8,128)(2,1)S(1)} %collective-permute-done.refs_1_, bf16[512,768]{1,0:T(8,128)(2,1)S(1)} %collective-permute-done.1.refs_2_, bf16[512,768]{1,0:T(8,128)(2,1)} %collective-permute-done.2.refs_3_, ...), custom_call_target="tpu_custom_call" | custom-call | flops 9999999827968 | bytes 1000000000 | tf_op jit(solution)/shard_map/project_qkv/pallas_call | solution.py:286
  77.9 2.2 collective-permute-done.19
  80.6 2.3 pad_maximum_fusion.2.refs_12_
  83.0 8.0 %collective-permute-done.23.refs_3_ = bf16[128,512]{1,0:T(8,128)(2,1)} collective-permute-done((bf16[128,512]{1,0:T(8,128)(2,1)S(1)}, bf16[128,512]{1,0:T(8,128)(2,1)}, u32[]{:S(2)}, u32[]{:S(2)}) %collective-permute-start.23) | collective-permute-done | bytes 131104 | tf_op jit(solution)/shard_map/ppermute | solution.py:132
  92.0 3.2 attend.2
  100.3 13.7 %attend.3 = (bf16[512,1024]{1,0:T(8,128)(2,1)}, bf16[16,512,512]{2,1,0:T(8,128)(2,1)}) custom-call(bf16[640,3072]{1,0:T(8,128)(2,1)} %project_qkv.1.qkv_ref, s32[512,1]{1,0:T(8,128)} %copy.43.column_ref, s32[1,512]{1,0:T(1,128)} %bitcast.167), custom_call_target="tpu_custom_call" | custom-call | flops 9999999827968 | bytes 1000000000 | tf_op jit(solution)/shard_map/attend/pallas_call | solution.py:61
  118.1 4.6 collective-permute-done.22.refs_2_
  122.7 3.4 collective-permute-done.20.refs_1_
  132.3 10.3 %first_norm.1 = (f32[640,1024]{1,0:T(8,128)}, f32[640,1]{1,0:T(8,128)S(1)}, bf16[640,1024]{1,0:T(8,128)(2,1)S(1)}) custom-call(bf16[256,512]{1,0:T(8,128)(2,1)} %refs_0_.12, bf16[256,512]{1,0:T(8,128)(2,1)} %collective-permute-done.18.refs_1_, bf16[256,512]{1,0:T(8,128)(2,1)} %collective-permute-done.21.refs_2_, ...), custom_call_target="tpu_custom_call" | custom-call | flops 9999999827968 | bytes 1000000000 | tf_op jit(solution)/shard_map/first_norm/pallas_call | solution.py:389
  146.6 3.0 collective-permute-done.40.refs_8_
  151.1 14.3 %project_hidden.1 = (bf16[640,4096]{1,0:T(8,128)(2,1)}, bf16[640,4096]{1,0:T(8,128)(2,1)}) custom-call(bf16[512,1024]{1,0:T(8,128)(2,1)} %refs_0_.11, bf16[512,1024]{1,0:T(8,128)(2,1)} %collective-permute-done.20.refs_1_, bf16[512,1024]{1,0:T(8,128)(2,1)} %collective-permute-done.22.refs_2_, bf16[256,1024]{1,0:T(8,128)(2,1)} %collective-permute-done.35.refs_3_, ...), custom_call_target="tpu_custom_call" | custom-call | flops 10000000 | bytes 1000 | tf_op jit(solution)/shard_map/project_hidden/pallas_call | solution.py:311
  165.4 4.4 collective-permute-done.33.refs_1_
  173.6 10.6 %collective-permute-done.42.refs_3_ = bf16[512,512]{1,0:T(8,128)(2,1)} collective-permute-done((bf16[512,512]{1,0:T(8,128)(2,1)S(1)}, bf16[512,512]{1,0:T(8,128)(2,1)}, u32[]{:S(2)}, u32[]{:S(2)}) %collective-permute-start.42) | collective-permute-done | bytes 524320 | tf_op jit(solution)/shard_map/ppermute | solution.py:132
  187.2 17.8 %second_norm.1 = (f32[640,512]{1,0:T(8,128)}, bf16[640,512]{1,0:T(8,128)(2,1)}, f32[640,1024]{1,0:T(8,128)}, bf16[640,1024]{1,0:T(8,128)(2,1)}, f32[3,1024]{1,0:T(4,128)S(1)}) custom-call(bf16[1024,512]{1,0:T(8,128)(2,1)S(1)} %copy-done.22, bf16[1024,512]{1,0:T(8,128)(2,1)S(1)} %collective-permute-done.33.refs_1_, ...), custom_call_target="tpu_custom_call" | custom-call | flops 9999999827968 | bytes 1000000000 | tf_op jit(solution)/shard_map/second_norm/pallas_call | solution.py:440
  206.3 10.4 %grad_down.2 = (bf16[4,1024,512]{2,1,0:T(8,128)(2,1)S(1)}, bf16[4,1024,512]{2,1,0:T(8,128)(2,1)}) custom-call(bf16[640,4096]{1,0:T(8,128)(2,1)} %get-tuple-element.179.refs_10_.left_ref, bf16[640,1024]{1,0:T(8,128)(2,1)S(1)} %copy-done.39), custom_call_target="tpu_custom_call" | custom-call | flops 9999999827968 | bytes 1000000000 | tf_op jit(solution)/shard_map/grad_down/pallas_call | solution.py:612
  220.1 10.1 %hidden_back.1 = (bf16[640,4096]{1,0:T(8,128)(2,1)}, f32[1,4096]{1,0:T(1,128)S(1)}) custom-call(bf16[1024,512]{1,0:T(8,128)(2,1)S(1)} %copy-done.22, bf16[1024,512]{1,0:T(8,128)(2,1)S(1)} %collective-permute-done.33.refs_1_, bf16[1024,512]{1,0:T(8,128)(2,1)S(1)} %collective-permute-done.34.refs_2_, bf16[512,512]{1,0:T(8,128)(2,1)} %collective-permute-done.42.refs_3_, ...), custom_call_target="tpu_custom_call" | custom-call | flops 9999999827968 | bytes 1000000000 | tf_op jit(solution)/shard_map/hidden_back/pallas_call | solution.py:536
  232.1 4.2 collective-permute-done.49
  236.3 2.8 fusion.20
  243.3 10.6 %grad_up.2 = (bf16[4,512,1024]{2,1,0:T(8,128)(2,1)S(1)}, bf16[4,512,1024]{2,1,0:T(8,128)(2,1)}) custom-call(bf16[640,1024]{1,0:T(8,128)(2,1)S(1)} %copy-done.10, bf16[640,4096]{1,0:T(8,128)(2,1)} %get-tuple-element.196.right_ref.refs_10_), custom_call_target="tpu_custom_call" | custom-call | flops 9999999827968 | bytes 1000000000 | tf_op jit(solution)/shard_map/grad_up/pallas_call | solution.py:587
  255.9 17.6 %first_back.1 = (f32[640,1024]{1,0:T(8,128)}, bf16[640,1024]{1,0:T(8,128)(2,1)}, f32[3,1024]{1,0:T(4,128)S(1)}) custom-call(bf16[512,1024]{1,0:T(8,128)(2,1)} %refs_0_.11, bf16[512,1024]{1,0:T(8,128)(2,1)} %collective-permute-done.20.refs_1_, bf16[512,1024]{1,0:T(8,128)(2,1)} %collective-permute-done.22.refs_2_, ...), custom_call_target="tpu_custom_call" | custom-call | flops 10000000 | bytes 1000 | tf_op jit(solution)/shard_map/first_back/pallas_call | solution.py:480
  274.9 3.4 heads_back.1.grad_ref
  284.8 3.4 fusion.10
  290.1 3.5 attend_back.2
  296.7 3.1 fusion.24
  301.9 14.9 %attend_back.3 = bf16[512,3072]{1,0:T(8,128)(2,1)} custom-call(bf16[640,3072]{1,0:T(8,128)(2,1)} %project_qkv.1.qkv_ref, bf16[16,512,512]{2,1,0:T(8,128)(2,1)} %get-tuple-element.210.probs_ref, bf16[640,1024]{1,0:T(8,128)(2,1)} %copy-done.8), custom_call_target="tpu_custom_call" | custom-call | flops 9999999827968 | bytes 1000000000 | tf_op jit(solution)/shard_map/attend_back/pallas_call | solution.py:107
  318.9 3.9 broadcast_select_fusion.9
  329.6 8.9 %grad_up.3 = (bf16[4,512,768]{2,1,0:T(8,128)(2,1)S(1)}, bf16[4,512,768]{2,1,0:T(8,128)(2,1)}) custom-call(bf16[640,1024]{1,0:T(8,128)(2,1)S(1)} %copy-done.13, bf16[640,3072]{1,0:T(8,128)(2,1)} %pad_maximum_fusion.right_ref.refs_8_), custom_call_target="tpu_custom_call" | custom-call | flops 9999999827968 | bytes 1000000000 | tf_op jit(solution)/shard_map/grad_up/pallas_call | solution.py:587
  341.7 2.6 collective-permute-start.68
  344.3 3.4 fusion.4
  349.7 3.8 grad_down.3
  353.6 3.1 collective-permute-done.68
  358.5 3.2 collective-permute-done.67
  362.5 3.9 broadcast_select_fusion.6
  372.8 11.2 %input_back.1 = (f32[640,512]{1,0:T(8,128)}, bf16[640,512]{1,0:T(8,128)(2,1)S(1)}, f32[1,3072]{1,0:T(1,128)S(1)}) custom-call(bf16[512,768]{1,0:T(8,128)(2,1)S(1)} %copy-done.24, bf16[512,768]{1,0:T(8,128)(2,1)S(1)} %copy-done.26, bf16[512,768]{1,0:T(8,128)(2,1)S(1)} %copy-done.28, bf16[512,768]{1,0:T(8,128)(2,1)} %collective-permute-done.2.refs_3_, ...), custom_call_target="tpu_custom_call" | custom-call | flops 9999999827968 | bytes 1000000000 | tf_op jit(solution)/shard_map/input_back/pallas_call | solution.py:506
  385.8 3.0 collective-permute-done.72
  399.4 8.5 %collective-permute-done.78 = bf16[256,768]{1,0:T(8,128)(2,1)S(1)} collective-permute-done((bf16[256,768]{1,0:T(8,128)(2,1)S(1)}, bf16[256,768]{1,0:T(8,128)(2,1)S(1)}, u32[]{:S(2)}, u32[]{:S(2)}) %collective-permute-start.78) | collective-permute-done | bytes 393248 | tf_op jit(solution)/shard_map/ppermute | solution.py:128
  413.1 2.4 collective-permute-start.82
  418.7 17.5 %collective-permute-done.84 = bf16[256,768]{1,0:T(8,128)(2,1)S(1)} collective-permute-done((bf16[256,768]{1,0:T(8,128)(2,1)S(1)}, bf16[256,768]{1,0:T(8,128)(2,1)S(1)}, u32[]{:S(2)}, u32[]{:S(2)}) %collective-permute-start.84) | collective-permute-done | bytes 393248 | tf_op jit(solution)/shard_map/ppermute | solution.py:650
  441.5 2.5 collective-permute-start.89
  452.1 6.4 %collective-permute-done.89 = bf16[256,1024]{1,0:T(8,128)(2,1)} collective-permute-done((bf16[256,1024]{1,0:T(8,128)(2,1)}, bf16[256,1024]{1,0:T(8,128)(2,1)}, u32[]{:S(2)}, u32[]{:S(2)}) %collective-permute-start.89) | collective-permute-done | bytes 524320 | tf_op jit(solution)/shard_map/ppermute | solution.py:650
  462.9 2.5 collective-permute-start.96
  466.0 7.4 %collective-permute-done.92 = bf16[128,768]{1,0:T(8,128)(2,1)S(1)} collective-permute-done((bf16[128,768]{1,0:T(8,128)(2,1)S(1)}, bf16[128,768]{1,0:T(8,128)(2,1)S(1)}, u32[]{:S(2)}, u32[]{:S(2)}) %collective-permute-start.92) | collective-permute-done | bytes 196640 | tf_op jit(solution)/shard_map/ppermute | solution.py:650
  477.1 7.1 %collective-permute-done.94 = bf16[256,768]{1,0:T(8,128)(2,1)S(1)} collective-permute-done((bf16[256,768]{1,0:T(8,128)(2,1)S(1)}, bf16[256,768]{1,0:T(8,128)(2,1)S(1)}, u32[]{:S(2)}, u32[]{:S(2)}) %collective-permute-start.94) | collective-permute-done | bytes 393248 | tf_op jit(solution)/shard_map/ppermute | solution.py:650
  (476 shorter events, 171.2 us)
Async XLA Ops:
  0.7 24.9 %collective-permute-start = (bf16[512,768]{1,0:T(8,128)(2,1)}, bf16[512,768]{1,0:T(8,128)(2,1)S(1)}, u32[]{:S(2)}, u32[]{:S(2)}) collective-permute-start(bf16[512,768]{1,0:T(8,128)(2,1)} %refs_0_.13), channel_id=1, source_target_pairs={{0,1},{1,0},{2,3},{3,2},{4,5},{5,4},{6,7},{7,6},{8,9},{9,8},{10,11... | collective-permute-start | bytes 2359304 | tf_op jit(solution)/shard_map/ppermute | solution.py:132
  3.7 22.4 %collective-permute-start.1 = (bf16[512,768]{1,0:T(8,128)(2,1)}, bf16[512,768]{1,0:T(8,128)(2,1)S(1)}, u32[]{:S(2)}, u32[]{:S(2)}) collective-permute-start(bf16[512,768]{1,0:T(8,128)(2,1)} %refs_0_.13), channel_id=1, source_target_pairs={{0,4},{2,6},{4,0},{6,2},{1,5},{3,7},{5,1},{7,3},{8,12},{10,14},{12... | collective-permute-start | bytes 2359304 | tf_op jit(solution)/shard_map/ppermute | solution.py:128
  11.3 22.1 %collective-permute-start.9 = (f32[3840]{0:T(1024)S(1)}, f32[3840]{0:T(1024)S(1)}, u32[]{:S(2)}, u32[]{:S(2)}) collective-permute-start(f32[3840]{0:T(1024)S(1)} %constant_dynamic-update-slice_fusion.8), channel_id=1, source_target_pairs={{0,2},{2,0},{4,6},{6,4},{1,3},{3,1},{5,7},{7,5},{8,10},{10,8},{12,... | collective-permute-start | bytes 46088 | tf_op jit(solution)/shard_map/ppermute | solution.py:124
  27.9 17.0 %collective-permute-start.7 = (bf16[640,512]{1,0:T(8,128)(2,1)}, bf16[640,512]{1,0:T(8,128)(2,1)}, u32[]{:S(2)}, u32[]{:S(2)}) collective-permute-start(bf16[640,512]{1,0:T(8,128)(2,1)} %get-tuple-element.347), channel_id=1, source_target_pairs={{0,1},{1,0},{2,3},{3,2},{4,5},{5,4},{6,7},{7,6},{8,9},{9,8},{10,11... | collective-permute-start | bytes 1966088 | tf_op jit(solution)/shard_map/ppermute | solution.py:132
  33.3 28.9 %collective-permute-start.3 = (bf16[512,768]{1,0:T(8,128)(2,1)S(1)}, bf16[512,768]{1,0:T(8,128)(2,1)S(1)}, u32[]{:S(2)}, u32[]{:S(2)}) collective-permute-start(bf16[512,768]{1,0:T(8,128)(2,1)S(1)} %copy-done.23), channel_id=1, source_target_pairs={{0,2},{2,0},{4,6},{6,4},{1,3},{3,1},{5,7},{7,5},{8,10},{10,8},{12,... | collective-permute-start | bytes 2359304 | tf_op jit(solution)/shard_map/ppermute | solution.py:124
  38.8 20.1 %collective-permute-start.2 = (bf16[512,768]{1,0:T(8,128)(2,1)S(1)}, bf16[512,768]{1,0:T(8,128)(2,1)}, u32[]{:S(2)}, u32[]{:S(2)}) collective-permute-start(bf16[512,768]{1,0:T(8,128)(2,1)S(1)} %collective-permute-done.refs_1_), channel_id=1, source_target_pairs={{0,4},{2,6},{4,0},{6,2},{1,5},{3,7},{5,1},{7,3},{8,12},{10,14},{12... | collective-permute-start | bytes 2359304 | tf_op jit(solution)/shard_map/ppermute | solution.py:128
  58.9 17.5 %collective-permute-start.21 = (bf16[256,512]{1,0:T(8,128)(2,1)}, bf16[256,512]{1,0:T(8,128)(2,1)}, u32[]{:S(2)}, u32[]{:S(2)}) collective-permute-start(bf16[256,512]{1,0:T(8,128)(2,1)} %refs_0_.12), channel_id=1, source_target_pairs={{0,4},{2,6},{4,0},{6,2},{1,5},{3,7},{5,1},{7,3},{8,12},{10,14},{12... | collective-permute-start | bytes 786440 | tf_op jit(solution)/shard_map/ppermute | solution.py:128
  62.3 17.8 %collective-permute-start.19 = (bf16[640,512]{1,0:T(8,128)(2,1)}, bf16[640,512]{1,0:T(8,128)(2,1)}, u32[]{:S(2)}, u32[]{:S(2)}) collective-permute-start(bf16[640,512]{1,0:T(8,128)(2,1)} %get-tuple-element.341), channel_id=1, source_target_pairs={{0,1},{1,0},{2,3},{3,2},{4,5},{5,4},{6,7},{7,6},{8,9},{9,8},{10,11... | collective-permute-start | bytes 1966088 | tf_op jit(solution)/shard_map/ppermute | solution.py:132
  73.3 17.7 %collective-permute-start.15 = (bf16[128,768]{1,0:T(8,128)(2,1)S(1)}, bf16[128,768]{1,0:T(8,128)(2,1)S(1)}, u32[]{:S(2)}, u32[]{:S(2)}) collective-permute-start(bf16[128,768]{1,0:T(8,128)(2,1)S(1)} %get-tuple-element.369), channel_id=1, source_target_pairs={{0,1},{1,0},{2,3},{3,2},{4,5},{5,4},{6,7},{7,6},{8,9},{9,8},{10,11... | collective-permute-start | bytes 589832 | tf_op jit(solution)/shard_map/ppermute | solution.py:175
  74.6 16.9 %collective-permute-start.16 = (bf16[128,768]{1,0:T(8,128)(2,1)S(1)}, bf16[128,768]{1,0:T(8,128)(2,1)S(1)}, u32[]{:S(2)}, u32[]{:S(2)}) collective-permute-start(bf16[128,768]{1,0:T(8,128)(2,1)S(1)} %get-tuple-element.368), channel_id=1, source_target_pairs={{0,2},{1,3},{2,0},{3,1},{4,6},{5,7},{6,4},{7,5},{8,10},{9,11},{10,... | collective-permute-start | bytes 589832 | tf_op jit(solution)/shard_map/ppermute | solution.py:175
  74.6 17.0 %collective-permute-start.17 = (bf16[128,768]{1,0:T(8,128)(2,1)S(1)}, bf16[128,768]{1,0:T(8,128)(2,1)S(1)}, u32[]{:S(2)}, u32[]{:S(2)}) collective-permute-start(bf16[128,768]{1,0:T(8,128)(2,1)S(1)} %get-tuple-element.367), channel_id=1, source_target_pairs={{0,3},{1,2},{2,1},{3,0},{4,7},{5,6},{6,5},{7,4},{8,11},{9,10},{10,... | collective-permute-start | bytes 589832 | tf_op jit(solution)/shard_map/ppermute | solution.py:175
  97.3 25.4 %collective-permute-start.22 = (bf16[512,1024]{1,0:T(8,128)(2,1)}, bf16[512,1024]{1,0:T(8,128)(2,1)}, u32[]{:S(2)}, u32[]{:S(2)}) collective-permute-start(bf16[512,1024]{1,0:T(8,128)(2,1)} %refs_0_.11), channel_id=1, source_target_pairs={{0,4},{2,6},{4,0},{6,2},{1,5},{3,7},{5,1},{7,3},{8,12},{10,14},{12... | collective-permute-start | bytes 3145736 | tf_op jit(solution)/shard_map/ppermute | solution.py:128
  97.8 16.2 %collective-permute-start.30 = (bf16[128,256]{1,0:T(8,128)(2,1)}, bf16[128,256]{1,0:T(8,128)(2,1)}, u32[]{:S(2)}, u32[]{:S(2)}) collective-permute-start(bf16[128,256]{1,0:T(8,128)(2,1)} %get-tuple-element.384), channel_id=1, source_target_pairs={{0,1},{1,0},{2,3},{3,2},{4,5},{5,4},{6,7},{7,6},{8,9},{9,8},{10,11... | collective-permute-start | bytes 196616 | tf_op jit(solution)/shard_map/ppermute | solution.py:181
  100.0 26.1 %collective-permute-start.20 = (bf16[512,1024]{1,0:T(8,128)(2,1)}, bf16[512,1024]{1,0:T(8,128)(2,1)}, u32[]{:S(2)}, u32[]{:S(2)}) collective-permute-start(bf16[512,1024]{1,0:T(8,128)(2,1)} %refs_0_.11), channel_id=1, source_target_pairs={{0,1},{1,0},{2,3},{3,2},{4,5},{5,4},{6,7},{7,6},{8,9},{9,8},{10,11... | collective-permute-start | bytes 3145736 | tf_op jit(solution)/shard_map/ppermute | solution.py:132
  114.0 30.2 %collective-permute-start.37 = (bf16[512,1024]{1,0:T(8,128)(2,1)}, bf16[512,1024]{1,0:T(8,128)(2,1)}, u32[]{:S(2)}, u32[]{:S(2)}) collective-permute-start(bf16[512,1024]{1,0:T(8,128)(2,1)} %refs_0_.11), channel_id=1, source_target_pairs={{0,2},{2,0},{4,6},{6,4},{1,3},{3,1},{5,7},{7,5},{8,10},{10,8},{12,... | collective-permute-start | bytes 3145736 | tf_op jit(solution)/shard_map/ppermute | solution.py:124
  144.3 25.6 %collective-permute-start.33 = (bf16[1024,512]{1,0:T(8,128)(2,1)S(1)}, bf16[1024,512]{1,0:T(8,128)(2,1)S(1)}, u32[]{:S(2)}, u32[]{:S(2)}) collective-permute-start(bf16[1024,512]{1,0:T(8,128)(2,1)S(1)} %copy-done.22), channel_id=1, source_target_pairs={{0,1},{1,0},{2,3},{3,2},{4,5},{5,4},{6,7},{7,6},{8,9},{9,8},{10,11... | collective-permute-start | bytes 3145736 | tf_op jit(solution)/shard_map/ppermute | solution.py:132
  145.6 25.2 %collective-permute-start.34 = (bf16[1024,512]{1,0:T(8,128)(2,1)S(1)}, bf16[1024,512]{1,0:T(8,128)(2,1)S(1)}, u32[]{:S(2)}, u32[]{:S(2)}) collective-permute-start(bf16[1024,512]{1,0:T(8,128)(2,1)S(1)} %copy-done.22), channel_id=1, source_target_pairs={{0,4},{2,6},{4,0},{6,2},{1,5},{3,7},{5,1},{7,3},{8,12},{10,14},{12... | collective-permute-start | bytes 3145736 | tf_op jit(solution)/shard_map/ppermute | solution.py:128
  149.6 35.2 %collective-permute-start.44 = (bf16[1024,512]{1,0:T(8,128)(2,1)S(1)}, bf16[1024,512]{1,0:T(8,128)(2,1)}, u32[]{:S(2)}, u32[]{:S(2)}) collective-permute-start(bf16[1024,512]{1,0:T(8,128)(2,1)S(1)} %copy-done.22), channel_id=1, source_target_pairs={{0,2},{2,0},{4,6},{6,4},{1,3},{3,1},{5,7},{7,5},{8,10},{10,8},{12,... | collective-permute-start | bytes 3145736 | tf_op jit(solution)/shard_map/ppermute | solution.py:124
  218.8 17.5 %collective-permute-start.50 = (bf16[4,1024,512]{2,1,0:T(8,128)(2,1)}, bf16[4,1024,512]{2,1,0:T(8,128)(2,1)}, u32[]{:S(2)}, u32[]{:S(2)}) collective-permute-start(bf16[4,1024,512]{2,1,0:T(8,128)(2,1)} %get-tuple-element.185), channel_id=1, source_target_pairs={{0,2},{2,0},{4,6},{6,4},{1,3},{3,1},{5,7},{7,5},{8,10},{10,8},{12,... | collective-permute-start | bytes 12582920 | tf_op jit(solution)/shard_map/ppermute | solution.py:124
  219.0 17.3 %collective-permute-start.49 = (bf16[640,512]{1,0:T(8,128)(2,1)}, bf16[640,512]{1,0:T(8,128)(2,1)}, u32[]{:S(2)}, u32[]{:S(2)}) collective-permute-start(bf16[640,512]{1,0:T(8,128)(2,1)} %get-tuple-element.183), channel_id=1, source_target_pairs={{0,1},{1,0},{2,3},{3,2},{4,5},{5,4},{6,7},{7,6},{8,9},{9,8},{10,11... | collective-permute-start | bytes 1966088 | tf_op jit(solution)/shard_map/ppermute | solution.py:132
  241.2 43.5 %collective-permute-start.55 = (bf16[1024,512]{1,0:T(8,128)(2,1)}, bf16[1024,512]{1,0:T(8,128)(2,1)}, u32[]{:S(2)}, u32[]{:S(2)}) collective-permute-start(bf16[1024,512]{1,0:T(8,128)(2,1)} %pad_maximum_fusion.5), channel_id=1, source_target_pairs={{0,4},{2,6},{4,0},{6,2},{1,5},{3,7},{5,1},{7,3},{8,12},{10,14},{12... | collective-permute-start | bytes 3145736 | tf_op jit(solution)/shard_map/ppermute | solution.py:128
  242.4 42.4 %collective-permute-start.56 = (bf16[1024,512]{1,0:T(8,128)(2,1)}, bf16[1024,512]{1,0:T(8,128)(2,1)}, u32[]{:S(2)}, u32[]{:S(2)}) collective-permute-start(bf16[1024,512]{1,0:T(8,128)(2,1)} %pad_maximum_fusion.4), channel_id=1, source_target_pairs={{0,1},{1,0},{2,3},{3,2},{4,5},{5,4},{6,7},{7,6},{8,9},{9,8},{10,11... | collective-permute-start | bytes 3145736 | tf_op jit(solution)/shard_map/ppermute | solution.py:132
  288.2 28.6 %collective-permute-start.60 = (bf16[512,512]{1,0:T(8,128)(2,1)}, bf16[512,512]{1,0:T(8,128)(2,1)}, u32[]{:S(2)}, u32[]{:S(2)}) collective-permute-start(bf16[512,512]{1,0:T(8,128)(2,1)} %get-tuple-element.205), channel_id=1, source_target_pairs={{0,4},{2,6},{4,0},{6,2},{1,5},{3,7},{5,1},{7,3},{8,12},{10,14},{12... | collective-permute-start | bytes 1572872 | tf_op jit(solution)/shard_map/ppermute | solution.py:128
  289.2 28.8 %collective-permute-start.59 = (bf16[512,512]{1,0:T(8,128)(2,1)}, bf16[512,512]{1,0:T(8,128)(2,1)}, u32[]{:S(2)}, u32[]{:S(2)}) collective-permute-start(bf16[512,512]{1,0:T(8,128)(2,1)} %get-tuple-element.204), channel_id=1, source_target_pairs={{0,1},{1,0},{2,3},{3,2},{4,5},{5,4},{6,7},{7,6},{8,9},{9,8},{10,11... | collective-permute-start | bytes 1572872 | tf_op jit(solution)/shard_map/ppermute | solution.py:132
  294.6 28.2 %collective-permute-start.62 = (bf16[128,768]{1,0:T(8,128)(2,1)}, bf16[128,768]{1,0:T(8,128)(2,1)}, u32[]{:S(2)}, u32[]{:S(2)}) collective-permute-start(bf16[128,768]{1,0:T(8,128)(2,1)} %get-tuple-element.364), channel_id=1, source_target_pairs={{0,1},{1,0},{2,3},{3,2},{4,5},{5,4},{6,7},{7,6},{8,9},{9,8},{10,11... | collective-permute-start | bytes 589832 | tf_op jit(solution)/shard_map/ppermute | solution.py:181
  295.7 28.7 %collective-permute-start.63 = (bf16[128,768]{1,0:T(8,128)(2,1)}, bf16[128,768]{1,0:T(8,128)(2,1)}, u32[]{:S(2)}, u32[]{:S(2)}) collective-permute-start(bf16[128,768]{1,0:T(8,128)(2,1)} %get-tuple-element.363), channel_id=1, source_target_pairs={{0,2},{1,3},{2,0},{3,1},{4,6},{5,7},{6,4},{7,5},{8,10},{9,11},{10,... | collective-permute-start | bytes 589832 | tf_op jit(solution)/shard_map/ppermute | solution.py:181
  295.7 28.7 %collective-permute-start.64 = (bf16[128,768]{1,0:T(8,128)(2,1)}, bf16[128,768]{1,0:T(8,128)(2,1)}, u32[]{:S(2)}, u32[]{:S(2)}) collective-permute-start(bf16[128,768]{1,0:T(8,128)(2,1)} %get-tuple-element.362), channel_id=1, source_target_pairs={{0,3},{1,2},{2,1},{3,0},{4,7},{5,6},{6,5},{7,4},{8,11},{9,10},{10,... | collective-permute-start | bytes 589832 | tf_op jit(solution)/shard_map/ppermute | solution.py:181
  316.8 27.5 %collective-permute-start.57 = (bf16[512,1024]{1,0:T(8,128)(2,1)}, bf16[512,1024]{1,0:T(8,128)(2,1)}, u32[]{:S(2)}, u32[]{:S(2)}) collective-permute-start(bf16[512,1024]{1,0:T(8,128)(2,1)} %pad_maximum_fusion.7), channel_id=1, source_target_pairs={{0,4},{2,6},{4,0},{6,2},{1,5},{3,7},{5,1},{7,3},{8,12},{10,14},{12... | collective-permute-start | bytes 3145736 | tf_op jit(solution)/shard_map/ppermute | solution.py:128
  318.1 26.3 %collective-permute-start.58 = (bf16[512,1024]{1,0:T(8,128)(2,1)}, bf16[512,1024]{1,0:T(8,128)(2,1)}, u32[]{:S(2)}, u32[]{:S(2)}) collective-permute-start(bf16[512,1024]{1,0:T(8,128)(2,1)} %pad_maximum_fusion.6), channel_id=1, source_target_pairs={{0,1},{1,0},{2,3},{3,2},{4,5},{5,4},{6,7},{7,6},{8,9},{9,8},{10,11... | collective-permute-start | bytes 3145736 | tf_op jit(solution)/shard_map/ppermute | solution.py:132
  338.5 28.4 %collective-permute-start.66 = (bf16[4,512,768]{2,1,0:T(8,128)(2,1)}, bf16[4,512,768]{2,1,0:T(8,128)(2,1)}, u32[]{:S(2)}, u32[]{:S(2)}) collective-permute-start(bf16[4,512,768]{2,1,0:T(8,128)(2,1)} %get-tuple-element.219), channel_id=1, source_target_pairs={{0,2},{2,0},{4,6},{6,4},{1,3},{3,1},{5,7},{7,5},{8,10},{10,8},{12,... | collective-permute-start | bytes 9437192 | tf_op jit(solution)/shard_map/ppermute | solution.py:124
  353.5 42.5 %collective-permute-start.65 = (bf16[4,256,512]{2,1,0:T(8,128)(2,1)}, bf16[4,256,512]{2,1,0:T(8,128)(2,1)}, u32[]{:S(2)}, u32[]{:S(2)}) collective-permute-start(bf16[4,256,512]{2,1,0:T(8,128)(2,1)} %get-tuple-element.228), channel_id=1, source_target_pairs={{0,2},{2,0},{4,6},{6,4},{1,3},{3,1},{5,7},{7,5},{8,10},{10,8},{12,... | collective-permute-start | bytes 3145736 | tf_op jit(solution)/shard_map/ppermute | solution.py:124
  358.5 33.8 %collective-permute-start.71 = (bf16[256,512]{1,0:T(8,128)(2,1)}, bf16[256,512]{1,0:T(8,128)(2,1)}, u32[]{:S(2)}, u32[]{:S(2)}) collective-permute-start(bf16[256,512]{1,0:T(8,128)(2,1)} %add_convert_fusion.16), channel_id=1, source_target_pairs={{0,16},{8,24},{16,0},{24,8},{1,17},{9,25},{17,1},{25,9},{2,18},{10... | collective-permute-start | bytes 786440 | tf_op jit(solution)/shard_map/ppermute | solution.py:650
  366.4 27.8 %collective-permute-start.70 = (bf16[256,1024]{1,0:T(8,128)(2,1)}, bf16[256,1024]{1,0:T(8,128)(2,1)}, u32[]{:S(2)}, u32[]{:S(2)}) collective-permute-start(bf16[256,1024]{1,0:T(8,128)(2,1)} %get-tuple-element.237), channel_id=1, source_target_pairs={{0,8},{8,0},{16,24},{24,16},{1,9},{9,1},{17,25},{25,17},{2,10},{10... | collective-permute-start | bytes 1572872 | tf_op jit(solution)/shard_map/ppermute | solution.py:650
  370.6 18.1 %collective-permute-start.72 = (bf16[512,768]{1,0:T(8,128)(2,1)}, bf16[512,768]{1,0:T(8,128)(2,1)}, u32[]{:S(2)}, u32[]{:S(2)}) collective-permute-start(bf16[512,768]{1,0:T(8,128)(2,1)} %pad_maximum_fusion.12), channel_id=1, source_target_pairs={{0,4},{2,6},{4,0},{6,2},{1,5},{3,7},{5,1},{7,3},{8,12},{10,14},{12... | collective-permute-start | bytes 2359304 | tf_op jit(solution)/shard_map/ppermute | solution.py:128
  371.6 17.8 %collective-permute-start.73 = (bf16[512,768]{1,0:T(8,128)(2,1)}, bf16[512,768]{1,0:T(8,128)(2,1)}, u32[]{:S(2)}, u32[]{:S(2)}) collective-permute-start(bf16[512,768]{1,0:T(8,128)(2,1)} %pad_maximum_fusion.11), channel_id=1, source_target_pairs={{0,1},{1,0},{2,3},{3,2},{4,5},{5,4},{6,7},{7,6},{8,9},{9,8},{10,11... | collective-permute-start | bytes 2359304 | tf_op jit(solution)/shard_map/ppermute | solution.py:132
  391.0 18.0 %collective-permute-start.79 = (bf16[256,768]{1,0:T(8,128)(2,1)S(1)}, bf16[256,768]{1,0:T(8,128)(2,1)S(1)}, u32[]{:S(2)}, u32[]{:S(2)}) collective-permute-start(bf16[256,768]{1,0:T(8,128)(2,1)S(1)} %get-tuple-element.247), channel_id=1, source_target_pairs={{0,1},{1,0},{2,3},{3,2},{4,5},{5,4},{6,7},{7,6},{8,9},{9,8},{10,11... | collective-permute-start | bytes 1179656 | tf_op jit(solution)/shard_map/ppermute | solution.py:132
  395.5 16.5 %collective-permute-start.77 = (bf16[128,1024]{1,0:T(8,128)(2,1)S(1)}, bf16[128,1024]{1,0:T(8,128)(2,1)S(1)}, u32[]{:S(2)}, u32[]{:S(2)}) collective-permute-start(bf16[128,1024]{1,0:T(8,128)(2,1)S(1)} %broadcast_select_fusion.15), channel_id=1, source_target_pairs={{0,16},{8,24},{16,0},{24,8},{1,17},{9,25},{17,1},{25,9},{2,18},{10... | collective-permute-start | bytes 786440 | tf_op jit(solution)/shard_map/ppermute | solution.py:650
  396.0 17.1 %collective-permute-start.76 = (f32[12288]{0:T(1024)S(1)}, f32[12288]{0:T(1024)S(1)}, u32[]{:S(2)}, u32[]{:S(2)}) collective-permute-start(f32[12288]{0:T(1024)S(1)} %pad_maximum_fusion.25), channel_id=1, source_target_pairs={{0,2},{2,0},{4,6},{6,4},{1,3},{3,1},{5,7},{7,5},{8,10},{10,8},{12,... | collective-permute-start | bytes 147464 | tf_op jit(solution)/shard_map/ppermute | solution.py:124
  398.4 17.1 %collective-permute-start.74 = (bf16[256,512]{1,0:T(8,128)(2,1)S(1)}, bf16[256,512]{1,0:T(8,128)(2,1)S(1)}, u32[]{:S(2)}, u32[]{:S(2)}) collective-permute-start(bf16[256,512]{1,0:T(8,128)(2,1)S(1)} %pad_maximum_fusion.23), channel_id=1, source_target_pairs={{0,4},{2,6},{4,0},{6,2},{1,5},{3,7},{5,1},{7,3},{8,12},{10,14},{12... | collective-permute-start | bytes 786440 | tf_op jit(solution)/shard_map/ppermute | solution.py:128
  409.0 38.1 %collective-permute-start.90 = (bf16[512,512]{1,0:T(8,128)(2,1)}, bf16[512,512]{1,0:T(8,128)(2,1)}, u32[]{:S(2)}, u32[]{:S(2)}) collective-permute-start(bf16[512,512]{1,0:T(8,128)(2,1)} %pad_maximum_fusion.18), channel_id=1, source_target_pairs={{0,8},{8,0},{16,24},{24,16},{1,9},{9,1},{17,25},{25,17},{2,10},{10... | collective-permute-start | bytes 1572872 | tf_op jit(solution)/shard_map/ppermute | solution.py:650
  412.0 24.2 %collective-permute-start.84 = (bf16[256,768]{1,0:T(8,128)(2,1)S(1)}, bf16[256,768]{1,0:T(8,128)(2,1)S(1)}, u32[]{:S(2)}, u32[]{:S(2)}) collective-permute-start(bf16[256,768]{1,0:T(8,128)(2,1)S(1)} %get-tuple-element.259), channel_id=1, source_target_pairs={{0,8},{8,0},{16,24},{24,16},{1,9},{9,1},{17,25},{25,17},{2,10},{10... | collective-permute-start | bytes 1179656 | tf_op jit(solution)/shard_map/ppermute | solution.py:650
  413.1 26.5 %collective-permute-start.82 = (bf16[128,1024]{1,0:T(8,128)(2,1)S(1)}, bf16[128,1024]{1,0:T(8,128)(2,1)S(1)}, u32[]{:S(2)}, u32[]{:S(2)}) collective-permute-start(bf16[128,1024]{1,0:T(8,128)(2,1)S(1)} %add_convert_fusion.15), channel_id=1, source_target_pairs={{0,16},{8,24},{16,0},{24,8},{1,17},{9,25},{17,1},{25,9},{2,18},{10... | collective-permute-start | bytes 786440 | tf_op jit(solution)/shard_map/ppermute | solution.py:650
  415.5 22.5 %collective-permute-start.83 = (f32[12288]{0:T(1024)S(1)}, f32[12288]{0:T(1024)S(1)}, u32[]{:S(2)}, u32[]{:S(2)}) collective-permute-start(f32[12288]{0:T(1024)S(1)} %fusion.43), channel_id=1, source_target_pairs={{0,4},{2,6},{4,0},{6,2},{1,5},{3,7},{5,1},{7,3},{8,12},{10,14},{12... | collective-permute-start | bytes 147464 | tf_op jit(solution)/shard_map/ppermute | solution.py:128
  417.7 23.8 %collective-permute-start.81 = (bf16[128,512]{1,0:T(8,128)(2,1)S(1)}, bf16[128,512]{1,0:T(8,128)(2,1)S(1)}, u32[]{:S(2)}, u32[]{:S(2)}) collective-permute-start(bf16[128,512]{1,0:T(8,128)(2,1)S(1)} %get-tuple-element.267), channel_id=1, source_target_pairs={{0,4},{2,6},{4,0},{6,2},{1,5},{3,7},{5,1},{7,3},{8,12},{10,14},{12... | collective-permute-start | bytes 393224 | tf_op jit(solution)/shard_map/ppermute | solution.py:128
  438.0 23.3 %collective-permute-start.88 = (bf16[128,768]{1,0:T(8,128)(2,1)}, bf16[128,768]{1,0:T(8,128)(2,1)}, u32[]{:S(2)}, u32[]{:S(2)}) collective-permute-start(bf16[128,768]{1,0:T(8,128)(2,1)} %broadcast_select_fusion.21), channel_id=1, source_target_pairs={{0,16},{8,24},{16,0},{24,8},{1,17},{9,25},{17,1},{25,9},{2,18},{10... | collective-permute-start | bytes 589832 | tf_op jit(solution)/shard_map/ppermute | solution.py:650
  441.5 17.0 %collective-permute-start.89 = (bf16[256,1024]{1,0:T(8,128)(2,1)}, bf16[256,1024]{1,0:T(8,128)(2,1)}, u32[]{:S(2)}, u32[]{:S(2)}) collective-permute-start(bf16[256,1024]{1,0:T(8,128)(2,1)} %pad_maximum_fusion.19), channel_id=1, source_target_pairs={{0,8},{8,0},{16,24},{24,16},{1,9},{9,1},{17,25},{25,17},{2,10},{10... | collective-permute-start | bytes 1572872 | tf_op jit(solution)/shard_map/ppermute | solution.py:650
  445.7 19.6 %collective-permute-start.85 = (bf16[128,512]{1,0:T(8,128)(2,1)}, bf16[128,512]{1,0:T(8,128)(2,1)S(1)}, u32[]{:S(2)}, u32[]{:S(2)}) collective-permute-start(bf16[128,512]{1,0:T(8,128)(2,1)} %get-tuple-element.276), channel_id=1, source_target_pairs={{0,8},{8,0},{16,24},{24,16},{1,9},{9,1},{17,25},{25,17},{2,10},{10... | collective-permute-start | bytes 393224 | tf_op jit(solution)/shard_map/ppermute | solution.py:650
  445.8 39.9 %collective-permute-start.95 = (bf16[640,512]{1,0:T(8,128)(2,1)S(1)}, bf16[640,512]{1,0:T(8,128)(2,1)}, u32[]{:S(2)}, u32[]{:S(2)}) collective-permute-start(bf16[640,512]{1,0:T(8,128)(2,1)S(1)} %copy-done.36), channel_id=1, source_target_pairs={{0,1},{1,0},{2,3},{3,2},{4,5},{5,4},{6,7},{7,6},{8,9},{9,8},{10,11... | collective-permute-start | bytes 1966088 | tf_op jit(solution)/shard_map/ppermute | solution.py:132
  (123 other events, 1142.7 us)

commit v6 on v5

--- a/solution.py
+++ b/solution.py
@@ -340,10 +340,10 @@
 
 
 def each_rows(count, body):
-    @pl.loop(0, count // (2 * ROWS))
+    @pl.loop(0, count // (4 * ROWS))
     def _(step):
-        for part in range(2):
-            body(pl.ds(pl.multiple_of((2 * step + part) * ROWS, ROWS), ROWS))
+        for part in range(4):
+            body(pl.ds(pl.multiple_of((4 * step + part) * ROWS, ROWS), ROWS))
 
 
 def add_rows(partial, place, value):
@@ -863,25 +863,25 @@
     qv_sums = jnp.concatenate([column_sums[:, 0], column_sums[:, 2]], 1)
     sums = jnp.concatenate([halves.reshape(-1), ordered(ff_in_bias_part).reshape(-1), qv_sums.reshape(-1)])
     sums = VectorSum(sums, own_part, n_dp)
-    qkv_sum.send_last(in_leave)
-    event = ff_out_pairs.step(qkv_sum.last[0])
+    event = ff_out_pairs.step(in_leave)
     event = ff_in_pairs.step(event)
+    qkv_sum.send_last(event)
+    event = sums.step(qkv_sum.last[0])
+    out_sum.send(event)
+    event = ff_in_pairs.step(out_sum.sent[0])
+    event = ff_out_pairs.step(event)
     event = sums.step(event)
-    out_sum.send(event)
-    qkv_pairs = PairSum(qkv_sum.result(*out_sum.sent), n_dp)
-    event = qkv_pairs.step(out_sum.sent[0])
-    event = ff_in_pairs.step(event)
+    qkv_pairs = PairSum(qkv_sum.result(event), n_dp)
+    event = qkv_pairs.step(event)
+    out_sum.send_last(event)
+    event = ff_in_pairs.step(out_sum.last[0])
     event = sums.step(event)
-    out_sum.send_last(event)
-    event = qkv_pairs.step(out_sum.last[0])
-    event = sums.step(event)
-    in_other = swap_col(after(in_leave, event))
-    event = ff_in_pairs.step(event)
+    event = qkv_pairs.step(event)
     out_pairs = PairSum(out_sum.result(event), n_dp)
     event = out_pairs.step(event)
     event = sums.step(event)
-
-    every = [ff_out_pairs, ff_in_pairs, qkv_pairs, sums, out_pairs]
+    in_other = swap_col(after(in_leave, event))
+    every = [ff_out_pairs, qkv_pairs, ff_in_pairs, out_pairs, sums]
     while any(pairs.plan for pairs in every):
         for pairs in every:
             event = pairs.step(event)
@@ -889,7 +889,7 @@
     layer_out = give_back(out_mine, after(out_other, event), odd, col)
     for pairs in every:
         pairs.take(event)
-    ff_out_grad, ff_in_grad, qkv_grad, early, out_w_grad = [pairs.result() for pairs in every]
+    ff_out_grad, qkv_grad, ff_in_grad, out_w_grad, early = [pairs.result() for pairs in every]
     halves = early[: 6 * 512].reshape(6, 512)
     return (
         layer_out,

time: 499 us -> 477 us (0.956)
  waiting for transfers between devices: 129 us -> 112 us
    ppermute x16, waiting for transfers between devices: 42.1 us -> 30.3 us  [step(): self.other = lax.ppermute(leaving, 'dp', pairs)]
    unnamed x144 -> x150, local copies, waits for them, and re-layouts: 20.9 us -> 21.5 us
  transfers between devices with their start and end apart: 98 -> 98, of which waited for: 30 -> 31; matrix products, arithmetic and copies ran while one was open for 20% -> 21% of each run, Pallas kernels for 27% -> 28%
where the time goes in v6:
time: 477 us; the launch traced here: 472 us
  Pallas kernels  158 us (33%)
  waiting for transfers between devices  112 us (23%)
  starting transfers between devices  75.7 us (16%)
  other arithmetic  70.1 us (15%)
  local copies, waits for them, and re-layouts  53.6 us (11%)
    ppermute x21, waiting for transfers between devices, swap_col(): return lax.ppermute(value, 'col', [(0, 1), (1, 0)])  46.2 us
    ppermute x16, waiting for transfers between devices, step(): self.other = lax.ppermute(leaving, 'dp', pairs)  30.3 us
    ppermute x19, waiting for transfers between devices, swap_row(): return lax.ppermute(value, 'row', [(i, i ^ 2) for i in range(4)])  27.5 us
    convert_element_type x16, other arithmetic, add(): return total.astype(BF16)  23.6 us
    ppermute x19, starting transfers between devices, swap_row(): return lax.ppermute(value, 'row', [(i, i ^ 2) for i in range(4)])  22.5 us
    ppermute x21, starting transfers between devices, swap_col(): return lax.ppermute(value, 'col', [(0, 1), (1, 0)])  22.3 us
    unnamed x150, local copies, waits for them, and re-layouts  21.5 us
    pallas_call x2, Pallas kernels, grad_up(): dense(grad_up_kernel, [whole(left), columns_of(right)], [two_blocks(out)]...  19.5 us
  transfers between devices with their start and end apart: 98, of which 31 were waited for; matrix products, arithmetic and copies ran while one was open for 21% of the time, Pallas kernels for 28%

profile of v6, /device:TPU:0, one launch (start us, length us, event | category | flops | bytes accessed | tf_op | source)
XLA Modules:
  0.0 471.5 jit_solution(8503937014679422058)
XLA Ops:
  0.7 3.0 collective-permute-start
  11.3 10.5 %collective-permute-done.8 = f32[3840]{0:T(1024)S(1)} collective-permute-done((f32[3840]{0:T(1024)S(1)}, f32[3840]{0:T(1024)S(1)}, u32[]{:S(2)}, u32[]{:S(2)}) %collective-permute-start.8) | collective-permute-done | bytes 15392 | tf_op jit(solution)/shard_map/ppermute | solution.py:132
  41.6 3.3 collective-permute-done.7
  44.9 2.5 pad_maximum_fusion.1.refs_8_.refs_11_.left_ref
  49.9 9.0 %collective-permute-done.2.refs_3_ = bf16[512,768]{1,0:T(8,128)(2,1)} collective-permute-done((bf16[512,768]{1,0:T(8,128)(2,1)S(1)}, bf16[512,768]{1,0:T(8,128)(2,1)}, u32[]{:S(2)}, u32[]{:S(2)}) %collective-permute-start.2) | collective-permute-done | bytes 786464 | tf_op jit(solution)/shard_map/ppermute | solution.py:128
  64.0 8.0 %project_qkv.1.qkv_ref = bf16[640,3072]{1,0:T(8,128)(2,1)} custom-call(bf16[512,768]{1,0:T(8,128)(2,1)S(1)} %copy-done.23, bf16[512,768]{1,0:T(8,128)(2,1)S(1)} %collective-permute-done.refs_1_, bf16[512,768]{1,0:T(8,128)(2,1)S(1)} %collective-permute-done.1.refs_2_, bf16[512,768]{1,0:T(8,128)(2,1)} %collective-permute-done.2.refs_3_, ...), custom_call_target="tpu_custom_call" | custom-call | flops 9999999827968 | bytes 1000000000 | tf_op jit(solution)/shard_map/project_qkv/pallas_call | solution.py:286
  77.9 2.2 collective-permute-done.19
  80.6 2.3 pad_maximum_fusion.2.refs_12_
  83.0 8.0 %collective-permute-done.23.refs_3_ = bf16[128,512]{1,0:T(8,128)(2,1)} collective-permute-done((bf16[128,512]{1,0:T(8,128)(2,1)S(1)}, bf16[128,512]{1,0:T(8,128)(2,1)}, u32[]{:S(2)}, u32[]{:S(2)}) %collective-permute-start.23) | collective-permute-done | bytes 131104 | tf_op jit(solution)/shard_map/ppermute | solution.py:132
  92.0 3.2 attend.2
  100.3 13.7 %attend.3 = (bf16[512,1024]{1,0:T(8,128)(2,1)}, bf16[16,512,512]{2,1,0:T(8,128)(2,1)}) custom-call(bf16[640,3072]{1,0:T(8,128)(2,1)} %project_qkv.1.qkv_ref, s32[512,1]{1,0:T(8,128)} %copy.43.column_ref, s32[1,512]{1,0:T(1,128)} %bitcast.167), custom_call_target="tpu_custom_call" | custom-call | flops 9999999827968 | bytes 1000000000 | tf_op jit(solution)/shard_map/attend/pallas_call | solution.py:61
  118.0 4.7 collective-permute-done.22.refs_2_
  122.7 3.4 collective-permute-done.20.refs_1_
  132.3 9.5 %first_norm.1 = (f32[640,1024]{1,0:T(8,128)}, f32[640,1]{1,0:T(8,128)S(1)}, bf16[640,1024]{1,0:T(8,128)(2,1)S(1)}) custom-call(bf16[256,512]{1,0:T(8,128)(2,1)} %refs_0_.12, bf16[256,512]{1,0:T(8,128)(2,1)} %collective-permute-done.18.refs_1_, bf16[256,512]{1,0:T(8,128)(2,1)} %collective-permute-done.21.refs_2_, ...), custom_call_target="tpu_custom_call" | custom-call | flops 9999999827968 | bytes 1000000000 | tf_op jit(solution)/shard_map/first_norm/pallas_call | solution.py:389
  146.6 2.7 collective-permute-done.40.refs_8_
  150.8 14.4 %project_hidden.1 = (bf16[640,4096]{1,0:T(8,128)(2,1)}, bf16[640,4096]{1,0:T(8,128)(2,1)}) custom-call(bf16[512,1024]{1,0:T(8,128)(2,1)} %refs_0_.11, bf16[512,1024]{1,0:T(8,128)(2,1)} %collective-permute-done.20.refs_1_, bf16[512,1024]{1,0:T(8,128)(2,1)} %collective-permute-done.22.refs_2_, bf16[256,1024]{1,0:T(8,128)(2,1)} %collective-permute-done.35.refs_3_, ...), custom_call_target="tpu_custom_call" | custom-call | flops 10000000 | bytes 1000 | tf_op jit(solution)/shard_map/project_hidden/pallas_call | solution.py:311
  165.2 4.3 collective-permute-done.33.refs_1_
  173.6 10.0 %collective-permute-done.42.refs_3_ = bf16[512,512]{1,0:T(8,128)(2,1)} collective-permute-done((bf16[512,512]{1,0:T(8,128)(2,1)S(1)}, bf16[512,512]{1,0:T(8,128)(2,1)}, u32[]{:S(2)}, u32[]{:S(2)}) %collective-permute-start.42) | collective-permute-done | bytes 524320 | tf_op jit(solution)/shard_map/ppermute | solution.py:132
  186.7 16.1 %second_norm.1 = (f32[640,512]{1,0:T(8,128)}, bf16[640,512]{1,0:T(8,128)(2,1)}, f32[640,1024]{1,0:T(8,128)}, bf16[640,1024]{1,0:T(8,128)(2,1)}, f32[3,1024]{1,0:T(4,128)S(1)}) custom-call(bf16[1024,512]{1,0:T(8,128)(2,1)S(1)} %copy-done.22, bf16[1024,512]{1,0:T(8,128)(2,1)S(1)} %collective-permute-done.33.refs_1_, ...), custom_call_target="tpu_custom_call" | custom-call | flops 9999999827968 | bytes 1000000000 | tf_op jit(solution)/shard_map/second_norm/pallas_call | solution.py:440
  204.1 10.4 %grad_down.2 = (bf16[4,1024,512]{2,1,0:T(8,128)(2,1)S(1)}, bf16[4,1024,512]{2,1,0:T(8,128)(2,1)}) custom-call(bf16[640,4096]{1,0:T(8,128)(2,1)} %get-tuple-element.179.refs_10_.left_ref, bf16[640,1024]{1,0:T(8,128)(2,1)S(1)} %copy-done.39), custom_call_target="tpu_custom_call" | custom-call | flops 9999999827968 | bytes 1000000000 | tf_op jit(solution)/shard_map/grad_down/pallas_call | solution.py:612
  217.8 10.2 %hidden_back.1 = (bf16[640,4096]{1,0:T(8,128)(2,1)}, f32[1,4096]{1,0:T(1,128)S(1)}) custom-call(bf16[1024,512]{1,0:T(8,128)(2,1)S(1)} %copy-done.22, bf16[1024,512]{1,0:T(8,128)(2,1)S(1)} %collective-permute-done.33.refs_1_, bf16[1024,512]{1,0:T(8,128)(2,1)S(1)} %collective-permute-done.34.refs_2_, bf16[512,512]{1,0:T(8,128)(2,1)} %collective-permute-done.42.refs_3_, ...), custom_call_target="tpu_custom_call" | custom-call | flops 9999999827968 | bytes 1000000000 | tf_op jit(solution)/shard_map/hidden_back/pallas_call | solution.py:536
  229.8 4.3 collective-permute-done.49
  234.1 2.8 fusion.20
  241.6 10.7 %grad_up.2 = (bf16[4,512,1024]{2,1,0:T(8,128)(2,1)S(1)}, bf16[4,512,1024]{2,1,0:T(8,128)(2,1)}) custom-call(bf16[640,1024]{1,0:T(8,128)(2,1)S(1)} %copy-done.10, bf16[640,4096]{1,0:T(8,128)(2,1)} %get-tuple-element.196.right_ref.refs_10_), custom_call_target="tpu_custom_call" | custom-call | flops 9999999827968 | bytes 1000000000 | tf_op jit(solution)/shard_map/grad_up/pallas_call | solution.py:587
  254.2 16.5 %first_back.1 = (f32[640,1024]{1,0:T(8,128)}, bf16[640,1024]{1,0:T(8,128)(2,1)}, f32[3,1024]{1,0:T(4,128)S(1)}) custom-call(bf16[512,1024]{1,0:T(8,128)(2,1)} %refs_0_.11, bf16[512,1024]{1,0:T(8,128)(2,1)} %collective-permute-done.20.refs_1_, bf16[512,1024]{1,0:T(8,128)(2,1)} %collective-permute-done.22.refs_2_, ...), custom_call_target="tpu_custom_call" | custom-call | flops 10000000 | bytes 1000 | tf_op jit(solution)/shard_map/first_back/pallas_call | solution.py:480
  272.0 3.4 heads_back.1.grad_ref
  281.9 3.4 fusion.10
  286.8 3.5 attend_back.2
  293.4 3.1 fusion.24
  298.6 14.9 %attend_back.3 = bf16[512,3072]{1,0:T(8,128)(2,1)} custom-call(bf16[640,3072]{1,0:T(8,128)(2,1)} %project_qkv.1.qkv_ref, bf16[16,512,512]{2,1,0:T(8,128)(2,1)} %get-tuple-element.210.probs_ref, bf16[640,1024]{1,0:T(8,128)(2,1)} %copy-done.8), custom_call_target="tpu_custom_call" | custom-call | flops 9999999827968 | bytes 1000000000 | tf_op jit(solution)/shard_map/attend_back/pallas_call | solution.py:107
  316.1 3.9 broadcast_select_fusion.9
  324.5 2.2 pad_maximum_fusion.right_ref.refs_8_
  326.7 8.9 %grad_up.3 = (bf16[4,512,768]{2,1,0:T(8,128)(2,1)S(1)}, bf16[4,512,768]{2,1,0:T(8,128)(2,1)}) custom-call(bf16[640,1024]{1,0:T(8,128)(2,1)S(1)} %copy-done.13, bf16[640,3072]{1,0:T(8,128)(2,1)} %pad_maximum_fusion.right_ref.refs_8_), custom_call_target="tpu_custom_call" | custom-call | flops 9999999827968 | bytes 1000000000 | tf_op jit(solution)/shard_map/grad_up/pallas_call | solution.py:587
  338.8 2.6 collective-permute-start.68
  341.4 3.4 fusion.4
  346.5 3.8 grad_down.3
  350.4 3.4 collective-permute-done.68
  355.6 3.2 collective-permute-done.67
  359.0 3.9 broadcast_select_fusion.6
  369.8 11.0 %input_back.1 = (f32[640,512]{1,0:T(8,128)}, bf16[640,512]{1,0:T(8,128)(2,1)S(1)}, f32[1,3072]{1,0:T(1,128)S(1)}) custom-call(bf16[512,768]{1,0:T(8,128)(2,1)S(1)} %copy-done.24, bf16[512,768]{1,0:T(8,128)(2,1)S(1)} %copy-done.26, bf16[512,768]{1,0:T(8,128)(2,1)S(1)} %copy-done.28, bf16[512,768]{1,0:T(8,128)(2,1)} %collective-permute-done.2.refs_3_, ...), custom_call_target="tpu_custom_call" | custom-call | flops 9999999827968 | bytes 1000000000 | tf_op jit(solution)/shard_map/input_back/pallas_call | solution.py:506
  394.2 9.9 %collective-permute-done.79 = bf16[128,1024]{1,0:T(8,128)(2,1)S(1)} collective-permute-done((bf16[128,1024]{1,0:T(8,128)(2,1)}, bf16[128,1024]{1,0:T(8,128)(2,1)S(1)}, u32[]{:S(2)}, u32[]{:S(2)}) %collective-permute-start.79) | collective-permute-done | bytes 262176 | tf_op jit(solution)/shard_map/ppermute | solution.py:650
  409.3 5.9 %collective-permute-done.76 = bf16[256,768]{1,0:T(8,128)(2,1)S(1)} collective-permute-done((bf16[256,768]{1,0:T(8,128)(2,1)S(1)}, bf16[256,768]{1,0:T(8,128)(2,1)S(1)}, u32[]{:S(2)}, u32[]{:S(2)}) %collective-permute-start.76) | collective-permute-done | bytes 393248 | tf_op jit(solution)/shard_map/ppermute | solution.py:128
  424.6 5.5 %collective-permute-done.83 = bf16[256,768]{1,0:T(8,128)(2,1)S(1)} collective-permute-done((bf16[256,768]{1,0:T(8,128)(2,1)S(1)}, bf16[256,768]{1,0:T(8,128)(2,1)S(1)}, u32[]{:S(2)}, u32[]{:S(2)}) %collective-permute-start.83) | collective-permute-done | bytes 393248 | tf_op jit(solution)/shard_map/ppermute | solution.py:650
  433.2 2.7 collective-permute-start.86
  444.7 3.0 collective-permute-start.89
  447.8 4.7 collective-permute-done.89
  454.9 2.8 collective-permute-done.90
  460.0 2.8 collective-permute-done.97
  (482 shorter events, 171.5 us)
Async XLA Ops:
  0.7 24.9 %collective-permute-start = (bf16[512,768]{1,0:T(8,128)(2,1)}, bf16[512,768]{1,0:T(8,128)(2,1)S(1)}, u32[]{:S(2)}, u32[]{:S(2)}) collective-permute-start(bf16[512,768]{1,0:T(8,128)(2,1)} %refs_0_.13), channel_id=1, source_target_pairs={{0,1},{1,0},{2,3},{3,2},{4,5},{5,4},{6,7},{7,6},{8,9},{9,8},{10,11... | collective-permute-start | bytes 2359304 | tf_op jit(solution)/shard_map/ppermute | solution.py:132
  3.7 22.4 %collective-permute-start.1 = (bf16[512,768]{1,0:T(8,128)(2,1)}, bf16[512,768]{1,0:T(8,128)(2,1)S(1)}, u32[]{:S(2)}, u32[]{:S(2)}) collective-permute-start(bf16[512,768]{1,0:T(8,128)(2,1)} %refs_0_.13), channel_id=1, source_target_pairs={{0,4},{2,6},{4,0},{6,2},{1,5},{3,7},{5,1},{7,3},{8,12},{10,14},{12... | collective-permute-start | bytes 2359304 | tf_op jit(solution)/shard_map/ppermute | solution.py:128
  11.3 22.1 %collective-permute-start.9 = (f32[3840]{0:T(1024)S(1)}, f32[3840]{0:T(1024)S(1)}, u32[]{:S(2)}, u32[]{:S(2)}) collective-permute-start(f32[3840]{0:T(1024)S(1)} %constant_dynamic-update-slice_fusion.8), channel_id=1, source_target_pairs={{0,2},{2,0},{4,6},{6,4},{1,3},{3,1},{5,7},{7,5},{8,10},{10,8},{12,... | collective-permute-start | bytes 46088 | tf_op jit(solution)/shard_map/ppermute | solution.py:124
  27.9 17.0 %collective-permute-start.7 = (bf16[640,512]{1,0:T(8,128)(2,1)}, bf16[640,512]{1,0:T(8,128)(2,1)}, u32[]{:S(2)}, u32[]{:S(2)}) collective-permute-start(bf16[640,512]{1,0:T(8,128)(2,1)} %get-tuple-element.347), channel_id=1, source_target_pairs={{0,1},{1,0},{2,3},{3,2},{4,5},{5,4},{6,7},{7,6},{8,9},{9,8},{10,11... | collective-permute-start | bytes 1966088 | tf_op jit(solution)/shard_map/ppermute | solution.py:132
  33.3 28.9 %collective-permute-start.3 = (bf16[512,768]{1,0:T(8,128)(2,1)S(1)}, bf16[512,768]{1,0:T(8,128)(2,1)S(1)}, u32[]{:S(2)}, u32[]{:S(2)}) collective-permute-start(bf16[512,768]{1,0:T(8,128)(2,1)S(1)} %copy-done.23), channel_id=1, source_target_pairs={{0,2},{2,0},{4,6},{6,4},{1,3},{3,1},{5,7},{7,5},{8,10},{10,8},{12,... | collective-permute-start | bytes 2359304 | tf_op jit(solution)/shard_map/ppermute | solution.py:124
  38.8 20.1 %collective-permute-start.2 = (bf16[512,768]{1,0:T(8,128)(2,1)S(1)}, bf16[512,768]{1,0:T(8,128)(2,1)}, u32[]{:S(2)}, u32[]{:S(2)}) collective-permute-start(bf16[512,768]{1,0:T(8,128)(2,1)S(1)} %collective-permute-done.refs_1_), channel_id=1, source_target_pairs={{0,4},{2,6},{4,0},{6,2},{1,5},{3,7},{5,1},{7,3},{8,12},{10,14},{12... | collective-permute-start | bytes 2359304 | tf_op jit(solution)/shard_map/ppermute | solution.py:128
  58.9 17.5 %collective-permute-start.21 = (bf16[256,512]{1,0:T(8,128)(2,1)}, bf16[256,512]{1,0:T(8,128)(2,1)}, u32[]{:S(2)}, u32[]{:S(2)}) collective-permute-start(bf16[256,512]{1,0:T(8,128)(2,1)} %refs_0_.12), channel_id=1, source_target_pairs={{0,4},{2,6},{4,0},{6,2},{1,5},{3,7},{5,1},{7,3},{8,12},{10,14},{12... | collective-permute-start | bytes 786440 | tf_op jit(solution)/shard_map/ppermute | solution.py:128
  62.3 17.8 %collective-permute-start.19 = (bf16[640,512]{1,0:T(8,128)(2,1)}, bf16[640,512]{1,0:T(8,128)(2,1)}, u32[]{:S(2)}, u32[]{:S(2)}) collective-permute-start(bf16[640,512]{1,0:T(8,128)(2,1)} %get-tuple-element.341), channel_id=1, source_target_pairs={{0,1},{1,0},{2,3},{3,2},{4,5},{5,4},{6,7},{7,6},{8,9},{9,8},{10,11... | collective-permute-start | bytes 1966088 | tf_op jit(solution)/shard_map/ppermute | solution.py:132
  73.2 17.7 %collective-permute-start.15 = (bf16[128,768]{1,0:T(8,128)(2,1)S(1)}, bf16[128,768]{1,0:T(8,128)(2,1)S(1)}, u32[]{:S(2)}, u32[]{:S(2)}) collective-permute-start(bf16[128,768]{1,0:T(8,128)(2,1)S(1)} %get-tuple-element.369), channel_id=1, source_target_pairs={{0,1},{1,0},{2,3},{3,2},{4,5},{5,4},{6,7},{7,6},{8,9},{9,8},{10,11... | collective-permute-start | bytes 589832 | tf_op jit(solution)/shard_map/ppermute | solution.py:175
  74.6 16.9 %collective-permute-start.16 = (bf16[128,768]{1,0:T(8,128)(2,1)S(1)}, bf16[128,768]{1,0:T(8,128)(2,1)S(1)}, u32[]{:S(2)}, u32[]{:S(2)}) collective-permute-start(bf16[128,768]{1,0:T(8,128)(2,1)S(1)} %get-tuple-element.368), channel_id=1, source_target_pairs={{0,2},{1,3},{2,0},{3,1},{4,6},{5,7},{6,4},{7,5},{8,10},{9,11},{10,... | collective-permute-start | bytes 589832 | tf_op jit(solution)/shard_map/ppermute | solution.py:175
  74.6 16.9 %collective-permute-start.17 = (bf16[128,768]{1,0:T(8,128)(2,1)S(1)}, bf16[128,768]{1,0:T(8,128)(2,1)S(1)}, u32[]{:S(2)}, u32[]{:S(2)}) collective-permute-start(bf16[128,768]{1,0:T(8,128)(2,1)S(1)} %get-tuple-element.367), channel_id=1, source_target_pairs={{0,3},{1,2},{2,1},{3,0},{4,7},{5,6},{6,5},{7,4},{8,11},{9,10},{10,... | collective-permute-start | bytes 589832 | tf_op jit(solution)/shard_map/ppermute | solution.py:175
  97.3 25.5 %collective-permute-start.22 = (bf16[512,1024]{1,0:T(8,128)(2,1)}, bf16[512,1024]{1,0:T(8,128)(2,1)}, u32[]{:S(2)}, u32[]{:S(2)}) collective-permute-start(bf16[512,1024]{1,0:T(8,128)(2,1)} %refs_0_.11), channel_id=1, source_target_pairs={{0,4},{2,6},{4,0},{6,2},{1,5},{3,7},{5,1},{7,3},{8,12},{10,14},{12... | collective-permute-start | bytes 3145736 | tf_op jit(solution)/shard_map/ppermute | solution.py:128
  97.8 16.2 %collective-permute-start.30 = (bf16[128,256]{1,0:T(8,128)(2,1)}, bf16[128,256]{1,0:T(8,128)(2,1)}, u32[]{:S(2)}, u32[]{:S(2)}) collective-permute-start(bf16[128,256]{1,0:T(8,128)(2,1)} %get-tuple-element.384), channel_id=1, source_target_pairs={{0,1},{1,0},{2,3},{3,2},{4,5},{5,4},{6,7},{7,6},{8,9},{9,8},{10,11... | collective-permute-start | bytes 196616 | tf_op jit(solution)/shard_map/ppermute | solution.py:181
  98.2 15.9 %collective-permute-start.31 = (bf16[128,256]{1,0:T(8,128)(2,1)}, bf16[128,256]{1,0:T(8,128)(2,1)}, u32[]{:S(2)}, u32[]{:S(2)}) collective-permute-start(bf16[128,256]{1,0:T(8,128)(2,1)} %get-tuple-element.383), channel_id=1, source_target_pairs={{0,2},{1,3},{2,0},{3,1},{4,6},{5,7},{6,4},{7,5},{8,10},{9,11},{10,... | collective-permute-start | bytes 196616 | tf_op jit(solution)/shard_map/ppermute | solution.py:181
  98.2 15.9 %collective-permute-start.32 = (bf16[128,256]{1,0:T(8,128)(2,1)}, bf16[128,256]{1,0:T(8,128)(2,1)}, u32[]{:S(2)}, u32[]{:S(2)}) collective-permute-start(bf16[128,256]{1,0:T(8,128)(2,1)} %get-tuple-element.382), channel_id=1, source_target_pairs={{0,3},{1,2},{2,1},{3,0},{4,7},{5,6},{6,5},{7,4},{8,11},{9,10},{10,... | collective-permute-start | bytes 196616 | tf_op jit(solution)/shard_map/ppermute | solution.py:181
  100.0 26.1 %collective-permute-start.20 = (bf16[512,1024]{1,0:T(8,128)(2,1)}, bf16[512,1024]{1,0:T(8,128)(2,1)}, u32[]{:S(2)}, u32[]{:S(2)}) collective-permute-start(bf16[512,1024]{1,0:T(8,128)(2,1)} %refs_0_.11), channel_id=1, source_target_pairs={{0,1},{1,0},{2,3},{3,2},{4,5},{5,4},{6,7},{7,6},{8,9},{9,8},{10,11... | collective-permute-start | bytes 3145736 | tf_op jit(solution)/shard_map/ppermute | solution.py:132
  114.0 29.9 %collective-permute-start.37 = (bf16[512,1024]{1,0:T(8,128)(2,1)}, bf16[512,1024]{1,0:T(8,128)(2,1)}, u32[]{:S(2)}, u32[]{:S(2)}) collective-permute-start(bf16[512,1024]{1,0:T(8,128)(2,1)} %refs_0_.11), channel_id=1, source_target_pairs={{0,2},{2,0},{4,6},{6,4},{1,3},{3,1},{5,7},{7,5},{8,10},{10,8},{12,... | collective-permute-start | bytes 3145736 | tf_op jit(solution)/shard_map/ppermute | solution.py:124
  143.9 25.6 %collective-permute-start.33 = (bf16[1024,512]{1,0:T(8,128)(2,1)S(1)}, bf16[1024,512]{1,0:T(8,128)(2,1)S(1)}, u32[]{:S(2)}, u32[]{:S(2)}) collective-permute-start(bf16[1024,512]{1,0:T(8,128)(2,1)S(1)} %copy-done.22), channel_id=1, source_target_pairs={{0,1},{1,0},{2,3},{3,2},{4,5},{5,4},{6,7},{7,6},{8,9},{9,8},{10,11... | collective-permute-start | bytes 3145736 | tf_op jit(solution)/shard_map/ppermute | solution.py:132
  145.0 25.2 %collective-permute-start.34 = (bf16[1024,512]{1,0:T(8,128)(2,1)S(1)}, bf16[1024,512]{1,0:T(8,128)(2,1)S(1)}, u32[]{:S(2)}, u32[]{:S(2)}) collective-permute-start(bf16[1024,512]{1,0:T(8,128)(2,1)S(1)} %copy-done.22), channel_id=1, source_target_pairs={{0,4},{2,6},{4,0},{6,2},{1,5},{3,7},{5,1},{7,3},{8,12},{10,14},{12... | collective-permute-start | bytes 3145736 | tf_op jit(solution)/shard_map/ppermute | solution.py:128
  149.3 35.2 %collective-permute-start.44 = (bf16[1024,512]{1,0:T(8,128)(2,1)S(1)}, bf16[1024,512]{1,0:T(8,128)(2,1)}, u32[]{:S(2)}, u32[]{:S(2)}) collective-permute-start(bf16[1024,512]{1,0:T(8,128)(2,1)S(1)} %copy-done.22), channel_id=1, source_target_pairs={{0,2},{2,0},{4,6},{6,4},{1,3},{3,1},{5,7},{7,5},{8,10},{10,8},{12,... | collective-permute-start | bytes 3145736 | tf_op jit(solution)/shard_map/ppermute | solution.py:124
  216.6 17.5 %collective-permute-start.50 = (bf16[4,1024,512]{2,1,0:T(8,128)(2,1)}, bf16[4,1024,512]{2,1,0:T(8,128)(2,1)}, u32[]{:S(2)}, u32[]{:S(2)}) collective-permute-start(bf16[4,1024,512]{2,1,0:T(8,128)(2,1)} %get-tuple-element.185), channel_id=1, source_target_pairs={{0,2},{2,0},{4,6},{6,4},{1,3},{3,1},{5,7},{7,5},{8,10},{10,8},{12,... | collective-permute-start | bytes 12582920 | tf_op jit(solution)/shard_map/ppermute | solution.py:124
  216.7 17.3 %collective-permute-start.49 = (bf16[640,512]{1,0:T(8,128)(2,1)}, bf16[640,512]{1,0:T(8,128)(2,1)}, u32[]{:S(2)}, u32[]{:S(2)}) collective-permute-start(bf16[640,512]{1,0:T(8,128)(2,1)} %get-tuple-element.183), channel_id=1, source_target_pairs={{0,1},{1,0},{2,3},{3,2},{4,5},{5,4},{6,7},{7,6},{8,9},{9,8},{10,11... | collective-permute-start | bytes 1966088 | tf_op jit(solution)/shard_map/ppermute | solution.py:132
  239.0 42.9 %collective-permute-start.55 = (bf16[1024,512]{1,0:T(8,128)(2,1)}, bf16[1024,512]{1,0:T(8,128)(2,1)}, u32[]{:S(2)}, u32[]{:S(2)}) collective-permute-start(bf16[1024,512]{1,0:T(8,128)(2,1)} %pad_maximum_fusion.5), channel_id=1, source_target_pairs={{0,4},{2,6},{4,0},{6,2},{1,5},{3,7},{5,1},{7,3},{8,12},{10,14},{12... | collective-permute-start | bytes 3145736 | tf_op jit(solution)/shard_map/ppermute | solution.py:128
  240.6 41.2 %collective-permute-start.56 = (bf16[1024,512]{1,0:T(8,128)(2,1)}, bf16[1024,512]{1,0:T(8,128)(2,1)}, u32[]{:S(2)}, u32[]{:S(2)}) collective-permute-start(bf16[1024,512]{1,0:T(8,128)(2,1)} %pad_maximum_fusion.4), channel_id=1, source_target_pairs={{0,1},{1,0},{2,3},{3,2},{4,5},{5,4},{6,7},{7,6},{8,9},{9,8},{10,11... | collective-permute-start | bytes 3145736 | tf_op jit(solution)/shard_map/ppermute | solution.py:132
  285.3 28.2 %collective-permute-start.60 = (bf16[512,512]{1,0:T(8,128)(2,1)}, bf16[512,512]{1,0:T(8,128)(2,1)}, u32[]{:S(2)}, u32[]{:S(2)}) collective-permute-start(bf16[512,512]{1,0:T(8,128)(2,1)} %get-tuple-element.205), channel_id=1, source_target_pairs={{0,4},{2,6},{4,0},{6,2},{1,5},{3,7},{5,1},{7,3},{8,12},{10,14},{12... | collective-permute-start | bytes 1572872 | tf_op jit(solution)/shard_map/ppermute | solution.py:128
  285.8 29.3 %collective-permute-start.59 = (bf16[512,512]{1,0:T(8,128)(2,1)}, bf16[512,512]{1,0:T(8,128)(2,1)}, u32[]{:S(2)}, u32[]{:S(2)}) collective-permute-start(bf16[512,512]{1,0:T(8,128)(2,1)} %get-tuple-element.204), channel_id=1, source_target_pairs={{0,1},{1,0},{2,3},{3,2},{4,5},{5,4},{6,7},{7,6},{8,9},{9,8},{10,11... | collective-permute-start | bytes 1572872 | tf_op jit(solution)/shard_map/ppermute | solution.py:132
  291.3 28.7 %collective-permute-start.62 = (bf16[128,768]{1,0:T(8,128)(2,1)}, bf16[128,768]{1,0:T(8,128)(2,1)}, u32[]{:S(2)}, u32[]{:S(2)}) collective-permute-start(bf16[128,768]{1,0:T(8,128)(2,1)} %get-tuple-element.364), channel_id=1, source_target_pairs={{0,1},{1,0},{2,3},{3,2},{4,5},{5,4},{6,7},{7,6},{8,9},{9,8},{10,11... | collective-permute-start | bytes 589832 | tf_op jit(solution)/shard_map/ppermute | solution.py:181
  292.3 29.2 %collective-permute-start.63 = (bf16[128,768]{1,0:T(8,128)(2,1)}, bf16[128,768]{1,0:T(8,128)(2,1)}, u32[]{:S(2)}, u32[]{:S(2)}) collective-permute-start(bf16[128,768]{1,0:T(8,128)(2,1)} %get-tuple-element.363), channel_id=1, source_target_pairs={{0,2},{1,3},{2,0},{3,1},{4,6},{5,7},{6,4},{7,5},{8,10},{9,11},{10,... | collective-permute-start | bytes 589832 | tf_op jit(solution)/shard_map/ppermute | solution.py:181
  292.3 29.2 %collective-permute-start.64 = (bf16[128,768]{1,0:T(8,128)(2,1)}, bf16[128,768]{1,0:T(8,128)(2,1)}, u32[]{:S(2)}, u32[]{:S(2)}) collective-permute-start(bf16[128,768]{1,0:T(8,128)(2,1)} %get-tuple-element.362), channel_id=1, source_target_pairs={{0,3},{1,2},{2,1},{3,0},{4,7},{5,6},{6,5},{7,4},{8,11},{9,10},{10,... | collective-permute-start | bytes 589832 | tf_op jit(solution)/shard_map/ppermute | solution.py:181
  313.5 27.9 %collective-permute-start.57 = (bf16[512,1024]{1,0:T(8,128)(2,1)}, bf16[512,1024]{1,0:T(8,128)(2,1)}, u32[]{:S(2)}, u32[]{:S(2)}) collective-permute-start(bf16[512,1024]{1,0:T(8,128)(2,1)} %pad_maximum_fusion.7), channel_id=1, source_target_pairs={{0,4},{2,6},{4,0},{6,2},{1,5},{3,7},{5,1},{7,3},{8,12},{10,14},{12... | collective-permute-start | bytes 3145736 | tf_op jit(solution)/shard_map/ppermute | solution.py:128
  315.2 26.2 %collective-permute-start.58 = (bf16[512,1024]{1,0:T(8,128)(2,1)}, bf16[512,1024]{1,0:T(8,128)(2,1)}, u32[]{:S(2)}, u32[]{:S(2)}) collective-permute-start(bf16[512,1024]{1,0:T(8,128)(2,1)} %pad_maximum_fusion.6), channel_id=1, source_target_pairs={{0,1},{1,0},{2,3},{3,2},{4,5},{5,4},{6,7},{7,6},{8,9},{9,8},{10,11... | collective-permute-start | bytes 3145736 | tf_op jit(solution)/shard_map/ppermute | solution.py:132
  319.9 15.7 %collective-permute-start.61 = (bf16[512,512]{1,0:T(8,128)(2,1)}, bf16[512,512]{1,0:T(8,128)(2,1)}, u32[]{:S(2)}, u32[]{:S(2)}) collective-permute-start(bf16[512,512]{1,0:T(8,128)(2,1)} %get-tuple-element.214), channel_id=1, source_target_pairs={{0,8},{8,0},{16,24},{24,16},{1,9},{9,1},{17,25},{25,17},{2,10},{10... | collective-permute-start | bytes 1572872 | tf_op jit(solution)/shard_map/ppermute | solution.py:650
  335.6 27.8 %collective-permute-start.66 = (bf16[4,512,768]{2,1,0:T(8,128)(2,1)}, bf16[4,512,768]{2,1,0:T(8,128)(2,1)}, u32[]{:S(2)}, u32[]{:S(2)}) collective-permute-start(bf16[4,512,768]{2,1,0:T(8,128)(2,1)} %get-tuple-element.219), channel_id=1, source_target_pairs={{0,2},{2,0},{4,6},{6,4},{1,3},{3,1},{5,7},{7,5},{8,10},{10,8},{12,... | collective-permute-start | bytes 9437192 | tf_op jit(solution)/shard_map/ppermute | solution.py:124
  338.8 15.1 %collective-permute-start.68 = (bf16[256,512]{1,0:T(8,128)(2,1)}, bf16[256,512]{1,0:T(8,128)(2,1)}, u32[]{:S(2)}, u32[]{:S(2)}) collective-permute-start(bf16[256,512]{1,0:T(8,128)(2,1)} %broadcast_select_fusion.18), channel_id=1, source_target_pairs={{0,16},{8,24},{16,0},{24,8},{1,17},{9,25},{17,1},{25,9},{2,18},{10... | collective-permute-start | bytes 786440 | tf_op jit(solution)/shard_map/ppermute | solution.py:650
  350.3 41.5 %collective-permute-start.65 = (bf16[4,256,512]{2,1,0:T(8,128)(2,1)}, bf16[4,256,512]{2,1,0:T(8,128)(2,1)}, u32[]{:S(2)}, u32[]{:S(2)}) collective-permute-start(bf16[4,256,512]{2,1,0:T(8,128)(2,1)} %get-tuple-element.228), channel_id=1, source_target_pairs={{0,2},{2,0},{4,6},{6,4},{1,3},{3,1},{5,7},{7,5},{8,10},{10,8},{12,... | collective-permute-start | bytes 3145736 | tf_op jit(solution)/shard_map/ppermute | solution.py:124
  355.6 25.3 %collective-permute-start.73 = (bf16[256,512]{1,0:T(8,128)(2,1)}, bf16[256,512]{1,0:T(8,128)(2,1)}, u32[]{:S(2)}, u32[]{:S(2)}) collective-permute-start(bf16[256,512]{1,0:T(8,128)(2,1)} %add_convert_fusion.16), channel_id=1, source_target_pairs={{0,16},{8,24},{16,0},{24,8},{1,17},{9,25},{17,1},{25,9},{2,18},{10... | collective-permute-start | bytes 786440 | tf_op jit(solution)/shard_map/ppermute | solution.py:650
  363.0 21.7 %collective-permute-start.72 = (bf16[256,1024]{1,0:T(8,128)(2,1)}, bf16[256,1024]{1,0:T(8,128)(2,1)}, u32[]{:S(2)}, u32[]{:S(2)}) collective-permute-start(bf16[256,1024]{1,0:T(8,128)(2,1)} %get-tuple-element.237), channel_id=1, source_target_pairs={{0,8},{8,0},{16,24},{24,16},{1,9},{9,1},{17,25},{25,17},{2,10},{10... | collective-permute-start | bytes 1572872 | tf_op jit(solution)/shard_map/ppermute | solution.py:650
  367.1 21.9 %collective-permute-start.70 = (bf16[512,768]{1,0:T(8,128)(2,1)}, bf16[512,768]{1,0:T(8,128)(2,1)}, u32[]{:S(2)}, u32[]{:S(2)}) collective-permute-start(bf16[512,768]{1,0:T(8,128)(2,1)} %pad_maximum_fusion.12), channel_id=1, source_target_pairs={{0,4},{2,6},{4,0},{6,2},{1,5},{3,7},{5,1},{7,3},{8,12},{10,14},{12... | collective-permute-start | bytes 2359304 | tf_op jit(solution)/shard_map/ppermute | solution.py:128
  368.7 20.4 %collective-permute-start.71 = (bf16[512,768]{1,0:T(8,128)(2,1)}, bf16[512,768]{1,0:T(8,128)(2,1)}, u32[]{:S(2)}, u32[]{:S(2)}) collective-permute-start(bf16[512,768]{1,0:T(8,128)(2,1)} %pad_maximum_fusion.11), channel_id=1, source_target_pairs={{0,1},{1,0},{2,3},{3,2},{4,5},{5,4},{6,7},{7,6},{8,9},{9,8},{10,11... | collective-permute-start | bytes 2359304 | tf_op jit(solution)/shard_map/ppermute | solution.py:132
  383.1 21.2 %collective-permute-start.78 = (bf16[512,512]{1,0:T(8,128)(2,1)}, bf16[512,512]{1,0:T(8,128)(2,1)}, u32[]{:S(2)}, u32[]{:S(2)}) collective-permute-start(bf16[512,512]{1,0:T(8,128)(2,1)} %pad_maximum_fusion.17), channel_id=1, source_target_pairs={{0,8},{8,0},{16,24},{24,16},{1,9},{9,1},{17,25},{25,17},{2,10},{10... | collective-permute-start | bytes 1572872 | tf_op jit(solution)/shard_map/ppermute | solution.py:650
  388.4 15.7 %collective-permute-start.79 = (bf16[128,1024]{1,0:T(8,128)(2,1)}, bf16[128,1024]{1,0:T(8,128)(2,1)S(1)}, u32[]{:S(2)}, u32[]{:S(2)}) collective-permute-start(bf16[128,1024]{1,0:T(8,128)(2,1)} %broadcast_select_fusion.15), channel_id=1, source_target_pairs={{0,16},{8,24},{16,0},{24,8},{1,17},{9,25},{17,1},{25,9},{2,18},{10... | collective-permute-start | bytes 786440 | tf_op jit(solution)/shard_map/ppermute | solution.py:650
  390.7 25.1 %collective-permute-start.80 = (bf16[256,768]{1,0:T(8,128)(2,1)S(1)}, bf16[256,768]{1,0:T(8,128)(2,1)S(1)}, u32[]{:S(2)}, u32[]{:S(2)}) collective-permute-start(bf16[256,768]{1,0:T(8,128)(2,1)S(1)} %get-tuple-element.251), channel_id=1, source_target_pairs={{0,1},{1,0},{2,3},{3,2},{4,5},{5,4},{6,7},{7,6},{8,9},{9,8},{10,11... | collective-permute-start | bytes 1179656 | tf_op jit(solution)/shard_map/ppermute | solution.py:132
  391.8 16.0 %collective-permute-start.77 = (f32[12288]{0:T(1024)S(1)}, f32[12288]{0:T(1024)S(1)}, u32[]{:S(2)}, u32[]{:S(2)}) collective-permute-start(f32[12288]{0:T(1024)S(1)} %pad_maximum_fusion.24), channel_id=1, source_target_pairs={{0,2},{2,0},{4,6},{6,4},{1,3},{3,1},{5,7},{7,5},{8,10},{10,8},{12,... | collective-permute-start | bytes 147464 | tf_op jit(solution)/shard_map/ppermute | solution.py:124
  393.1 26.3 %collective-permute-start.75 = (bf16[256,512]{1,0:T(8,128)(2,1)S(1)}, bf16[256,512]{1,0:T(8,128)(2,1)S(1)}, u32[]{:S(2)}, u32[]{:S(2)}) collective-permute-start(bf16[256,512]{1,0:T(8,128)(2,1)S(1)} %pad_maximum_fusion.21), channel_id=1, source_target_pairs={{0,1},{1,0},{2,3},{3,2},{4,5},{5,4},{6,7},{7,6},{8,9},{9,8},{10,11... | collective-permute-start | bytes 786440 | tf_op jit(solution)/shard_map/ppermute | solution.py:132
  404.3 17.1 %collective-permute-start.85 = (bf16[128,1024]{1,0:T(8,128)(2,1)S(1)}, bf16[128,1024]{1,0:T(8,128)(2,1)S(1)}, u32[]{:S(2)}, u32[]{:S(2)}) collective-permute-start(bf16[128,1024]{1,0:T(8,128)(2,1)S(1)} %add_convert_fusion.15), channel_id=1, source_target_pairs={{0,16},{8,24},{16,0},{24,8},{1,17},{9,25},{17,1},{25,9},{2,18},{10... | collective-permute-start | bytes 786440 | tf_op jit(solution)/shard_map/ppermute | solution.py:650
  421.5 21.3 %collective-permute-start.87 = (bf16[256,1024]{1,0:T(8,128)(2,1)S(1)}, bf16[256,1024]{1,0:T(8,128)(2,1)S(1)}, u32[]{:S(2)}, u32[]{:S(2)}) collective-permute-start(bf16[256,1024]{1,0:T(8,128)(2,1)S(1)} %pad_maximum_fusion.18), channel_id=1, source_target_pairs={{0,8},{8,0},{16,24},{24,16},{1,9},{9,1},{17,25},{25,17},{2,10},{10... | collective-permute-start | bytes 1572872 | tf_op jit(solution)/shard_map/ppermute | solution.py:650
  440.9 22.8 %collective-permute-start.92 = (bf16[640,512]{1,0:T(8,128)(2,1)S(1)}, bf16[640,512]{1,0:T(8,128)(2,1)S(1)}, u32[]{:S(2)}, u32[]{:S(2)}) collective-permute-start(bf16[640,512]{1,0:T(8,128)(2,1)S(1)} %copy-done.36), channel_id=1, source_target_pairs={{0,1},{1,0},{2,3},{3,2},{4,5},{5,4},{6,7},{7,6},{8,9},{9,8},{10,11... | collective-permute-start | bytes 1966088 | tf_op jit(solution)/shard_map/ppermute | solution.py:132
  442.7 16.5 %collective-permute-start.93 = (bf16[128,768]{1,0:T(8,128)(2,1)S(1)}, bf16[128,768]{1,0:T(8,128)(2,1)S(1)}, u32[]{:S(2)}, u32[]{:S(2)}) collective-permute-start(bf16[128,768]{1,0:T(8,128)(2,1)S(1)} %add_convert_fusion.17), channel_id=1, source_target_pairs={{0,16},{8,24},{16,0},{24,8},{1,17},{9,25},{17,1},{25,9},{2,18},{10... | collective-permute-start | bytes 589832 | tf_op jit(solution)/shard_map/ppermute | solution.py:650
  (126 other events, 1131.2 us)

commit v7 on v6

--- a/solution.py
+++ b/solution.py
@@ -772,7 +772,7 @@
     qkv_w = Shards(D // 2, qkv_weight, qkv_beside, qkv_across, qkv_corner)
     out_beside = swap_col(after(out_weight, x))
     out_across = swap_row(after(out_weight, qkv_corner))
-    incoming = own_rows(after(out_grad, out_beside), odd, col)
+    incoming = own_rows(after(out_grad, x), odd, col)
     ff_in_across = swap_row(after(ff_in_weight, out_across))
 
     vec = packed[:2, : 6 * 512].reshape(2, 6, 512).transpose(1, 0, 2).reshape(6, D)

time: 477 us -> 476 us (level)
  waiting for transfers between devices: 112 us -> 117 us
  local copies, waits for them, and re-layouts: 53.6 us -> 48.7 us
    ppermute x21, waiting for transfers between devices: 46.2 us -> 60.2 us  [swap_col(): return lax.ppermute(value, 'col', [(0, 1), (1, 0)])]
    ppermute x19, waiting for transfers between devices: 27.5 us -> 18.8 us  [swap_row(): return lax.ppermute(value, 'row', [(i, i ^ 2) for i in range(4)])]
    another operation x9, local copies, waits for them, and re-layouts: 5.89 us -> 0.29 us  [local(): jnp.stack([near[0], near[1], far[0], far[1], near[2], near[3], far[2], fa...]
    unnamed x150 -> x158, local copies, waits for them, and re-layouts: 21.5 us -> 23.2 us
  transfers between devices with their start and end apart: 98 -> 98, of which waited for: 31 -> 32; matrix products, arithmetic and copies ran while one was open for 21% -> 20% of each run, Pallas kernels for 28% -> 28%
where the time goes in v7:
time: 476 us; the launch traced here: 471 us
  Pallas kernels  158 us (33%)
  waiting for transfers between devices  117 us (25%)
  starting transfers between devices  73.4 us (15%)
  other arithmetic  70.2 us (15%)
  local copies, waits for them, and re-layouts  48.7 us (10%)
    ppermute x21, waiting for transfers between devices, swap_col(): return lax.ppermute(value, 'col', [(0, 1), (1, 0)])  60.2 us
    ppermute x16, waiting for transfers between devices, step(): self.other = lax.ppermute(leaving, 'dp', pairs)  29.9 us
    convert_element_type x16, other arithmetic, add(): return total.astype(BF16)  23.6 us
    unnamed x158, local copies, waits for them, and re-layouts  23.2 us
    ppermute x21, starting transfers between devices, swap_col(): return lax.ppermute(value, 'col', [(0, 1), (1, 0)])  22.9 us
    pallas_call x2, Pallas kernels, grad_up(): dense(grad_up_kernel, [whole(left), columns_of(right)], [two_blocks(out)]...  19.5 us
    ppermute x19, starting transfers between devices, swap_row(): return lax.ppermute(value, 'row', [(i, i ^ 2) for i in range(4)])  19.4 us
    ppermute x16, starting transfers between devices, step(): self.other = lax.ppermute(leaving, 'dp', pairs)  18.8 us
  transfers between devices with their start and end apart: 98, of which 32 were waited for; matrix products, arithmetic and copies ran while one was open for 20% of the time, Pallas kernels for 28%

profile of v7, /device:TPU:0, one launch (start us, length us, event | category | flops | bytes accessed | tf_op | source)
XLA Modules:
  0.0 470.7 jit_solution(3384646205625707410)
XLA Ops:
  0.7 3.0 collective-permute-start
  11.3 10.5 %collective-permute-done.8 = f32[3840]{0:T(1024)S(1)} collective-permute-done((f32[3840]{0:T(1024)S(1)}, f32[3840]{0:T(1024)S(1)}, u32[]{:S(2)}, u32[]{:S(2)}) %collective-permute-start.8) | collective-permute-done | bytes 15392 | tf_op jit(solution)/shard_map/ppermute | solution.py:132
  37.7 11.7 %collective-permute-done.7 = bf16[640,512]{1,0:T(8,128)(2,1)} collective-permute-done((bf16[640,512]{1,0:T(8,128)(2,1)}, bf16[640,512]{1,0:T(8,128)(2,1)}, u32[]{:S(2)}, u32[]{:S(2)}) %collective-permute-start.7) | collective-permute-done | bytes 655392 | tf_op jit(solution)/shard_map/ppermute | solution.py:132
  49.5 2.6 pad_maximum_fusion.1.refs_8_.refs_11_.left_ref
  59.8 8.1 %project_qkv.1.qkv_ref = bf16[640,3072]{1,0:T(8,128)(2,1)} custom-call(bf16[512,768]{1,0:T(8,128)(2,1)S(1)} %copy-done.23, bf16[512,768]{1,0:T(8,128)(2,1)S(1)} %collective-permute-done.refs_1_, bf16[512,768]{1,0:T(8,128)(2,1)S(1)} %collective-permute-done.1.refs_2_, bf16[512,768]{1,0:T(8,128)(2,1)S(1)} %collective-permute-done.2.refs_3_, ...), custom_call_target="tpu_custom_call" | custom-call | flops 9999999827968 | bytes 1000000000 | tf_op jit(solution)/shard_map/project_qkv/pallas_call | solution.py:286
  69.7 9.0 %collective-permute-done.22.refs_1_ = bf16[256,512]{1,0:T(8,128)(2,1)} collective-permute-done((bf16[256,512]{1,0:T(8,128)(2,1)}, bf16[256,512]{1,0:T(8,128)(2,1)}, u32[]{:S(2)}, u32[]{:S(2)}) %collective-permute-start.22) | collective-permute-done | bytes 262176 | tf_op jit(solution)/shard_map/ppermute | solution.py:132
  83.2 2.3 pad_maximum_fusion.2.refs_12_
  86.2 3.4 collective-permute-done.23.refs_3_
  90.6 3.2 attend.2
  100.1 13.7 %attend.3 = (bf16[512,1024]{1,0:T(8,128)(2,1)}, bf16[16,512,512]{2,1,0:T(8,128)(2,1)}) custom-call(bf16[640,3072]{1,0:T(8,128)(2,1)} %project_qkv.1.qkv_ref, s32[512,1]{1,0:T(8,128)} %copy.43.column_ref, s32[1,512]{1,0:T(1,128)} %bitcast.167), custom_call_target="tpu_custom_call" | custom-call | flops 9999999827968 | bytes 1000000000 | tf_op jit(solution)/shard_map/attend/pallas_call | solution.py:61
  117.9 3.4 collective-permute-done.21.refs_2_
  121.3 4.6 collective-permute-done.19.refs_1_
  130.9 9.5 %first_norm.1 = (f32[640,1024]{1,0:T(8,128)}, f32[640,1]{1,0:T(8,128)S(1)}, bf16[640,1024]{1,0:T(8,128)(2,1)S(1)}) custom-call(bf16[256,512]{1,0:T(8,128)(2,1)} %refs_0_.12, bf16[256,512]{1,0:T(8,128)(2,1)} %collective-permute-done.22.refs_1_, bf16[256,512]{1,0:T(8,128)(2,1)} %collective-permute-done.20.refs_2_, ...), custom_call_target="tpu_custom_call" | custom-call | flops 9999999827968 | bytes 1000000000 | tf_op jit(solution)/shard_map/first_norm/pallas_call | solution.py:389
  145.4 3.6 collective-permute-done.40.refs_8_
  150.5 14.3 %project_hidden.1 = (bf16[640,4096]{1,0:T(8,128)(2,1)}, bf16[640,4096]{1,0:T(8,128)(2,1)}) custom-call(bf16[512,1024]{1,0:T(8,128)(2,1)} %refs_0_.11, bf16[512,1024]{1,0:T(8,128)(2,1)} %collective-permute-done.19.refs_1_, bf16[512,1024]{1,0:T(8,128)(2,1)} %collective-permute-done.21.refs_2_, bf16[256,1024]{1,0:T(8,128)(2,1)} %collective-permute-done.35.refs_3_, ...), custom_call_target="tpu_custom_call" | custom-call | flops 10000000 | bytes 1000 | tf_op jit(solution)/shard_map/project_hidden/pallas_call | solution.py:311
  164.9 4.3 collective-permute-done.33.refs_1_
  172.1 11.1 %collective-permute-done.42.refs_3_ = bf16[512,512]{1,0:T(8,128)(2,1)} collective-permute-done((bf16[512,512]{1,0:T(8,128)(2,1)S(1)}, bf16[512,512]{1,0:T(8,128)(2,1)}, u32[]{:S(2)}, u32[]{:S(2)}) %collective-permute-start.42) | collective-permute-done | bytes 524320 | tf_op jit(solution)/shard_map/ppermute | solution.py:132
  186.4 16.1 %second_norm.1 = (f32[640,512]{1,0:T(8,128)}, bf16[640,512]{1,0:T(8,128)(2,1)}, f32[640,1024]{1,0:T(8,128)}, bf16[640,1024]{1,0:T(8,128)(2,1)}, f32[3,1024]{1,0:T(4,128)S(1)}) custom-call(bf16[1024,512]{1,0:T(8,128)(2,1)S(1)} %copy-done.22, bf16[1024,512]{1,0:T(8,128)(2,1)S(1)} %collective-permute-done.33.refs_1_, ...), custom_call_target="tpu_custom_call" | custom-call | flops 9999999827968 | bytes 1000000000 | tf_op jit(solution)/shard_map/second_norm/pallas_call | solution.py:440
  203.8 10.4 %grad_down.2 = (bf16[4,1024,512]{2,1,0:T(8,128)(2,1)S(1)}, bf16[4,1024,512]{2,1,0:T(8,128)(2,1)}) custom-call(bf16[640,4096]{1,0:T(8,128)(2,1)} %get-tuple-element.179.refs_10_.left_ref, bf16[640,1024]{1,0:T(8,128)(2,1)S(1)} %copy-done.41), custom_call_target="tpu_custom_call" | custom-call | flops 9999999827968 | bytes 1000000000 | tf_op jit(solution)/shard_map/grad_down/pallas_call | solution.py:612
  214.2 2.1 copy-done.1
  217.4 10.2 %hidden_back.1 = (bf16[640,4096]{1,0:T(8,128)(2,1)}, f32[1,4096]{1,0:T(1,128)S(1)}) custom-call(bf16[1024,512]{1,0:T(8,128)(2,1)S(1)} %copy-done.22, bf16[1024,512]{1,0:T(8,128)(2,1)S(1)} %collective-permute-done.33.refs_1_, bf16[1024,512]{1,0:T(8,128)(2,1)S(1)} %collective-permute-done.34.refs_2_, bf16[512,512]{1,0:T(8,128)(2,1)} %collective-permute-done.42.refs_3_, ...), custom_call_target="tpu_custom_call" | custom-call | flops 9999999827968 | bytes 1000000000 | tf_op jit(solution)/shard_map/hidden_back/pallas_call | solution.py:536
  229.4 4.3 collective-permute-done.49
  233.8 2.8 fusion.20
  240.1 10.6 %grad_up.2 = (bf16[4,512,1024]{2,1,0:T(8,128)(2,1)S(1)}, bf16[4,512,1024]{2,1,0:T(8,128)(2,1)}) custom-call(bf16[640,1024]{1,0:T(8,128)(2,1)S(1)} %copy-done.10, bf16[640,4096]{1,0:T(8,128)(2,1)} %get-tuple-element.196.right_ref.refs_10_), custom_call_target="tpu_custom_call" | custom-call | flops 9999999827968 | bytes 1000000000 | tf_op jit(solution)/shard_map/grad_up/pallas_call | solution.py:587
  252.7 16.5 %first_back.1 = (f32[640,1024]{1,0:T(8,128)}, bf16[640,1024]{1,0:T(8,128)(2,1)}, f32[3,1024]{1,0:T(4,128)S(1)}) custom-call(bf16[512,1024]{1,0:T(8,128)(2,1)} %refs_0_.11, bf16[512,1024]{1,0:T(8,128)(2,1)} %collective-permute-done.19.refs_1_, bf16[512,1024]{1,0:T(8,128)(2,1)} %collective-permute-done.21.refs_2_, ...), custom_call_target="tpu_custom_call" | custom-call | flops 10000000 | bytes 1000 | tf_op jit(solution)/shard_map/first_back/pallas_call | solution.py:480
  270.5 3.4 heads_back.1.grad_ref
  280.5 3.4 fusion.10
  286.5 3.6 attend_back.2
  293.1 3.1 fusion.24
  298.3 14.9 %attend_back.3 = bf16[512,3072]{1,0:T(8,128)(2,1)} custom-call(bf16[640,3072]{1,0:T(8,128)(2,1)} %project_qkv.1.qkv_ref, bf16[16,512,512]{2,1,0:T(8,128)(2,1)} %get-tuple-element.210.probs_ref, bf16[640,1024]{1,0:T(8,128)(2,1)} %copy-done.8), custom_call_target="tpu_custom_call" | custom-call | flops 9999999827968 | bytes 1000000000 | tf_op jit(solution)/shard_map/attend_back/pallas_call | solution.py:107
  314.7 3.9 broadcast_select_fusion.9
  323.1 2.2 pad_maximum_fusion.right_ref.refs_8_
  325.3 8.9 %grad_up.3 = (bf16[4,512,768]{2,1,0:T(8,128)(2,1)S(1)}, bf16[4,512,768]{2,1,0:T(8,128)(2,1)}) custom-call(bf16[640,1024]{1,0:T(8,128)(2,1)S(1)} %copy-done.13, bf16[640,3072]{1,0:T(8,128)(2,1)} %pad_maximum_fusion.right_ref.refs_8_), custom_call_target="tpu_custom_call" | custom-call | flops 9999999827968 | bytes 1000000000 | tf_op jit(solution)/shard_map/grad_up/pallas_call | solution.py:587
  337.3 2.6 collective-permute-start.68
  339.9 3.4 fusion.4
  346.0 3.8 grad_down.3
  349.9 2.5 collective-permute-done.68
  354.2 3.2 collective-permute-done.67
  358.6 3.9 broadcast_select_fusion.6
  368.4 11.1 %input_back.1 = (f32[640,512]{1,0:T(8,128)}, bf16[640,512]{1,0:T(8,128)(2,1)S(1)}, f32[1,3072]{1,0:T(1,128)S(1)}) custom-call(bf16[512,768]{1,0:T(8,128)(2,1)S(1)} %copy-done.24, bf16[512,768]{1,0:T(8,128)(2,1)S(1)} %copy-done.26, bf16[512,768]{1,0:T(8,128)(2,1)S(1)} %copy-done.28, bf16[512,768]{1,0:T(8,128)(2,1)S(1)} %copy-done.32, ...), custom_call_target="tpu_custom_call" | custom-call | flops 9999999827968 | bytes 1000000000 | tf_op jit(solution)/shard_map/input_back/pallas_call | solution.py:506
  392.9 10.0 %collective-permute-done.79 = bf16[128,1024]{1,0:T(8,128)(2,1)S(1)} collective-permute-done((bf16[128,1024]{1,0:T(8,128)(2,1)}, bf16[128,1024]{1,0:T(8,128)(2,1)S(1)}, u32[]{:S(2)}, u32[]{:S(2)}) %collective-permute-start.79) | collective-permute-done | bytes 262176 | tf_op jit(solution)/shard_map/ppermute | solution.py:650
  408.0 6.0 %collective-permute-done.76 = bf16[256,768]{1,0:T(8,128)(2,1)S(1)} collective-permute-done((bf16[256,768]{1,0:T(8,128)(2,1)S(1)}, bf16[256,768]{1,0:T(8,128)(2,1)S(1)}, u32[]{:S(2)}, u32[]{:S(2)}) %collective-permute-start.76) | collective-permute-done | bytes 393248 | tf_op jit(solution)/shard_map/ppermute | solution.py:128
  423.4 6.2 %collective-permute-done.83 = bf16[256,768]{1,0:T(8,128)(2,1)S(1)} collective-permute-done((bf16[256,768]{1,0:T(8,128)(2,1)S(1)}, bf16[256,768]{1,0:T(8,128)(2,1)S(1)}, u32[]{:S(2)}, u32[]{:S(2)}) %collective-permute-start.83) | collective-permute-done | bytes 393248 | tf_op jit(solution)/shard_map/ppermute | solution.py:650
  432.5 2.7 collective-permute-start.86
  444.1 2.7 collective-permute-start.89
  447.2 4.4 collective-permute-done.89
  454.0 2.9 collective-permute-done.90
  459.2 2.8 collective-permute-done.97
  (490 shorter events, 165.1 us)
Async XLA Ops:
  0.7 27.9 %collective-permute-start = (bf16[512,768]{1,0:T(8,128)(2,1)}, bf16[512,768]{1,0:T(8,128)(2,1)S(1)}, u32[]{:S(2)}, u32[]{:S(2)}) collective-permute-start(bf16[512,768]{1,0:T(8,128)(2,1)} %refs_0_.13), channel_id=1, source_target_pairs={{0,1},{1,0},{2,3},{3,2},{4,5},{5,4},{6,7},{7,6},{8,9},{9,8},{10,11... | collective-permute-start | bytes 2359304 | tf_op jit(solution)/shard_map/ppermute | solution.py:132
  3.7 24.9 %collective-permute-start.1 = (bf16[512,768]{1,0:T(8,128)(2,1)}, bf16[512,768]{1,0:T(8,128)(2,1)S(1)}, u32[]{:S(2)}, u32[]{:S(2)}) collective-permute-start(bf16[512,768]{1,0:T(8,128)(2,1)} %refs_0_.13), channel_id=1, source_target_pairs={{0,4},{2,6},{4,0},{6,2},{1,5},{3,7},{5,1},{7,3},{8,12},{10,14},{12... | collective-permute-start | bytes 2359304 | tf_op jit(solution)/shard_map/ppermute | solution.py:128
  27.6 28.1 %collective-permute-start.3 = (bf16[512,768]{1,0:T(8,128)(2,1)}, bf16[512,768]{1,0:T(8,128)(2,1)S(1)}, u32[]{:S(2)}, u32[]{:S(2)}) collective-permute-start(bf16[512,768]{1,0:T(8,128)(2,1)} %refs_0_.13), channel_id=1, source_target_pairs={{0,2},{2,0},{4,6},{6,4},{1,3},{3,1},{5,7},{7,5},{8,10},{10,8},{12,... | collective-permute-start | bytes 2359304 | tf_op jit(solution)/shard_map/ppermute | solution.py:124
  32.5 17.0 %collective-permute-start.7 = (bf16[640,512]{1,0:T(8,128)(2,1)}, bf16[640,512]{1,0:T(8,128)(2,1)}, u32[]{:S(2)}, u32[]{:S(2)}) collective-permute-start(bf16[640,512]{1,0:T(8,128)(2,1)} %get-tuple-element.347), channel_id=1, source_target_pairs={{0,1},{1,0},{2,3},{3,2},{4,5},{5,4},{6,7},{7,6},{8,9},{9,8},{10,11... | collective-permute-start | bytes 1966088 | tf_op jit(solution)/shard_map/ppermute | solution.py:132
  34.2 19.2 %collective-permute-start.2 = (bf16[512,768]{1,0:T(8,128)(2,1)S(1)}, bf16[512,768]{1,0:T(8,128)(2,1)S(1)}, u32[]{:S(2)}, u32[]{:S(2)}) collective-permute-start(bf16[512,768]{1,0:T(8,128)(2,1)S(1)} %collective-permute-done.refs_1_), channel_id=1, source_target_pairs={{0,4},{2,6},{4,0},{6,2},{1,5},{3,7},{5,1},{7,3},{8,12},{10,14},{12... | collective-permute-start | bytes 2359304 | tf_op jit(solution)/shard_map/ppermute | solution.py:128
  37.2 20.1 %collective-permute-start.4 = (bf16[512,768]{1,0:T(8,128)(2,1)S(1)}, bf16[512,768]{1,0:T(8,128)(2,1)S(1)}, u32[]{:S(2)}, u32[]{:S(2)}) collective-permute-start(bf16[512,768]{1,0:T(8,128)(2,1)S(1)} %collective-permute-done.refs_1_), channel_id=1, source_target_pairs={{0,2},{2,0},{4,6},{6,4},{1,3},{3,1},{5,7},{7,5},{8,10},{10,8},{12,... | collective-permute-start | bytes 2359304 | tf_op jit(solution)/shard_map/ppermute | solution.py:124
  37.2 21.6 %collective-permute-start.5 = (bf16[512,768]{1,0:T(8,128)(2,1)S(1)}, bf16[512,768]{1,0:T(8,128)(2,1)S(1)}, u32[]{:S(2)}, u32[]{:S(2)}) collective-permute-start(bf16[512,768]{1,0:T(8,128)(2,1)S(1)} %collective-permute-done.1.refs_2_), channel_id=1, source_target_pairs={{0,2},{2,0},{4,6},{6,4},{1,3},{3,1},{5,7},{7,5},{8,10},{10,8},{12,... | collective-permute-start | bytes 2359304 | tf_op jit(solution)/shard_map/ppermute | solution.py:124
  55.2 27.0 %collective-permute-start.18 = (bf16[640,512]{1,0:T(8,128)(2,1)}, bf16[640,512]{1,0:T(8,128)(2,1)}, u32[]{:S(2)}, u32[]{:S(2)}) collective-permute-start(bf16[640,512]{1,0:T(8,128)(2,1)} %get-tuple-element.341), channel_id=1, source_target_pairs={{0,1},{1,0},{2,3},{3,2},{4,5},{5,4},{6,7},{7,6},{8,9},{9,8},{10,11... | collective-permute-start | bytes 1966088 | tf_op jit(solution)/shard_map/ppermute | solution.py:132
  55.7 23.0 %collective-permute-start.22 = (bf16[256,512]{1,0:T(8,128)(2,1)}, bf16[256,512]{1,0:T(8,128)(2,1)}, u32[]{:S(2)}, u32[]{:S(2)}) collective-permute-start(bf16[256,512]{1,0:T(8,128)(2,1)} %refs_0_.12), channel_id=1, source_target_pairs={{0,1},{1,0},{2,3},{3,2},{4,5},{5,4},{6,7},{7,6},{8,9},{9,8},{10,11... | collective-permute-start | bytes 786440 | tf_op jit(solution)/shard_map/ppermute | solution.py:132
  57.3 22.4 %collective-permute-start.20 = (bf16[256,512]{1,0:T(8,128)(2,1)}, bf16[256,512]{1,0:T(8,128)(2,1)}, u32[]{:S(2)}, u32[]{:S(2)}) collective-permute-start(bf16[256,512]{1,0:T(8,128)(2,1)} %refs_0_.12), channel_id=1, source_target_pairs={{0,4},{2,6},{4,0},{6,2},{1,5},{3,7},{5,1},{7,3},{8,12},{10,14},{12... | collective-permute-start | bytes 786440 | tf_op jit(solution)/shard_map/ppermute | solution.py:128
  69.1 20.4 %collective-permute-start.15 = (bf16[128,768]{1,0:T(8,128)(2,1)S(1)}, bf16[128,768]{1,0:T(8,128)(2,1)S(1)}, u32[]{:S(2)}, u32[]{:S(2)}) collective-permute-start(bf16[128,768]{1,0:T(8,128)(2,1)S(1)} %get-tuple-element.369), channel_id=1, source_target_pairs={{0,1},{1,0},{2,3},{3,2},{4,5},{5,4},{6,7},{7,6},{8,9},{9,8},{10,11... | collective-permute-start | bytes 589832 | tf_op jit(solution)/shard_map/ppermute | solution.py:175
  69.7 20.3 %collective-permute-start.16 = (bf16[128,768]{1,0:T(8,128)(2,1)S(1)}, bf16[128,768]{1,0:T(8,128)(2,1)S(1)}, u32[]{:S(2)}, u32[]{:S(2)}) collective-permute-start(bf16[128,768]{1,0:T(8,128)(2,1)S(1)} %get-tuple-element.368), channel_id=1, source_target_pairs={{0,2},{1,3},{2,0},{3,1},{4,6},{5,7},{6,4},{7,5},{8,10},{9,11},{10,... | collective-permute-start | bytes 589832 | tf_op jit(solution)/shard_map/ppermute | solution.py:175
  95.9 25.4 %collective-permute-start.21 = (bf16[512,1024]{1,0:T(8,128)(2,1)}, bf16[512,1024]{1,0:T(8,128)(2,1)}, u32[]{:S(2)}, u32[]{:S(2)}) collective-permute-start(bf16[512,1024]{1,0:T(8,128)(2,1)} %refs_0_.11), channel_id=1, source_target_pairs={{0,4},{2,6},{4,0},{6,2},{1,5},{3,7},{5,1},{7,3},{8,12},{10,14},{12... | collective-permute-start | bytes 3145736 | tf_op jit(solution)/shard_map/ppermute | solution.py:128
  97.4 16.4 %collective-permute-start.30 = (bf16[128,256]{1,0:T(8,128)(2,1)}, bf16[128,256]{1,0:T(8,128)(2,1)}, u32[]{:S(2)}, u32[]{:S(2)}) collective-permute-start(bf16[128,256]{1,0:T(8,128)(2,1)} %get-tuple-element.384), channel_id=1, source_target_pairs={{0,1},{1,0},{2,3},{3,2},{4,5},{5,4},{6,7},{7,6},{8,9},{9,8},{10,11... | collective-permute-start | bytes 196616 | tf_op jit(solution)/shard_map/ppermute | solution.py:181
  98.0 15.9 %collective-permute-start.31 = (bf16[128,256]{1,0:T(8,128)(2,1)}, bf16[128,256]{1,0:T(8,128)(2,1)}, u32[]{:S(2)}, u32[]{:S(2)}) collective-permute-start(bf16[128,256]{1,0:T(8,128)(2,1)} %get-tuple-element.383), channel_id=1, source_target_pairs={{0,2},{1,3},{2,0},{3,1},{4,6},{5,7},{6,4},{7,5},{8,10},{9,11},{10,... | collective-permute-start | bytes 196616 | tf_op jit(solution)/shard_map/ppermute | solution.py:181
  98.0 15.9 %collective-permute-start.32 = (bf16[128,256]{1,0:T(8,128)(2,1)}, bf16[128,256]{1,0:T(8,128)(2,1)}, u32[]{:S(2)}, u32[]{:S(2)}) collective-permute-start(bf16[128,256]{1,0:T(8,128)(2,1)} %get-tuple-element.382), channel_id=1, source_target_pairs={{0,3},{1,2},{2,1},{3,0},{4,7},{5,6},{6,5},{7,4},{8,11},{9,10},{10,... | collective-permute-start | bytes 196616 | tf_op jit(solution)/shard_map/ppermute | solution.py:181
  99.6 26.3 %collective-permute-start.19 = (bf16[512,1024]{1,0:T(8,128)(2,1)}, bf16[512,1024]{1,0:T(8,128)(2,1)}, u32[]{:S(2)}, u32[]{:S(2)}) collective-permute-start(bf16[512,1024]{1,0:T(8,128)(2,1)} %refs_0_.11), channel_id=1, source_target_pairs={{0,1},{1,0},{2,3},{3,2},{4,5},{5,4},{6,7},{7,6},{8,9},{9,8},{10,11... | collective-permute-start | bytes 3145736 | tf_op jit(solution)/shard_map/ppermute | solution.py:132
  113.8 29.8 %collective-permute-start.37 = (bf16[512,1024]{1,0:T(8,128)(2,1)}, bf16[512,1024]{1,0:T(8,128)(2,1)}, u32[]{:S(2)}, u32[]{:S(2)}) collective-permute-start(bf16[512,1024]{1,0:T(8,128)(2,1)} %refs_0_.11), channel_id=1, source_target_pairs={{0,2},{2,0},{4,6},{6,4},{1,3},{3,1},{5,7},{7,5},{8,10},{10,8},{12,... | collective-permute-start | bytes 3145736 | tf_op jit(solution)/shard_map/ppermute | solution.py:124
  143.6 25.6 %collective-permute-start.33 = (bf16[1024,512]{1,0:T(8,128)(2,1)S(1)}, bf16[1024,512]{1,0:T(8,128)(2,1)S(1)}, u32[]{:S(2)}, u32[]{:S(2)}) collective-permute-start(bf16[1024,512]{1,0:T(8,128)(2,1)S(1)} %copy-done.22), channel_id=1, source_target_pairs={{0,1},{1,0},{2,3},{3,2},{4,5},{5,4},{6,7},{7,6},{8,9},{9,8},{10,11... | collective-permute-start | bytes 3145736 | tf_op jit(solution)/shard_map/ppermute | solution.py:132
  144.6 25.2 %collective-permute-start.34 = (bf16[1024,512]{1,0:T(8,128)(2,1)S(1)}, bf16[1024,512]{1,0:T(8,128)(2,1)S(1)}, u32[]{:S(2)}, u32[]{:S(2)}) collective-permute-start(bf16[1024,512]{1,0:T(8,128)(2,1)S(1)} %copy-done.22), channel_id=1, source_target_pairs={{0,4},{2,6},{4,0},{6,2},{1,5},{3,7},{5,1},{7,3},{8,12},{10,14},{12... | collective-permute-start | bytes 3145736 | tf_op jit(solution)/shard_map/ppermute | solution.py:128
  149.0 35.2 %collective-permute-start.44 = (bf16[1024,512]{1,0:T(8,128)(2,1)S(1)}, bf16[1024,512]{1,0:T(8,128)(2,1)}, u32[]{:S(2)}, u32[]{:S(2)}) collective-permute-start(bf16[1024,512]{1,0:T(8,128)(2,1)S(1)} %copy-done.22), channel_id=1, source_target_pairs={{0,2},{2,0},{4,6},{6,4},{1,3},{3,1},{5,7},{7,5},{8,10},{10,8},{12,... | collective-permute-start | bytes 3145736 | tf_op jit(solution)/shard_map/ppermute | solution.py:124
  216.3 17.5 %collective-permute-start.50 = (bf16[4,1024,512]{2,1,0:T(8,128)(2,1)}, bf16[4,1024,512]{2,1,0:T(8,128)(2,1)}, u32[]{:S(2)}, u32[]{:S(2)}) collective-permute-start(bf16[4,1024,512]{2,1,0:T(8,128)(2,1)} %get-tuple-element.185), channel_id=1, source_target_pairs={{0,2},{2,0},{4,6},{6,4},{1,3},{3,1},{5,7},{7,5},{8,10},{10,8},{12,... | collective-permute-start | bytes 12582920 | tf_op jit(solution)/shard_map/ppermute | solution.py:124
  216.4 17.3 %collective-permute-start.49 = (bf16[640,512]{1,0:T(8,128)(2,1)}, bf16[640,512]{1,0:T(8,128)(2,1)}, u32[]{:S(2)}, u32[]{:S(2)}) collective-permute-start(bf16[640,512]{1,0:T(8,128)(2,1)} %get-tuple-element.183), channel_id=1, source_target_pairs={{0,1},{1,0},{2,3},{3,2},{4,5},{5,4},{6,7},{7,6},{8,9},{9,8},{10,11... | collective-permute-start | bytes 1966088 | tf_op jit(solution)/shard_map/ppermute | solution.py:132
  238.7 41.8 %collective-permute-start.55 = (bf16[1024,512]{1,0:T(8,128)(2,1)}, bf16[1024,512]{1,0:T(8,128)(2,1)}, u32[]{:S(2)}, u32[]{:S(2)}) collective-permute-start(bf16[1024,512]{1,0:T(8,128)(2,1)} %pad_maximum_fusion.5), channel_id=1, source_target_pairs={{0,4},{2,6},{4,0},{6,2},{1,5},{3,7},{5,1},{7,3},{8,12},{10,14},{12... | collective-permute-start | bytes 3145736 | tf_op jit(solution)/shard_map/ppermute | solution.py:128
  239.1 41.4 %collective-permute-start.56 = (bf16[1024,512]{1,0:T(8,128)(2,1)}, bf16[1024,512]{1,0:T(8,128)(2,1)}, u32[]{:S(2)}, u32[]{:S(2)}) collective-permute-start(bf16[1024,512]{1,0:T(8,128)(2,1)} %pad_maximum_fusion.4), channel_id=1, source_target_pairs={{0,1},{1,0},{2,3},{3,2},{4,5},{5,4},{6,7},{7,6},{8,9},{9,8},{10,11... | collective-permute-start | bytes 3145736 | tf_op jit(solution)/shard_map/ppermute | solution.py:132
  283.9 29.3 %collective-permute-start.60 = (bf16[512,512]{1,0:T(8,128)(2,1)}, bf16[512,512]{1,0:T(8,128)(2,1)}, u32[]{:S(2)}, u32[]{:S(2)}) collective-permute-start(bf16[512,512]{1,0:T(8,128)(2,1)} %get-tuple-element.205), channel_id=1, source_target_pairs={{0,4},{2,6},{4,0},{6,2},{1,5},{3,7},{5,1},{7,3},{8,12},{10,14},{12... | collective-permute-start | bytes 1572872 | tf_op jit(solution)/shard_map/ppermute | solution.py:128
  285.3 28.3 %collective-permute-start.59 = (bf16[512,512]{1,0:T(8,128)(2,1)}, bf16[512,512]{1,0:T(8,128)(2,1)}, u32[]{:S(2)}, u32[]{:S(2)}) collective-permute-start(bf16[512,512]{1,0:T(8,128)(2,1)} %get-tuple-element.204), channel_id=1, source_target_pairs={{0,1},{1,0},{2,3},{3,2},{4,5},{5,4},{6,7},{7,6},{8,9},{9,8},{10,11... | collective-permute-start | bytes 1572872 | tf_op jit(solution)/shard_map/ppermute | solution.py:132
  290.9 27.6 %collective-permute-start.62 = (bf16[128,768]{1,0:T(8,128)(2,1)}, bf16[128,768]{1,0:T(8,128)(2,1)}, u32[]{:S(2)}, u32[]{:S(2)}) collective-permute-start(bf16[128,768]{1,0:T(8,128)(2,1)} %get-tuple-element.364), channel_id=1, source_target_pairs={{0,1},{1,0},{2,3},{3,2},{4,5},{5,4},{6,7},{7,6},{8,9},{9,8},{10,11... | collective-permute-start | bytes 589832 | tf_op jit(solution)/shard_map/ppermute | solution.py:181
  291.8 28.3 %collective-permute-start.63 = (bf16[128,768]{1,0:T(8,128)(2,1)}, bf16[128,768]{1,0:T(8,128)(2,1)}, u32[]{:S(2)}, u32[]{:S(2)}) collective-permute-start(bf16[128,768]{1,0:T(8,128)(2,1)} %get-tuple-element.363), channel_id=1, source_target_pairs={{0,2},{1,3},{2,0},{3,1},{4,6},{5,7},{6,4},{7,5},{8,10},{9,11},{10,... | collective-permute-start | bytes 589832 | tf_op jit(solution)/shard_map/ppermute | solution.py:181
  291.8 28.3 %collective-permute-start.64 = (bf16[128,768]{1,0:T(8,128)(2,1)}, bf16[128,768]{1,0:T(8,128)(2,1)}, u32[]{:S(2)}, u32[]{:S(2)}) collective-permute-start(bf16[128,768]{1,0:T(8,128)(2,1)} %get-tuple-element.362), channel_id=1, source_target_pairs={{0,3},{1,2},{2,1},{3,0},{4,7},{5,6},{6,5},{7,4},{8,11},{9,10},{10,... | collective-permute-start | bytes 589832 | tf_op jit(solution)/shard_map/ppermute | solution.py:181
  313.1 26.8 %collective-permute-start.57 = (bf16[512,1024]{1,0:T(8,128)(2,1)}, bf16[512,1024]{1,0:T(8,128)(2,1)}, u32[]{:S(2)}, u32[]{:S(2)}) collective-permute-start(bf16[512,1024]{1,0:T(8,128)(2,1)} %pad_maximum_fusion.7), channel_id=1, source_target_pairs={{0,4},{2,6},{4,0},{6,2},{1,5},{3,7},{5,1},{7,3},{8,12},{10,14},{12... | collective-permute-start | bytes 3145736 | tf_op jit(solution)/shard_map/ppermute | solution.py:128
  313.6 26.3 %collective-permute-start.58 = (bf16[512,1024]{1,0:T(8,128)(2,1)}, bf16[512,1024]{1,0:T(8,128)(2,1)}, u32[]{:S(2)}, u32[]{:S(2)}) collective-permute-start(bf16[512,1024]{1,0:T(8,128)(2,1)} %pad_maximum_fusion.6), channel_id=1, source_target_pairs={{0,1},{1,0},{2,3},{3,2},{4,5},{5,4},{6,7},{7,6},{8,9},{9,8},{10,11... | collective-permute-start | bytes 3145736 | tf_op jit(solution)/shard_map/ppermute | solution.py:132
  318.5 15.6 %collective-permute-start.61 = (bf16[512,512]{1,0:T(8,128)(2,1)}, bf16[512,512]{1,0:T(8,128)(2,1)}, u32[]{:S(2)}, u32[]{:S(2)}) collective-permute-start(bf16[512,512]{1,0:T(8,128)(2,1)} %get-tuple-element.214), channel_id=1, source_target_pairs={{0,8},{8,0},{16,24},{24,16},{1,9},{9,1},{17,25},{25,17},{2,10},{10... | collective-permute-start | bytes 1572872 | tf_op jit(solution)/shard_map/ppermute | solution.py:650
  334.1 28.8 %collective-permute-start.66 = (bf16[4,512,768]{2,1,0:T(8,128)(2,1)}, bf16[4,512,768]{2,1,0:T(8,128)(2,1)}, u32[]{:S(2)}, u32[]{:S(2)}) collective-permute-start(bf16[4,512,768]{2,1,0:T(8,128)(2,1)} %get-tuple-element.219), channel_id=1, source_target_pairs={{0,2},{2,0},{4,6},{6,4},{1,3},{3,1},{5,7},{7,5},{8,10},{10,8},{12,... | collective-permute-start | bytes 9437192 | tf_op jit(solution)/shard_map/ppermute | solution.py:124
  349.9 40.8 %collective-permute-start.65 = (bf16[4,256,512]{2,1,0:T(8,128)(2,1)}, bf16[4,256,512]{2,1,0:T(8,128)(2,1)}, u32[]{:S(2)}, u32[]{:S(2)}) collective-permute-start(bf16[4,256,512]{2,1,0:T(8,128)(2,1)} %get-tuple-element.228), channel_id=1, source_target_pairs={{0,2},{2,0},{4,6},{6,4},{1,3},{3,1},{5,7},{7,5},{8,10},{10,8},{12,... | collective-permute-start | bytes 3145736 | tf_op jit(solution)/shard_map/ppermute | solution.py:124
  354.2 25.4 %collective-permute-start.73 = (bf16[256,512]{1,0:T(8,128)(2,1)}, bf16[256,512]{1,0:T(8,128)(2,1)}, u32[]{:S(2)}, u32[]{:S(2)}) collective-permute-start(bf16[256,512]{1,0:T(8,128)(2,1)} %add_convert_fusion.16), channel_id=1, source_target_pairs={{0,16},{8,24},{16,0},{24,8},{1,17},{9,25},{17,1},{25,9},{2,18},{10... | collective-permute-start | bytes 786440 | tf_op jit(solution)/shard_map/ppermute | solution.py:650
  362.5 20.9 %collective-permute-start.72 = (bf16[256,1024]{1,0:T(8,128)(2,1)}, bf16[256,1024]{1,0:T(8,128)(2,1)}, u32[]{:S(2)}, u32[]{:S(2)}) collective-permute-start(bf16[256,1024]{1,0:T(8,128)(2,1)} %get-tuple-element.237), channel_id=1, source_target_pairs={{0,8},{8,0},{16,24},{24,16},{1,9},{9,1},{17,25},{25,17},{2,10},{10... | collective-permute-start | bytes 1572872 | tf_op jit(solution)/shard_map/ppermute | solution.py:650
  366.7 21.0 %collective-permute-start.70 = (bf16[512,768]{1,0:T(8,128)(2,1)}, bf16[512,768]{1,0:T(8,128)(2,1)}, u32[]{:S(2)}, u32[]{:S(2)}) collective-permute-start(bf16[512,768]{1,0:T(8,128)(2,1)} %pad_maximum_fusion.12), channel_id=1, source_target_pairs={{0,4},{2,6},{4,0},{6,2},{1,5},{3,7},{5,1},{7,3},{8,12},{10,14},{12... | collective-permute-start | bytes 2359304 | tf_op jit(solution)/shard_map/ppermute | solution.py:128
  367.2 20.5 %collective-permute-start.71 = (bf16[512,768]{1,0:T(8,128)(2,1)}, bf16[512,768]{1,0:T(8,128)(2,1)}, u32[]{:S(2)}, u32[]{:S(2)}) collective-permute-start(bf16[512,768]{1,0:T(8,128)(2,1)} %pad_maximum_fusion.11), channel_id=1, source_target_pairs={{0,1},{1,0},{2,3},{3,2},{4,5},{5,4},{6,7},{7,6},{8,9},{9,8},{10,11... | collective-permute-start | bytes 2359304 | tf_op jit(solution)/shard_map/ppermute | solution.py:132
  381.7 21.3 %collective-permute-start.78 = (bf16[512,512]{1,0:T(8,128)(2,1)}, bf16[512,512]{1,0:T(8,128)(2,1)}, u32[]{:S(2)}, u32[]{:S(2)}) collective-permute-start(bf16[512,512]{1,0:T(8,128)(2,1)} %pad_maximum_fusion.17), channel_id=1, source_target_pairs={{0,8},{8,0},{16,24},{24,16},{1,9},{9,1},{17,25},{25,17},{2,10},{10... | collective-permute-start | bytes 1572872 | tf_op jit(solution)/shard_map/ppermute | solution.py:650
  387.1 15.8 %collective-permute-start.79 = (bf16[128,1024]{1,0:T(8,128)(2,1)}, bf16[128,1024]{1,0:T(8,128)(2,1)S(1)}, u32[]{:S(2)}, u32[]{:S(2)}) collective-permute-start(bf16[128,1024]{1,0:T(8,128)(2,1)} %broadcast_select_fusion.15), channel_id=1, source_target_pairs={{0,16},{8,24},{16,0},{24,8},{1,17},{9,25},{17,1},{25,9},{2,18},{10... | collective-permute-start | bytes 786440 | tf_op jit(solution)/shard_map/ppermute | solution.py:650
  389.4 26.0 %collective-permute-start.80 = (bf16[256,768]{1,0:T(8,128)(2,1)S(1)}, bf16[256,768]{1,0:T(8,128)(2,1)S(1)}, u32[]{:S(2)}, u32[]{:S(2)}) collective-permute-start(bf16[256,768]{1,0:T(8,128)(2,1)S(1)} %get-tuple-element.251), channel_id=1, source_target_pairs={{0,1},{1,0},{2,3},{3,2},{4,5},{5,4},{6,7},{7,6},{8,9},{9,8},{10,11... | collective-permute-start | bytes 1179656 | tf_op jit(solution)/shard_map/ppermute | solution.py:132
  390.6 16.8 %collective-permute-start.77 = (f32[12288]{0:T(1024)S(1)}, f32[12288]{0:T(1024)S(1)}, u32[]{:S(2)}, u32[]{:S(2)}) collective-permute-start(f32[12288]{0:T(1024)S(1)} %pad_maximum_fusion.24), channel_id=1, source_target_pairs={{0,2},{2,0},{4,6},{6,4},{1,3},{3,1},{5,7},{7,5},{8,10},{10,8},{12,... | collective-permute-start | bytes 147464 | tf_op jit(solution)/shard_map/ppermute | solution.py:124
  391.9 26.2 %collective-permute-start.75 = (bf16[256,512]{1,0:T(8,128)(2,1)S(1)}, bf16[256,512]{1,0:T(8,128)(2,1)S(1)}, u32[]{:S(2)}, u32[]{:S(2)}) collective-permute-start(bf16[256,512]{1,0:T(8,128)(2,1)S(1)} %pad_maximum_fusion.21), channel_id=1, source_target_pairs={{0,1},{1,0},{2,3},{3,2},{4,5},{5,4},{6,7},{7,6},{8,9},{9,8},{10,11... | collective-permute-start | bytes 786440 | tf_op jit(solution)/shard_map/ppermute | solution.py:132
  403.0 17.1 %collective-permute-start.85 = (bf16[128,1024]{1,0:T(8,128)(2,1)S(1)}, bf16[128,1024]{1,0:T(8,128)(2,1)S(1)}, u32[]{:S(2)}, u32[]{:S(2)}) collective-permute-start(bf16[128,1024]{1,0:T(8,128)(2,1)S(1)} %add_convert_fusion.15), channel_id=1, source_target_pairs={{0,16},{8,24},{16,0},{24,8},{1,17},{9,25},{17,1},{25,9},{2,18},{10... | collective-permute-start | bytes 786440 | tf_op jit(solution)/shard_map/ppermute | solution.py:650
  420.2 22.0 %collective-permute-start.87 = (bf16[256,1024]{1,0:T(8,128)(2,1)S(1)}, bf16[256,1024]{1,0:T(8,128)(2,1)S(1)}, u32[]{:S(2)}, u32[]{:S(2)}) collective-permute-start(bf16[256,1024]{1,0:T(8,128)(2,1)S(1)} %pad_maximum_fusion.18), channel_id=1, source_target_pairs={{0,8},{8,0},{16,24},{24,16},{1,9},{9,1},{17,25},{25,17},{2,10},{10... | collective-permute-start | bytes 1572872 | tf_op jit(solution)/shard_map/ppermute | solution.py:650
  440.2 22.7 %collective-permute-start.92 = (bf16[640,512]{1,0:T(8,128)(2,1)S(1)}, bf16[640,512]{1,0:T(8,128)(2,1)S(1)}, u32[]{:S(2)}, u32[]{:S(2)}) collective-permute-start(bf16[640,512]{1,0:T(8,128)(2,1)S(1)} %copy-done.38), channel_id=1, source_target_pairs={{0,1},{1,0},{2,3},{3,2},{4,5},{5,4},{6,7},{7,6},{8,9},{9,8},{10,11... | collective-permute-start | bytes 1966088 | tf_op jit(solution)/shard_map/ppermute | solution.py:132
  441.8 16.5 %collective-permute-start.93 = (bf16[128,768]{1,0:T(8,128)(2,1)S(1)}, bf16[128,768]{1,0:T(8,128)(2,1)S(1)}, u32[]{:S(2)}, u32[]{:S(2)}) collective-permute-start(bf16[128,768]{1,0:T(8,128)(2,1)S(1)} %add_convert_fusion.17), channel_id=1, source_target_pairs={{0,16},{8,24},{16,0},{24,8},{1,17},{9,25},{17,1},{25,9},{2,18},{10... | collective-permute-start | bytes 589832 | tf_op jit(solution)/shard_map/ppermute | solution.py:650
  (130 other events, 1077.7 us)
